TPU v7x, 256 devices: a whole 4x4x8 slice. The times are simulated.
256 devices in a mesh: shard: 64 (over z, y, core), tp: 4 (over x).
Axes of the slice: x: 4, y: 4, z: 8, core: 2. Of those that a mesh axis runs over, the one named last changes fastest.
Arguments:
- person_embedding: bfloat16 [128, 256], P('shard'), may hold values from -6 to 6
- catalog_embedding: bfloat16 [524288, 256], P(('shard', 'tp')), may hold values from -1.7 to 1.7
- catalog_attributes: bfloat16 [524288, 768], P(('shard', 'tp')), may hold values from -6 to 6
- kept_part_entries: int32 [128, 256, 8], P(None, ('shard', 'tp')), may hold values from 0 to 2047
- valid_slot_number: int32 [128, 256], P(None, ('shard', 'tp')), may hold values from 1 to 8, 1024 in all within a row
- pair_attributes: bfloat16 [128, 1024, 2048], P('shard', None, 'tp'), may hold values from -6 to 6
- lowrank_v_matrix: bfloat16 [2, 3072, 512], P(None, 'tp'), may hold values from -0.109375 to 0.109375
- lowrank_u_matrix: bfloat16 [2, 512, 3072], P(None, None, 'tp'), may hold values from -0.25 to 0.25
- interaction_offset: float32 [2, 3072], P(None, 'tp'), may hold values from -3 to 3
- final_projection: bfloat16 [3072], P('tp'), may hold values from -0.109375 to 0.109375
- similarity_coefficient: float32 [1], replicated, may hold values from 0.5 to 1.5
Outputs:
- ranked_scores: float32 [128, 1024], P('shard')
Inputs may be any that keep to these rules, and one draw needn't show every extreme that they name: Only the first valid_slot_number[u, b] slots of kept_part_entries[u, b] are read; each is a row of shard b. `valid_slot_number`: each user has exactly 1024 survivors over all shards, and for each user some shard gives 8.
All inputs are finite; a program needn't handle non-finite values.
Results may differ from a plain program's by a relative error of at most 0.017.
Values may be sent and summed in bfloat16 or wider, within the bound.
No kernel may reach another device: no remote copies, remote signals or barrier semaphores. Data moves between devices by JAX's collectives and lax.ppermute only.
A program may use at most 64 MiB of HBM per device.

v0:
```python
import jax
import jax.numpy as jnp
from jax import lax
from jax.sharding import PartitionSpec as P


def on_device(
    person_embedding,
    catalog_embedding,
    catalog_attributes,
    kept_part_entries,
    valid_slot_number,
    pair_attributes,
    lowrank_v_matrix,
    lowrank_u_matrix,
    interaction_offset,
    final_projection,
    similarity_coefficient,
):
    part_number = lax.axis_size("shard")
    model_split_number = lax.axis_size("tp")
    users_all = lax.all_gather(person_embedding, "shard", axis=0, tiled=True)
    person_sum = users_all.shape[0]
    persons_of_group = person_sum // part_number
    kept_capacity = kept_part_entries.shape[2]
    part_holders = part_number * model_split_number
    surv = pair_attributes.shape[1]
    requested_rows = kept_part_entries[:, 0, :]
    vec_rows = jnp.take(catalog_embedding, requested_rows, axis=0)
    feat_rows = jnp.take(catalog_attributes, requested_rows, axis=0)
    message_content = jnp.concatenate([vec_rows, feat_rows], axis=2)
    person_fourth = message_content.shape[2] // model_split_number
    message_content = message_content.reshape(
        person_sum, kept_capacity, model_split_number, person_fourth
    ).transpose(0, 2, 1, 3)
    raw_predictions = jnp.einsum(
        "ue,uce->uc", users_all, vec_rows, preferred_element_type=jnp.float32
    )
    logit_out = jnp.broadcast_to(
        raw_predictions[:, None, :], (person_sum, model_split_number, kept_capacity)
    )
    output_count = jnp.broadcast_to(
        valid_slot_number[:, None, :], (person_sum, model_split_number, 1)
    )
    all_scores = jnp.einsum(
        "ue,ie->ui", users_all, catalog_embedding, preferred_element_type=jnp.float32
    )
    best_local = jnp.max(all_scores, axis=1)
    parcel = (message_content, logit_out, output_count)
    holder_numbers = jnp.arange(part_holders, dtype=jnp.int32)
    received_thing = (
        lax.all_to_all(
            lax.all_to_all(parcel[0], "shard", split_axis=0, concat_axis=2, tiled=True),
            "tp",
            split_axis=1,
            concat_axis=2,
            tiled=True,
        ),
        lax.all_to_all(
            lax.all_to_all(
                parcel[1].astype(jnp.bfloat16), "shard", split_axis=0, concat_axis=2, tiled=True
            ),
            "tp",
            split_axis=1,
            concat_axis=2,
            tiled=True,
        ).astype(jnp.float32),
        lax.all_to_all(
            lax.all_to_all(parcel[2], "shard", split_axis=0, concat_axis=2, tiled=True),
            "tp",
            split_axis=1,
            concat_axis=2,
            tiled=True,
        ),
    )
    counts_b = (
        received_thing[2]
        .reshape(persons_of_group, model_split_number, part_number)
        .transpose(0, 2, 1)
        .reshape(persons_of_group, part_holders)
    )
    base = (
        holder_numbers % model_split_number * (part_number * kept_capacity)
        + holder_numbers // model_split_number * kept_capacity
    )
    best_all = lax.pmax(best_local, ("shard", "tp"))
    best = lax.dynamic_slice_in_dim(
        best_all, lax.axis_index("shard") * persons_of_group, persons_of_group
    )
    received_entries = received_thing[0].reshape(
        persons_of_group, part_holders * kept_capacity, person_fourth
    )
    received_predictions = received_thing[1].reshape(persons_of_group, part_holders * kept_capacity)
    beginning_positions = jnp.cumsum(counts_b, axis=1).astype(jnp.int32) - counts_b
    permutation = jnp.arange(surv, dtype=jnp.int32)
    holder_lookup = (
        jnp.sum(
            (beginning_positions[:, None, :] <= permutation[None, :, None]).astype(jnp.int32),
            axis=2,
        )
        - 1
    )
    beginning_lookup = jnp.take_along_axis(beginning_positions, holder_lookup, axis=1)
    source = base[holder_lookup] + (permutation[None, :] - beginning_lookup)
    picked = jnp.take_along_axis(received_entries, source[:, :, None], axis=1)
    logit_kept = jnp.take_along_axis(received_predictions, source, axis=1)
    x_first = jnp.concatenate([picked, pair_attributes], axis=2).reshape(
        persons_of_group * surv, -1
    )
    x_now = x_first
    for layer in range(lowrank_v_matrix.shape[0]):
        partial_proj = jnp.dot(
            x_now, lowrank_v_matrix[layer], preferred_element_type=jnp.float32
        ).astype(jnp.bfloat16)
        proj = lax.psum(partial_proj, "tp").astype(jnp.float32).astype(jnp.bfloat16)
        hidden = jnp.dot(proj, lowrank_u_matrix[layer], preferred_element_type=jnp.float32)
        x_now = (
            x_first.astype(jnp.float32) * (hidden + interaction_offset[layer][None, :])
            + x_now.astype(jnp.float32)
        ).astype(jnp.bfloat16)
    partial_score = jnp.sum(
        x_now.astype(jnp.float32) * final_projection.astype(jnp.float32)[None, :], axis=1
    )
    score = lax.psum(partial_score, "tp").reshape(persons_of_group, surv)
    return score + similarity_coefficient[0] * (logit_kept - best[:, None])


def solution(mesh):
    return jax.shard_map(
        on_device,
        mesh=mesh,
        in_specs=(
            P("shard", None),
            P(("shard", "tp"), None),
            P(("shard", "tp"), None),
            P(None, ("shard", "tp"), None),
            P(None, ("shard", "tp")),
            P("shard", None, "tp"),
            P(None, "tp", None),
            P(None, None, "tp"),
            P(None, "tp"),
            P("tp"),
            P(),
        ),
        out_specs=P("shard", None),
        check_vma=False,
    )
```

profile of v0, /device:TPU:1, one launch (start us, length us, event | category | flops | bytes accessed | tf_op | source)
XLA Modules:
  0.0 452.3 jit_solution(14513417889235415655)
XLA Ops:
  6.5 1.6 broadcast_in_dim.60
  8.2 13.2 %all-to-all-start = ((s32[128,4,1]{1,2,0:T(1,128)}), s32[128,4,1]{1,2,0:T(1,128)S(1)}, u32[]{:S(2)}, u32[]{:S(2)}) async-start(s32[128,4,1]{1,2,0:T(1,128)} %broadcast_in_dim.60), calls=%async_computation | async-start | bytes 131072 | tf_op jit(solution)/shard_map/all_to_all | solution.py:69
  21.3 0.7 compare_and_fusion.1
  22.0 0.7 compare_select_fusion.4
  22.7 0.1 copy.69
  22.8 0.1 copy.70
  22.9 0.1 reshape.222
  23.0 5.9 %gather_fusion.1 = bf16[1024,256]{1,0:T(8,128)(2,1)} fusion(bf16[2048,256]{1,0:T(8,128)(2,1)} %param.12, s32[1024]{0:T(1024)S(1)} %broadcast_clamp_fusion), kind=kCustom, calls=%fused_computation.1 | custom fusion | bytes 1052672 | tf_op jit(solution)/shard_map/jit(_take)/gather | solution.py:29
  29.0 5.2 %gather_fusion.2 = bf16[1024,768]{1,0:T(8,128)(2,1)} fusion(bf16[2048,768]{1,0:T(8,128)(2,1)S(1)} %copy-done, s32[1024]{0:T(1024)S(1)} %broadcast_clamp_fusion), kind=kCustom, calls=%fused_computation.2 | custom fusion | bytes 3149824 | tf_op jit(solution)/shard_map/jit(_take)/gather | solution.py:30
  34.2 2.8 bitcast_select_fusion
  37.0 1.0 bitcast_select_fusion.1
  38.1 0.1 copy.66
  38.2 0.7 reshape.269
  38.8 4.0 all-to-all-start.1
  42.8 3.1 pad_maximum_fusion.1
  45.9 1.0 all-to-all-done.1
  46.9 11.9 %all-to-all-start.2 = ((bf16[128,4,8,256]{3,2,1,0:T(8,128)(2,1)}), bf16[128,4,8,256]{3,2,1,0:T(8,128)(2,1)}, u32[]{:S(2)}, u32[]{:S(2)}) async-start(bf16[128,4,8,256]{3,2,1,0:T(8,128)(2,1)} %bitcast.113), calls=%async_computation.2 | async-start | bytes 4194304 | tf_op jit(solution)/shard_map/all_to_all | solution.py:53
  58.8 0.5 broadcast.269
  59.3 0.7 reduce.6
  60.0 0.1 reshape.270
  60.1 0.1 copy.67
  60.2 0.1 reshape.206
  60.3 0.1 reshape.204
  60.4 0.6 reduce-window.6
  61.0 47.4 %all-to-all-done.2 = bf16[128,4,8,256]{3,2,1,0:T(8,128)(2,1)} async-done(((bf16[128,4,8,256]{3,2,1,0:T(8,128)(2,1)}), bf16[128,4,8,256]{3,2,1,0:T(8,128)(2,1)}, u32[]{:S(2)}, u32[]{:S(2)}) %all-to-all-start.2) | async-done | bytes 2097184 | tf_op jit(solution)/shard_map/all_to_all | solution.py:53
  108.4 1.7 copy.93
  110.1 1.4 copy.73
  111.5 4.4 all-to-all-start.3
  116.0 0.2 slice_reduce_fusion.2
  116.2 0.2 reduce-window.9
  116.4 0.1 add_bitcast_fusion
  116.5 0.4 convert_reduce_fusion
  116.9 17.7 %gather_fusion.3 = s32[2048]{0:T(1024)S(1)} fusion(s32[2,256]{1,0:T(2,128)S(1)} %bitcast_subtract_fusion, s32[2048]{0:T(1024)S(1)} %bitcast.109), kind=kCustom, calls=%fused_computation.3 | custom fusion | bytes 32768 | tf_op jit(solution)/shard_map/jit(take_along_axis)/gather | solution.py:103
  134.7 13.1 %gather_fusion = s32[2048]{0:T(1024)S(1)} fusion(s32[256]{0:T(256)S(1)} %fusion.22, s32[2048]{0:T(1024)S(1)} %bitcast_clamp_fusion), kind=kCustom, calls=%fused_computation | custom fusion | bytes 24576 | tf_op jit(solution)/shard_map/gather | solution.py:104
  147.9 3.0 copy.74
  151.0 35.4 %gather_fusion.4 = bf16[2048,256]{1,0:T(8,128)(2,1)} fusion(bf16[2,2048,256]{2,1,0:T(8,128)(2,1)} %bitcast.110, s32[2048]{0:T(1024)S(1)} %bitcast.107), kind=kCustom, calls=%fused_computation.4 | custom fusion | bytes 2113536 | tf_op jit(solution)/shard_map/jit(take_along_axis)/gather | solution.py:105
  186.3 1.6 broadcast_select_fusion
  188.0 0.3 copy-done.2
  188.3 0.2 pad_maximum_fusion
  188.5 1.7 copy-done.1
  190.2 0.1 copy-done.7
  190.3 3.2 convolution_convert_fusion.1
  193.5 0.2 all-reduce.5.cloned.1.call-start
  193.7 0.4 copy-done.4
  194.2 4.8 %copy.81 = bf16[2048,768]{0,1:T(8,128)(2,1)} copy(bf16[2048,768]{1,0:T(8,128)(2,1)} %bitcast.112) | data formatting | bytes 6291456 | tf_op jit(solution)/shard_map/reshape | solution.py:107
  199.0 56.6 %all-reduce.3.cloned.1.call-done = bf16[2048,512]{1,0:T(8,128)(2,1)} async-done(((bf16[2048,512]{1,0:T(8,128)(2,1)}), bf16[2048,512]{1,0:T(8,128)(2,1)}) %all-reduce.3.cloned.1.call-update) | async-done | bytes 2097168 | tf_op jit(solution)/shard_map/psum | solution.py:115
  255.6 5.0 %fusion.2 = bf16[2048,768]{0,1:T(8,128)(2,1)S(1)} fusion(bf16[2048,768]{0,1:T(8,128)(2,1)} %copy.81, bf16[2048,512]{1,0:T(8,128)(2,1)} %all-reduce.3.cloned.1.call-done, f32[768]{0:T(1024)S(1)} %get-tuple-element.6, bf16[2,512,768]{2,1,0:T(8,128)(2,1)} %param.18), kind=kOutput, calls=%fused_computation.10 | convolution fusion | flops 1618477056 | bytes 9178112 | tf_op jit(solution)/shard_map/dot_general | solution.py:116
  260.7 1.7 copy-done.9
  262.4 3.3 convolution_convert_fusion
  265.7 0.6 copy-done.6
  266.3 45.1 %all-gather = bf16[64,2,256]{2,1,0:T(2,128)(2,1)S(1)} all-gather(bf16[1,2,256]{2,1,0:T(2,128)(2,1)S(1)} %bitcast.122), channel_id=1, replica_groups=mesh['shard'=64,'tp'=4] {'shard'}, dimensions={0}, use_global_device_ids=true | all-gather | bytes 66560 | tf_op jit(solution)/shard_map/all_gather | solution.py:22
  311.5 1.3 fusion.25
  312.8 0.7 broadcast_in_dim.69
  313.5 7.2 %all-to-all-start.4 = ((bf16[128,4,8]{2,1,0:T(4,128)(2,1)}), bf16[128,4,8]{2,1,0:T(4,128)(2,1)S(1)}, u32[]{:S(2)}, u32[]{:S(2)}) async-start(bf16[128,4,8]{2,1,0:T(4,128)(2,1)} %broadcast_in_dim.69), calls=%async_computation.4 | async-start | bytes 262144 | tf_op jit(solution)/shard_map/all_to_all | solution.py:60
  320.8 11.1 %all-to-all-done.4 = bf16[128,4,8]{2,1,0:T(4,128)(2,1)S(1)} async-done(((bf16[128,4,8]{2,1,0:T(4,128)(2,1)}), bf16[128,4,8]{2,1,0:T(4,128)(2,1)S(1)}, u32[]{:S(2)}, u32[]{:S(2)}) %all-to-all-start.4) | async-done | bytes 8224 | tf_op jit(solution)/shard_map/all_to_all | solution.py:60
  331.9 0.8 reshape.265
  332.6 3.2 all-to-all-start.5
  335.9 1.8 convolution_reduce_fusion
  338.4 74.1 %pmax.7 = f32[128]{0:T(128)S(1)} all-reduce(f32[128]{0:T(128)S(1)} %convolution_reduce_fusion), channel_id=1, replica_groups=mesh['shard'=64,'tp'=4] {'shard','tp'}, use_global_device_ids=true, to_apply=%region_8.9 | all-reduce | flops 128 | bytes 1024 | tf_op jit(solution)/shard_map/pmax | solution.py:86
  412.5 0.1 dynamic_slice.3
  412.5 17.7 %gather_fusion.5 = f32[2048]{0:T(1024)S(1)} fusion(f32[2,2048]{1,0:T(2,128)S(1)} %convert.1, s32[2048]{0:T(1024)S(1)} %bitcast.108), kind=kCustom, calls=%fused_computation.5 | custom fusion | bytes 32768 | tf_op jit(solution)/shard_map/jit(take_along_axis)/gather | solution.py:106
  430.3 6.4 %multiply_reduce_fusion = f32[2048]{0:T(1024)S(1)} fusion(f32[768]{0:T(1024)S(1)} %convert_element_type.54, bf16[2048,768]{0,1:T(8,128)(2,1)} %copy-done.9, f32[768]{0:T(1024)S(1)} %get-tuple-element.5, bf16[2048,512]{1,0:T(8,128)(2,1)} %all-reduce.5.cloned.1.call-done, bf16[2048,768]{0,1:T(8,128)(2,1)} %copy.81, bf16[2,512,768]{2,1,0:T(8,128)(2,1)} %param.18), kind=kOutput, calls=%fused_computation.11 | convolution fusion | flops 1624766464 | bytes 9189376 | tf_op jit(solution)/shard_map/dot_general | solution.py:116
  436.7 8.0 %psum.23 = f32[2,1024]{1,0:T(2,128)S(1)} all-reduce(f32[2,1024]{1,0:T(2,128)S(1)} %reshape.210), channel_id=1, replica_groups=mesh['shard'=64,'tp'=4] {'tp'}, use_global_device_ids=true, to_apply=%region_6.7 | all-reduce | flops 2048 | bytes 16384 | tf_op jit(solution)/shard_map/psum | solution.py:124
  444.7 0.7 multiply_add_fusion.1
  (45 shorter events, 0.5 us)
Async XLA Ops:
  6.5 22.4 %copy-start = (bf16[2048,768]{1,0:T(8,128)(2,1)S(1)}, bf16[2048,768]{1,0:T(8,128)(2,1)}, u32[]{:S(2)}) copy-start(bf16[2048,768]{1,0:T(8,128)(2,1)} %param.13) | copy-start | bytes 9437188
  8.2 29.9 %all-to-all-start = ((s32[128,4,1]{1,2,0:T(1,128)}), s32[128,4,1]{1,2,0:T(1,128)S(1)}, u32[]{:S(2)}, u32[]{:S(2)}) async-start(s32[128,4,1]{1,2,0:T(1,128)} %broadcast_in_dim.60), calls=%async_computation | async-start | bytes 131072 | tf_op jit(solution)/shard_map/all_to_all | solution.py:69
  34.2 2.9 copy-start.3
  38.8 8.0 %all-to-all-start.1 = ((s32[4,1,128]{2,1,0:T(1,128)}), s32[4,1,128]{2,1,0:T(1,128)S(1)}, u32[]{:S(2)}, u32[]{:S(2)}) async-start(s32[4,1,128]{2,1,0:T(1,128)} %reshape.269), calls=%async_computation.1 | async-start | bytes 4096 | tf_op jit(solution)/shard_map/all_to_all | solution.py:68
  46.9 61.5 %all-to-all-start.2 = ((bf16[128,4,8,256]{3,2,1,0:T(8,128)(2,1)}), bf16[128,4,8,256]{3,2,1,0:T(8,128)(2,1)}, u32[]{:S(2)}, u32[]{:S(2)}) async-start(bf16[128,4,8,256]{3,2,1,0:T(8,128)(2,1)} %bitcast.113), calls=%async_computation.2 | async-start | bytes 4194304 | tf_op jit(solution)/shard_map/all_to_all | solution.py:53
  111.5 36.4 %all-to-all-start.3 = ((bf16[2,4,512,256]{3,2,0,1:T(8,128)(2,1)}), bf16[2,4,512,256]{3,2,0,1:T(8,128)(2,1)}, u32[]{:S(2)}, u32[]{:S(2)}) async-start(bf16[2,4,512,256]{3,2,0,1:T(8,128)(2,1)} %copy.73), calls=%async_computation.3 | async-start | bytes 4194304 | tf_op jit(solution)/shard_map/all_to_all | solution.py:52
  116.0 139.6 %all-reduce.3.cloned.1.call-start = ((), (), s32[]{:S(2)}) async-start(), calls=%async_computation.6 | async-start | bytes 4194304 | tf_op jit(solution)/shard_map/psum | solution.py:115
  186.3 1.9 copy-start.2
  188.2 2.0 copy-start.7
  188.5 1.7 copy-start.1
  193.5 0.7 copy-start.4
  193.5 236.8 %all-reduce.5.cloned.1.call-start = ((), (), s32[]{:S(2)}) async-start(), calls=%async_computation.7 | async-start | bytes 4194304 | tf_op jit(solution)/shard_map/psum | solution.py:115
  255.6 6.8 %copy-start.8 = (bf16[2,768,512]{2,1,0:T(8,128)(2,1)S(1)}, bf16[2,768,512]{2,1,0:T(8,128)(2,1)}, u32[]{:S(2)}) copy-start(bf16[2,768,512]{2,1,0:T(8,128)(2,1)} %param.17) | copy-start | bytes 4718596
  260.6 1.7 copy-start.9
  265.6 0.7 copy-start.6
  265.6 72.7 %copy-start.5 = (bf16[768]{0:T(1024)(128)(2,1)S(1)}, bf16[768]{0:T(1024)(128)(2,1)}, u32[]{:S(2)}) copy-start(bf16[768]{0:T(1024)(128)(2,1)} %param.20) | copy-start | bytes 4612
  313.5 18.3 %all-to-all-start.4 = ((bf16[128,4,8]{2,1,0:T(4,128)(2,1)}), bf16[128,4,8]{2,1,0:T(4,128)(2,1)S(1)}, u32[]{:S(2)}, u32[]{:S(2)}) async-start(bf16[128,4,8]{2,1,0:T(4,128)(2,1)} %broadcast_in_dim.69), calls=%async_computation.4 | async-start | bytes 262144 | tf_op jit(solution)/shard_map/all_to_all | solution.py:60
  332.6 79.9 %all-to-all-start.5 = ((bf16[2,4,512]{2,0,1:T(2,128)(2,1)}), bf16[2,4,512]{2,0,1:T(2,128)(2,1)S(1)}, u32[]{:S(2)}, u32[]{:S(2)}) async-start(bf16[2,4,512]{2,0,1:T(2,128)(2,1)} %reshape.265), calls=%async_computation.5 | async-start | bytes 16384 | tf_op jit(solution)/shard_map/all_to_all | solution.py:59
Sparse Core Ops, SparseCore 0:
  193.6 61.9 all-reduce.2
  265.8 63.6 all-reduce.4
where the time goes:
time: 455 us; the launch traced here: 452 us
  blocking collectives  127 us (28%)
  local copies, waits for them, and re-layouts  116 us (25%)
  waiting for transfers between devices  116 us (25%)
  starting transfers between devices  44.2 us (10%)
  matrix products  21 us (5%)
  between operations  14.4 us (3%)
  other arithmetic  12.9 us (3%)
    pmax x1, blocking collectives, on_device(): best_all = lax.pmax(best_local, ('shard', 'tp'))  74.1 us
    psum x2, waiting for transfers between devices, on_device(): proj = lax.psum(partial_proj, 'tp').astype(jnp.float32).astype(jnp.bfloat16)  56.7 us
    all_to_all x1, waiting for transfers between devices, on_device(): lax.all_to_all(parcel[0], 'shard', split_axis=0, concat_axis=2, tiled=True)  47.4 us
    all_gather x1, blocking collectives, on_device(): users_all = lax.all_gather(person_embedding, 'shard', axis=0, tiled=True)  45.1 us
    gather x1, local copies, waits for them, and re-layouts, on_device(): picked = jnp.take_along_axis(received_entries, source[:, :, None], axis=1)  35.4 us
    gather x3, local copies, waits for them, and re-layouts, on_device(): jnp.take_along_axis(beginning_positions, holder_lookup, axis=1)  17.7 us
    gather x2, local copies, waits for them, and re-layouts, on_device(): logit_kept = jnp.take_along_axis(received_predictions, source, axis=1)  17.7 us
    gather x3, local copies, waits for them, and re-layouts, on_device(): source = base[holder_lookup] + (permutation[None, :] - beginning_lookup)  13.2 us
  transfers between devices with their start and end apart: 8, of which 4 were waited for; matrix products, arithmetic and copies ran while one was open for 18% of the time, Pallas kernels for 0%

commit v1 on v0

v1 whole, which is shorter than its diff:
```python
import functools

import jax
import jax.numpy as jnp
from jax import lax
from jax.experimental import pallas as pl
from jax.experimental.pallas import tpu as pltpu
from jax.sharding import PartitionSpec as P

BF = jnp.bfloat16
F32 = jnp.float32
AXES = ("shard", "tp")
VMEM = pltpu.CompilerParams(vmem_limit_bytes=56 * 1024 * 1024)


def group_perm(groups, step, member=lambda x, c: True):
    pairs = []
    for g in range(groups):
        for c in range(2):
            for x in range(4):
                if member(x, c):
                    x2, c2 = step(x, c)
                    pairs.append((g * 8 + c * 4 + x, g * 8 + c2 * 4 + x2))
    return pairs


def is_home(x, c):
    return x // 2 == c


def is_away(x, c):
    return x // 2 != c


def near(x, c):
    return (x ^ 1, x // 2) if is_home(x, c) else (x ^ 3, x // 2)


def dot(a, b):
    return jnp.dot(a, b, preferred_element_type=F32)


def dot_nt(a, b):
    return lax.dot_general(a, b, (((1,), (1,)), ((), ())), preferred_element_type=F32)


def pick_kernel(rows_ref, emb_ref, attr_ref, out_ref):
    rows = rows_ref[...]
    n = rows.shape[0]
    items = emb_ref.shape[0]
    hot = (lax.broadcasted_iota(jnp.int32, (n, items), 1) == rows).astype(BF)
    unused = rows < 0
    odd = (lax.broadcasted_iota(jnp.int32, (n, 1), 0) // 8) % 2 == 1
    quarters = [
        jnp.where(unused, jnp.inf, dot(hot, emb_ref[...])),
        jnp.where(unused, jnp.inf, dot(hot, attr_ref[:, 0:256])),
        jnp.where(unused, jnp.inf, dot(hot, attr_ref[:, 256:512])),
        jnp.where(unused, jnp.inf, dot(hot, attr_ref[:, 512:768])),
    ]
    for c in range(2):
        low, high = quarters[2 * c], quarters[2 * c + 1]
        first = jnp.where(odd, low, high).astype(BF)
        second = jnp.where(odd, high, low).astype(BF)
        for g in range(n // 32):
            out_ref[g, c, :, 0:256] = first[g * 32 : (g + 1) * 32]
            out_ref[g, c, :, 256:512] = second[g * 32 : (g + 1) * 32]


def pick_rows(rows, emb, attr):
    n = rows.shape[0]
    steps = 4
    block = n // steps
    return pl.pallas_call(
        pick_kernel,
        grid=(steps,),
        in_specs=[
            pl.BlockSpec((block, 1), lambda i: (i, 0)),
            pl.BlockSpec(emb.shape, lambda i: (0, 0)),
            pl.BlockSpec(attr.shape, lambda i: (0, 0)),
        ],
        out_specs=pl.BlockSpec((block // 32, 2, 32, 512), lambda i: (i, 0, 0, 0)),
        out_shape=jax.ShapeDtypeStruct((n // 32, 2, 32, 512), BF),
        compiler_params=VMEM,
        cost_estimate=pl.CostEstimate(
            flops=2 * n * 2048 * 1024, bytes_accessed=6 << 20, transcendentals=0
        ),
        name="pick_rows",
    )(rows, emb, attr)


def first_kernel(
    recv_ref, ca_ref, cb_ref, va_ref, vb_ref, u_ref, pay_ref, piece_ref, logit_ref, clean, place
):
    step = pl.program_id(0)
    slots = recv_ref.shape[0]
    blk = 256

    @pl.when(step == 0)
    def _():
        r = lax.broadcasted_iota(jnp.int32, (blk, blk), 0)
        q = lax.broadcasted_iota(jnp.int32, (blk, blk), 1)
        upper = (r <= q).astype(BF)
        lane0 = (lax.broadcasted_iota(jnp.int32, (16, 128), 1) == 0).astype(BF)
        before = jnp.zeros((16, 1), F32)
        for i in range(slots // blk):
            got = recv_ref[i * blk : (i + 1) * blk, :].astype(F32)
            live = got < jnp.inf
            clean[i * blk : (i + 1) * blk, :] = jnp.where(live, got, 0.0).astype(BF)
            flags = dot_nt(lane0, live[:, 0:128].astype(F32).astype(BF))
            upto = dot(flags.astype(BF), upper) + before
            place[:, i * blk : (i + 1) * blk] = jnp.where(flags > 0.5, upto - 1.0, -1.0)
            before = upto[:, blk - 1 : blk]

    rows = pay_ref.shape[0]
    k = (lax.broadcasted_iota(jnp.int32, (rows, slots), 0) + step * rows).astype(F32)
    hot = (k == place[0:1, :]).astype(BF)
    pay = dot(hot, clean[...]).astype(BF)
    pay_ref[...] = pay
    piece = (
        dot(pay[:, 0:256], va_ref[0:256])
        + dot(ca_ref[...], va_ref[256:768])
        + dot(pay[:, 256:512], vb_ref[0:256])
        + dot(cb_ref[...], vb_ref[256:768])
    )
    piece_ref[...] = piece.astype(BF)
    logit_ref[...] = dot_nt(u_ref[...], pay)


def first_layer(recv, ctx_a, ctx_b, v_a, v_b, u_rows):
    surv = ctx_a.shape[0]
    steps = 4
    rows = surv // steps

    def full(a):
        return pl.BlockSpec(a.shape, lambda i: (0,) * a.ndim)

    by_row = pl.BlockSpec((rows, 512), lambda i: (i, 0))
    return pl.pallas_call(
        first_kernel,
        grid=(steps,),
        in_specs=[full(recv), by_row, by_row, full(v_a), full(v_b), full(u_rows)],
        out_specs=[by_row, by_row, pl.BlockSpec((16, rows), lambda i: (0, i))],
        out_shape=[
            jax.ShapeDtypeStruct((surv, 512), BF),
            jax.ShapeDtypeStruct((surv, 512), BF),
            jax.ShapeDtypeStruct((16, surv), F32),
        ],
        scratch_shapes=[pltpu.VMEM(recv.shape, BF), pltpu.VMEM((16, recv.shape[0]), F32)],
        compiler_params=VMEM,
        cost_estimate=pl.CostEstimate(flops=4 << 30, bytes_accessed=8 << 20, transcendentals=0),
        name="first_layer",
    )(recv, ctx_a, ctx_b, v_a, v_b, u_rows)


def cross(x0, hidden, offset, x):
    x0 = x0.astype(F32)
    return (x0 * (hidden + offset) + x.astype(F32)).astype(BF)


def second_kernel(
    mine_ref, other_ref, pay_ref, ca_ref, cb_ref, ua_ref, ub_ref, ba_ref, bb_ref, va_ref, vb_ref,
    xa_ref, xb_ref, piece_ref,
):
    proj = (mine_ref[...].astype(F32) + other_ref[...].astype(F32)).astype(BF)
    piece = None
    for x_ref, u_ref, b_ref, v_ref, c_ref, at in (
        (xa_ref, ua_ref, ba_ref, va_ref, ca_ref, 0),
        (xb_ref, ub_ref, bb_ref, vb_ref, cb_ref, 256),
    ):
        hidden = dot(proj, u_ref[...])
        pay = pay_ref[:, at : at + 256]
        x_ref[:, 0:256] = cross(pay, hidden[:, 0:256], b_ref[0:1, 0:256], pay)
        x_ref[:, 256:768] = cross(c_ref[...], hidden[:, 256:768], b_ref[0:1, 256:768], c_ref[...])
        term = dot(x_ref[...], v_ref[...])
        piece = term if piece is None else piece + term
    piece_ref[...] = piece.astype(BF)


def second_layer(mine, other, pay, ctx_a, ctx_b, u_a, u_b, b_a, b_b, v_a, v_b):
    surv = pay.shape[0]
    steps = 4
    rows = surv // steps

    def full(a):
        return pl.BlockSpec(a.shape, lambda i: (0,) * a.ndim)

    by_row = pl.BlockSpec((rows, 512), lambda i: (i, 0))
    wide = pl.BlockSpec((rows, 768), lambda i: (i, 0))
    return pl.pallas_call(
        second_kernel,
        grid=(steps,),
        in_specs=[by_row] * 5 + [full(a) for a in (u_a, u_b, b_a, b_b, v_a, v_b)],
        out_specs=[wide, wide, by_row],
        out_shape=[
            jax.ShapeDtypeStruct((surv, 768), BF),
            jax.ShapeDtypeStruct((surv, 768), BF),
            jax.ShapeDtypeStruct((surv, 512), BF),
        ],
        compiler_params=VMEM,
        cost_estimate=pl.CostEstimate(flops=7 << 29, bytes_accessed=12 << 20, transcendentals=0),
        name="second_layer",
    )(mine, other, pay, ctx_a, ctx_b, u_a, u_b, b_a, b_b, v_a, v_b)


def last_kernel(
    mine_ref, other_ref, pay_ref, ca_ref, cb_ref, xa_ref, xb_ref, ua_ref, ub_ref, ba_ref, bb_ref,
    fa_ref, fb_ref, extra_ref, score_ref,
):
    proj = (mine_ref[...].astype(F32) + other_ref[...].astype(F32)).astype(BF)
    score = extra_ref[...]
    for x_ref, u_ref, b_ref, f_ref, c_ref, at in (
        (xa_ref, ua_ref, ba_ref, fa_ref, ca_ref, 0),
        (xb_ref, ub_ref, bb_ref, fb_ref, cb_ref, 256),
    ):
        hidden = dot(proj, u_ref[...])
        pay = pay_ref[:, at : at + 256]
        low = cross(pay, hidden[:, 0:256], b_ref[0:1, 0:256], x_ref[:, 0:256])
        high = cross(c_ref[...], hidden[:, 256:768], b_ref[0:1, 256:768], x_ref[:, 256:768])
        score = score + dot_nt(f_ref[:, 0:256], low) + dot_nt(f_ref[:, 256:768], high)
    score_ref[...] = score


def last_layer(mine, other, pay, ctx_a, ctx_b, x_a, x_b, u_a, u_b, b_a, b_b, f_a, f_b, extra):
    surv = pay.shape[0]
    steps = 4
    rows = surv // steps

    def full(a):
        return pl.BlockSpec(a.shape, lambda i: (0,) * a.ndim)

    by_row = pl.BlockSpec((rows, 512), lambda i: (i, 0))
    wide = pl.BlockSpec((rows, 768), lambda i: (i, 0))
    lanes = pl.BlockSpec((16, rows), lambda i: (0, i))
    return pl.pallas_call(
        last_kernel,
        grid=(steps,),
        in_specs=[by_row] * 5
        + [wide, wide]
        + [full(a) for a in (u_a, u_b, b_a, b_b, f_a, f_b)]
        + [lanes],
        out_specs=lanes,
        out_shape=jax.ShapeDtypeStruct((16, surv), F32),
        compiler_params=VMEM,
        cost_estimate=pl.CostEstimate(flops=7 << 28, bytes_accessed=10 << 20, transcendentals=0),
        name="last_layer",
    )(mine, other, pay, ctx_a, ctx_b, x_a, x_b, u_a, u_b, b_a, b_b, f_a, f_b, extra)


def on_device(
    person_embedding,
    catalog_embedding,
    catalog_attributes,
    kept_part_entries,
    valid_slot_number,
    pair_attributes,
    lowrank_v_matrix,
    lowrank_u_matrix,
    interaction_offset,
    final_projection,
    similarity_coefficient,
):
    shards = lax.axis_size("shard")
    groups = shards // 2
    x = lax.axis_index("tp")
    core = lax.axis_index("shard") % 2
    home = x // 2 == core
    parity = x % 2
    move = functools.partial(lax.ppermute, axis_name=AXES)
    to_core = group_perm(groups, lambda x, c: (x, 1 - c))
    to_near = group_perm(groups, near)
    home_on = group_perm(groups, lambda x, c: (x ^ 3, c), is_home)
    away_swap = group_perm(groups, lambda x, c: (x ^ 1, c), is_away)
    ctx_near = group_perm(groups, lambda x, c: (x ^ 1, c) if is_home(x, c) else (x ^ 3, 1 - c))
    ctx_far = group_perm(groups, lambda x, c: (x ^ 2, 1 - c), is_away)

    persons, _, kept = kept_part_entries.shape
    slot = jnp.arange(kept, dtype=jnp.int32)[None, :]
    rows = jnp.where(slot < valid_slot_number, kept_part_entries[:, 0, :], -1)
    parcel = pick_rows(rows.reshape(persons * kept, 1), catalog_embedding, catalog_attributes)
    parcel = parcel.reshape(persons * 2, kept, 512)
    recv = lax.all_to_all(parcel, AXES, split_axis=0, concat_axis=0, tiled=True)
    recv = recv.reshape(persons * 2 * kept, 512)

    ctx_a = move(lax.dynamic_index_in_dim(pair_attributes, 1 - parity, 0, False), perm=ctx_near)
    ctx_own = lax.dynamic_index_in_dim(pair_attributes, parity, 0, False)
    ctx_b = jnp.where(home, ctx_own, move(ctx_own, perm=ctx_far))

    small = jnp.concatenate([interaction_offset, final_projection[None, :].astype(F32)], 0)
    v_a = move(lowrank_v_matrix, perm=to_near)
    u_a = move(lowrank_u_matrix, perm=to_near)
    small_a = move(small, perm=to_near)
    v_b = jnp.where(home, lowrank_v_matrix, move(v_a, perm=home_on))
    u_b = jnp.where(home, lowrank_u_matrix, move(u_a, perm=away_swap))
    small_b = jnp.where(home, small, move(small_a, perm=home_on))

    users = person_embedding[None]
    width = 1
    while width < shards:
        pairs = [(i, i ^ width) for i in range(shards)]
        users = jnp.concatenate([users, lax.ppermute(users, "shard", pairs)], 0)
        width *= 2
    all_scores = jnp.einsum(
        "ue,ie->ui", users.reshape(persons, -1), catalog_embedding, preferred_element_type=F32
    )
    best = jnp.max(all_scores, axis=1).reshape(shards, persons // shards)
    while width > 1:
        width //= 2
        pairs = [(i, i ^ width) for i in range(shards)]
        best = jnp.maximum(best[:width], lax.ppermute(best[width:], "shard", pairs))
    for flip in (1, 2):
        best = jnp.maximum(best, lax.ppermute(best, "tp", [(i, i ^ flip) for i in range(4)]))

    emb_other = move(person_embedding, perm=to_core)
    query = lax.dynamic_slice_in_dim(jnp.where(home, person_embedding, emb_other), parity, 1, 0)
    query = jnp.where(core == 0, query, jnp.zeros_like(query))
    zero = jnp.zeros_like(query)
    query = jnp.where(
        parity == 1, jnp.concatenate([query, zero], 1), jnp.concatenate([zero, query], 1)
    )
    query = jnp.broadcast_to(query, (16, 512))

    pay, piece, logit = first_layer(recv, ctx_a, ctx_b, v_a[0], v_b[0], query)
    other = move(piece, perm=to_core)
    x_a, x_b, piece1 = second_layer(
        piece, other, pay, ctx_a, ctx_b, u_a[0], u_b[0], small_a[0:1], small_b[0:1], v_a[1], v_b[1]
    )
    other1 = move(piece1, perm=to_core)
    top = jnp.where(home, lax.dynamic_slice_in_dim(best, parity, 1, 1), 0.0)
    extra = similarity_coefficient[0] * (logit - top)
    f_a = jnp.broadcast_to(small_a[2:3], (16, 768)).astype(BF)
    f_b = jnp.broadcast_to(small_b[2:3], (16, 768)).astype(BF)
    score = last_layer(
        piece1, other1, pay, ctx_a, ctx_b, x_a, x_b, u_a[1], u_b[1], small_a[1:2], small_b[1:2],
        f_a, f_b, extra,
    )[0:1]
    score = score + move(score, perm=to_core)
    score_a = move(score, perm=to_near)
    score_b = jnp.where(home, score, move(score, perm=ctx_far))
    return jnp.where(
        parity == 1,
        jnp.concatenate([score_a, score_b], 0),
        jnp.concatenate([score_b, score_a], 0),
    )


def solution(mesh):
    return jax.shard_map(
        on_device,
        mesh=mesh,
        in_specs=(
            P("shard", None),
            P(("shard", "tp"), None),
            P(("shard", "tp"), None),
            P(None, ("shard", "tp"), None),
            P(None, ("shard", "tp")),
            P("shard", None, "tp"),
            P(None, "tp", None),
            P(None, None, "tp"),
            P(None, "tp"),
            P("tp"),
            P(),
        ),
        out_specs=P("shard", None),
        check_vma=False,
    )
```

time: 455 us -> 224 us (0.49)
  blocking collectives: 127 us -> 0 us
  local copies, waits for them, and re-layouts: 116 us -> 15.4 us
  Pallas kernels: 0 us -> 32.1 us
  starting transfers between devices: 44.2 us -> 75.7 us
  waiting for transfers between devices: 116 us -> 87.9 us
  matrix products: 21 us -> 1.78 us
  between operations: 14.4 us -> 0.93 us
    gather x11 -> x0, local copies, waits for them, and re-layouts: 95.1 us -> none  [the longest x1 35.4 us: on_device(): picked = jnp.take_along_axis(received_entries, source[:, :, None], axis=1)]
    ppermute x0 -> x28, waiting for transfers between devices: none -> 87.9 us  [the longest x1 61.5 us: on_device(): small_a = move(small, perm=to_near)]
    pmax x1 -> x0, blocking collectives: 74.1 us -> none  [on_device(): best_all = lax.pmax(best_local, ('shard', 'tp'))]
    all_to_all x6 -> x1, waiting for transfers between devices: 59.4 us -> 0.01 us  [on_device(): recv = lax.all_to_all(parcel, AXES, split_axis=0, concat_axis=0, tiled=True)]
    ppermute x0 -> x28, starting transfers between devices: none -> 59.1 us  [the longest x6 12.7 us: on_device(): best = jnp.maximum(best[:width], lax.ppermute(best[width:], 'shard', pairs))]
    psum x2 -> x0, waiting for transfers between devices: 56.7 us -> none  [on_device(): proj = lax.psum(partial_proj, 'tp').astype(jnp.float32).astype(jnp.bfloat16)]
    all_gather x1 -> x0, blocking collectives: 45.1 us -> none  [on_device(): users_all = lax.all_gather(person_embedding, 'shard', axis=0, tiled=True)]
    pallas_call x0 -> x4, Pallas kernels: none -> 32.1 us  [the longest x1 8.48 us: first_layer(): pl.pallas_call(first_kernel, grid=(steps,), in_specs=[full(recv), by_row,...]
  transfers between devices with their start and end apart: 8 -> 29, of which waited for: 4 -> 16; matrix products, arithmetic and copies ran while one was open for 18% -> 9% of each run, Pallas kernels for 0% -> 7%
where the time goes in v1:
time: 224 us; the launch traced here: 223 us
  waiting for transfers between devices  87.9 us (39%)
  starting transfers between devices  75.7 us (34%)
  Pallas kernels  32.1 us (14%)
  local copies, waits for them, and re-layouts  15.4 us (7%)
  other arithmetic  9.07 us (4%)
    ppermute x1, waiting for transfers between devices, on_device(): small_a = move(small, perm=to_near)  61.5 us
    all_to_all x1, starting transfers between devices, on_device(): recv = lax.all_to_all(parcel, AXES, split_axis=0, concat_axis=0, tiled=True)  16.7 us
    ppermute x6, starting transfers between devices, on_device(): best = jnp.maximum(best[:width], lax.ppermute(best[width:], 'shard', pairs))  12.7 us
    ppermute x6, starting transfers between devices, on_device(): users = jnp.concatenate([users, lax.ppermute(users, 'shard', pairs)], 0)  9.49 us
    pallas_call x1, Pallas kernels, first_layer(): pl.pallas_call(first_kernel, grid=(steps,), in_specs=[full(recv), by_row,...  8.48 us
    pallas_call x1, Pallas kernels, pick_rows(): pl.pallas_call(pick_kernel, grid=(steps,), in_specs=[pl.BlockSpec((block,...  8.36 us
    ppermute x6, waiting for transfers between devices, on_device(): users = jnp.concatenate([users, lax.ppermute(users, 'shard', pairs)], 0)  8.35 us
    pallas_call x1, Pallas kernels, second_layer(): pl.pallas_call(second_kernel, grid=(steps,), in_specs=[by_row] * 5 + [ful...  7.78 us
  transfers between devices with their start and end apart: 29, of which 16 were waited for; matrix products, arithmetic and copies ran while one was open for 9% of the time, Pallas kernels for 7%

profile of v1, /device:TPU:1, one launch (start us, length us, event | category | flops | bytes accessed | tf_op | source)
XLA Modules:
  0.0 222.9 jit_solution(970121970910327682)
XLA Ops:
  0.0 0.8 copy.13
  1.0 0.7 iota_compare_fusion
  2.0 0.8 broadcast_select_fusion.3.rows_ref
  2.8 8.4 %pick_rows.1 = bf16[32,2,32,512]{3,2,1,0:T(8,128)(2,1)} custom-call(s32[1024,1]{1,0:T(8,128)} %broadcast_select_fusion.3.rows_ref, bf16[2048,256]{1,0:T(8,128)(2,1)} %emb_ref.1, bf16[2048,768]{1,0:T(8,128)(2,1)} %attr_ref.1), custom_call_target="tpu_custom_call" | custom-call | flops 4294967296 | bytes 6291456 | tf_op jit(solution)/shard_map/pick_rows/pallas_call | solution.py:73
  11.2 16.7 %all-to-all-start = ((bf16[256,8,512]{2,1,0:T(8,128)(2,1)}), bf16[256,8,512]{2,1,0:T(8,128)(2,1)}, u32[]{:S(2)}, u32[]{:S(2)}) async-start(bf16[256,8,512]{2,1,0:T(8,128)(2,1)} %bitcast.35), calls=%async_computation | async-start | bytes 4194304 | tf_op jit(solution)/shard_map/all_to_all | solution.py:281
  27.8 2.3 %collective-permute-start.4 = (bf16[2,256]{1,0:T(2,128)(2,1)S(1)}, bf16[2,256]{1,0:T(2,128)(2,1)S(1)}, u32[]{:S(2)}, u32[]{:S(2)}) collective-permute-start(bf16[2,256]{1,0:T(2,128)(2,1)S(1)} %copy-done.4), channel_id=1, source_target_pairs={{0,4},{1,5},{2,6},{3,7},{4,0},{5,1},{6,2},{7,3},{8,12},{9,13},{10,... | collective-permute-start | bytes 3080 | tf_op jit(solution)/shard_map/ppermute | solution.py:313
  30.2 1.1 dynamic-slice_bitcast_fusion
  31.4 3.2 %collective-permute-start.1 = (bf16[1024,512]{1,0:T(8,128)(2,1)S(1)}, bf16[1024,512]{1,0:T(8,128)(2,1)}, u32[]{:S(2)}, u32[]{:S(2)}) collective-permute-start(bf16[1024,512]{1,0:T(8,128)(2,1)S(1)} %get-tuple-element.17), channel_id=1, source_target_pairs={{2,4},{3,5},{4,2},{5,3},{10,12},{11,13},{12,10},{13,11},{18,20},{1... | collective-permute-start | bytes 3145736 | tf_op jit(solution)/shard_map/ppermute | solution.py:286
  34.6 1.0 collective-permute-start.2
  35.6 2.0 collective-permute-start
  38.4 1.0 collective-permute-start.6
  39.4 1.3 collective-permute-start.12
  40.7 1.6 collective-permute-done.12
  42.4 2.8 %collective-permute-start.13 = (bf16[4,2,256]{2,1,0:T(2,128)(2,1)S(1)}, bf16[4,2,256]{2,1,0:T(2,128)(2,1)S(1)}, u32[]{:S(2)}, u32[]{:S(2)}) collective-permute-start(bf16[4,2,256]{2,1,0:T(2,128)(2,1)S(1)} %pad_maximum_fusion.2), channel_id=1, source_target_pairs={{0,16},{4,20},{8,24},{12,28},{16,0},{20,4},{24,8},{28,12},{32,48},... | collective-permute-start | bytes 12296 | tf_op jit(solution)/shard_map/ppermute | solution.py:300
  45.2 1.7 collective-permute-done.13
  46.8 3.5 %collective-permute-start.8 = (f32[3,768]{1,0:T(4,128)S(1)}, f32[3,768]{1,0:T(4,128)S(1)}, u32[]{:S(2)}, u32[]{:S(2)}) collective-permute-start(f32[3,768]{1,0:T(4,128)S(1)} %pad_maximum_fusion), channel_id=1, source_target_pairs={{0,1},{1,0},{2,5},{3,4},{4,3},{5,2},{6,7},{7,6},{8,9},{9,8},{10,13... | collective-permute-start | bytes 27656 | tf_op jit(solution)/shard_map/ppermute | solution.py:291
  50.4 61.5 %collective-permute-done.8 = f32[3,768]{1,0:T(4,128)S(1)} collective-permute-done((f32[3,768]{1,0:T(4,128)S(1)}, f32[3,768]{1,0:T(4,128)S(1)}, u32[]{:S(2)}, u32[]{:S(2)}) %collective-permute-start.8) | collective-permute-done | bytes 9248 | tf_op jit(solution)/shard_map/ppermute | solution.py:291
  112.6 1.7 collective-permute-done.14
  114.3 1.3 collective-permute-start.9
  115.6 4.3 %collective-permute-done.9 = f32[3,768]{1,0:T(4,128)S(1)} collective-permute-done((f32[3,768]{1,0:T(4,128)S(1)}, f32[3,768]{1,0:T(4,128)S(1)}, u32[]{:S(2)}, u32[]{:S(2)}) %collective-permute-start.9) | collective-permute-done | bytes 9248 | tf_op jit(solution)/shard_map/ppermute | solution.py:294
  120.0 1.2 collective-permute-start.15
  121.2 1.3 collective-permute-start.3
  122.5 1.1 collective-permute-done.15
  123.7 4.0 %collective-permute-start.16 = (bf16[32,2,256]{2,1,0:T(2,128)(2,1)S(1)}, bf16[32,2,256]{2,1,0:T(2,128)(2,1)S(1)}, u32[]{:S(2)}, u32[]{:S(2)}) collective-permute-start(bf16[32,2,256]{2,1,0:T(2,128)(2,1)S(1)} %get-tuple-element.27), channel_id=1, source_target_pairs={{0,128},{4,132},{8,136},{12,140},{16,144},{20,148},{24,152},{28,15... | collective-permute-start | bytes 98312 | tf_op jit(solution)/shard_map/ppermute | solution.py:300
  128.2 2.2 collective-permute-done.16
  130.5 1.8 convolution_reduce_fusion
  132.5 4.3 %collective-permute-start.17 = (f32[32,2]{1,0:T(8,128)S(1)}, f32[32,2]{1,0:T(8,128)S(1)}, u32[]{:S(2)}, u32[]{:S(2)}) collective-permute-start(f32[32,2]{1,0:T(8,128)S(1)} %slice.122), channel_id=1, source_target_pairs={{0,128},{4,132},{8,136},{12,140},{16,144},{20,148},{24,152},{28,15... | collective-permute-start | bytes 776 | tf_op jit(solution)/shard_map/ppermute | solution.py:309
  136.9 2.2 collective-permute-done.17
  139.1 1.1 collective-permute-start.18
  140.2 2.3 %broadcast_select_fusion.2.cb_ref = bf16[1024,512]{1,0:T(8,128)(2,1)} fusion(bf16[1024,512]{1,0:T(8,128)(2,1)S(1)} %get-tuple-element.17, bf16[1024,512]{1,0:T(8,128)(2,1)} %collective-permute-done.1, pred[]{:T(512)} %eq.14), kind=kLoop, calls=%fused_computation.5 | loop fusion | flops 524288 | bytes 3145729 | tf_op jit(solution)/shard_map/jit(_where)/select_n | solution.py:286
  142.5 2.1 collective-permute-start.7
  144.6 2.6 %slice_bitcast_fusion.3 = (bf16[768,512]{1,0:T(8,128)(2,1)}, bf16[768,512]{1,0:T(8,128)(2,1)}) fusion(bf16[2,768,512]{2,1,0:T(8,128)(2,1)} %collective-permute-done.2), kind=kLoop, calls=%fused_computation.9 | loop fusion | bytes 3145728 | tf_op jit(solution)/shard_map/squeeze | solution.py:325
  147.4 1.2 slice_bitcast_fusion.2
  148.7 0.6 broadcast_in_dim.30.u_ref
  149.3 8.5 %first_layer.1 = (bf16[1024,512]{1,0:T(8,128)(2,1)}, bf16[1024,512]{1,0:T(8,128)(2,1)}, f32[16,1024]{1,0:T(8,128)}) custom-call(bf16[2048,512]{1,0:T(8,128)(2,1)} %bitcast.2.recv_ref, bf16[1024,512]{1,0:T(8,128)(2,1)} %collective-permute-done.ca_ref, bf16[1024,512]{1,0:T(8,128)(2,1)} %broadcast_select_fusion.2.cb_ref, ...), custom_call_target="tpu_custom_call" | custom-call | flops 4294967296 | bytes 8388608 | tf_op jit(solution)/shard_map/first_layer/pallas_call | solution.py:138
  157.7 6.0 %collective-permute-start.5 = (bf16[1024,512]{1,0:T(8,128)(2,1)}, bf16[1024,512]{1,0:T(8,128)(2,1)S(1)}, u32[]{:S(2)}, u32[]{:S(2)}) collective-permute-start(bf16[1024,512]{1,0:T(8,128)(2,1)} %get-tuple-element.11.mine_ref), channel_id=1, source_target_pairs={{0,4},{1,5},{2,6},{3,7},{4,0},{5,1},{6,2},{7,3},{8,12},{9,13},{10,... | collective-permute-start | bytes 3145736 | tf_op jit(solution)/shard_map/ppermute | solution.py:323
  163.7 1.0 collective-permute-start.19
  164.7 2.6 %slice_bitcast_fusion.1 = (bf16[512,768]{1,0:T(8,128)(2,1)}, bf16[512,768]{1,0:T(8,128)(2,1)}) fusion(bf16[2,512,768]{2,1,0:T(8,128)(2,1)} %collective-permute-done.6), kind=kLoop, calls=%fused_computation.7 | loop fusion | bytes 3145728 | tf_op jit(solution)/shard_map/squeeze | solution.py:333
  167.3 1.6 broadcast_select_fusion
  168.9 1.3 slice_bitcast_fusion
  170.2 1.0 copy-done.7
  171.2 7.8 %second_layer.1 = (bf16[1024,768]{1,0:T(8,128)(2,1)}, bf16[1024,768]{1,0:T(8,128)(2,1)}, bf16[1024,512]{1,0:T(8,128)(2,1)}) custom-call(bf16[1024,512]{1,0:T(8,128)(2,1)} %get-tuple-element.11.mine_ref, bf16[1024,512]{1,0:T(8,128)(2,1)} %copy-done.7, bf16[1024,512]{1,0:T(8,128)(2,1)} %get-tuple-element.12.pay_ref, ...), custom_call_target="tpu_custom_call" | custom-call | flops 3758096384 | bytes 12582912 | tf_op jit(solution)/shard_map/second_layer/pallas_call | solution.py:189
  179.0 2.4 %collective-permute-start.20 = (f32[4,2]{1,0:T(4,128)S(1)}, f32[4,2]{1,0:T(4,128)S(1)}, u32[]{:S(2)}, u32[]{:S(2)}) collective-permute-start(f32[4,2]{1,0:T(4,128)S(1)} %slice.128), channel_id=1, source_target_pairs={{0,16},{4,20},{8,24},{12,28},{16,0},{20,4},{24,8},{28,12},{32,48},... | collective-permute-start | bytes 104 | tf_op jit(solution)/shard_map/ppermute | solution.py:309
  181.4 1.6 collective-permute-done.20
  183.1 1.1 collective-permute-start.21
  184.1 1.4 collective-permute-done.21
  185.5 2.8 %collective-permute-start.22 = (f32[1,2]{1,0:T(1,128)S(1)}, f32[1,2]{1,0:T(1,128)S(1)}, u32[]{:S(2)}, u32[]{:S(2)}) collective-permute-start(f32[1,2]{1,0:T(1,128)S(1)} %slice.132), channel_id=1, source_target_pairs={{0,4},{4,0},{8,12},{12,8},{16,20},{20,16},{24,28},{28,24},{32,36},... | collective-permute-start | bytes 32 | tf_op jit(solution)/shard_map/ppermute | solution.py:309
  188.3 0.8 collective-permute-done.22
  189.1 2.4 %collective-permute-done.23 = f32[1,2]{1,0:T(1,128)S(1)} collective-permute-done((f32[1,2]{1,0:T(1,128)S(1)}, f32[1,2]{1,0:T(1,128)S(1)}, u32[]{:S(2)}, u32[]{:S(2)}) %collective-permute-start.23) | collective-permute-done | bytes 40 | tf_op jit(solution)/shard_map/ppermute | solution.py:311
  191.5 5.1 %collective-permute-start.24 = (f32[1,2]{1,0:T(1,128)S(1)}, f32[1,2]{1,0:T(1,128)S(1)}, u32[]{:S(2)}, u32[]{:S(2)}) collective-permute-start(f32[1,2]{1,0:T(1,128)S(1)} %max.30), channel_id=1, source_target_pairs={{0,2},{1,3},{2,0},{3,1},{4,6},{5,7},{6,4},{7,5},{8,10},{9,11},{10,... | collective-permute-start | bytes 32 | tf_op jit(solution)/shard_map/ppermute | solution.py:311
  196.6 0.9 collective-permute-done.24
  197.5 0.6 fusion.6
  198.2 1.3 subtract_multiply_fusion.extra_ref
  199.4 0.6 broadcast_in_dim.32.fb_ref
  200.7 7.5 %last_layer.1 = f32[16,1024]{1,0:T(8,128)} custom-call(bf16[1024,512]{1,0:T(8,128)(2,1)} %get-tuple-element.13.mine_ref, bf16[1024,512]{1,0:T(8,128)(2,1)} %copy-done.2, bf16[1024,512]{1,0:T(8,128)(2,1)} %get-tuple-element.12.pay_ref, bf16[1024,512]{1,0:T(8,128)(2,1)} %collective-permute-done.ca_ref, bf16[1024,512]{1,0:T(8,128)(2,1)} %broadcast_select_fusion.2.cb_ref, ...), custom_call_target="tpu_custom_call" | custom-call | flops 1879048192 | bytes 10485760 | tf_op jit(solution)/shard_map/last_layer/pallas_call | solution.py:234
  208.2 0.8 slice.152
  208.9 2.1 collective-permute-start.25
  211.0 0.8 collective-permute-done.25
  211.8 0.8 slice_add_fusion
  212.6 5.4 %collective-permute-start.27 = (f32[1,1024]{1,0:T(1,128)S(1)}, f32[1,1024]{1,0:T(1,128)S(1)}, u32[]{:S(2)}, u32[]{:S(2)}) collective-permute-start(f32[1,1024]{1,0:T(1,128)S(1)} %slice_add_fusion), channel_id=1, source_target_pairs={{2,4},{3,5},{4,2},{5,3},{10,12},{11,13},{12,10},{13,11},{18,20},{1... | collective-permute-start | bytes 12296 | tf_op jit(solution)/shard_map/ppermute | solution.py:338
  218.0 0.7 collective-permute-start.26
  218.6 0.6 collective-permute-done.27
  219.2 3.0 %collective-permute-done.26 = f32[1,1024]{1,0:T(1,128)S(1)} collective-permute-done((f32[1,1024]{1,0:T(1,128)S(1)}, f32[1,1024]{1,0:T(1,128)S(1)}, u32[]{:S(2)}, u32[]{:S(2)}) %collective-permute-start.26) | collective-permute-done | bytes 4128 | tf_op jit(solution)/shard_map/ppermute | solution.py:337
  222.3 0.6 maximum_select_fusion
  (73 shorter events, 3.4 us)
Async XLA Ops:
  11.1 16.7 %copy-start.4 = (bf16[2,256]{1,0:T(2,128)(2,1)S(1)}, bf16[2,256]{1,0:T(2,128)(2,1)}, u32[]{:S(2)}) copy-start(bf16[2,256]{1,0:T(2,128)(2,1)} %param.11) | copy-start | bytes 3076
  11.2 19.1 %copy-start = (bf16[2,1024,512]{2,1,0:T(8,128)(2,1)S(1)}, bf16[2,1024,512]{2,1,0:T(8,128)(2,1)}, u32[]{:S(2)}) copy-start(bf16[2,1024,512]{2,1,0:T(8,128)(2,1)} %param.16) | copy-start | bytes 6291460
  11.2 137.5 %all-to-all-start = ((bf16[256,8,512]{2,1,0:T(8,128)(2,1)}), bf16[256,8,512]{2,1,0:T(8,128)(2,1)}, u32[]{:S(2)}, u32[]{:S(2)}) async-start(bf16[256,8,512]{2,1,0:T(8,128)(2,1)} %bitcast.35), calls=%async_computation | async-start | bytes 4194304 | tf_op jit(solution)/shard_map/all_to_all | solution.py:281
  27.8 11.6 %collective-permute-start.4 = (bf16[2,256]{1,0:T(2,128)(2,1)S(1)}, bf16[2,256]{1,0:T(2,128)(2,1)S(1)}, u32[]{:S(2)}, u32[]{:S(2)}) collective-permute-start(bf16[2,256]{1,0:T(2,128)(2,1)S(1)} %copy-done.4), channel_id=1, source_target_pairs={{0,4},{1,5},{2,6},{3,7},{4,0},{5,1},{6,2},{7,3},{8,12},{9,13},{10,... | collective-permute-start | bytes 3080 | tf_op jit(solution)/shard_map/ppermute | solution.py:313
  30.1 8.2 %collective-permute-start.11 = (bf16[1,2,256]{2,1,0:T(2,128)(2,1)S(1)}, bf16[1,2,256]{2,1,0:T(2,128)(2,1)S(1)}, u32[]{:S(2)}, u32[]{:S(2)}) collective-permute-start(bf16[1,2,256]{2,1,0:T(2,128)(2,1)S(1)} %bitcast.36), channel_id=1, source_target_pairs={{0,4},{4,0},{8,12},{12,8},{16,20},{20,16},{24,28},{28,24},{32,36},... | collective-permute-start | bytes 3080 | tf_op jit(solution)/shard_map/ppermute | solution.py:300
  30.2 7.4 %copy-start.6 = (bf16[768]{0:T(1024)(128)(2,1)S(1)}, bf16[768]{0:T(1024)(128)(2,1)}, u32[]{:S(2)}) copy-start(bf16[768]{0:T(1024)(128)(2,1)} %param.20) | copy-start | bytes 4612
  30.2 7.4 %copy-start.5 = (f32[2,768]{1,0:T(2,128)S(1)}, f32[2,768]{1,0:T(2,128)}, u32[]{:S(2)}) copy-start(f32[2,768]{1,0:T(2,128)} %param.19) | copy-start | bytes 18436
  31.4 108.8 %collective-permute-start.1 = (bf16[1024,512]{1,0:T(8,128)(2,1)S(1)}, bf16[1024,512]{1,0:T(8,128)(2,1)}, u32[]{:S(2)}, u32[]{:S(2)}) collective-permute-start(bf16[1024,512]{1,0:T(8,128)(2,1)S(1)} %get-tuple-element.17), channel_id=1, source_target_pairs={{2,4},{3,5},{4,2},{5,3},{10,12},{11,13},{12,10},{13,11},{18,20},{1... | collective-permute-start | bytes 3145736 | tf_op jit(solution)/shard_map/ppermute | solution.py:286
  34.6 86.6 %collective-permute-start.2 = (bf16[2,768,512]{2,1,0:T(8,128)(2,1)}, bf16[2,768,512]{2,1,0:T(8,128)(2,1)}, u32[]{:S(2)}, u32[]{:S(2)}) collective-permute-start(bf16[2,768,512]{2,1,0:T(8,128)(2,1)} %param.17), channel_id=1, source_target_pairs={{0,1},{1,0},{2,5},{3,4},{4,3},{5,2},{6,7},{7,6},{8,9},{9,8},{10,13... | collective-permute-start | bytes 4718600 | tf_op jit(solution)/shard_map/ppermute | solution.py:289
  35.6 113.0 %collective-permute-start = (bf16[1024,512]{1,0:T(8,128)(2,1)}, bf16[1024,512]{1,0:T(8,128)(2,1)}, u32[]{:S(2)}, u32[]{:S(2)}) collective-permute-start(bf16[1024,512]{1,0:T(8,128)(2,1)} %get-tuple-element.18), channel_id=1, source_target_pairs={{0,1},{1,0},{2,5},{3,4},{4,3},{5,2},{6,7},{7,6},{8,9},{9,8},{10,13... | collective-permute-start | bytes 3145736 | tf_op jit(solution)/shard_map/ppermute | solution.py:284
  38.4 104.1 %collective-permute-start.6 = (bf16[2,512,768]{2,1,0:T(8,128)(2,1)}, bf16[2,512,768]{2,1,0:T(8,128)(2,1)}, u32[]{:S(2)}, u32[]{:S(2)}) collective-permute-start(bf16[2,512,768]{2,1,0:T(8,128)(2,1)} %param.18), channel_id=1, source_target_pairs={{0,1},{1,0},{2,5},{3,4},{4,3},{5,2},{6,7},{7,6},{8,9},{9,8},{10,13... | collective-permute-start | bytes 4718600 | tf_op jit(solution)/shard_map/ppermute | solution.py:290
  39.4 2.9 %collective-permute-start.12 = (bf16[2,2,256]{2,1,0:T(2,128)(2,1)S(1)}, bf16[2,2,256]{2,1,0:T(2,128)(2,1)S(1)}, u32[]{:S(2)}, u32[]{:S(2)}) collective-permute-start(bf16[2,2,256]{2,1,0:T(2,128)(2,1)S(1)} %pad_maximum_fusion.3), channel_id=1, source_target_pairs={{0,8},{4,12},{8,0},{12,4},{16,24},{20,28},{24,16},{28,20},{32,40},... | collective-permute-start | bytes 6152 | tf_op jit(solution)/shard_map/ppermute | solution.py:300
  42.4 4.4 %collective-permute-start.13 = (bf16[4,2,256]{2,1,0:T(2,128)(2,1)S(1)}, bf16[4,2,256]{2,1,0:T(2,128)(2,1)S(1)}, u32[]{:S(2)}, u32[]{:S(2)}) collective-permute-start(bf16[4,2,256]{2,1,0:T(2,128)(2,1)S(1)} %pad_maximum_fusion.2), channel_id=1, source_target_pairs={{0,16},{4,20},{8,24},{12,28},{16,0},{20,4},{24,8},{28,12},{32,48},... | collective-permute-start | bytes 12296 | tf_op jit(solution)/shard_map/ppermute | solution.py:300
  46.8 65.0 %collective-permute-start.8 = (f32[3,768]{1,0:T(4,128)S(1)}, f32[3,768]{1,0:T(4,128)S(1)}, u32[]{:S(2)}, u32[]{:S(2)}) collective-permute-start(f32[3,768]{1,0:T(4,128)S(1)} %pad_maximum_fusion), channel_id=1, source_target_pairs={{0,1},{1,0},{2,5},{3,4},{4,3},{5,2},{6,7},{7,6},{8,9},{9,8},{10,13... | collective-permute-start | bytes 27656 | tf_op jit(solution)/shard_map/ppermute | solution.py:291
  111.8 2.5 %collective-permute-start.14 = (bf16[8,2,256]{2,1,0:T(2,128)(2,1)S(1)}, bf16[8,2,256]{2,1,0:T(2,128)(2,1)S(1)}, u32[]{:S(2)}, u32[]{:S(2)}) collective-permute-start(bf16[8,2,256]{2,1,0:T(2,128)(2,1)S(1)} %pad_maximum_fusion.1), channel_id=1, source_target_pairs={{0,32},{4,36},{8,40},{12,44},{16,48},{20,52},{24,56},{28,60},{32,0... | collective-permute-start | bytes 24584 | tf_op jit(solution)/shard_map/ppermute | solution.py:300
  114.3 5.6 %collective-permute-start.9 = (f32[3,768]{1,0:T(4,128)S(1)}, f32[3,768]{1,0:T(4,128)S(1)}, u32[]{:S(2)}, u32[]{:S(2)}) collective-permute-start(f32[3,768]{1,0:T(4,128)S(1)} %collective-permute-done.8), channel_id=1, source_target_pairs={{0,3},{1,2},{6,5},{7,4},{8,11},{9,10},{14,13},{15,12},{16,19},{17,... | collective-permute-start | bytes 27656 | tf_op jit(solution)/shard_map/ppermute | solution.py:294
  120.0 3.7 %collective-permute-start.15 = (bf16[16,2,256]{2,1,0:T(2,128)(2,1)S(1)}, bf16[16,2,256]{2,1,0:T(2,128)(2,1)S(1)}, u32[]{:S(2)}, u32[]{:S(2)}) collective-permute-start(bf16[16,2,256]{2,1,0:T(2,128)(2,1)S(1)} %get-tuple-element.35), channel_id=1, source_target_pairs={{0,64},{4,68},{8,72},{12,76},{16,80},{20,84},{24,88},{28,92},{32,9... | collective-permute-start | bytes 49160 | tf_op jit(solution)/shard_map/ppermute | solution.py:300
  121.2 26.0 %collective-permute-start.3 = (bf16[2,768,512]{2,1,0:T(8,128)(2,1)}, bf16[2,768,512]{2,1,0:T(8,128)(2,1)S(1)}, u32[]{:S(2)}, u32[]{:S(2)}) collective-permute-start(bf16[2,768,512]{2,1,0:T(8,128)(2,1)} %collective-permute-done.2), channel_id=1, source_target_pairs={{0,3},{1,2},{6,5},{7,4},{8,11},{9,10},{14,13},{15,12},{16,19},{17,... | collective-permute-start | bytes 4718600 | tf_op jit(solution)/shard_map/ppermute | solution.py:292
  123.7 6.8 %collective-permute-start.16 = (bf16[32,2,256]{2,1,0:T(2,128)(2,1)S(1)}, bf16[32,2,256]{2,1,0:T(2,128)(2,1)S(1)}, u32[]{:S(2)}, u32[]{:S(2)}) collective-permute-start(bf16[32,2,256]{2,1,0:T(2,128)(2,1)S(1)} %get-tuple-element.27), channel_id=1, source_target_pairs={{0,128},{4,132},{8,136},{12,140},{16,144},{20,148},{24,152},{28,15... | collective-permute-start | bytes 98312 | tf_op jit(solution)/shard_map/ppermute | solution.py:300
  132.5 6.6 %collective-permute-start.17 = (f32[32,2]{1,0:T(8,128)S(1)}, f32[32,2]{1,0:T(8,128)S(1)}, u32[]{:S(2)}, u32[]{:S(2)}) collective-permute-start(f32[32,2]{1,0:T(8,128)S(1)} %slice.122), channel_id=1, source_target_pairs={{0,128},{4,132},{8,136},{12,140},{16,144},{20,148},{24,152},{28,15... | collective-permute-start | bytes 776 | tf_op jit(solution)/shard_map/ppermute | solution.py:309
  139.1 24.6 %collective-permute-start.18 = (f32[16,2]{1,0:T(8,128)S(1)}, f32[16,2]{1,0:T(8,128)S(1)}, u32[]{:S(2)}, u32[]{:S(2)}) collective-permute-start(f32[16,2]{1,0:T(8,128)S(1)} %slice.149), channel_id=1, source_target_pairs={{0,64},{4,68},{8,72},{12,76},{16,80},{20,84},{24,88},{28,92},{32,9... | collective-permute-start | bytes 392 | tf_op jit(solution)/shard_map/ppermute | solution.py:309
  142.5 24.8 %collective-permute-start.7 = (bf16[2,512,768]{2,1,0:T(8,128)(2,1)}, bf16[2,512,768]{2,1,0:T(8,128)(2,1)}, u32[]{:S(2)}, u32[]{:S(2)}) collective-permute-start(bf16[2,512,768]{2,1,0:T(8,128)(2,1)} %collective-permute-done.6), channel_id=1, source_target_pairs={{2,3},{3,2},{4,5},{5,4},{10,11},{11,10},{12,13},{13,12},{18,19},{1... | collective-permute-start | bytes 4718600 | tf_op jit(solution)/shard_map/ppermute | solution.py:293
  157.7 12.5 %collective-permute-start.5 = (bf16[1024,512]{1,0:T(8,128)(2,1)}, bf16[1024,512]{1,0:T(8,128)(2,1)S(1)}, u32[]{:S(2)}, u32[]{:S(2)}) collective-permute-start(bf16[1024,512]{1,0:T(8,128)(2,1)} %get-tuple-element.11.mine_ref), channel_id=1, source_target_pairs={{0,4},{1,5},{2,6},{3,7},{4,0},{5,1},{6,2},{7,3},{8,12},{9,13},{10,... | collective-permute-start | bytes 3145736 | tf_op jit(solution)/shard_map/ppermute | solution.py:323
  163.7 3.6 %copy-start.1 = (bf16[2,512,768]{2,1,0:T(8,128)(2,1)S(1)}, bf16[2,512,768]{2,1,0:T(8,128)(2,1)}, u32[]{:S(2)}) copy-start(bf16[2,512,768]{2,1,0:T(8,128)(2,1)} %param.18) | copy-start | bytes 4718596
  163.7 15.3 %collective-permute-start.19 = (f32[8,2]{1,0:T(8,128)S(1)}, f32[8,2]{1,0:T(8,128)S(1)}, u32[]{:S(2)}, u32[]{:S(2)}) collective-permute-start(f32[8,2]{1,0:T(8,128)S(1)} %slice.151), channel_id=1, source_target_pairs={{0,32},{4,36},{8,40},{12,44},{16,48},{20,52},{24,56},{28,60},{32,0... | collective-permute-start | bytes 200 | tf_op jit(solution)/shard_map/ppermute | solution.py:309
  170.2 1.0 copy-start.7
  171.2 27.0 %copy-start.3 = (f32[16,1024]{1,0:T(8,128)S(1)}, f32[16,1024]{1,0:T(8,128)}, u32[]{:S(2)}) copy-start(f32[16,1024]{1,0:T(8,128)} %get-tuple-element.16) | copy-start | bytes 196612
  179.0 20.4 %collective-permute-start.10 = (bf16[1024,512]{1,0:T(8,128)(2,1)}, bf16[1024,512]{1,0:T(8,128)(2,1)S(1)}, u32[]{:S(2)}, u32[]{:S(2)}) collective-permute-start(bf16[1024,512]{1,0:T(8,128)(2,1)} %get-tuple-element.13.mine_ref), channel_id=1, source_target_pairs={{0,4},{1,5},{2,6},{3,7},{4,0},{5,1},{6,2},{7,3},{8,12},{9,13},{10,... | collective-permute-start | bytes 3145736 | tf_op jit(solution)/shard_map/ppermute | solution.py:327
  179.0 4.0 %collective-permute-start.20 = (f32[4,2]{1,0:T(4,128)S(1)}, f32[4,2]{1,0:T(4,128)S(1)}, u32[]{:S(2)}, u32[]{:S(2)}) collective-permute-start(f32[4,2]{1,0:T(4,128)S(1)} %slice.128), channel_id=1, source_target_pairs={{0,16},{4,20},{8,24},{12,28},{16,0},{20,4},{24,8},{28,12},{32,48},... | collective-permute-start | bytes 104 | tf_op jit(solution)/shard_map/ppermute | solution.py:309
  183.1 2.4 %collective-permute-start.21 = (f32[2,2]{1,0:T(2,128)S(1)}, f32[2,2]{1,0:T(2,128)S(1)}, u32[]{:S(2)}, u32[]{:S(2)}) collective-permute-start(f32[2,2]{1,0:T(2,128)S(1)} %slice.130), channel_id=1, source_target_pairs={{0,8},{4,12},{8,0},{12,4},{16,24},{20,28},{24,16},{28,20},{32,40},... | collective-permute-start | bytes 56 | tf_op jit(solution)/shard_map/ppermute | solution.py:309
  185.5 3.6 %collective-permute-start.22 = (f32[1,2]{1,0:T(1,128)S(1)}, f32[1,2]{1,0:T(1,128)S(1)}, u32[]{:S(2)}, u32[]{:S(2)}) collective-permute-start(f32[1,2]{1,0:T(1,128)S(1)} %slice.132), channel_id=1, source_target_pairs={{0,4},{4,0},{8,12},{12,8},{16,20},{20,16},{24,28},{28,24},{32,36},... | collective-permute-start | bytes 32 | tf_op jit(solution)/shard_map/ppermute | solution.py:309
  189.1 2.4 %collective-permute-start.23 = (f32[1,2]{1,0:T(1,128)S(1)}, f32[1,2]{1,0:T(1,128)S(1)}, u32[]{:S(2)}, u32[]{:S(2)}) collective-permute-start(f32[1,2]{1,0:T(1,128)S(1)} %slice_maximum_fusion.4), channel_id=1, source_target_pairs={{0,1},{1,0},{2,3},{3,2},{4,5},{5,4},{6,7},{7,6},{8,9},{9,8},{10,11... | collective-permute-start | bytes 32 | tf_op jit(solution)/shard_map/ppermute | solution.py:311
  191.5 6.0 %collective-permute-start.24 = (f32[1,2]{1,0:T(1,128)S(1)}, f32[1,2]{1,0:T(1,128)S(1)}, u32[]{:S(2)}, u32[]{:S(2)}) collective-permute-start(f32[1,2]{1,0:T(1,128)S(1)} %max.30), channel_id=1, source_target_pairs={{0,2},{1,3},{2,0},{3,1},{4,6},{5,7},{6,4},{7,5},{8,10},{9,11},{10,... | collective-permute-start | bytes 32 | tf_op jit(solution)/shard_map/ppermute | solution.py:311
  199.4 1.2 copy-start.2
  208.9 2.9 %collective-permute-start.25 = (f32[1,1024]{1,0:T(1,128)S(1)}, f32[1,1024]{1,0:T(1,128)S(1)}, u32[]{:S(2)}, u32[]{:S(2)}) collective-permute-start(f32[1,1024]{1,0:T(1,128)S(1)} %slice.152), channel_id=1, source_target_pairs={{0,4},{1,5},{2,6},{3,7},{4,0},{5,1},{6,2},{7,3},{8,12},{9,13},{10,... | collective-permute-start | bytes 12296 | tf_op jit(solution)/shard_map/ppermute | solution.py:336
  212.6 6.7 %collective-permute-start.27 = (f32[1,1024]{1,0:T(1,128)S(1)}, f32[1,1024]{1,0:T(1,128)S(1)}, u32[]{:S(2)}, u32[]{:S(2)}) collective-permute-start(f32[1,1024]{1,0:T(1,128)S(1)} %slice_add_fusion), channel_id=1, source_target_pairs={{2,4},{3,5},{4,2},{5,3},{10,12},{11,13},{12,10},{13,11},{18,20},{1... | collective-permute-start | bytes 12296 | tf_op jit(solution)/shard_map/ppermute | solution.py:338
  218.0 4.3 %collective-permute-start.26 = (f32[1,1024]{1,0:T(1,128)S(1)}, f32[1,1024]{1,0:T(1,128)S(1)}, u32[]{:S(2)}, u32[]{:S(2)}) collective-permute-start(f32[1,1024]{1,0:T(1,128)S(1)} %slice_add_fusion), channel_id=1, source_target_pairs={{0,1},{1,0},{2,5},{3,4},{4,3},{5,2},{6,7},{7,6},{8,9},{9,8},{10,13... | collective-permute-start | bytes 12296 | tf_op jit(solution)/shard_map/ppermute | solution.py:337

commit v2 on v0

v2 whole, which is shorter than its diff:
```python
import functools

import jax
import jax.numpy as jnp
from jax import lax
from jax.experimental import pallas as pl
from jax.experimental.pallas import tpu as pltpu
from jax.sharding import PartitionSpec as P

BF = jnp.bfloat16
F32 = jnp.float32
AXES = ("shard", "tp")
VMEM = pl.BlockSpec(memory_space=pltpu.VMEM)
SMEM = pl.BlockSpec(memory_space=pltpu.SMEM)
PARAMS = pltpu.CompilerParams(vmem_limit_bytes=24 * 1024 * 1024)


def group_perm(groups, step, member=lambda x, c: True, turn=lambda x, c: 0):
    pairs = []
    for g in range(groups):
        for c in range(2):
            for x in range(4):
                if member(x, c):
                    x2, c2 = step(x, c)
                    g2 = g // 4 * 4 + (g + turn(x, c)) % 4
                    pairs.append((g * 8 + c * 4 + x, g2 * 8 + c2 * 4 + x2))
    return pairs


def is_home(x, c):
    return x // 2 == c


def is_away(x, c):
    return x // 2 != c


def near(x, c):
    return (x ^ 1, x // 2) if is_home(x, c) else (x ^ 3, x // 2)


def dot(a, b):
    return jnp.dot(a, b, preferred_element_type=F32)


def dot_nt(a, b):
    return lax.dot_general(a, b, (((1,), (1,)), ((), ())), preferred_element_type=F32)


def in_vmem(kernel, name, outs, scratch, mflops, mbytes, scalars, arrays):
    return pl.pallas_call(
        kernel,
        in_specs=[SMEM] * len(scalars) + [VMEM] * len(arrays),
        out_specs=[VMEM] * len(outs),
        out_shape=[jax.ShapeDtypeStruct(shape, dtype) for shape, dtype in outs],
        scratch_shapes=scratch,
        compiler_params=PARAMS,
        cost_estimate=pl.CostEstimate(
            flops=mflops << 20, bytes_accessed=mbytes << 20, transcendentals=0
        ),
        name=name,
    )(*scalars, *arrays)


def pick_kernel(kept_ref, count_ref, emb_ref, attr_ref, out_ref):
    slots, persons = kept_ref.shape
    items = emb_ref.shape[0]
    live = lax.broadcasted_iota(jnp.int32, (slots, persons), 0) < count_ref[...]
    wanted = jnp.where(live, kept_ref[...], 4095)
    digits = jnp.concatenate([wanted >> 6, wanted & 63], 0).astype(F32).astype(BF)
    n = 256
    for at in range(0, persons * slots, n):
        row = lax.broadcasted_iota(jnp.int32, (n, persons), 0) + at
        owner = (row // slots == lax.broadcasted_iota(jnp.int32, (n, persons), 1)).astype(BF)
        both = dot_nt(owner, digits)
        lane = lax.broadcasted_iota(jnp.int32, (n, 2 * slots), 1)
        slot = lax.broadcasted_iota(jnp.int32, (n, 2 * slots), 0) % slots
        high = jnp.where(lane == slot, both * 64.0, 0.0)
        low = jnp.where(lane == slot + slots, both, 0.0)
        rows = jnp.sum(high + low, axis=1, keepdims=True).astype(jnp.int32)
        hot = (lax.broadcasted_iota(jnp.int32, (n, items), 1) == rows).astype(BF)
        unused = rows >= items
        odd = (lax.broadcasted_iota(jnp.int32, (n, 1), 0) // slots) % 2 == 1
        for c in range(2):
            tables = (
                (emb_ref[...], attr_ref[:, 0:256])
                if c == 0
                else (attr_ref[:, 256:512], attr_ref[:, 512:768])
            )
            low, high = (jnp.where(unused, jnp.inf, dot(hot, t)) for t in tables)
            first = jnp.where(odd, low, high).astype(BF)
            second = jnp.where(odd, high, low).astype(BF)
            for g in range(n // 32):
                out_ref[at // 32 + g, c, :, 0:256] = first[g * 32 : (g + 1) * 32]
                out_ref[at // 32 + g, c, :, 256:512] = second[g * 32 : (g + 1) * 32]


def choose(flags, layer, own, near_x, far_x, near_y, far_y, dst_a, dst_b):
    home = flags[0] == 1
    by_x = flags[1] == layer
    dst_a[...] = jnp.where(by_x, near_x[...], near_y[...])
    dst_b[...] = jnp.where(home, own[layer], jnp.where(by_x, far_x[...], far_y[...]))


def first_kernel(
    flags, recv_ref, ca_ref, cb_ref, u_ref, v0, v1, v2, v3, v4, pay_ref, piece_ref, logit_ref,
    clean, place, va_ref, vb_ref,
):
    slots = recv_ref.shape[0]
    blk = 256
    choose(flags, 0, v0, v1, v2, v3, v4, va_ref, vb_ref)
    r = lax.broadcasted_iota(jnp.int32, (blk, blk), 0)
    q = lax.broadcasted_iota(jnp.int32, (blk, blk), 1)
    upper = (r <= q).astype(BF)
    lane0 = (lax.broadcasted_iota(jnp.int32, (16, 128), 1) == 0).astype(BF)
    before = jnp.zeros((16, 1), F32)
    for i in range(slots // blk):
        got = recv_ref[i * blk : (i + 1) * blk, :].astype(F32)
        live = got < jnp.inf
        clean[i * blk : (i + 1) * blk, :] = jnp.where(live, got, 0.0).astype(BF)
        marks = dot_nt(lane0, live[:, 0:128].astype(F32).astype(BF))
        upto = dot(marks.astype(BF), upper) + before
        place[:, i * blk : (i + 1) * blk] = jnp.where(marks > 0.5, upto - 1.0, -1.0)
        before = upto[:, blk - 1 : blk]
    rows = 256
    for at in range(0, pay_ref.shape[0], rows):
        here = pl.ds(at, rows)
        k = (lax.broadcasted_iota(jnp.int32, (rows, slots), 0) + at).astype(F32)
        hot = (k == place[0:1, :]).astype(BF)
        pay = dot(hot, clean[...]).astype(BF)
        pay_ref[here] = pay
        piece = (
            dot(pay[:, 0:256], va_ref[0:256])
            + dot(ca_ref[here], va_ref[256:768])
            + dot(pay[:, 256:512], vb_ref[0:256])
            + dot(cb_ref[here], vb_ref[256:768])
        )
        piece_ref[here] = piece.astype(BF)
        logit_ref[:, here] = dot_nt(u_ref[...], pay)


def cross(x0, hidden, offset, x):
    x0 = x0.astype(F32)
    return (x0 * (hidden + offset) + x.astype(F32)).astype(BF)


def second_kernel(
    flags, mine_ref, other_ref, pay_ref, ca_ref, cb_ref, ba_ref, bb_ref,
    u0, u1, u2, u3, u4, v0, v1, v2, v3, v4,
    xa_ref, xb_ref, piece_ref, ua_ref, ub_ref, va_ref, vb_ref,
):
    choose(flags, 0, u0, u1, u2, u3, u4, ua_ref, ub_ref)
    choose(flags, 1, v0, v1, v2, v3, v4, va_ref, vb_ref)
    rows = 256
    for start in range(0, pay_ref.shape[0], rows):
        here = pl.ds(start, rows)
        proj = (mine_ref[here].astype(F32) + other_ref[here].astype(F32)).astype(BF)
        piece = None
        for x_ref, u_ref, b_ref, v_ref, c_ref, at in (
            (xa_ref, ua_ref, ba_ref, va_ref, ca_ref, 0),
            (xb_ref, ub_ref, bb_ref, vb_ref, cb_ref, 256),
        ):
            hidden = dot(proj, u_ref[...])
            pay = pay_ref[here, at : at + 256]
            ctx = c_ref[here]
            x_ref[here, 0:256] = cross(pay, hidden[:, 0:256], b_ref[0:1, 0:256], pay)
            x_ref[here, 256:768] = cross(ctx, hidden[:, 256:768], b_ref[0:1, 256:768], ctx)
            term = dot(x_ref[here], v_ref[...])
            piece = term if piece is None else piece + term
        piece_ref[here] = piece.astype(BF)


def last_kernel(
    flags, coefficient, mine_ref, other_ref, pay_ref, ca_ref, cb_ref, xa_ref, xb_ref,
    sa_ref, sb_ref, logit_ref, u0, u1, u2, u3, u4, score_ref, ua_ref, ub_ref,
):
    choose(flags, 1, u0, u1, u2, u3, u4, ua_ref, ub_ref)
    rows = 256
    for start in range(0, pay_ref.shape[0], rows):
        here = pl.ds(start, rows)
        proj = (mine_ref[here].astype(F32) + other_ref[here].astype(F32)).astype(BF)
        score = coefficient[0] * logit_ref[:, here]
        for x_ref, u_ref, s_ref, c_ref, at in (
            (xa_ref, ua_ref, sa_ref, ca_ref, 0),
            (xb_ref, ub_ref, sb_ref, cb_ref, 256),
        ):
            hidden = dot(proj, u_ref[...])
            low = cross(
                pay_ref[here, at : at + 256], hidden[:, 0:256], s_ref[1:2, 0:256], x_ref[here, 0:256]
            )
            high = cross(
                c_ref[here], hidden[:, 256:768], s_ref[1:2, 256:768], x_ref[here, 256:768]
            )
            out = jnp.broadcast_to(s_ref[2:3, :], (16, 768)).astype(BF)
            score = score + dot_nt(out[:, 0:256], low) + dot_nt(out[:, 256:768], high)
        score_ref[:, here] = score


def on_device(
    person_embedding,
    catalog_embedding,
    catalog_attributes,
    kept_part_entries,
    valid_slot_number,
    pair_attributes,
    lowrank_v_matrix,
    lowrank_u_matrix,
    interaction_offset,
    final_projection,
    similarity_coefficient,
):
    shards = lax.axis_size("shard")
    groups = shards // 2
    x = lax.axis_index("tp")
    core = lax.axis_index("shard") % 2
    home = x // 2 == core
    parity = x % 2
    move = functools.partial(lax.ppermute, axis_name=AXES)
    to_core = group_perm(groups, lambda x, c: (x, 1 - c))
    to_near = group_perm(groups, near)
    home_on = group_perm(groups, lambda x, c: (x ^ 3, c), is_home)
    away_swap = group_perm(groups, lambda x, c: (x ^ 1, c), is_away)
    ctx_near = group_perm(groups, lambda x, c: (x ^ 1, c) if is_home(x, c) else (x ^ 3, 1 - c))
    ctx_far = group_perm(groups, lambda x, c: (x ^ 2, 1 - c), is_away)
    stay = lambda x, c: (x, c)
    y_up = group_perm(groups, stay, turn=lambda x, c: 1)
    y_mixed = group_perm(groups, stay, turn=lambda x, c: -1 if is_home(x, c) else 1)
    y_down = group_perm(groups, stay, is_away, lambda x, c: -1)
    by = lax.axis_index("shard") // 2 % 2
    flags = jnp.stack([home.astype(jnp.int32), by])

    persons, _, kept = kept_part_entries.shape
    small = jnp.concatenate([interaction_offset, final_projection[None, :].astype(F32)], 0)
    small_a = move(small, perm=to_near)
    small_b = move(small, perm=ctx_far)
    emb_other = move(person_embedding, perm=to_core)
    masks = (16, 32, 8, 2, 4, 1)
    users = person_embedding[None]

    def double(users, mask):
        pairs = [(i, i ^ mask) for i in range(shards)]
        return jnp.concatenate([users, lax.ppermute(users, "shard", pairs)], 0)

    for mask in masks[:3]:
        users = double(users, mask)

    v_mine = lax.dynamic_index_in_dim(lowrank_v_matrix, by, 0, False)
    u_mine = lax.dynamic_index_in_dim(lowrank_u_matrix, by, 0, False)
    v_near = move(v_mine, perm=to_near)

    (parcel,) = in_vmem(
        pick_kernel, "pick_rows", [((persons // 4, 2, 4 * kept, 512), BF)], [], 4096, 6, [],
        [
            kept_part_entries[:, 0, :].T,
            valid_slot_number.T,
            catalog_embedding,
            catalog_attributes,
        ],
    )
    parcel = parcel.reshape(persons * 2, kept, 512)
    parcel, v_near, small_a, small_b, emb_other, users = lax.optimization_barrier(
        (parcel, v_near, small_a, small_b, emb_other, users)
    )
    recv = lax.all_to_all(parcel, AXES, split_axis=0, concat_axis=0, tiled=True)
    recv = recv.reshape(persons * 2 * kept, 512)

    u_near = move(u_mine, perm=to_near)
    v_far = move(v_near, perm=home_on)
    u_far = move(u_near, perm=away_swap)
    vs = (lowrank_v_matrix, v_near, v_far, move(v_near, perm=y_up), move(v_far, perm=y_down))
    us = (lowrank_u_matrix, u_near, u_far, move(u_near, perm=y_mixed), move(u_far, perm=y_down))
    small_b = jnp.where(home, small, small_b)

    ctx_a = move(lax.dynamic_index_in_dim(pair_attributes, 1 - parity, 0, False), perm=ctx_near)
    ctx_own = lax.dynamic_index_in_dim(pair_attributes, parity, 0, False)
    ctx_b = jnp.where(home, ctx_own, move(ctx_own, perm=ctx_far))

    for mask in masks[3:]:
        users = double(users, mask)
    all_scores = jnp.einsum(
        "ue,ie->ui", users.reshape(persons, -1), catalog_embedding, preferred_element_type=F32
    )
    best = jnp.max(all_scores, axis=1).reshape(shards, persons // shards)

    def halve(best, mask):
        half = best.shape[0] // 2
        pairs = [(i, i ^ mask) for i in range(shards)]
        return jnp.maximum(best[:half], lax.ppermute(best[half:], "shard", pairs))

    def over_x(best, flip):
        return jnp.maximum(best, lax.ppermute(best, "tp", [(i, i ^ flip) for i in range(4)]))

    for mask in masks[:2:-1]:
        best = halve(best, mask)

    query = lax.dynamic_slice_in_dim(jnp.where(home, person_embedding, emb_other), parity, 1, 0)
    query = jnp.where(core == 0, query, jnp.zeros_like(query))
    zero = jnp.zeros_like(query)
    query = jnp.where(
        parity == 1, jnp.concatenate([query, zero], 1), jnp.concatenate([zero, query], 1)
    )
    query = jnp.broadcast_to(query, (16, 512))

    surv = pair_attributes.shape[1]
    tall, wide, lanes = ((surv, 512), BF), ((surv, 768), BF), ((16, surv), F32)
    v_pair = [pltpu.VMEM((768, 512), BF)] * 2
    u_pair = [pltpu.VMEM((512, 768), BF)] * 2
    recv, best = lax.optimization_barrier((recv, best))
    step = over_x(best, 1)
    pay, piece, logit = in_vmem(
        first_kernel, "first_layer", [tall, tall, lanes],
        [pltpu.VMEM(recv.shape, BF), pltpu.VMEM((16, recv.shape[0]), F32)] + v_pair,
        4096, 8, [flags], [recv, ctx_a, ctx_b, query, *vs],
    )
    piece, best = lax.optimization_barrier((piece, step))
    other, best = lax.optimization_barrier((move(piece, perm=to_core), over_x(best, 2)))
    step = halve(best, masks[2])
    x_a, x_b, piece1 = in_vmem(
        second_kernel, "second_layer", [wide, wide, tall], u_pair + v_pair, 3584, 12, [flags],
        [piece, other, pay, ctx_a, ctx_b, small_a, small_b, *us, *vs],
    )
    piece1, best = lax.optimization_barrier((piece1, step))
    other1, best = lax.optimization_barrier((move(piece1, perm=to_core), halve(best, masks[1])))
    step = halve(best, masks[0])
    (score,) = in_vmem(
        last_kernel, "last_layer", [lanes], u_pair, 1792, 10, [flags, similarity_coefficient],
        [piece1, other1, pay, ctx_a, ctx_b, x_a, x_b, small_a, small_b, logit, *us],
    )
    score, best = lax.optimization_barrier((score, step))
    top = jnp.where(home, lax.dynamic_slice_in_dim(best, parity, 1, 1), 0.0)
    score = score[0:1] - similarity_coefficient[0] * top
    score = score + move(score, perm=to_core)
    score_a = move(score, perm=to_near)
    score_b = jnp.where(home, score, move(score, perm=ctx_far))
    return jnp.where(
        parity == 1,
        jnp.concatenate([score_a, score_b], 0),
        jnp.concatenate([score_b, score_a], 0),
    )


def solution(mesh):
    return jax.shard_map(
        on_device,
        mesh=mesh,
        in_specs=(
            P("shard", None),
            P(("shard", "tp"), None),
            P(("shard", "tp"), None),
            P(None, ("shard", "tp"), None),
            P(None, ("shard", "tp")),
            P("shard", None, "tp"),
            P(None, "tp", None),
            P(None, None, "tp"),
            P(None, "tp"),
            P("tp"),
            P(),
        ),
        out_specs=P("shard", None),
        check_vma=False,
    )
```

time: 455 us -> 183 us (0.40)
  blocking collectives: 127 us -> 0 us
  local copies, waits for them, and re-layouts: 116 us -> 9.37 us
  waiting for transfers between devices: 116 us -> 64.7 us
  starting transfers between devices: 44.2 us -> 76.3 us
  Pallas kernels: 0 us -> 25.4 us
  matrix products: 21 us -> 0.56 us
  between operations: 14.4 us -> 1.63 us
  other arithmetic: 12.9 us -> 4.4 us
    gather x11 -> x0, local copies, waits for them, and re-layouts: 95.1 us -> none  [the longest x1 35.4 us: on_device(): picked = jnp.take_along_axis(received_entries, source[:, :, None], axis=1)]
    pmax x1 -> x0, blocking collectives: 74.1 us -> none  [on_device(): best_all = lax.pmax(best_local, ('shard', 'tp'))]
    ppermute x0 -> x32, starting transfers between devices: none -> 65.4 us  [the longest x6 19.3 us: double(): return jnp.concatenate([users, lax.ppermute(users, 'shard', pairs)], 0)]
    ppermute x0 -> x32, waiting for transfers between devices: none -> 64.7 us  [the longest x1 30.1 us: on_device(): v_far = move(v_near, perm=home_on)]
    all_to_all x6 -> x1, waiting for transfers between devices: 59.4 us -> 0.01 us  [on_device(): recv = lax.all_to_all(parcel, AXES, split_axis=0, concat_axis=0, tiled=True)]
    psum x2 -> x0, waiting for transfers between devices: 56.7 us -> none  [on_device(): proj = lax.psum(partial_proj, 'tp').astype(jnp.float32).astype(jnp.bfloat16)]
    all_gather x1 -> x0, blocking collectives: 45.1 us -> none  [on_device(): users_all = lax.all_gather(person_embedding, 'shard', axis=0, tiled=True)]
    all_to_all x6 -> x1, starting transfers between devices: 44 us -> 11 us  [on_device(): recv = lax.all_to_all(parcel, AXES, split_axis=0, concat_axis=0, tiled=True)]
  transfers between devices with their start and end apart: 8 -> 33, of which waited for: 4 -> 13; matrix products, arithmetic and copies ran while one was open for 18% -> 5% of each run, Pallas kernels for 0% -> 14%
where the time goes in v2:
time: 183 us; the launch traced here: 182 us
  starting transfers between devices  76.3 us (42%)
  waiting for transfers between devices  64.7 us (35%)
  Pallas kernels  25.4 us (14%)
  local copies, waits for them, and re-layouts  9.37 us (5%)
  other arithmetic  4.4 us (2%)
    ppermute x1, waiting for transfers between devices, on_device(): v_far = move(v_near, perm=home_on)  30.1 us
    pallas_call x4, Pallas kernels, in_vmem(): pl.pallas_call(kernel, in_specs=[SMEM] * len(scalars) + [VMEM] * len(arra...  25.4 us
    ppermute x6, starting transfers between devices, double(): return jnp.concatenate([users, lax.ppermute(users, 'shard', pairs)], 0)  19.3 us
    ppermute x6, starting transfers between devices, halve(): return jnp.maximum(best[:half], lax.ppermute(best[half:], 'shard', pairs))  11.1 us
    all_to_all x1, starting transfers between devices, on_device(): recv = lax.all_to_all(parcel, AXES, split_axis=0, concat_axis=0, tiled=True)  11 us
    ppermute x1, waiting for transfers between devices, on_device(): move(u_far, perm=y_down)  8.09 us
    ppermute x6, waiting for transfers between devices, halve(): return jnp.maximum(best[:half], lax.ppermute(best[half:], 'shard', pairs))  7.88 us
    ppermute x1, waiting for transfers between devices, on_device(): u_near = move(u_mine, perm=to_near)  6.42 us
  transfers between devices with their start and end apart: 33, of which 13 were waited for; matrix products, arithmetic and copies ran while one was open for 5% of the time, Pallas kernels for 14%

profile of v2, /device:TPU:1, one launch (start us, length us, event | category | flops | bytes accessed | tf_op | source)
XLA Modules:
  0.0 182.5 jit_solution(851583601773415109)
XLA Ops:
  0.0 3.9 %collective-permute-start.4 = (bf16[1,2,256]{2,1,0:T(2,128)(2,1)}, bf16[1,2,256]{2,1,0:T(2,128)(2,1)S(1)}, u32[]{:S(2)}, u32[]{:S(2)}) collective-permute-start(bf16[1,2,256]{2,1,0:T(2,128)(2,1)} %bitcast.25), channel_id=1, source_target_pairs={{0,64},{4,68},{8,72},{12,76},{16,80},{20,84},{24,88},{28,92},{32,9... | collective-permute-start | bytes 3080 | tf_op jit(solution)/shard_map/ppermute | solution.py:242
  3.9 1.2 dynamic-slice_bitcast_fusion.3
  5.1 3.4 %collective-permute-start = (bf16[768,512]{1,0:T(8,128)(2,1)S(1)}, bf16[768,512]{1,0:T(8,128)(2,1)}, u32[]{:S(2)}, u32[]{:S(2)}) collective-permute-start(bf16[768,512]{1,0:T(8,128)(2,1)S(1)} %dynamic-slice_bitcast_fusion.3), channel_id=1, source_target_pairs={{0,1},{1,0},{2,5},{3,4},{4,3},{5,2},{6,7},{7,6},{8,9},{9,8},{10,13... | collective-permute-start | bytes 2359304 | tf_op jit(solution)/shard_map/ppermute | solution.py:249
  8.6 5.2 %collective-permute-start.5 = (bf16[2,2,256]{2,1,0:T(2,128)(2,1)S(1)}, bf16[2,2,256]{2,1,0:T(2,128)(2,1)S(1)}, u32[]{:S(2)}, u32[]{:S(2)}) collective-permute-start(bf16[2,2,256]{2,1,0:T(2,128)(2,1)S(1)} %pad_maximum_fusion.6), channel_id=1, source_target_pairs={{0,128},{4,132},{8,136},{12,140},{16,144},{20,148},{24,152},{28,15... | collective-permute-start | bytes 6152 | tf_op jit(solution)/shard_map/ppermute | solution.py:242
  13.8 2.3 %collective-permute-start.1 = (f32[3,768]{1,0:T(4,128)S(1)}, f32[3,768]{1,0:T(4,128)S(1)}, u32[]{:S(2)}, u32[]{:S(2)}) collective-permute-start(f32[3,768]{1,0:T(4,128)S(1)} %pad_maximum_fusion.3), channel_id=1, source_target_pairs={{0,1},{1,0},{2,5},{3,4},{4,3},{5,2},{6,7},{7,6},{8,9},{9,8},{10,13... | collective-permute-start | bytes 27656 | tf_op jit(solution)/shard_map/ppermute | solution.py:234
  16.1 2.2 %collective-permute-start.2 = (f32[3,768]{1,0:T(4,128)S(1)}, f32[3,768]{1,0:T(4,128)S(1)}, u32[]{:S(2)}, u32[]{:S(2)}) collective-permute-start(f32[3,768]{1,0:T(4,128)S(1)} %pad_maximum_fusion.3), channel_id=1, source_target_pairs={{2,4},{3,5},{4,2},{5,3},{10,12},{11,13},{12,10},{13,11},{18,20},{1... | collective-permute-start | bytes 27656 | tf_op jit(solution)/shard_map/ppermute | solution.py:235
  18.3 0.1 collective-permute-start.3
  18.4 0.8 collective-permute-start.6
  19.2 1.9 %copy-done.4 = bf16[2048,768]{1,0:T(8,128)(2,1)S(1)} copy-done((bf16[2048,768]{1,0:T(8,128)(2,1)S(1)}, bf16[2048,768]{1,0:T(8,128)(2,1)}, u32[]{:S(2)}) %copy-start.4) | copy-done | bytes 3145752
  21.1 6.8 %pick_rows.1 = bf16[32,2,32,512]{3,2,1,0:T(8,128)(2,1)} custom-call(s32[8,128]{1,0:T(8,128)S(1)} %bitcast.23, s32[1,128]{1,0:T(1,128)S(1)} %bitcast.24, bf16[2048,256]{1,0:T(8,128)(2,1)S(1)} %copy-done.3, bf16[2048,768]{1,0:T(8,128)(2,1)S(1)} %copy-done.4), custom_call_target="tpu_custom_call" | custom-call | flops 4294967296 | bytes 6291456 | tf_op jit(solution)/shard_map/pick_rows/pallas_call | solution.py:51
  28.0 0.6 copy-done.10
  28.5 11.0 %all-to-all-start = ((bf16[256,8,512]{2,1,0:T(8,128)(2,1)}), bf16[256,8,512]{2,1,0:T(8,128)(2,1)}, u32[]{:S(2)}, u32[]{:S(2)}) async-start(bf16[256,8,512]{2,1,0:T(8,128)(2,1)} %bitcast.5), calls=%async_computation | async-start | bytes 4194304 | tf_op jit(solution)/shard_map/all_to_all | solution.py:264
  39.5 1.5 collective-permute-start.7
  41.0 1.7 collective-permute-done.7
  42.8 3.3 %collective-permute-start.8 = (bf16[16,2,256]{2,1,0:T(2,128)(2,1)S(1)}, bf16[16,2,256]{2,1,0:T(2,128)(2,1)S(1)}, u32[]{:S(2)}, u32[]{:S(2)}) collective-permute-start(bf16[16,2,256]{2,1,0:T(2,128)(2,1)S(1)} %pad_maximum_fusion.2), channel_id=1, source_target_pairs={{0,16},{4,20},{8,24},{12,28},{16,0},{20,4},{24,8},{28,12},{32,48},... | collective-permute-start | bytes 49160 | tf_op jit(solution)/shard_map/ppermute | solution.py:242
  46.1 3.0 %dynamic-slice_bitcast_fusion = (bf16[1024,512]{1,0:T(8,128)(2,1)}, bf16[1024,512]{1,0:T(8,128)(2,1)}) fusion(bf16[2,1024,512]{2,1,0:T(8,128)(2,1)} %param.16, s32[]{:T(128)S(6)} %select_n.110, s32[]{:T(128)S(6)} %select_n.108), kind=kLoop, calls=%fused_computation.1 | loop fusion | bytes 4194312 | tf_op jit(solution)/shard_map/jit(dynamic_index_in_dim)/squeeze | solution.py:275
  49.1 5.4 %collective-permute-start.14 = (bf16[1024,512]{1,0:T(8,128)(2,1)}, bf16[1024,512]{1,0:T(8,128)(2,1)}, u32[]{:S(2)}, u32[]{:S(2)}) collective-permute-start(bf16[1024,512]{1,0:T(8,128)(2,1)} %get-tuple-element.53), channel_id=1, source_target_pairs={{2,4},{3,5},{4,2},{5,3},{10,12},{11,13},{12,10},{13,11},{18,20},{1... | collective-permute-start | bytes 3145736 | tf_op jit(solution)/shard_map/ppermute | solution.py:276
  54.5 0.4 collective-permute-start.13
  55.0 1.3 collective-permute-start.15
  56.3 4.6 %collective-permute-start.9 = (bf16[32,2,256]{2,1,0:T(2,128)(2,1)S(1)}, bf16[32,2,256]{2,1,0:T(2,128)(2,1)}, u32[]{:S(2)}, u32[]{:S(2)}) collective-permute-start(bf16[32,2,256]{2,1,0:T(2,128)(2,1)S(1)} %pad_maximum_fusion.1), channel_id=1, source_target_pairs={{0,4},{4,0},{8,12},{12,8},{16,20},{20,16},{24,28},{28,24},{32,36},... | collective-permute-start | bytes 98312 | tf_op jit(solution)/shard_map/ppermute | solution.py:242
  60.9 1.0 dynamic-slice_bitcast_fusion.2
  61.8 0.1 collective-permute-start.21
  61.9 0.9 pad_maximum_fusion
  62.8 0.6 convolution_reduce_fusion
  63.4 0.1 fusion.1
  63.5 0.1 slice.64
  63.6 0.4 collective-permute-start.10
  64.0 0.1 slice.62
  64.1 0.7 collective-permute-done.10
  64.8 0.3 collective-permute-start.11
  65.1 4.4 %collective-permute-done.11 = f32[16,2]{1,0:T(8,128)S(1)} collective-permute-done((f32[16,2]{1,0:T(8,128)S(1)}, f32[16,2]{1,0:T(8,128)S(1)}, u32[]{:S(2)}, u32[]{:S(2)}) %collective-permute-start.11) | collective-permute-done | bytes 160 | tf_op jit(solution)/shard_map/ppermute | solution.py:288
  69.6 30.1 %collective-permute-done.15.v2 = bf16[768,512]{1,0:T(8,128)(2,1)} collective-permute-done((bf16[768,512]{1,0:T(8,128)(2,1)}, bf16[768,512]{1,0:T(8,128)(2,1)}, u32[]{:S(2)}, u32[]{:S(2)}) %collective-permute-start.15) | collective-permute-done | bytes 786464 | tf_op jit(solution)/shard_map/ppermute | solution.py:268
  99.7 3.7 %collective-permute-start.17 = (bf16[768,512]{1,0:T(8,128)(2,1)}, bf16[768,512]{1,0:T(8,128)(2,1)}, u32[]{:S(2)}, u32[]{:S(2)}) collective-permute-start(bf16[768,512]{1,0:T(8,128)(2,1)} %collective-permute-done.15.v2), channel_id=1, source_target_pairs={{2,26},{3,27},{4,28},{5,29},{10,2},{11,3},{12,4},{13,5},{18,10},{1... | collective-permute-start | bytes 2359304 | tf_op jit(solution)/shard_map/ppermute | solution.py:270
  103.4 0.7 broadcast_select_fusion.5
  104.1 6.4 %collective-permute-done.21.u1 = bf16[512,768]{1,0:T(8,128)(2,1)S(1)} collective-permute-done((bf16[512,768]{1,0:T(8,128)(2,1)}, bf16[512,768]{1,0:T(8,128)(2,1)S(1)}, u32[]{:S(2)}, u32[]{:S(2)}) %collective-permute-start.21) | collective-permute-done | bytes 786464 | tf_op jit(solution)/shard_map/ppermute | solution.py:267
  110.5 0.7 collective-permute-start.12
  111.2 1.8 collective-permute-done.12
  113.0 2.2 %collective-permute-start.22 = (bf16[512,768]{1,0:T(8,128)(2,1)S(1)}, bf16[512,768]{1,0:T(8,128)(2,1)}, u32[]{:S(2)}, u32[]{:S(2)}) collective-permute-start(bf16[512,768]{1,0:T(8,128)(2,1)S(1)} %collective-permute-done.21.u1), channel_id=1, source_target_pairs={{2,3},{3,2},{4,5},{5,4},{10,11},{11,10},{12,13},{13,12},{18,19},{1... | collective-permute-start | bytes 2359304 | tf_op jit(solution)/shard_map/ppermute | solution.py:269
  115.2 1.4 broadcast_select_fusion.cb_ref
  116.6 1.3 collective-permute-start.18
  117.9 1.4 copy-done.1
  119.3 7.7 %first_layer.1 = (bf16[1024,512]{1,0:T(8,128)(2,1)S(1)}, bf16[1024,512]{1,0:T(8,128)(2,1)S(1)}, f32[16,1024]{1,0:T(8,128)S(1)}) custom-call(s32[2]{0:T(128)S(1)} %pad_add_fusion.flags, bf16[2048,512]{1,0:T(8,128)(2,1)} %bitcast.8.recv_ref, bf16[1024,512]{1,0:T(8,128)(2,1)} %collective-permute-done.13.ca_ref, ...), custom_call_target="tpu_custom_call" | custom-call | flops 4294967296 | bytes 8388608 | tf_op jit(solution)/shard_map/first_layer/pallas_call | solution.py:51
  127.0 0.1 collective-permute-start.19
  127.1 0.8 collective-permute-start.23
  127.9 3.9 %collective-permute-start.24 = (bf16[512,768]{1,0:T(8,128)(2,1)}, bf16[512,768]{1,0:T(8,128)(2,1)S(1)}, u32[]{:S(2)}, u32[]{:S(2)}) collective-permute-start(bf16[512,768]{1,0:T(8,128)(2,1)} %collective-permute-done.22.u2), channel_id=1, source_target_pairs={{2,26},{3,27},{4,28},{5,29},{10,2},{11,3},{12,4},{13,5},{18,10},{1... | collective-permute-start | bytes 2359304 | tf_op jit(solution)/shard_map/ppermute | solution.py:271
  131.8 0.3 collective-permute-start.20
  132.1 3.7 %collective-permute-done.20 = f32[8,2]{1,0:T(8,128)S(1)} collective-permute-done((f32[8,2]{1,0:T(8,128)S(1)}, f32[8,2]{1,0:T(8,128)S(1)}, u32[]{:S(2)}, u32[]{:S(2)}) %collective-permute-start.20) | collective-permute-done | bytes 96 | tf_op jit(solution)/shard_map/ppermute | solution.py:291
  135.8 1.3 collective-permute-start.25
  137.2 2.1 %collective-permute-done.23.u3 = bf16[512,768]{1,0:T(8,128)(2,1)S(1)} collective-permute-done((bf16[512,768]{1,0:T(8,128)(2,1)S(1)}, bf16[512,768]{1,0:T(8,128)(2,1)S(1)}, u32[]{:S(2)}, u32[]{:S(2)}) %collective-permute-start.23) | collective-permute-done | bytes 786464 | tf_op jit(solution)/shard_map/ppermute | solution.py:271
  139.2 8.1 %collective-permute-done.24.u4 = bf16[512,768]{1,0:T(8,128)(2,1)S(1)} collective-permute-done((bf16[512,768]{1,0:T(8,128)(2,1)}, bf16[512,768]{1,0:T(8,128)(2,1)S(1)}, u32[]{:S(2)}, u32[]{:S(2)}) %collective-permute-start.24) | collective-permute-done | bytes 786464 | tf_op jit(solution)/shard_map/ppermute | solution.py:271
  147.3 6.4 %second_layer.1 = (bf16[1024,768]{1,0:T(8,128)(2,1)S(1)}, bf16[1024,768]{1,0:T(8,128)(2,1)S(1)}, bf16[1024,512]{1,0:T(8,128)(2,1)S(1)}) custom-call(s32[2]{0:T(128)S(1)} %pad_add_fusion.flags, bf16[1024,512]{1,0:T(8,128)(2,1)S(1)} %get-tuple-element.36.mine_ref, bf16[1024,512]{1,0:T(8,128)(2,1)S(1)} %collective-permute-done.19.other_ref, ...), custom_call_target="tpu_custom_call" | custom-call | flops 3758096384 | bytes 12582912 | tf_op jit(solution)/shard_map/second_layer/pallas_call | solution.py:51
  153.7 0.1 collective-permute-start.26
  154.5 5.6 %collective-permute-start.27 = (f32[2,2]{1,0:T(2,128)S(1)}, f32[2,2]{1,0:T(2,128)S(1)}, u32[]{:S(2)}, u32[]{:S(2)}) collective-permute-start(f32[2,2]{1,0:T(2,128)S(1)} %slice.72), channel_id=1, source_target_pairs={{0,128},{4,132},{8,136},{12,140},{16,144},{20,148},{24,152},{28,15... | collective-permute-start | bytes 56 | tf_op jit(solution)/shard_map/ppermute | solution.py:288
  160.0 1.0 collective-permute-done.27
  161.0 2.9 %collective-permute-start.28 = (f32[1,2]{1,0:T(1,128)S(1)}, f32[1,2]{1,0:T(1,128)S(1)}, u32[]{:S(2)}, u32[]{:S(2)}) collective-permute-start(f32[1,2]{1,0:T(1,128)S(1)} %slice.74), channel_id=1, source_target_pairs={{0,64},{4,68},{8,72},{12,76},{16,80},{20,84},{24,88},{28,92},{32,9... | collective-permute-start | bytes 32 | tf_op jit(solution)/shard_map/ppermute | solution.py:288
  163.9 4.6 %last_layer.1 = f32[16,1024]{1,0:T(8,128)S(1)} custom-call(s32[2]{0:T(128)S(1)} %pad_add_fusion.flags, f32[1]{0:T(128)} %copy.12.coefficient, bf16[1024,512]{1,0:T(8,128)(2,1)S(1)} %get-tuple-element.44.mine_ref, bf16[1024,512]{1,0:T(8,128)(2,1)S(1)} %collective-permute-done.26.other_ref, bf16[1024,512]{1,0:T(8,128)(2,1)S(1)} %get-tuple-element.39.pay_ref, ...), custom_call_target="tpu_custom_call" | custom-call | flops 1879048192 | bytes 10485760 | tf_op jit(solution)/shard_map/last_layer/pallas_call | solution.py:51
  168.6 0.6 fusion.2
  169.7 2.0 %collective-permute-start.29 = (f32[1,1024]{1,0:T(1,128)S(1)}, f32[1,1024]{1,0:T(1,128)S(1)}, u32[]{:S(2)}, u32[]{:S(2)}) collective-permute-start(f32[1,1024]{1,0:T(1,128)S(1)} %slice_subtract_fusion), channel_id=1, source_target_pairs={{0,4},{1,5},{2,6},{3,7},{4,0},{5,1},{6,2},{7,3},{8,12},{9,13},{10,... | collective-permute-start | bytes 12296 | tf_op jit(solution)/shard_map/ppermute | solution.py:332
  171.7 0.8 collective-permute-done.29
  172.6 4.9 %collective-permute-start.31 = (f32[1,1024]{1,0:T(1,128)S(1)}, f32[1,1024]{1,0:T(1,128)S(1)}, u32[]{:S(2)}, u32[]{:S(2)}) collective-permute-start(f32[1,1024]{1,0:T(1,128)S(1)} %fusion.5), channel_id=1, source_target_pairs={{2,4},{3,5},{4,2},{5,3},{10,12},{11,13},{12,10},{13,11},{18,20},{1... | collective-permute-start | bytes 12296 | tf_op jit(solution)/shard_map/ppermute | solution.py:334
  177.5 0.5 collective-permute-start.30
  178.0 0.9 collective-permute-done.31
  179.0 2.8 %collective-permute-done.30 = f32[1,1024]{1,0:T(1,128)S(1)} collective-permute-done((f32[1,1024]{1,0:T(1,128)S(1)}, f32[1,1024]{1,0:T(1,128)S(1)}, u32[]{:S(2)}, u32[]{:S(2)}) %collective-permute-start.30) | collective-permute-done | bytes 4128 | tf_op jit(solution)/shard_map/ppermute | solution.py:333
  181.8 0.6 maximum_select_fusion
  (74 shorter events, 0.5 us)
Async XLA Ops:
  0.0 8.6 %copy-start.9 = (bf16[2,256]{1,0:T(2,128)(2,1)S(1)}, bf16[2,256]{1,0:T(2,128)(2,1)}, u32[]{:S(2)}) copy-start(bf16[2,256]{1,0:T(2,128)(2,1)} %param.11) | copy-start | bytes 3076
  0.0 8.5 %copy-start.12 = (bf16[768]{0:T(1024)(128)(2,1)S(1)}, bf16[768]{0:T(1024)(128)(2,1)}, u32[]{:S(2)}) copy-start(bf16[768]{0:T(1024)(128)(2,1)} %param.20) | copy-start | bytes 4612
  0.0 13.8 %copy-start.7 = (f32[2,768]{1,0:T(2,128)S(1)}, f32[2,768]{1,0:T(2,128)}, u32[]{:S(2)}) copy-start(f32[2,768]{1,0:T(2,128)} %param.19) | copy-start | bytes 18436
  0.0 19.2 %copy-start.5 = (s32[128,1,8]{0,2,1:T(8,128)S(1)}, s32[128,1,8]{0,2,1:T(8,128)}, u32[]{:S(2)}) copy-start(s32[128,1,8]{0,2,1:T(8,128)} %param.14) | copy-start | bytes 12292
  0.0 19.2 %copy-start.6 = (s32[128,1]{0,1:T(1,128)S(1)}, s32[128,1]{0,1:T(1,128)}, u32[]{:S(2)}) copy-start(s32[128,1]{0,1:T(1,128)} %param.15) | copy-start | bytes 1540
  0.0 19.2 %copy-start.3 = (bf16[2048,256]{1,0:T(8,128)(2,1)S(1)}, bf16[2048,256]{1,0:T(8,128)(2,1)}, u32[]{:S(2)}) copy-start(bf16[2048,256]{1,0:T(8,128)(2,1)} %emb_ref.1) | copy-start | bytes 3145732
  0.0 8.5 %collective-permute-start.4 = (bf16[1,2,256]{2,1,0:T(2,128)(2,1)}, bf16[1,2,256]{2,1,0:T(2,128)(2,1)S(1)}, u32[]{:S(2)}, u32[]{:S(2)}) collective-permute-start(bf16[1,2,256]{2,1,0:T(2,128)(2,1)} %bitcast.25), channel_id=1, source_target_pairs={{0,64},{4,68},{8,72},{12,76},{16,80},{20,84},{24,88},{28,92},{32,9... | collective-permute-start | bytes 3080 | tf_op jit(solution)/shard_map/ppermute | solution.py:242
  5.1 22.8 %collective-permute-start = (bf16[768,512]{1,0:T(8,128)(2,1)S(1)}, bf16[768,512]{1,0:T(8,128)(2,1)}, u32[]{:S(2)}, u32[]{:S(2)}) collective-permute-start(bf16[768,512]{1,0:T(8,128)(2,1)S(1)} %dynamic-slice_bitcast_fusion.3), channel_id=1, source_target_pairs={{0,1},{1,0},{2,5},{3,4},{4,3},{5,2},{6,7},{7,6},{8,9},{9,8},{10,13... | collective-permute-start | bytes 2359304 | tf_op jit(solution)/shard_map/ppermute | solution.py:249
  8.6 9.8 %collective-permute-start.5 = (bf16[2,2,256]{2,1,0:T(2,128)(2,1)S(1)}, bf16[2,2,256]{2,1,0:T(2,128)(2,1)S(1)}, u32[]{:S(2)}, u32[]{:S(2)}) collective-permute-start(bf16[2,2,256]{2,1,0:T(2,128)(2,1)S(1)} %pad_maximum_fusion.6), channel_id=1, source_target_pairs={{0,128},{4,132},{8,136},{12,140},{16,144},{20,148},{24,152},{28,15... | collective-permute-start | bytes 6152 | tf_op jit(solution)/shard_map/ppermute | solution.py:242
  13.8 14.1 %collective-permute-start.1 = (f32[3,768]{1,0:T(4,128)S(1)}, f32[3,768]{1,0:T(4,128)S(1)}, u32[]{:S(2)}, u32[]{:S(2)}) collective-permute-start(f32[3,768]{1,0:T(4,128)S(1)} %pad_maximum_fusion.3), channel_id=1, source_target_pairs={{0,1},{1,0},{2,5},{3,4},{4,3},{5,2},{6,7},{7,6},{8,9},{9,8},{10,13... | collective-permute-start | bytes 27656 | tf_op jit(solution)/shard_map/ppermute | solution.py:234
  16.1 11.9 %collective-permute-start.2 = (f32[3,768]{1,0:T(4,128)S(1)}, f32[3,768]{1,0:T(4,128)S(1)}, u32[]{:S(2)}, u32[]{:S(2)}) collective-permute-start(f32[3,768]{1,0:T(4,128)S(1)} %pad_maximum_fusion.3), channel_id=1, source_target_pairs={{2,4},{3,5},{4,2},{5,3},{10,12},{11,13},{12,10},{13,11},{18,20},{1... | collective-permute-start | bytes 27656 | tf_op jit(solution)/shard_map/ppermute | solution.py:235
  18.3 9.6 %collective-permute-start.3 = (bf16[2,256]{1,0:T(2,128)(2,1)S(1)}, bf16[2,256]{1,0:T(2,128)(2,1)S(1)}, u32[]{:S(2)}, u32[]{:S(2)}) collective-permute-start(bf16[2,256]{1,0:T(2,128)(2,1)S(1)} %copy-done.9), channel_id=1, source_target_pairs={{0,4},{1,5},{2,6},{3,7},{4,0},{5,1},{6,2},{7,3},{8,12},{9,13},{10,... | collective-permute-start | bytes 3080 | tf_op jit(solution)/shard_map/ppermute | solution.py:236
  18.4 9.5 %collective-permute-start.6 = (bf16[4,2,256]{2,1,0:T(2,128)(2,1)S(1)}, bf16[4,2,256]{2,1,0:T(2,128)(2,1)S(1)}, u32[]{:S(2)}, u32[]{:S(2)}) collective-permute-start(bf16[4,2,256]{2,1,0:T(2,128)(2,1)S(1)} %pad_maximum_fusion.5), channel_id=1, source_target_pairs={{0,32},{4,36},{8,40},{12,44},{16,48},{20,52},{24,56},{28,60},{32,0... | collective-permute-start | bytes 12296 | tf_op jit(solution)/shard_map/ppermute | solution.py:242
  19.2 1.9 %copy-start.4 = (bf16[2048,768]{1,0:T(8,128)(2,1)S(1)}, bf16[2048,768]{1,0:T(8,128)(2,1)}, u32[]{:S(2)}) copy-start(bf16[2048,768]{1,0:T(8,128)(2,1)} %attr_ref.1) | copy-start | bytes 9437188
  27.9 13.1 %copy-start.13 = (bf16[2,256]{1,0:T(2,128)(2,1)}, bf16[2,256]{1,0:T(2,128)(2,1)S(1)}, u32[]{:S(2)}) copy-start(bf16[2,256]{1,0:T(2,128)(2,1)S(1)} %collective-permute-done.3) | copy-start | bytes 3076
  27.9 0.6 copy-start.10
  28.5 88.0 %all-to-all-start = ((bf16[256,8,512]{2,1,0:T(8,128)(2,1)}), bf16[256,8,512]{2,1,0:T(8,128)(2,1)}, u32[]{:S(2)}, u32[]{:S(2)}) async-start(bf16[256,8,512]{2,1,0:T(8,128)(2,1)} %bitcast.5), calls=%async_computation | async-start | bytes 4194304 | tf_op jit(solution)/shard_map/all_to_all | solution.py:264
  39.5 3.2 %collective-permute-start.7 = (bf16[8,2,256]{2,1,0:T(2,128)(2,1)S(1)}, bf16[8,2,256]{2,1,0:T(2,128)(2,1)S(1)}, u32[]{:S(2)}, u32[]{:S(2)}) collective-permute-start(bf16[8,2,256]{2,1,0:T(2,128)(2,1)S(1)} %pad_maximum_fusion.4), channel_id=1, source_target_pairs={{0,8},{4,12},{8,0},{12,4},{16,24},{20,28},{24,16},{28,20},{32,40},... | collective-permute-start | bytes 24584 | tf_op jit(solution)/shard_map/ppermute | solution.py:242
  42.8 18.1 %copy-start = (bf16[2,512,768]{2,1,0:T(8,128)(2,1)S(1)}, bf16[2,512,768]{2,1,0:T(8,128)(2,1)}, u32[]{:S(2)}) copy-start(bf16[2,512,768]{2,1,0:T(8,128)(2,1)} %u0.3) | copy-start | bytes 4718596
  42.8 13.5 %collective-permute-start.8 = (bf16[16,2,256]{2,1,0:T(2,128)(2,1)S(1)}, bf16[16,2,256]{2,1,0:T(2,128)(2,1)S(1)}, u32[]{:S(2)}, u32[]{:S(2)}) collective-permute-start(bf16[16,2,256]{2,1,0:T(2,128)(2,1)S(1)} %pad_maximum_fusion.2), channel_id=1, source_target_pairs={{0,16},{4,20},{8,24},{12,28},{16,0},{20,4},{24,8},{28,12},{32,48},... | collective-permute-start | bytes 49160 | tf_op jit(solution)/shard_map/ppermute | solution.py:242
  49.1 66.1 %collective-permute-start.14 = (bf16[1024,512]{1,0:T(8,128)(2,1)}, bf16[1024,512]{1,0:T(8,128)(2,1)}, u32[]{:S(2)}, u32[]{:S(2)}) collective-permute-start(bf16[1024,512]{1,0:T(8,128)(2,1)} %get-tuple-element.53), channel_id=1, source_target_pairs={{2,4},{3,5},{4,2},{5,3},{10,12},{11,13},{12,10},{13,11},{18,20},{1... | collective-permute-start | bytes 3145736 | tf_op jit(solution)/shard_map/ppermute | solution.py:276
  54.5 63.3 %collective-permute-start.13 = (bf16[1024,512]{1,0:T(8,128)(2,1)}, bf16[1024,512]{1,0:T(8,128)(2,1)}, u32[]{:S(2)}, u32[]{:S(2)}) collective-permute-start(bf16[1024,512]{1,0:T(8,128)(2,1)} %get-tuple-element.54), channel_id=1, source_target_pairs={{0,1},{1,0},{2,5},{3,4},{4,3},{5,2},{6,7},{7,6},{8,9},{9,8},{10,13... | collective-permute-start | bytes 3145736 | tf_op jit(solution)/shard_map/ppermute | solution.py:274
  55.0 44.7 %collective-permute-start.15 = (bf16[768,512]{1,0:T(8,128)(2,1)}, bf16[768,512]{1,0:T(8,128)(2,1)}, u32[]{:S(2)}, u32[]{:S(2)}) collective-permute-start(bf16[768,512]{1,0:T(8,128)(2,1)} %collective-permute-done.v1), channel_id=1, source_target_pairs={{0,3},{1,2},{6,5},{7,4},{8,11},{9,10},{14,13},{15,12},{16,19},{17,... | collective-permute-start | bytes 2359304 | tf_op jit(solution)/shard_map/ppermute | solution.py:268
  56.3 5.6 %collective-permute-start.9 = (bf16[32,2,256]{2,1,0:T(2,128)(2,1)S(1)}, bf16[32,2,256]{2,1,0:T(2,128)(2,1)}, u32[]{:S(2)}, u32[]{:S(2)}) collective-permute-start(bf16[32,2,256]{2,1,0:T(2,128)(2,1)S(1)} %pad_maximum_fusion.1), channel_id=1, source_target_pairs={{0,4},{4,0},{8,12},{12,8},{16,20},{20,16},{24,28},{28,24},{32,36},... | collective-permute-start | bytes 98312 | tf_op jit(solution)/shard_map/ppermute | solution.py:242
  61.8 48.7 %collective-permute-start.21 = (bf16[512,768]{1,0:T(8,128)(2,1)}, bf16[512,768]{1,0:T(8,128)(2,1)S(1)}, u32[]{:S(2)}, u32[]{:S(2)}) collective-permute-start(bf16[512,768]{1,0:T(8,128)(2,1)} %dynamic-slice_bitcast_fusion.2), channel_id=1, source_target_pairs={{0,1},{1,0},{2,5},{3,4},{4,3},{5,2},{6,7},{7,6},{8,9},{9,8},{10,13... | collective-permute-start | bytes 2359304 | tf_op jit(solution)/shard_map/ppermute | solution.py:267
  63.6 1.3 collective-permute-start.10
  64.8 4.7 %collective-permute-start.11 = (f32[16,2]{1,0:T(8,128)S(1)}, f32[16,2]{1,0:T(8,128)S(1)}, u32[]{:S(2)}, u32[]{:S(2)}) collective-permute-start(f32[16,2]{1,0:T(8,128)S(1)} %slice.77), channel_id=1, source_target_pairs={{0,16},{4,20},{8,24},{12,28},{16,0},{20,4},{24,8},{28,12},{32,48},... | collective-permute-start | bytes 392 | tf_op jit(solution)/shard_map/ppermute | solution.py:288
  69.6 48.3 %collective-permute-start.16 = (bf16[768,512]{1,0:T(8,128)(2,1)}, bf16[768,512]{1,0:T(8,128)(2,1)}, u32[]{:S(2)}, u32[]{:S(2)}) collective-permute-start(bf16[768,512]{1,0:T(8,128)(2,1)} %collective-permute-done.v1), channel_id=1, source_target_pairs={{0,8},{1,9},{2,10},{3,11},{4,12},{5,13},{6,14},{7,15},{8,16},{9,17... | collective-permute-start | bytes 2359304 | tf_op jit(solution)/shard_map/ppermute | solution.py:270
  99.7 18.2 %collective-permute-start.17 = (bf16[768,512]{1,0:T(8,128)(2,1)}, bf16[768,512]{1,0:T(8,128)(2,1)}, u32[]{:S(2)}, u32[]{:S(2)}) collective-permute-start(bf16[768,512]{1,0:T(8,128)(2,1)} %collective-permute-done.15.v2), channel_id=1, source_target_pairs={{2,26},{3,27},{4,28},{5,29},{10,2},{11,3},{12,4},{13,5},{18,10},{1... | collective-permute-start | bytes 2359304 | tf_op jit(solution)/shard_map/ppermute | solution.py:270
  110.5 2.5 %collective-permute-start.12 = (f32[8,2]{1,0:T(8,128)S(1)}, f32[8,2]{1,0:T(8,128)S(1)}, u32[]{:S(2)}, u32[]{:S(2)}) collective-permute-start(f32[8,2]{1,0:T(8,128)S(1)} %slice.79), channel_id=1, source_target_pairs={{0,8},{4,12},{8,0},{12,4},{16,24},{20,28},{24,16},{28,20},{32,40},... | collective-permute-start | bytes 200 | tf_op jit(solution)/shard_map/ppermute | solution.py:288
  113.0 14.9 %collective-permute-start.22 = (bf16[512,768]{1,0:T(8,128)(2,1)S(1)}, bf16[512,768]{1,0:T(8,128)(2,1)}, u32[]{:S(2)}, u32[]{:S(2)}) collective-permute-start(bf16[512,768]{1,0:T(8,128)(2,1)S(1)} %collective-permute-done.21.u1), channel_id=1, source_target_pairs={{2,3},{3,2},{4,5},{5,4},{10,11},{11,10},{12,13},{13,12},{18,19},{1... | collective-permute-start | bytes 2359304 | tf_op jit(solution)/shard_map/ppermute | solution.py:269
  116.6 10.4 %collective-permute-start.18 = (f32[8,2]{1,0:T(8,128)S(1)}, f32[8,2]{1,0:T(8,128)S(1)}, u32[]{:S(2)}, u32[]{:S(2)}) collective-permute-start(f32[8,2]{1,0:T(8,128)S(1)} %slice_maximum_fusion.1), channel_id=1, source_target_pairs={{0,1},{1,0},{2,3},{3,2},{4,5},{5,4},{6,7},{7,6},{8,9},{9,8},{10,11... | collective-permute-start | bytes 200 | tf_op jit(solution)/shard_map/ppermute | solution.py:291
  117.9 1.4 copy-start.1
  119.3 12.8 %copy-start.8 = (f32[2,768]{1,0:T(2,128)S(1)}, f32[2,768]{1,0:T(2,128)}, u32[]{:S(2)}) copy-start(f32[2,768]{1,0:T(2,128)} %param.19) | copy-start | bytes 18436
  119.3 12.8 %copy-start.11 = (f32[3,768]{1,0:T(4,128)S(1)}, f32[3,768]{1,0:T(4,128)}, u32[]{:S(2)}) copy-start(f32[3,768]{1,0:T(4,128)} %copy-done.10) | copy-start | bytes 27652
  119.3 28.1 %copy-start.2 = (bf16[2,768,512]{2,1,0:T(8,128)(2,1)S(1)}, bf16[2,768,512]{2,1,0:T(8,128)(2,1)}, u32[]{:S(2)}) copy-start(bf16[2,768,512]{2,1,0:T(8,128)(2,1)} %v0.3) | copy-start | bytes 4718596
  127.0 8.8 %collective-permute-start.19 = (bf16[1024,512]{1,0:T(8,128)(2,1)S(1)}, bf16[1024,512]{1,0:T(8,128)(2,1)S(1)}, u32[]{:S(2)}, u32[]{:S(2)}) collective-permute-start(bf16[1024,512]{1,0:T(8,128)(2,1)S(1)} %get-tuple-element.36.mine_ref), channel_id=1, source_target_pairs={{0,4},{1,5},{2,6},{3,7},{4,0},{5,1},{6,2},{7,3},{8,12},{9,13},{10,... | collective-permute-start | bytes 3145736 | tf_op jit(solution)/shard_map/ppermute | solution.py:316
  127.1 12.1 %collective-permute-start.23 = (bf16[512,768]{1,0:T(8,128)(2,1)S(1)}, bf16[512,768]{1,0:T(8,128)(2,1)S(1)}, u32[]{:S(2)}, u32[]{:S(2)}) collective-permute-start(bf16[512,768]{1,0:T(8,128)(2,1)S(1)} %collective-permute-done.21.u1), channel_id=1, source_target_pairs={{0,24},{1,25},{2,10},{3,11},{4,12},{5,13},{6,30},{7,31},{8,0},{9,1... | collective-permute-start | bytes 2359304 | tf_op jit(solution)/shard_map/ppermute | solution.py:271
  127.9 19.5 %collective-permute-start.24 = (bf16[512,768]{1,0:T(8,128)(2,1)}, bf16[512,768]{1,0:T(8,128)(2,1)S(1)}, u32[]{:S(2)}, u32[]{:S(2)}) collective-permute-start(bf16[512,768]{1,0:T(8,128)(2,1)} %collective-permute-done.22.u2), channel_id=1, source_target_pairs={{2,26},{3,27},{4,28},{5,29},{10,2},{11,3},{12,4},{13,5},{18,10},{1... | collective-permute-start | bytes 2359304 | tf_op jit(solution)/shard_map/ppermute | solution.py:271
  131.8 4.0 %collective-permute-start.20 = (f32[8,2]{1,0:T(8,128)S(1)}, f32[8,2]{1,0:T(8,128)S(1)}, u32[]{:S(2)}, u32[]{:S(2)}) collective-permute-start(f32[8,2]{1,0:T(8,128)S(1)} %max.27), channel_id=1, source_target_pairs={{0,2},{1,3},{2,0},{3,1},{4,6},{5,7},{6,4},{7,5},{8,10},{9,11},{10,... | collective-permute-start | bytes 200 | tf_op jit(solution)/shard_map/ppermute | solution.py:291
  135.8 17.9 %collective-permute-start.25 = (f32[4,2]{1,0:T(4,128)S(1)}, f32[4,2]{1,0:T(4,128)S(1)}, u32[]{:S(2)}, u32[]{:S(2)}) collective-permute-start(f32[4,2]{1,0:T(4,128)S(1)} %slice.70), channel_id=1, source_target_pairs={{0,32},{4,36},{8,40},{12,44},{16,48},{20,52},{24,56},{28,60},{32,0... | collective-permute-start | bytes 104 | tf_op jit(solution)/shard_map/ppermute | solution.py:288
  153.7 7.3 %collective-permute-start.26 = (bf16[1024,512]{1,0:T(8,128)(2,1)S(1)}, bf16[1024,512]{1,0:T(8,128)(2,1)S(1)}, u32[]{:S(2)}, u32[]{:S(2)}) collective-permute-start(bf16[1024,512]{1,0:T(8,128)(2,1)S(1)} %get-tuple-element.44.mine_ref), channel_id=1, source_target_pairs={{0,4},{1,5},{2,6},{3,7},{4,0},{5,1},{6,2},{7,3},{8,12},{9,13},{10,... | collective-permute-start | bytes 3145736 | tf_op jit(solution)/shard_map/ppermute | solution.py:323
  154.5 6.5 %collective-permute-start.27 = (f32[2,2]{1,0:T(2,128)S(1)}, f32[2,2]{1,0:T(2,128)S(1)}, u32[]{:S(2)}, u32[]{:S(2)}) collective-permute-start(f32[2,2]{1,0:T(2,128)S(1)} %slice.72), channel_id=1, source_target_pairs={{0,128},{4,132},{8,136},{12,140},{16,144},{20,148},{24,152},{28,15... | collective-permute-start | bytes 56 | tf_op jit(solution)/shard_map/ppermute | solution.py:288
  161.0 7.5 %collective-permute-start.28 = (f32[1,2]{1,0:T(1,128)S(1)}, f32[1,2]{1,0:T(1,128)S(1)}, u32[]{:S(2)}, u32[]{:S(2)}) collective-permute-start(f32[1,2]{1,0:T(1,128)S(1)} %slice.74), channel_id=1, source_target_pairs={{0,64},{4,68},{8,72},{12,76},{16,80},{20,84},{24,88},{28,92},{32,9... | collective-permute-start | bytes 32 | tf_op jit(solution)/shard_map/ppermute | solution.py:288
  169.7 2.9 %collective-permute-start.29 = (f32[1,1024]{1,0:T(1,128)S(1)}, f32[1,1024]{1,0:T(1,128)S(1)}, u32[]{:S(2)}, u32[]{:S(2)}) collective-permute-start(f32[1,1024]{1,0:T(1,128)S(1)} %slice_subtract_fusion), channel_id=1, source_target_pairs={{0,4},{1,5},{2,6},{3,7},{4,0},{5,1},{6,2},{7,3},{8,12},{9,13},{10,... | collective-permute-start | bytes 12296 | tf_op jit(solution)/shard_map/ppermute | solution.py:332
  172.6 6.4 %collective-permute-start.31 = (f32[1,1024]{1,0:T(1,128)S(1)}, f32[1,1024]{1,0:T(1,128)S(1)}, u32[]{:S(2)}, u32[]{:S(2)}) collective-permute-start(f32[1,1024]{1,0:T(1,128)S(1)} %fusion.5), channel_id=1, source_target_pairs={{2,4},{3,5},{4,2},{5,3},{10,12},{11,13},{12,10},{13,11},{18,20},{1... | collective-permute-start | bytes 12296 | tf_op jit(solution)/shard_map/ppermute | solution.py:334
  177.5 4.3 %collective-permute-start.30 = (f32[1,1024]{1,0:T(1,128)S(1)}, f32[1,1024]{1,0:T(1,128)S(1)}, u32[]{:S(2)}, u32[]{:S(2)}) collective-permute-start(f32[1,1024]{1,0:T(1,128)S(1)} %fusion.5), channel_id=1, source_target_pairs={{0,1},{1,0},{2,5},{3,4},{4,3},{5,2},{6,7},{7,6},{8,9},{9,8},{10,13... | collective-permute-start | bytes 12296 | tf_op jit(solution)/shard_map/ppermute | solution.py:333

commit v3 on v2

--- a/solution.py
+++ b/solution.py
@@ -11,6 +11,7 @@
 F32 = jnp.float32
 AXES = ("shard", "tp")
 VMEM = pl.BlockSpec(memory_space=pltpu.VMEM)
+PICK, CTX, FIRST = 4096, 20000, 15000
 SMEM = pl.BlockSpec(memory_space=pltpu.SMEM)
 PARAMS = pltpu.CompilerParams(vmem_limit_bytes=24 * 1024 * 1024)
 
@@ -102,13 +103,23 @@
     dst_b[...] = jnp.where(home, own[layer], jnp.where(by_x, far_x[...], far_y[...]))
 
 
+def context_kernel(
+    flags, ca_ref, cb_ref, v0, v1, v2, v3, v4, part_ref, pa_ref, pb_ref, va_ref, vb_ref
+):
+    choose(flags, 0, v0, v1, v2, v3, v4, va_ref, vb_ref)
+    pa_ref[...] = va_ref[0:256]
+    pb_ref[...] = vb_ref[0:256]
+    rows = 256
+    for at in range(0, part_ref.shape[0], rows):
+        here = pl.ds(at, rows)
+        part_ref[here] = dot(ca_ref[here], va_ref[256:768]) + dot(cb_ref[here], vb_ref[256:768])
+
+
 def first_kernel(
-    flags, recv_ref, ca_ref, cb_ref, u_ref, v0, v1, v2, v3, v4, pay_ref, piece_ref, logit_ref,
-    clean, place, va_ref, vb_ref,
+    recv_ref, part_ref, u_ref, pa_ref, pb_ref, pay_ref, piece_ref, logit_ref, clean, place
 ):
     slots = recv_ref.shape[0]
     blk = 256
-    choose(flags, 0, v0, v1, v2, v3, v4, va_ref, vb_ref)
     r = lax.broadcasted_iota(jnp.int32, (blk, blk), 0)
     q = lax.broadcasted_iota(jnp.int32, (blk, blk), 1)
     upper = (r <= q).astype(BF)
@@ -129,12 +140,7 @@
         hot = (k == place[0:1, :]).astype(BF)
         pay = dot(hot, clean[...]).astype(BF)
         pay_ref[here] = pay
-        piece = (
-            dot(pay[:, 0:256], va_ref[0:256])
-            + dot(ca_ref[here], va_ref[256:768])
-            + dot(pay[:, 256:512], vb_ref[0:256])
-            + dot(cb_ref[here], vb_ref[256:768])
-        )
+        piece = part_ref[here] + dot(pay[:, 0:256], pa_ref[...]) + dot(pay[:, 256:512], pb_ref[...])
         piece_ref[here] = piece.astype(BF)
         logit_ref[:, here] = dot_nt(u_ref[...], pay)
 
@@ -230,10 +236,6 @@
     flags = jnp.stack([home.astype(jnp.int32), by])
 
     persons, _, kept = kept_part_entries.shape
-    small = jnp.concatenate([interaction_offset, final_projection[None, :].astype(F32)], 0)
-    small_a = move(small, perm=to_near)
-    small_b = move(small, perm=ctx_far)
-    emb_other = move(person_embedding, perm=to_core)
     masks = (16, 32, 8, 2, 4, 1)
     users = person_embedding[None]
 
@@ -243,13 +245,12 @@
 
     for mask in masks[:3]:
         users = double(users, mask)
-
     v_mine = lax.dynamic_index_in_dim(lowrank_v_matrix, by, 0, False)
     u_mine = lax.dynamic_index_in_dim(lowrank_u_matrix, by, 0, False)
     v_near = move(v_mine, perm=to_near)
-
+    u_near = move(u_mine, perm=to_near)
     (parcel,) = in_vmem(
-        pick_kernel, "pick_rows", [((persons // 4, 2, 4 * kept, 512), BF)], [], 4096, 6, [],
+        pick_kernel, "pick_rows", [((persons // 4, 2, 4 * kept, 512), BF)], [], PICK, 6, [],
         [
             kept_part_entries[:, 0, :].T,
             valid_slot_number.T,
@@ -257,23 +258,33 @@
             catalog_attributes,
         ],
     )
+
     parcel = parcel.reshape(persons * 2, kept, 512)
-    parcel, v_near, small_a, small_b, emb_other, users = lax.optimization_barrier(
-        (parcel, v_near, small_a, small_b, emb_other, users)
-    )
+    parcel, v_near, u_near, users = lax.optimization_barrier((parcel, v_near, u_near, users))
     recv = lax.all_to_all(parcel, AXES, split_axis=0, concat_axis=0, tiled=True)
     recv = recv.reshape(persons * 2 * kept, 512)
 
-    u_near = move(u_mine, perm=to_near)
+    small = jnp.concatenate([interaction_offset, final_projection[None, :].astype(F32)], 0)
+    small, v_near, u_near = lax.optimization_barrier((small, v_near, u_near))
+    small_a = move(small, perm=to_near)
+    small_b = move(small, perm=ctx_far)
     v_far = move(v_near, perm=home_on)
     u_far = move(u_near, perm=away_swap)
-    vs = (lowrank_v_matrix, v_near, v_far, move(v_near, perm=y_up), move(v_far, perm=y_down))
-    us = (lowrank_u_matrix, u_near, u_far, move(u_near, perm=y_mixed), move(u_far, perm=y_down))
+    v_near_y = move(v_near, perm=y_up)
+    u_near_y = move(u_near, perm=y_mixed)
+
+    ctx_away = lax.dynamic_index_in_dim(pair_attributes, 1 - parity, 0, False)
+    ctx_own = lax.dynamic_index_in_dim(pair_attributes, parity, 0, False)
+    ctx_away, ctx_own, small_a, small_b = lax.optimization_barrier(
+        (ctx_away, ctx_own, small_a, small_b)
+    )
+    ctx_a = move(ctx_away, perm=ctx_near)
+    ctx_b = jnp.where(home, ctx_own, move(ctx_own, perm=ctx_far))
     small_b = jnp.where(home, small, small_b)
-
-    ctx_a = move(lax.dynamic_index_in_dim(pair_attributes, 1 - parity, 0, False), perm=ctx_near)
-    ctx_own = lax.dynamic_index_in_dim(pair_attributes, parity, 0, False)
-    ctx_b = jnp.where(home, ctx_own, move(ctx_own, perm=ctx_far))
+    v_far, users = lax.optimization_barrier((v_far, users))
+    ctx_a, u_far, u_near_y = lax.optimization_barrier((ctx_a, u_far, u_near_y))
+    vs = (lowrank_v_matrix, v_near, v_far, v_near_y, move(v_far, perm=y_down))
+    us = (lowrank_u_matrix, u_near, u_far, u_near_y, move(u_far, perm=y_down))
 
     for mask in masks[3:]:
         users = double(users, mask)
@@ -293,7 +304,7 @@
     for mask in masks[:2:-1]:
         best = halve(best, mask)
 
-    query = lax.dynamic_slice_in_dim(jnp.where(home, person_embedding, emb_other), parity, 1, 0)
+    query = lax.dynamic_slice_in_dim(jnp.where(home, person_embedding, users[shards // 2]), parity, 1, 0)
     query = jnp.where(core == 0, query, jnp.zeros_like(query))
     zero = jnp.zeros_like(query)
     query = jnp.where(
@@ -305,12 +316,17 @@
     tall, wide, lanes = ((surv, 512), BF), ((surv, 768), BF), ((16, surv), F32)
     v_pair = [pltpu.VMEM((768, 512), BF)] * 2
     u_pair = [pltpu.VMEM((512, 768), BF)] * 2
+    head = ((256, 512), BF)
+    part, head_a, head_b = in_vmem(
+        context_kernel, "context_part", [((surv, 512), F32), head, head], v_pair, CTX, 8, [flags],
+        [ctx_a, ctx_b, *vs],
+    )
     recv, best = lax.optimization_barrier((recv, best))
     step = over_x(best, 1)
     pay, piece, logit = in_vmem(
         first_kernel, "first_layer", [tall, tall, lanes],
-        [pltpu.VMEM(recv.shape, BF), pltpu.VMEM((16, recv.shape[0]), F32)] + v_pair,
-        4096, 8, [flags], [recv, ctx_a, ctx_b, query, *vs],
+        [pltpu.VMEM(recv.shape, BF), pltpu.VMEM((16, recv.shape[0]), F32)],
+        FIRST, 8, [], [recv, part, query, head_a, head_b],
     )
     piece, best = lax.optimization_barrier((piece, step))
     other, best = lax.optimization_barrier((move(piece, perm=to_core), over_x(best, 2)))

time: 183 us -> 177 us (0.967)
  waiting for transfers between devices: 64.7 us -> 50.1 us
  local copies, waits for them, and re-layouts: 9.37 us -> 20.2 us
  Pallas kernels: 25.4 us -> 23.5 us
    ppermute x1, waiting for transfers between devices: 30.1 us -> 0.01 us  [on_device(): v_far = move(v_near, perm=home_on)]
    ppermute x6, waiting for transfers between devices: 7.88 us -> 20.7 us  [halve(): return jnp.maximum(best[:half], lax.ppermute(best[half:], 'shard', pairs))]
    unnamed x28 -> x64, local copies, waits for them, and re-layouts: 3.92 us -> 14.7 us
    ppermute x1, waiting for transfers between devices: 0.01 us -> 10.4 us  [on_device(): ctx_b = jnp.where(home, ctx_own, move(ctx_own, perm=ctx_far))]
    ppermute x1, waiting for transfers between devices: 6.42 us -> 0.01 us  [on_device(): u_near = move(u_mine, perm=to_near)]
    ppermute x1, starting transfers between devices: 2.27 us -> 6.76 us  [on_device(): small_a = move(small, perm=to_near)]
    ppermute x6, starting transfers between devices: 19.3 us -> 15.1 us  [double(): return jnp.concatenate([users, lax.ppermute(users, 'shard', pairs)], 0)]
    ppermute x6, starting transfers between devices: 11.1 us -> 7.41 us  [halve(): return jnp.maximum(best[:half], lax.ppermute(best[half:], 'shard', pairs))]
  transfers between devices with their start and end apart: 33 -> 32, of which waited for: 13 -> 14; matrix products, arithmetic and copies ran while one was open for 5% -> 5% of each run, Pallas kernels for 14% -> 13%
where the time goes in v3:
time: 177 us; the launch traced here: 176 us
  starting transfers between devices  75 us (42%)
  waiting for transfers between devices  50.1 us (28%)
  Pallas kernels  23.5 us (13%)
  local copies, waits for them, and re-layouts  20.2 us (11%)
  other arithmetic  3.72 us (2%)
  matrix products  1.78 us (1%)
  between operations  1.77 us (1%)
    pallas_call x5, Pallas kernels, in_vmem(): pl.pallas_call(kernel, in_specs=[SMEM] * len(scalars) + [VMEM] * len(arra...  23.5 us
    ppermute x6, waiting for transfers between devices, halve(): return jnp.maximum(best[:half], lax.ppermute(best[half:], 'shard', pairs))  20.7 us
    ppermute x6, starting transfers between devices, double(): return jnp.concatenate([users, lax.ppermute(users, 'shard', pairs)], 0)  15.1 us
    unnamed x64, local copies, waits for them, and re-layouts  14.7 us
    all_to_all x1, starting transfers between devices, on_device(): recv = lax.all_to_all(parcel, AXES, split_axis=0, concat_axis=0, tiled=True)  13 us
    ppermute x1, waiting for transfers between devices, on_device(): ctx_b = jnp.where(home, ctx_own, move(ctx_own, perm=ctx_far))  10.4 us
    ppermute x6, starting transfers between devices, halve(): return jnp.maximum(best[:half], lax.ppermute(best[half:], 'shard', pairs))  7.41 us
    ppermute x1, starting transfers between devices, on_device(): small_a = move(small, perm=to_near)  6.76 us
  transfers between devices with their start and end apart: 32, of which 14 were waited for; matrix products, arithmetic and copies ran while one was open for 5% of the time, Pallas kernels for 13%

profile of v3, /device:TPU:1, one launch (start us, length us, event | category | flops | bytes accessed | tf_op | source)
XLA Modules:
  0.0 176.0 jit_solution(16611252854576924258)
XLA Ops:
  0.1 1.3 dynamic-slice_bitcast_fusion.3
  1.4 4.0 %collective-permute-start = (bf16[768,512]{1,0:T(8,128)(2,1)S(1)}, bf16[768,512]{1,0:T(8,128)(2,1)}, u32[]{:S(2)}, u32[]{:S(2)}) collective-permute-start(bf16[768,512]{1,0:T(8,128)(2,1)S(1)} %dynamic-slice_bitcast_fusion.3), channel_id=1, source_target_pairs={{0,1},{1,0},{2,5},{3,4},{4,3},{5,2},{6,7},{7,6},{8,9},{9,8},{10,13... | collective-permute-start | bytes 2359304 | tf_op jit(solution)/shard_map/ppermute | solution.py:250
  5.4 3.0 %collective-permute-start.2 = (bf16[1,2,256]{2,1,0:T(2,128)(2,1)}, bf16[1,2,256]{2,1,0:T(2,128)(2,1)S(1)}, u32[]{:S(2)}, u32[]{:S(2)}) collective-permute-start(bf16[1,2,256]{2,1,0:T(2,128)(2,1)} %bitcast.28), channel_id=1, source_target_pairs={{0,64},{4,68},{8,72},{12,76},{16,80},{20,84},{24,88},{28,92},{32,9... | collective-permute-start | bytes 3080 | tf_op jit(solution)/shard_map/ppermute | solution.py:244
  8.9 0.6 collective-permute-done.2
  9.5 6.4 %collective-permute-start.3 = (bf16[2,2,256]{2,1,0:T(2,128)(2,1)S(1)}, bf16[2,2,256]{2,1,0:T(2,128)(2,1)S(1)}, u32[]{:S(2)}, u32[]{:S(2)}) collective-permute-start(bf16[2,2,256]{2,1,0:T(2,128)(2,1)S(1)} %pad_maximum_fusion.6), channel_id=1, source_target_pairs={{0,128},{4,132},{8,136},{12,140},{16,144},{20,148},{24,152},{28,15... | collective-permute-start | bytes 6152 | tf_op jit(solution)/shard_map/ppermute | solution.py:244
  15.9 1.9 %copy-done.15 = bf16[2048,768]{1,0:T(8,128)(2,1)S(1)} copy-done((bf16[2048,768]{1,0:T(8,128)(2,1)S(1)}, bf16[2048,768]{1,0:T(8,128)(2,1)}, u32[]{:S(2)}) %copy-start.15) | copy-done | bytes 3145752
  17.8 5.3 %pick_rows.1 = bf16[32,2,32,512]{3,2,1,0:T(8,128)(2,1)S(1)} custom-call(s32[8,128]{1,0:T(8,128)S(1)} %bitcast.26, s32[1,128]{1,0:T(1,128)S(1)} %bitcast.27, bf16[2048,256]{1,0:T(8,128)(2,1)S(1)} %copy-done.7, bf16[2048,768]{1,0:T(8,128)(2,1)S(1)} %copy-done.15), custom_call_target="tpu_custom_call" | custom-call | flops 4294967296 | bytes 6291456 | tf_op jit(solution)/shard_map/pick_rows/pallas_call | solution.py:52
  23.2 1.4 copy-done.6
  24.6 0.8 collective-permute-start.4
  25.4 1.7 collective-permute-done.4
  27.2 1.3 collective-permute-start.5
  28.5 13.0 %all-to-all-start = ((bf16[256,8,512]{2,1,0:T(8,128)(2,1)}), bf16[256,8,512]{2,1,0:T(8,128)(2,1)}, u32[]{:S(2)}, u32[]{:S(2)}) async-start(bf16[256,8,512]{2,1,0:T(8,128)(2,1)} %bitcast.25), calls=%async_computation | async-start | bytes 4194304 | tf_op jit(solution)/shard_map/all_to_all | solution.py:264
  41.5 1.5 collective-permute-start.6
  43.0 1.7 collective-permute-done.6
  44.7 3.3 %collective-permute-start.7 = (bf16[16,2,256]{2,1,0:T(2,128)(2,1)S(1)}, bf16[16,2,256]{2,1,0:T(2,128)(2,1)S(1)}, u32[]{:S(2)}, u32[]{:S(2)}) collective-permute-start(bf16[16,2,256]{2,1,0:T(2,128)(2,1)S(1)} %pad_maximum_fusion.2), channel_id=1, source_target_pairs={{0,16},{4,20},{8,24},{12,28},{16,0},{20,4},{24,8},{28,12},{32,48},... | collective-permute-start | bytes 49160 | tf_op jit(solution)/shard_map/ppermute | solution.py:244
  48.0 6.8 %collective-permute-start.12 = (f32[3,768]{1,0:T(4,128)S(1)}, f32[3,768]{1,0:T(4,128)S(1)}, u32[]{:S(2)}, u32[]{:S(2)}) collective-permute-start(f32[3,768]{1,0:T(4,128)S(1)} %pad_maximum_fusion.3), channel_id=1, source_target_pairs={{0,1},{1,0},{2,5},{3,4},{4,3},{5,2},{6,7},{7,6},{8,9},{9,8},{10,13... | collective-permute-start | bytes 27656 | tf_op jit(solution)/shard_map/ppermute | solution.py:269
  54.8 1.9 %collective-permute-start.13 = (f32[3,768]{1,0:T(4,128)S(1)}, f32[3,768]{1,0:T(4,128)S(1)}, u32[]{:S(2)}, u32[]{:S(2)}) collective-permute-start(f32[3,768]{1,0:T(4,128)S(1)} %pad_maximum_fusion.3), channel_id=1, source_target_pairs={{2,4},{3,5},{4,2},{5,3},{10,12},{11,13},{12,10},{13,11},{18,20},{1... | collective-permute-start | bytes 27656 | tf_op jit(solution)/shard_map/ppermute | solution.py:270
  56.9 3.0 %dynamic-slice_bitcast_fusion = (bf16[1024,512]{1,0:T(8,128)(2,1)}, bf16[1024,512]{1,0:T(8,128)(2,1)}) fusion(bf16[2,1024,512]{2,1,0:T(8,128)(2,1)} %param.16, s32[]{:T(128)S(6)} %select_n.109, s32[]{:T(128)S(6)} %select_n.108), kind=kLoop, calls=%fused_computation.1 | loop fusion | bytes 4194312 | tf_op jit(solution)/shard_map/jit(dynamic_index_in_dim)/squeeze | solution.py:277
  59.9 2.5 %collective-permute-start.15 = (bf16[512,768]{1,0:T(8,128)(2,1)S(1)}, bf16[512,768]{1,0:T(8,128)(2,1)}, u32[]{:S(2)}, u32[]{:S(2)}) collective-permute-start(bf16[512,768]{1,0:T(8,128)(2,1)S(1)} %collective-permute-done.1.u1), channel_id=1, source_target_pairs={{2,3},{3,2},{4,5},{5,4},{10,11},{11,10},{12,13},{13,12},{18,19},{1... | collective-permute-start | bytes 2359304 | tf_op jit(solution)/shard_map/ppermute | solution.py:272
  62.4 0.6 copy-done.28
  63.0 4.6 %collective-permute-start.17 = (bf16[1024,512]{1,0:T(8,128)(2,1)}, bf16[1024,512]{1,0:T(8,128)(2,1)}, u32[]{:S(2)}, u32[]{:S(2)}) collective-permute-start(bf16[1024,512]{1,0:T(8,128)(2,1)} %get-tuple-element.53), channel_id=1, source_target_pairs={{2,4},{3,5},{4,2},{5,3},{10,12},{11,13},{12,10},{13,11},{18,20},{1... | collective-permute-start | bytes 3145736 | tf_op jit(solution)/shard_map/ppermute | solution.py:282
  67.6 1.2 collective-permute-start.14
  68.8 0.6 copy-done.26
  69.5 1.8 %convolution_reduce_fusion = f32[128]{0:T(128)S(1)} fusion(bf16[128,256]{1,0:T(8,128)(2,1)S(1)} %reshape.35, bf16[2048,256]{1,0:T(8,128)(2,1)} %emb_ref.1), kind=kOutput, calls=%fused_computation | convolution fusion | flops 134479744 | bytes 1114624 | tf_op jit(solution)/shard_map/ue,ie->ui/dot_general | solution.py:291
  72.1 0.7 collective-permute-done.9
  72.8 1.7 collective-permute-start.10
  74.4 16.4 %collective-permute-done.10 = f32[16,2]{1,0:T(8,128)S(1)} collective-permute-done((f32[16,2]{1,0:T(8,128)S(1)}, f32[16,2]{1,0:T(8,128)S(1)}, u32[]{:S(2)}, u32[]{:S(2)}) %collective-permute-start.10) | collective-permute-done | bytes 160 | tf_op jit(solution)/shard_map/ppermute | solution.py:299
  90.9 1.5 collective-permute-start.18
  92.3 1.3 collective-permute-done.11
  93.6 1.9 %collective-permute-start.19 = (bf16[768,512]{1,0:T(8,128)(2,1)}, bf16[768,512]{1,0:T(8,128)(2,1)S(1)}, u32[]{:S(2)}, u32[]{:S(2)}) collective-permute-start(bf16[768,512]{1,0:T(8,128)(2,1)} %copy-done.8), channel_id=1, source_target_pairs={{2,26},{3,27},{4,28},{5,29},{10,2},{11,3},{12,4},{13,5},{18,10},{1... | collective-permute-start | bytes 2359304 | tf_op jit(solution)/shard_map/ppermute | solution.py:286
  95.5 0.6 slice_bitcast_fusion
  96.2 0.7 broadcast_select_fusion.5
  96.9 1.0 copy-done.1
  97.9 10.4 %collective-permute-done.17 = bf16[1024,512]{1,0:T(8,128)(2,1)} collective-permute-done((bf16[1024,512]{1,0:T(8,128)(2,1)}, bf16[1024,512]{1,0:T(8,128)(2,1)}, u32[]{:S(2)}, u32[]{:S(2)}) %collective-permute-start.17) | collective-permute-done | bytes 1048608 | tf_op jit(solution)/shard_map/ppermute | solution.py:282
  108.3 1.4 broadcast_select_fusion.cb_ref
  109.7 1.3 collective-permute-done.18.v3
  111.1 1.1 copy-done.9
  112.2 2.5 %context_part.1 = (f32[1024,512]{1,0:T(8,128)S(1)}, bf16[256,512]{1,0:T(8,128)(2,1)S(1)}, bf16[256,512]{1,0:T(8,128)(2,1)S(1)}) custom-call(s32[2]{0:T(128)S(1)} %pad_add_fusion.flags, bf16[1024,512]{1,0:T(8,128)(2,1)S(1)} %copy-done.2, bf16[1024,512]{1,0:T(8,128)(2,1)S(1)} %broadcast_select_fusion.cb_ref, bf16[2,768,512]{2,1,0:T(8,128)(2,1)S(1)} %copy-done.4, ...), custom_call_target="tpu_custom_call" | custom-call | flops 20971520000 | bytes 8388608 | tf_op jit(solution)/shard_map/context_part/pallas_call | solution.py:52
  114.7 0.9 copy-done.11
  115.7 0.9 copy-done.13
  116.6 1.4 copy-done.18
  117.9 0.7 copy-done.20
  118.7 0.7 copy-done.22
  119.4 1.6 copy-done.19
  121.0 0.9 copy-done.21
  121.9 0.9 copy-done.23
  122.9 5.7 %first_layer.1 = (bf16[1024,512]{1,0:T(8,128)(2,1)S(1)}, bf16[1024,512]{1,0:T(8,128)(2,1)S(1)}, f32[16,1024]{1,0:T(8,128)S(1)}) custom-call(bf16[2048,512]{1,0:T(8,128)(2,1)} %bitcast.9.recv_ref, f32[1024,512]{1,0:T(8,128)S(1)} %copy-done.19, bf16[16,512]{1,0:T(8,128)(2,1)S(1)} %broadcast_in_dim.15.u_ref, bf16[256,512]{1,0:T(8,128)(2,1)S(1)} %copy-done.21, ...), custom_call_target="tpu_custom_call" | custom-call | flops 15728640000 | bytes 8388608 | tf_op jit(solution)/shard_map/first_layer/pallas_call | solution.py:52
  128.6 1.6 collective-permute-start.21
  130.2 2.8 %collective-permute-start.23 = (bf16[512,768]{1,0:T(8,128)(2,1)}, bf16[512,768]{1,0:T(8,128)(2,1)S(1)}, u32[]{:S(2)}, u32[]{:S(2)}) collective-permute-start(bf16[512,768]{1,0:T(8,128)(2,1)} %collective-permute-done.15.u2), channel_id=1, source_target_pairs={{2,26},{3,27},{4,28},{5,29},{10,2},{11,3},{12,4},{13,5},{18,10},{1... | collective-permute-start | bytes 2359304 | tf_op jit(solution)/shard_map/ppermute | solution.py:287
  133.0 1.3 collective-permute-start.22
  134.3 2.8 %collective-permute-done.22 = f32[8,2]{1,0:T(8,128)S(1)} collective-permute-done((f32[8,2]{1,0:T(8,128)S(1)}, f32[8,2]{1,0:T(8,128)S(1)}, u32[]{:S(2)}, u32[]{:S(2)}) %collective-permute-start.22) | collective-permute-done | bytes 96 | tf_op jit(solution)/shard_map/ppermute | solution.py:302
  137.4 5.7 %collective-permute-done.23.u4 = bf16[512,768]{1,0:T(8,128)(2,1)S(1)} collective-permute-done((bf16[512,768]{1,0:T(8,128)(2,1)}, bf16[512,768]{1,0:T(8,128)(2,1)S(1)}, u32[]{:S(2)}, u32[]{:S(2)}) %collective-permute-start.23) | collective-permute-done | bytes 786464 | tf_op jit(solution)/shard_map/ppermute | solution.py:287
  143.2 5.5 %second_layer.1 = (bf16[1024,768]{1,0:T(8,128)(2,1)S(1)}, bf16[1024,768]{1,0:T(8,128)(2,1)S(1)}, bf16[1024,512]{1,0:T(8,128)(2,1)S(1)}) custom-call(s32[2]{0:T(128)S(1)} %pad_add_fusion.flags, bf16[1024,512]{1,0:T(8,128)(2,1)S(1)} %get-tuple-element.60.mine_ref, bf16[1024,512]{1,0:T(8,128)(2,1)S(1)} %collective-permute-done.21.other_ref, ...), custom_call_target="tpu_custom_call" | custom-call | flops 3758096384 | bytes 12582912 | tf_op jit(solution)/shard_map/second_layer/pallas_call | solution.py:52
  149.5 4.1 %collective-permute-start.26 = (f32[2,2]{1,0:T(2,128)S(1)}, f32[2,2]{1,0:T(2,128)S(1)}, u32[]{:S(2)}, u32[]{:S(2)}) collective-permute-start(f32[2,2]{1,0:T(2,128)S(1)} %slice.76), channel_id=1, source_target_pairs={{0,128},{4,132},{8,136},{12,140},{16,144},{20,148},{24,152},{28,15... | collective-permute-start | bytes 56 | tf_op jit(solution)/shard_map/ppermute | solution.py:299
  153.6 2.3 %collective-permute-done.26 = f32[2,2]{1,0:T(2,128)S(1)} collective-permute-done((f32[2,2]{1,0:T(2,128)S(1)}, f32[2,2]{1,0:T(2,128)S(1)}, u32[]{:S(2)}, u32[]{:S(2)}) %collective-permute-start.26) | collective-permute-done | bytes 48 | tf_op jit(solution)/shard_map/ppermute | solution.py:299
  155.9 1.3 collective-permute-start.27
  157.2 4.5 %last_layer.1 = f32[16,1024]{1,0:T(8,128)S(1)} custom-call(s32[2]{0:T(128)S(1)} %pad_add_fusion.flags, f32[1]{0:T(128)} %copy.12.coefficient, bf16[1024,512]{1,0:T(8,128)(2,1)S(1)} %get-tuple-element.70.mine_ref, bf16[1024,512]{1,0:T(8,128)(2,1)S(1)} %collective-permute-done.25.other_ref, bf16[1024,512]{1,0:T(8,128)(2,1)S(1)} %get-tuple-element.63.pay_ref, ...), custom_call_target="tpu_custom_call" | custom-call | flops 1879048192 | bytes 10485760 | tf_op jit(solution)/shard_map/last_layer/pallas_call | solution.py:52
  161.7 0.6 fusion.2
  162.9 2.0 %collective-permute-start.28 = (f32[1,1024]{1,0:T(1,128)S(1)}, f32[1,1024]{1,0:T(1,128)S(1)}, u32[]{:S(2)}, u32[]{:S(2)}) collective-permute-start(f32[1,1024]{1,0:T(1,128)S(1)} %slice_subtract_fusion), channel_id=1, source_target_pairs={{0,4},{1,5},{2,6},{3,7},{4,0},{5,1},{6,2},{7,3},{8,12},{9,13},{10,... | collective-permute-start | bytes 12296 | tf_op jit(solution)/shard_map/ppermute | solution.py:348
  164.9 0.8 collective-permute-done.28
  165.7 5.4 %collective-permute-start.30 = (f32[1,1024]{1,0:T(1,128)S(1)}, f32[1,1024]{1,0:T(1,128)S(1)}, u32[]{:S(2)}, u32[]{:S(2)}) collective-permute-start(f32[1,1024]{1,0:T(1,128)S(1)} %fusion.5), channel_id=1, source_target_pairs={{2,4},{3,5},{4,2},{5,3},{10,12},{11,13},{12,10},{13,11},{18,20},{1... | collective-permute-start | bytes 12296 | tf_op jit(solution)/shard_map/ppermute | solution.py:350
  171.2 1.2 collective-permute-done.30
  172.4 3.0 %collective-permute-done.29 = f32[1,1024]{1,0:T(1,128)S(1)} collective-permute-done((f32[1,1024]{1,0:T(1,128)S(1)}, f32[1,1024]{1,0:T(1,128)S(1)}, u32[]{:S(2)}, u32[]{:S(2)}) %collective-permute-start.29) | collective-permute-done | bytes 4128 | tf_op jit(solution)/shard_map/ppermute | solution.py:349
  175.4 0.6 maximum_select_fusion
  (110 shorter events, 2.4 us)
Async XLA Ops:
  0.0 9.5 %copy-start.27 = (bf16[2,256]{1,0:T(2,128)(2,1)S(1)}, bf16[2,256]{1,0:T(2,128)(2,1)}, u32[]{:S(2)}) copy-start(bf16[2,256]{1,0:T(2,128)(2,1)} %param.11) | copy-start | bytes 3076
  0.0 8.4 %copy-start = (bf16[2,512,768]{2,1,0:T(8,128)(2,1)S(1)}, bf16[2,512,768]{2,1,0:T(8,128)(2,1)}, u32[]{:S(2)}) copy-start(bf16[2,512,768]{2,1,0:T(8,128)(2,1)} %u0.3) | copy-start | bytes 4718596
  0.0 15.9 %copy-start.16 = (s32[128,1,8]{0,2,1:T(8,128)S(1)}, s32[128,1,8]{0,2,1:T(8,128)}, u32[]{:S(2)}) copy-start(s32[128,1,8]{0,2,1:T(8,128)} %param.14) | copy-start | bytes 12292
  0.0 15.9 %copy-start.17 = (s32[128,1]{0,1:T(1,128)S(1)}, s32[128,1]{0,1:T(1,128)}, u32[]{:S(2)}) copy-start(s32[128,1]{0,1:T(1,128)} %param.15) | copy-start | bytes 1540
  0.0 15.9 %copy-start.7 = (bf16[2048,256]{1,0:T(8,128)(2,1)S(1)}, bf16[2048,256]{1,0:T(8,128)(2,1)}, u32[]{:S(2)}) copy-start(bf16[2048,256]{1,0:T(8,128)(2,1)} %emb_ref.1) | copy-start | bytes 3145732
  1.4 25.7 %collective-permute-start = (bf16[768,512]{1,0:T(8,128)(2,1)S(1)}, bf16[768,512]{1,0:T(8,128)(2,1)}, u32[]{:S(2)}, u32[]{:S(2)}) collective-permute-start(bf16[768,512]{1,0:T(8,128)(2,1)S(1)} %dynamic-slice_bitcast_fusion.3), channel_id=1, source_target_pairs={{0,1},{1,0},{2,5},{3,4},{4,3},{5,2},{6,7},{7,6},{8,9},{9,8},{10,13... | collective-permute-start | bytes 2359304 | tf_op jit(solution)/shard_map/ppermute | solution.py:250
  5.4 4.2 %collective-permute-start.2 = (bf16[1,2,256]{2,1,0:T(2,128)(2,1)}, bf16[1,2,256]{2,1,0:T(2,128)(2,1)S(1)}, u32[]{:S(2)}, u32[]{:S(2)}) collective-permute-start(bf16[1,2,256]{2,1,0:T(2,128)(2,1)} %bitcast.28), channel_id=1, source_target_pairs={{0,64},{4,68},{8,72},{12,76},{16,80},{20,84},{24,88},{28,92},{32,9... | collective-permute-start | bytes 3080 | tf_op jit(solution)/shard_map/ppermute | solution.py:244
  8.4 18.7 %collective-permute-start.1 = (bf16[512,768]{1,0:T(8,128)(2,1)S(1)}, bf16[512,768]{1,0:T(8,128)(2,1)S(1)}, u32[]{:S(2)}, u32[]{:S(2)}) collective-permute-start(bf16[512,768]{1,0:T(8,128)(2,1)S(1)} %dynamic-slice_bitcast_fusion.2), channel_id=1, source_target_pairs={{0,1},{1,0},{2,5},{3,4},{4,3},{5,2},{6,7},{7,6},{8,9},{9,8},{10,13... | collective-permute-start | bytes 2359304 | tf_op jit(solution)/shard_map/ppermute | solution.py:251
  9.5 15.0 %collective-permute-start.3 = (bf16[2,2,256]{2,1,0:T(2,128)(2,1)S(1)}, bf16[2,2,256]{2,1,0:T(2,128)(2,1)S(1)}, u32[]{:S(2)}, u32[]{:S(2)}) collective-permute-start(bf16[2,2,256]{2,1,0:T(2,128)(2,1)S(1)} %pad_maximum_fusion.6), channel_id=1, source_target_pairs={{0,128},{4,132},{8,136},{12,140},{16,144},{20,148},{24,152},{28,15... | collective-permute-start | bytes 6152 | tf_op jit(solution)/shard_map/ppermute | solution.py:244
  15.9 1.9 %copy-start.15 = (bf16[2048,768]{1,0:T(8,128)(2,1)S(1)}, bf16[2048,768]{1,0:T(8,128)(2,1)}, u32[]{:S(2)}) copy-start(bf16[2048,768]{1,0:T(8,128)(2,1)} %attr_ref.1) | copy-start | bytes 9437188
  17.8 6.7 %copy-start.31 = (bf16[768]{0:T(1024)(128)(2,1)S(1)}, bf16[768]{0:T(1024)(128)(2,1)}, u32[]{:S(2)}) copy-start(bf16[768]{0:T(1024)(128)(2,1)} %param.20) | copy-start | bytes 4612
  17.8 7.6 %copy-start.30 = (f32[2,768]{1,0:T(2,128)S(1)}, f32[2,768]{1,0:T(2,128)}, u32[]{:S(2)}) copy-start(f32[2,768]{1,0:T(2,128)} %param.19) | copy-start | bytes 18436
  23.2 1.4 copy-start.6
  24.6 2.5 %collective-permute-start.4 = (bf16[4,2,256]{2,1,0:T(2,128)(2,1)S(1)}, bf16[4,2,256]{2,1,0:T(2,128)(2,1)S(1)}, u32[]{:S(2)}, u32[]{:S(2)}) collective-permute-start(bf16[4,2,256]{2,1,0:T(2,128)(2,1)S(1)} %pad_maximum_fusion.5), channel_id=1, source_target_pairs={{0,32},{4,36},{8,40},{12,44},{16,48},{20,52},{24,56},{28,60},{32,0... | collective-permute-start | bytes 12296 | tf_op jit(solution)/shard_map/ppermute | solution.py:244
  25.4 29.4 %copy-start.24 = (f32[3,768]{1,0:T(4,128)}, f32[3,768]{1,0:T(4,128)S(1)}, u32[]{:S(2)}) copy-start(f32[3,768]{1,0:T(4,128)S(1)} %pad_maximum_fusion.3) | copy-start | bytes 27652
  27.2 14.3 %collective-permute-start.5 = (bf16[768,512]{1,0:T(8,128)(2,1)}, bf16[768,512]{1,0:T(8,128)(2,1)S(1)}, u32[]{:S(2)}, u32[]{:S(2)}) collective-permute-start(bf16[768,512]{1,0:T(8,128)(2,1)} %collective-permute-done.v1), channel_id=1, source_target_pairs={{0,3},{1,2},{6,5},{7,4},{8,11},{9,10},{14,13},{15,12},{16,19},{17,... | collective-permute-start | bytes 2359304 | tf_op jit(solution)/shard_map/ppermute | solution.py:271
  28.5 90.9 %all-to-all-start = ((bf16[256,8,512]{2,1,0:T(8,128)(2,1)}), bf16[256,8,512]{2,1,0:T(8,128)(2,1)}, u32[]{:S(2)}, u32[]{:S(2)}) async-start(bf16[256,8,512]{2,1,0:T(8,128)(2,1)} %bitcast.25), calls=%async_computation | async-start | bytes 4194304 | tf_op jit(solution)/shard_map/all_to_all | solution.py:264
  41.5 18.5 %copy-start.8 = (bf16[768,512]{1,0:T(8,128)(2,1)}, bf16[768,512]{1,0:T(8,128)(2,1)S(1)}, u32[]{:S(2)}) copy-start(bf16[768,512]{1,0:T(8,128)(2,1)S(1)} %collective-permute-done.5.v2) | copy-start | bytes 2359300
  41.5 3.2 %collective-permute-start.6 = (bf16[8,2,256]{2,1,0:T(2,128)(2,1)S(1)}, bf16[8,2,256]{2,1,0:T(2,128)(2,1)S(1)}, u32[]{:S(2)}, u32[]{:S(2)}) collective-permute-start(bf16[8,2,256]{2,1,0:T(2,128)(2,1)S(1)} %pad_maximum_fusion.4), channel_id=1, source_target_pairs={{0,8},{4,12},{8,0},{12,4},{16,24},{20,28},{24,16},{28,20},{32,40},... | collective-permute-start | bytes 24584 | tf_op jit(solution)/shard_map/ppermute | solution.py:244
  44.7 12.0 %collective-permute-start.7 = (bf16[16,2,256]{2,1,0:T(2,128)(2,1)S(1)}, bf16[16,2,256]{2,1,0:T(2,128)(2,1)S(1)}, u32[]{:S(2)}, u32[]{:S(2)}) collective-permute-start(bf16[16,2,256]{2,1,0:T(2,128)(2,1)S(1)} %pad_maximum_fusion.2), channel_id=1, source_target_pairs={{0,16},{4,20},{8,24},{12,28},{16,0},{20,4},{24,8},{28,12},{32,48},... | collective-permute-start | bytes 49160 | tf_op jit(solution)/shard_map/ppermute | solution.py:244
  48.0 14.4 %collective-permute-start.12 = (f32[3,768]{1,0:T(4,128)S(1)}, f32[3,768]{1,0:T(4,128)S(1)}, u32[]{:S(2)}, u32[]{:S(2)}) collective-permute-start(f32[3,768]{1,0:T(4,128)S(1)} %pad_maximum_fusion.3), channel_id=1, source_target_pairs={{0,1},{1,0},{2,5},{3,4},{4,3},{5,2},{6,7},{7,6},{8,9},{9,8},{10,13... | collective-permute-start | bytes 27656 | tf_op jit(solution)/shard_map/ppermute | solution.py:269
  54.8 7.6 %collective-permute-start.13 = (f32[3,768]{1,0:T(4,128)S(1)}, f32[3,768]{1,0:T(4,128)S(1)}, u32[]{:S(2)}, u32[]{:S(2)}) collective-permute-start(f32[3,768]{1,0:T(4,128)S(1)} %pad_maximum_fusion.3), channel_id=1, source_target_pairs={{2,4},{3,5},{4,2},{5,3},{10,12},{11,13},{12,10},{13,11},{18,20},{1... | collective-permute-start | bytes 27656 | tf_op jit(solution)/shard_map/ppermute | solution.py:270
  56.8 12.0 %collective-permute-start.8 = (bf16[32,2,256]{2,1,0:T(2,128)(2,1)S(1)}, bf16[32,2,256]{2,1,0:T(2,128)(2,1)S(1)}, u32[]{:S(2)}, u32[]{:S(2)}) collective-permute-start(bf16[32,2,256]{2,1,0:T(2,128)(2,1)S(1)} %pad_maximum_fusion.1), channel_id=1, source_target_pairs={{0,4},{4,0},{8,12},{12,8},{16,20},{20,16},{24,28},{28,24},{32,36},... | collective-permute-start | bytes 98312 | tf_op jit(solution)/shard_map/ppermute | solution.py:244
  59.9 30.9 %collective-permute-start.15 = (bf16[512,768]{1,0:T(8,128)(2,1)S(1)}, bf16[512,768]{1,0:T(8,128)(2,1)}, u32[]{:S(2)}, u32[]{:S(2)}) collective-permute-start(bf16[512,768]{1,0:T(8,128)(2,1)S(1)} %collective-permute-done.1.u1), channel_id=1, source_target_pairs={{2,3},{3,2},{4,5},{5,4},{10,11},{11,10},{12,13},{13,12},{18,19},{1... | collective-permute-start | bytes 2359304 | tf_op jit(solution)/shard_map/ppermute | solution.py:272
  62.4 0.6 copy-start.28
  63.0 45.3 %collective-permute-start.17 = (bf16[1024,512]{1,0:T(8,128)(2,1)}, bf16[1024,512]{1,0:T(8,128)(2,1)}, u32[]{:S(2)}, u32[]{:S(2)}) collective-permute-start(bf16[1024,512]{1,0:T(8,128)(2,1)} %get-tuple-element.53), channel_id=1, source_target_pairs={{2,4},{3,5},{4,2},{5,3},{10,12},{11,13},{12,10},{13,11},{18,20},{1... | collective-permute-start | bytes 3145736 | tf_op jit(solution)/shard_map/ppermute | solution.py:282
  67.6 29.3 %collective-permute-start.14 = (bf16[1024,512]{1,0:T(8,128)(2,1)}, bf16[1024,512]{1,0:T(8,128)(2,1)S(1)}, u32[]{:S(2)}, u32[]{:S(2)}) collective-permute-start(bf16[1024,512]{1,0:T(8,128)(2,1)} %get-tuple-element.50), channel_id=1, source_target_pairs={{0,1},{1,0},{2,5},{3,4},{4,3},{5,2},{6,7},{7,6},{8,9},{9,8},{10,13... | collective-permute-start | bytes 3145736 | tf_op jit(solution)/shard_map/ppermute | solution.py:281
  68.8 0.6 copy-start.26
  71.5 1.3 collective-permute-start.9
  71.7 25.2 %collective-permute-start.16 = (bf16[512,768]{1,0:T(8,128)(2,1)S(1)}, bf16[512,768]{1,0:T(8,128)(2,1)}, u32[]{:S(2)}, u32[]{:S(2)}) collective-permute-start(bf16[512,768]{1,0:T(8,128)(2,1)S(1)} %collective-permute-done.1.u1), channel_id=1, source_target_pairs={{0,24},{1,25},{2,10},{3,11},{4,12},{5,13},{6,30},{7,31},{8,0},{9,1... | collective-permute-start | bytes 2359304 | tf_op jit(solution)/shard_map/ppermute | solution.py:274
  72.8 18.1 %collective-permute-start.10 = (f32[16,2]{1,0:T(8,128)S(1)}, f32[16,2]{1,0:T(8,128)S(1)}, u32[]{:S(2)}, u32[]{:S(2)}) collective-permute-start(f32[16,2]{1,0:T(8,128)S(1)} %slice.81), channel_id=1, source_target_pairs={{0,16},{4,20},{8,24},{12,28},{16,0},{20,4},{24,8},{28,12},{32,48},... | collective-permute-start | bytes 392 | tf_op jit(solution)/shard_map/ppermute | solution.py:299
  74.4 36.7 %copy-start.4 = (bf16[2,768,512]{2,1,0:T(8,128)(2,1)S(1)}, bf16[2,768,512]{2,1,0:T(8,128)(2,1)}, u32[]{:S(2)}) copy-start(bf16[2,768,512]{2,1,0:T(8,128)(2,1)} %v0.3) | copy-start | bytes 4718596
  90.8 2.8 %collective-permute-start.11 = (f32[8,2]{1,0:T(8,128)S(1)}, f32[8,2]{1,0:T(8,128)S(1)}, u32[]{:S(2)}, u32[]{:S(2)}) collective-permute-start(f32[8,2]{1,0:T(8,128)S(1)} %slice.83), channel_id=1, source_target_pairs={{0,8},{4,12},{8,0},{12,4},{16,24},{20,28},{24,16},{28,20},{32,40},... | collective-permute-start | bytes 200 | tf_op jit(solution)/shard_map/ppermute | solution.py:299
  90.9 20.2 %collective-permute-start.18 = (bf16[768,512]{1,0:T(8,128)(2,1)}, bf16[768,512]{1,0:T(8,128)(2,1)S(1)}, u32[]{:S(2)}, u32[]{:S(2)}) collective-permute-start(bf16[768,512]{1,0:T(8,128)(2,1)} %collective-permute-done.v1), channel_id=1, source_target_pairs={{0,8},{1,9},{2,10},{3,11},{4,12},{5,13},{6,14},{7,15},{8,16},{9,17... | collective-permute-start | bytes 2359304 | tf_op jit(solution)/shard_map/ppermute | solution.py:273
  93.6 17.5 %collective-permute-start.19 = (bf16[768,512]{1,0:T(8,128)(2,1)}, bf16[768,512]{1,0:T(8,128)(2,1)S(1)}, u32[]{:S(2)}, u32[]{:S(2)}) collective-permute-start(bf16[768,512]{1,0:T(8,128)(2,1)} %copy-done.8), channel_id=1, source_target_pairs={{2,26},{3,27},{4,28},{5,29},{10,2},{11,3},{12,4},{13,5},{18,10},{1... | collective-permute-start | bytes 2359304 | tf_op jit(solution)/shard_map/ppermute | solution.py:286
  96.9 1.0 copy-start.1
  108.3 2.8 %copy-start.2 = (bf16[1024,512]{1,0:T(8,128)(2,1)S(1)}, bf16[1024,512]{1,0:T(8,128)(2,1)}, u32[]{:S(2)}) copy-start(bf16[1024,512]{1,0:T(8,128)(2,1)} %copy-done.1) | copy-start | bytes 3145732
  111.1 1.1 copy-start.9
  114.7 0.9 copy-start.11
  115.7 0.9 copy-start.13
  116.6 1.4 copy-start.18
  117.9 0.7 copy-start.20
  118.7 0.7 copy-start.22
  119.4 9.2 %collective-permute-start.20 = (f32[8,2]{1,0:T(8,128)S(1)}, f32[8,2]{1,0:T(8,128)S(1)}, u32[]{:S(2)}, u32[]{:S(2)}) collective-permute-start(f32[8,2]{1,0:T(8,128)S(1)} %slice_maximum_fusion.1), channel_id=1, source_target_pairs={{0,1},{1,0},{2,3},{3,2},{4,5},{5,4},{6,7},{7,6},{8,9},{9,8},{10,11... | collective-permute-start | bytes 200 | tf_op jit(solution)/shard_map/ppermute | solution.py:302
  119.4 1.6 copy-start.19
  121.0 0.9 copy-start.21
  121.9 0.9 copy-start.23
  122.9 11.4 %copy-start.25 = (f32[3,768]{1,0:T(4,128)S(1)}, f32[3,768]{1,0:T(4,128)}, u32[]{:S(2)}) copy-start(f32[3,768]{1,0:T(4,128)} %copy-done.24) | copy-start | bytes 27652
  122.9 11.4 %copy-start.29 = (f32[3,768]{1,0:T(4,128)S(1)}, f32[3,768]{1,0:T(4,128)}, u32[]{:S(2)}) copy-start(f32[3,768]{1,0:T(4,128)} %copy-done.28) | copy-start | bytes 27652
  122.9 20.3 %copy-start.3 = (bf16[1024,512]{1,0:T(8,128)(2,1)S(1)}, bf16[1024,512]{1,0:T(8,128)(2,1)}, u32[]{:S(2)}) copy-start(bf16[1024,512]{1,0:T(8,128)(2,1)} %copy-done.1) | copy-start | bytes 3145732
  122.9 20.3 %copy-start.5 = (bf16[2,768,512]{2,1,0:T(8,128)(2,1)S(1)}, bf16[2,768,512]{2,1,0:T(8,128)(2,1)}, u32[]{:S(2)}) copy-start(bf16[2,768,512]{2,1,0:T(8,128)(2,1)} %v0.3) | copy-start | bytes 4718596
  122.9 20.3 %copy-start.10 = (bf16[768,512]{1,0:T(8,128)(2,1)S(1)}, bf16[768,512]{1,0:T(8,128)(2,1)}, u32[]{:S(2)}) copy-start(bf16[768,512]{1,0:T(8,128)(2,1)} %copy-done.8) | copy-start | bytes 2359300
  122.9 20.3 %copy-start.12 = (bf16[768,512]{1,0:T(8,128)(2,1)S(1)}, bf16[768,512]{1,0:T(8,128)(2,1)}, u32[]{:S(2)}) copy-start(bf16[768,512]{1,0:T(8,128)(2,1)} %copy-done.11) | copy-start | bytes 2359300
  122.9 20.3 %copy-start.14 = (bf16[768,512]{1,0:T(8,128)(2,1)S(1)}, bf16[768,512]{1,0:T(8,128)(2,1)}, u32[]{:S(2)}) copy-start(bf16[768,512]{1,0:T(8,128)(2,1)} %copy-done.13) | copy-start | bytes 2359300
  128.6 8.5 %collective-permute-start.21 = (bf16[1024,512]{1,0:T(8,128)(2,1)S(1)}, bf16[1024,512]{1,0:T(8,128)(2,1)S(1)}, u32[]{:S(2)}, u32[]{:S(2)}) collective-permute-start(bf16[1024,512]{1,0:T(8,128)(2,1)S(1)} %get-tuple-element.60.mine_ref), channel_id=1, source_target_pairs={{0,4},{1,5},{2,6},{3,7},{4,0},{5,1},{6,2},{7,3},{8,12},{9,13},{10,... | collective-permute-start | bytes 3145736 | tf_op jit(solution)/shard_map/ppermute | solution.py:332
  130.2 12.9 %collective-permute-start.23 = (bf16[512,768]{1,0:T(8,128)(2,1)}, bf16[512,768]{1,0:T(8,128)(2,1)S(1)}, u32[]{:S(2)}, u32[]{:S(2)}) collective-permute-start(bf16[512,768]{1,0:T(8,128)(2,1)} %collective-permute-done.15.u2), channel_id=1, source_target_pairs={{2,26},{3,27},{4,28},{5,29},{10,2},{11,3},{12,4},{13,5},{18,10},{1... | collective-permute-start | bytes 2359304 | tf_op jit(solution)/shard_map/ppermute | solution.py:287
  133.0 4.0 %collective-permute-start.22 = (f32[8,2]{1,0:T(8,128)S(1)}, f32[8,2]{1,0:T(8,128)S(1)}, u32[]{:S(2)}, u32[]{:S(2)}) collective-permute-start(f32[8,2]{1,0:T(8,128)S(1)} %max.27), channel_id=1, source_target_pairs={{0,2},{1,3},{2,0},{3,1},{4,6},{5,7},{6,4},{7,5},{8,10},{9,11},{10,... | collective-permute-start | bytes 200 | tf_op jit(solution)/shard_map/ppermute | solution.py:302
  137.1 11.6 %collective-permute-start.24 = (f32[4,2]{1,0:T(4,128)S(1)}, f32[4,2]{1,0:T(4,128)S(1)}, u32[]{:S(2)}, u32[]{:S(2)}) collective-permute-start(f32[4,2]{1,0:T(4,128)S(1)} %slice.74), channel_id=1, source_target_pairs={{0,32},{4,36},{8,40},{12,44},{16,48},{20,52},{24,56},{28,60},{32,0... | collective-permute-start | bytes 104 | tf_op jit(solution)/shard_map/ppermute | solution.py:299
  148.7 7.2 %collective-permute-start.25 = (bf16[1024,512]{1,0:T(8,128)(2,1)S(1)}, bf16[1024,512]{1,0:T(8,128)(2,1)S(1)}, u32[]{:S(2)}, u32[]{:S(2)}) collective-permute-start(bf16[1024,512]{1,0:T(8,128)(2,1)S(1)} %get-tuple-element.70.mine_ref), channel_id=1, source_target_pairs={{0,4},{1,5},{2,6},{3,7},{4,0},{5,1},{6,2},{7,3},{8,12},{9,13},{10,... | collective-permute-start | bytes 3145736 | tf_op jit(solution)/shard_map/ppermute | solution.py:339
  149.5 6.4 %collective-permute-start.26 = (f32[2,2]{1,0:T(2,128)S(1)}, f32[2,2]{1,0:T(2,128)S(1)}, u32[]{:S(2)}, u32[]{:S(2)}) collective-permute-start(f32[2,2]{1,0:T(2,128)S(1)} %slice.76), channel_id=1, source_target_pairs={{0,128},{4,132},{8,136},{12,140},{16,144},{20,148},{24,152},{28,15... | collective-permute-start | bytes 56 | tf_op jit(solution)/shard_map/ppermute | solution.py:299
  155.9 5.8 %collective-permute-start.27 = (f32[1,2]{1,0:T(1,128)S(1)}, f32[1,2]{1,0:T(1,128)S(1)}, u32[]{:S(2)}, u32[]{:S(2)}) collective-permute-start(f32[1,2]{1,0:T(1,128)S(1)} %slice.78), channel_id=1, source_target_pairs={{0,64},{4,68},{8,72},{12,76},{16,80},{20,84},{24,88},{28,92},{32,9... | collective-permute-start | bytes 32 | tf_op jit(solution)/shard_map/ppermute | solution.py:299
  162.9 2.8 %collective-permute-start.28 = (f32[1,1024]{1,0:T(1,128)S(1)}, f32[1,1024]{1,0:T(1,128)S(1)}, u32[]{:S(2)}, u32[]{:S(2)}) collective-permute-start(f32[1,1024]{1,0:T(1,128)S(1)} %slice_subtract_fusion), channel_id=1, source_target_pairs={{0,4},{1,5},{2,6},{3,7},{4,0},{5,1},{6,2},{7,3},{8,12},{9,13},{10,... | collective-permute-start | bytes 12296 | tf_op jit(solution)/shard_map/ppermute | solution.py:348
  165.7 6.6 %collective-permute-start.30 = (f32[1,1024]{1,0:T(1,128)S(1)}, f32[1,1024]{1,0:T(1,128)S(1)}, u32[]{:S(2)}, u32[]{:S(2)}) collective-permute-start(f32[1,1024]{1,0:T(1,128)S(1)} %fusion.5), channel_id=1, source_target_pairs={{2,4},{3,5},{4,2},{5,3},{10,12},{11,13},{12,10},{13,11},{18,20},{1... | collective-permute-start | bytes 12296 | tf_op jit(solution)/shard_map/ppermute | solution.py:350
  171.1 4.3 %collective-permute-start.29 = (f32[1,1024]{1,0:T(1,128)S(1)}, f32[1,1024]{1,0:T(1,128)S(1)}, u32[]{:S(2)}, u32[]{:S(2)}) collective-permute-start(f32[1,1024]{1,0:T(1,128)S(1)} %fusion.5), channel_id=1, source_target_pairs={{0,1},{1,0},{2,5},{3,4},{4,3},{5,2},{6,7},{7,6},{8,9},{9,8},{10,13... | collective-permute-start | bytes 12296 | tf_op jit(solution)/shard_map/ppermute | solution.py:349

commit v4 on v3

v4 whole, which is shorter than its diff:
```python
import functools

import jax
import jax.numpy as jnp
from jax import lax
from jax.experimental import pallas as pl
from jax.experimental.pallas import tpu as pltpu
from jax.sharding import PartitionSpec as P

BF = jnp.bfloat16
F32 = jnp.float32
AXES = ("shard", "tp")
VMEM = pl.BlockSpec(memory_space=pltpu.VMEM)
PICK, CTX, FIRST = 4096, 20000, 15000
SMEM = pl.BlockSpec(memory_space=pltpu.SMEM)
ANY = pl.BlockSpec(memory_space=pl.ANY)


def grant(kbytes):
    return pltpu.CompilerParams(vmem_limit_bytes=kbytes * 1000)


def group_perm(groups, step, member=lambda x, c: True, turn=lambda x, c: 0):
    pairs = []
    for g in range(groups):
        for c in range(2):
            for x in range(4):
                if member(x, c):
                    x2, c2 = step(x, c)
                    g2 = g // 4 * 4 + (g + turn(x, c)) % 4
                    pairs.append((g * 8 + c * 4 + x, g2 * 8 + c2 * 4 + x2))
    return pairs


def is_home(x, c):
    return x // 2 == c


def is_away(x, c):
    return x // 2 != c


def near(x, c):
    return (x ^ 1, x // 2) if is_home(x, c) else (x ^ 3, x // 2)


def partners(shards):
    far_z = (6, 7, 4, 5, 2, 3, 0, 1)
    steps = []
    for of_z, of_y, of_core in (
        (lambda z: z ^ 1, None, None),
        (lambda z: z ^ 2, None, None),
        (lambda z: far_z[z], None, None),
        (None, 1, None),
        (None, 3, None),
        (None, None, 1),
    ):
        pairs = []
        for i in range(shards):
            z, y, c = i // 8, i // 2 % 4, i % 2
            z = of_z(z) if of_z else z
            y = y ^ of_y if of_y else y
            c = c ^ of_core if of_core else c
            pairs.append((i, z * 8 + y * 2 + c))
        steps.append(pairs)
    return steps


def dot(a, b):
    return jnp.dot(a, b, preferred_element_type=F32)


def dot_nt(a, b):
    return lax.dot_general(a, b, (((1,), (1,)), ((), ())), preferred_element_type=F32)


def call(kernel, name, kbytes, outs, scratch, mflops, mbytes, scalars, arrays, far, out_specs=None):
    return pl.pallas_call(
        kernel,
        in_specs=[SMEM] * len(scalars) + [VMEM] * len(arrays) + [ANY] * len(far),
        out_specs=out_specs or [VMEM] * len(outs),
        out_shape=[jax.ShapeDtypeStruct(shape, dtype) for shape, dtype in outs],
        scratch_shapes=scratch,
        compiler_params=grant(kbytes),
        cost_estimate=pl.CostEstimate(
            flops=mflops << 20, bytes_accessed=mbytes << 20, transcendentals=0
        ),
        name=name,
    )(*scalars, *arrays, *far)


def pick_kernel(kept_ref, count_ref, emb_ref, attr_ref, out_ref):
    slots, persons = kept_ref.shape
    items = emb_ref.shape[0]
    n = out_ref.shape[0] * 32
    at = pl.program_id(0) * n
    live = lax.broadcasted_iota(jnp.int32, (slots, persons), 0) < count_ref[...]
    wanted = jnp.where(live, kept_ref[...], 4095)
    digits = jnp.concatenate([wanted >> 6, wanted & 63], 0).astype(F32).astype(BF)
    row = lax.broadcasted_iota(jnp.int32, (n, persons), 0) + at
    owner = (row // slots == lax.broadcasted_iota(jnp.int32, (n, persons), 1)).astype(BF)
    both = dot_nt(owner, digits)
    lane = lax.broadcasted_iota(jnp.int32, (n, 2 * slots), 1)
    slot = lax.broadcasted_iota(jnp.int32, (n, 2 * slots), 0) % slots
    high = jnp.where(lane == slot, both * 64.0, 0.0)
    low = jnp.where(lane == slot + slots, both, 0.0)
    rows = jnp.sum(high + low, axis=1, keepdims=True).astype(jnp.int32)
    hot = (lax.broadcasted_iota(jnp.int32, (n, items), 1) == rows).astype(BF)
    unused = rows >= items
    odd = (lax.broadcasted_iota(jnp.int32, (n, 1), 0) // slots) % 2 == 1
    for c in range(2):
        tables = (
            (emb_ref[...], attr_ref[:, 0:256])
            if c == 0
            else (attr_ref[:, 256:512], attr_ref[:, 512:768])
        )
        low, high = (jnp.where(unused, jnp.inf, dot(hot, t)) for t in tables)
        first = jnp.where(odd, low, high).astype(BF)
        second = jnp.where(odd, high, low).astype(BF)
        for g in range(n // 32):
            out_ref[g, c, :, 0:256] = first[g * 32 : (g + 1) * 32]
            out_ref[g, c, :, 256:512] = second[g * 32 : (g + 1) * 32]


def pick_rows(kept, count, emb, attr):
    slots, persons = kept.shape
    steps = 4
    return pl.pallas_call(
        pick_kernel,
        grid=(steps,),
        in_specs=[VMEM] * 4,
        out_specs=pl.BlockSpec((persons // 4 // steps, 2, 4 * slots, 512), lambda i: (i, 0, 0, 0)),
        out_shape=jax.ShapeDtypeStruct((persons // 4, 2, 4 * slots, 512), BF),
        compiler_params=grant(58500),
        cost_estimate=pl.CostEstimate(
            flops=PICK << 20, bytes_accessed=6 << 20, transcendentals=0
        ),
        name="pick_rows",
    )(kept, count, emb, attr)


def fetch(flags, layer, sources, dst_a, dst_b, sems):
    own, near_x, far_x, near_y, far_y = sources
    home = flags[0] == 1
    by_x = flags[1] == layer
    pairs = (
        (by_x, near_x, dst_a, 0),
        (jnp.logical_not(by_x), near_y, dst_a, 0),
        (home, own.at[layer], dst_b, 1),
        (jnp.logical_and(jnp.logical_not(home), by_x), far_x, dst_b, 1),
        (jnp.logical_not(jnp.logical_or(home, by_x)), far_y, dst_b, 1),
    )
    for when, src, dst, i in pairs:

        @pl.when(when)
        def _(src=src, dst=dst, i=i):
            pltpu.make_async_copy(src, dst, sems.at[i]).start()


def fetched(sources, dst_a, dst_b, sems):
    pltpu.make_async_copy(sources[1], dst_a, sems.at[0]).wait()
    pltpu.make_async_copy(sources[1], dst_b, sems.at[1]).wait()


ROWS = 256


def block_copies(src, dst, sems):
    copies = []
    for i in range(dst.shape[0] // ROWS):
        here = pl.ds(i * ROWS, ROWS)
        copies.append(pltpu.make_async_copy(src.at[here], dst.at[here], sems.at[i]))
        copies[-1].start()
    return copies


def context_kernel(
    flags, ca_hbm, cb_hbm, v0, v1, v2, v3, v4, part_hbm, pa_hbm, pb_hbm,
    ca_ref, cb_ref, va_ref, vb_ref, part_ref, v_sems, a_sems, b_sems, out_sems, head_sems,
):
    vs = (v0, v1, v2, v3, v4)
    fetch(flags, 0, vs, va_ref, vb_ref, v_sems)
    a_copies = block_copies(ca_hbm, ca_ref, a_sems)
    b_copies = block_copies(cb_hbm, cb_ref, b_sems)
    fetched(vs, va_ref, vb_ref, v_sems)
    outs = [
        pltpu.make_async_copy(va_ref.at[0:256], pa_hbm, head_sems.at[0]),
        pltpu.make_async_copy(vb_ref.at[0:256], pb_hbm, head_sems.at[1]),
    ]
    for copy in outs:
        copy.start()
    for i in range(part_ref.shape[0] // ROWS):
        here = pl.ds(i * ROWS, ROWS)
        a_copies[i].wait()
        b_copies[i].wait()
        part_ref[here] = dot(ca_ref[here], va_ref[256:768]) + dot(cb_ref[here], vb_ref[256:768])
        outs.append(pltpu.make_async_copy(part_ref.at[here], part_hbm.at[here], out_sems.at[i]))
        outs[-1].start()
    for copy in outs:
        copy.wait()


def first_kernel(
    u_ref, recv_hbm, part_hbm, pa_hbm, pb_hbm, pay_ref, piece_ref, logit_ref,
    clean, place, recv_ref, part_ref, pa_ref, pb_ref, recv_sems, part_sems, head_sems,
):
    slots = recv_ref.shape[0]
    recv_copies = block_copies(recv_hbm, recv_ref, recv_sems)
    heads = [
        pltpu.make_async_copy(pa_hbm, pa_ref, head_sems.at[0]),
        pltpu.make_async_copy(pb_hbm, pb_ref, head_sems.at[1]),
    ]
    for copy in heads:
        copy.start()
    part_copies = block_copies(part_hbm, part_ref, part_sems)
    r = lax.broadcasted_iota(jnp.int32, (ROWS, ROWS), 0)
    q = lax.broadcasted_iota(jnp.int32, (ROWS, ROWS), 1)
    upper = (r <= q).astype(BF)
    lane0 = (lax.broadcasted_iota(jnp.int32, (16, 128), 1) == 0).astype(BF)
    before = jnp.zeros((16, 1), F32)
    for i in range(slots // ROWS):
        here = slice(i * ROWS, (i + 1) * ROWS)
        recv_copies[i].wait()
        got = recv_ref[here].astype(F32)
        live = got < jnp.inf
        clean[here] = jnp.where(live, got, 0.0).astype(BF)
        marks = dot_nt(lane0, live[:, 0:128].astype(F32).astype(BF))
        upto = dot(marks.astype(BF), upper) + before
        place[:, here] = jnp.where(marks > 0.5, upto - 1.0, -1.0)
        before = upto[:, ROWS - 1 : ROWS]
    for copy in heads:
        copy.wait()
    for i in range(pay_ref.shape[0] // ROWS):
        here = pl.ds(i * ROWS, ROWS)
        k = (lax.broadcasted_iota(jnp.int32, (ROWS, slots), 0) + i * ROWS).astype(F32)
        hot = (k == place[0:1, :]).astype(BF)
        pay = dot(hot, clean[...]).astype(BF)
        pay_ref[here] = pay
        part_copies[i].wait()
        piece = part_ref[here] + dot(pay[:, 0:256], pa_ref[...]) + dot(pay[:, 256:512], pb_ref[...])
        piece_ref[here] = piece.astype(BF)
        logit_ref[:, here] = dot_nt(u_ref[...], pay)


def cross(x0, hidden, offset, x):
    x0 = x0.astype(F32)
    return (x0 * (hidden + offset) + x.astype(F32)).astype(BF)


def second_kernel(
    flags, mine_ref, other_ref, pay_ref, ba_ref, bb_ref, ca_hbm, cb_hbm,
    u0, u1, u2, u3, u4, v0, v1, v2, v3, v4, xa_ref, xb_ref, piece_ref,
    ua_ref, ub_ref, va_ref, vb_ref, ca_ref, cb_ref, u_sems, v_sems, a_sems, b_sems,
):
    us, vs = (u0, u1, u2, u3, u4), (v0, v1, v2, v3, v4)
    fetch(flags, 0, us, ua_ref, ub_ref, u_sems)
    a_copies = block_copies(ca_hbm, ca_ref, a_sems)
    b_copies = block_copies(cb_hbm, cb_ref, b_sems)
    fetch(flags, 1, vs, va_ref, vb_ref, v_sems)
    fetched(us, ua_ref, ub_ref, u_sems)
    for i in range(pay_ref.shape[0] // ROWS):
        here = pl.ds(i * ROWS, ROWS)
        proj = (mine_ref[here].astype(F32) + other_ref[here].astype(F32)).astype(BF)
        a_copies[i].wait()
        b_copies[i].wait()
        slots = (
            (xa_ref, ua_ref, ba_ref, ca_ref, 0),
            (xb_ref, ub_ref, bb_ref, cb_ref, 256),
        )
        for x_ref, u_ref, b_ref, c_ref, at in slots:
            hidden = dot(proj, u_ref[...])
            pay = pay_ref[here, at : at + 256]
            ctx = c_ref[here]
            x_ref[here, 0:256] = cross(pay, hidden[:, 0:256], b_ref[0:1, 0:256], pay)
            x_ref[here, 256:768] = cross(ctx, hidden[:, 256:768], b_ref[0:1, 256:768], ctx)
        if i == 0:
            fetched(vs, va_ref, vb_ref, v_sems)
        piece = dot(xa_ref[here], va_ref[...]) + dot(xb_ref[here], vb_ref[...])
        piece_ref[here] = piece.astype(BF)


def last_kernel(
    flags, coefficient, mine_ref, other_ref, pay_ref, xa_ref, xb_ref, sa_ref, sb_ref, logit_ref,
    ca_hbm, cb_hbm, u0, u1, u2, u3, u4, score_ref,
    ua_ref, ub_ref, ca_ref, cb_ref, u_sems, a_sems, b_sems,
):
    us = (u0, u1, u2, u3, u4)
    fetch(flags, 1, us, ua_ref, ub_ref, u_sems)
    a_copies = block_copies(ca_hbm, ca_ref, a_sems)
    b_copies = block_copies(cb_hbm, cb_ref, b_sems)
    fetched(us, ua_ref, ub_ref, u_sems)
    for i in range(pay_ref.shape[0] // ROWS):
        here = pl.ds(i * ROWS, ROWS)
        proj = (mine_ref[here].astype(F32) + other_ref[here].astype(F32)).astype(BF)
        score = coefficient[0] * logit_ref[:, here]
        a_copies[i].wait()
        b_copies[i].wait()
        for x_ref, u_ref, s_ref, c_ref, at in (
            (xa_ref, ua_ref, sa_ref, ca_ref, 0),
            (xb_ref, ub_ref, sb_ref, cb_ref, 256),
        ):
            hidden = dot(proj, u_ref[...])
            low = cross(
                pay_ref[here, at : at + 256], hidden[:, 0:256], s_ref[1:2, 0:256], x_ref[here, 0:256]
            )
            high = cross(
                c_ref[here], hidden[:, 256:768], s_ref[1:2, 256:768], x_ref[here, 256:768]
            )
            out = jnp.broadcast_to(s_ref[2:3, :], (16, 768)).astype(BF)
            score = score + dot_nt(out[:, 0:256], low) + dot_nt(out[:, 256:768], high)
        score_ref[:, here] = score


def on_device(
    person_embedding,
    catalog_embedding,
    catalog_attributes,
    kept_part_entries,
    valid_slot_number,
    pair_attributes,
    lowrank_v_matrix,
    lowrank_u_matrix,
    interaction_offset,
    final_projection,
    similarity_coefficient,
):
    shards = lax.axis_size("shard")
    groups = shards // 2
    x = lax.axis_index("tp")
    core = lax.axis_index("shard") % 2
    home = x // 2 == core
    parity = x % 2
    move = functools.partial(lax.ppermute, axis_name=AXES)
    to_core = group_perm(groups, lambda x, c: (x, 1 - c))
    to_near = group_perm(groups, near)
    home_on = group_perm(groups, lambda x, c: (x ^ 3, c), is_home)
    away_swap = group_perm(groups, lambda x, c: (x ^ 1, c), is_away)
    ctx_near = group_perm(groups, lambda x, c: (x ^ 1, c) if is_home(x, c) else (x ^ 3, 1 - c))
    ctx_far = group_perm(groups, lambda x, c: (x ^ 2, 1 - c), is_away)
    stay = lambda x, c: (x, c)
    y_up = group_perm(groups, stay, turn=lambda x, c: 1)
    y_mixed = group_perm(groups, stay, turn=lambda x, c: -1 if is_home(x, c) else 1)
    y_down = group_perm(groups, stay, is_away, lambda x, c: -1)
    by = lax.axis_index("shard") // 2 % 2
    flags = jnp.stack([home.astype(jnp.int32), by])

    persons, _, kept = kept_part_entries.shape
    hops = partners(shards)
    users = person_embedding[None]

    def double(users, pairs):
        return jnp.concatenate([users, lax.ppermute(users, "shard", pairs)], 0)

    for pairs in hops[:3]:
        users = double(users, pairs)
    v_mine = lax.dynamic_index_in_dim(lowrank_v_matrix, by, 0, False)
    u_mine = lax.dynamic_index_in_dim(lowrank_u_matrix, by, 0, False)
    v_near = move(v_mine, perm=to_near)
    u_near = move(u_mine, perm=to_near)
    ctx_a = move(lax.dynamic_index_in_dim(pair_attributes, 1 - parity, 0, False), perm=ctx_near)
    ctx_own = lax.dynamic_index_in_dim(pair_attributes, parity, 0, False)
    parcel = pick_rows(
        kept_part_entries[:, 0, :].T, valid_slot_number.T, catalog_embedding, catalog_attributes
    )

    parcel = parcel.reshape(persons * 2, kept, 512)
    parcel, v_near, ctx_a, users = lax.optimization_barrier((parcel, v_near, ctx_a, users))
    recv = lax.all_to_all(parcel, AXES, split_axis=0, concat_axis=0, tiled=True)
    recv = recv.reshape(persons * 2 * kept, 512)

    small = jnp.concatenate([interaction_offset, final_projection[None, :].astype(F32)], 0)
    small, v_near = lax.optimization_barrier((small, v_near))
    small_a = move(small, perm=to_near)
    small_b = move(small, perm=ctx_far)
    v_far = move(v_near, perm=home_on)
    u_far = move(u_near, perm=away_swap)
    v_near_y = move(v_near, perm=y_up)
    u_near_y = move(u_near, perm=y_mixed)

    ctx_own, small_a, small_b = lax.optimization_barrier((ctx_own, small_a, small_b))
    ctx_b = jnp.where(home, ctx_own, move(ctx_own, perm=ctx_far))
    small_b = jnp.where(home, small, small_b)
    v_far, users = lax.optimization_barrier((v_far, users))
    v_far_y = move(v_far, perm=y_down)
    u_far_y = move(u_far, perm=y_down)
    ctx_a, u_far, u_near_y, u_far_y = lax.optimization_barrier((ctx_a, u_far, u_near_y, u_far_y))
    vs = (lowrank_v_matrix, v_near, v_far, v_near_y, v_far_y)
    us = (lowrank_u_matrix, u_near, u_far, u_near_y, u_far_y)

    for pairs in hops[3:]:
        users = double(users, pairs)
    all_scores = jnp.einsum(
        "ue,ie->ui", users.reshape(persons, -1), catalog_embedding, preferred_element_type=F32
    )
    best = jnp.max(all_scores, axis=1).reshape(shards, persons // shards)

    def halve(best, pairs):
        half = best.shape[0] // 2
        return jnp.maximum(best[:half], lax.ppermute(best[half:], "shard", pairs))

    def over_x(best, flip):
        return jnp.maximum(best, lax.ppermute(best, "tp", [(i, i ^ flip) for i in range(4)]))

    for pairs in hops[:2:-1]:
        best = halve(best, pairs)

    query = lax.dynamic_slice_in_dim(jnp.where(home, person_embedding, users[shards // 2]), parity, 1, 0)
    query = jnp.where(core == 0, query, jnp.zeros_like(query))
    zero = jnp.zeros_like(query)
    query = jnp.where(
        parity == 1, jnp.concatenate([query, zero], 1), jnp.concatenate([zero, query], 1)
    )
    query = jnp.broadcast_to(query, (16, 512))

    surv = pair_attributes.shape[1]
    blocks = surv // ROWS
    tall, wide, lanes = ((surv, 512), BF), ((surv, 768), BF), ((16, surv), F32)
    part_like, head = ((surv, 512), F32), ((256, 512), BF)
    v_pair = [pltpu.VMEM((768, 512), BF)] * 2
    u_pair = [pltpu.VMEM((512, 768), BF)] * 2
    ctx_pair = [pltpu.VMEM((surv, 512), BF)] * 2

    def sems(*counts):
        return [pltpu.SemaphoreType.DMA((n,)) for n in counts]

    part, head_a, head_b = call(
        context_kernel, "context_part", 62500, [part_like, head, head],
        ctx_pair + v_pair + [pltpu.VMEM(*part_like)] + sems(2, blocks, blocks, blocks, 2),
        CTX, 8, [flags], [], [ctx_a, ctx_b, *vs], [ANY] * 3,
    )
    recv, best = lax.optimization_barrier((recv, best))
    step = over_x(best, 1)
    pay, piece, logit = call(
        first_kernel, "first_layer", 61000, [tall, tall, lanes],
        [pltpu.VMEM(recv.shape, BF), pltpu.VMEM((16, recv.shape[0]), F32)]
        + [pltpu.VMEM(recv.shape, BF), pltpu.VMEM(*part_like)]
        + [pltpu.VMEM(*head)] * 2
        + sems(recv.shape[0] // ROWS, blocks, 2),
        FIRST, 8, [], [query], [recv, part, head_a, head_b],
    )
    piece, best = lax.optimization_barrier((piece, step))
    other, best = lax.optimization_barrier((move(piece, perm=to_core), over_x(best, 3)))
    step = halve(best, hops[2])
    x_a, x_b, piece1 = call(
        second_kernel, "second_layer", 55500, [wide, wide, tall],
        u_pair + v_pair + ctx_pair + sems(2, 2, blocks, blocks),
        3584, 12, [flags], [piece, other, pay, small_a, small_b], [ctx_a, ctx_b, *us, *vs],
    )
    piece1, best = lax.optimization_barrier((piece1, step))
    other1, best = lax.optimization_barrier((move(piece1, perm=to_core), halve(best, hops[1])))
    step = halve(best, hops[0])
    (score,) = call(
        last_kernel, "last_layer", 56500, [lanes], u_pair + ctx_pair + sems(2, blocks, blocks),
        1792, 10, [flags, similarity_coefficient],
        [piece1, other1, pay, x_a, x_b, small_a, small_b, logit], [ctx_a, ctx_b, *us],
    )
    score, best = lax.optimization_barrier((score, step))
    top = jnp.where(home, lax.dynamic_slice_in_dim(best, parity, 1, 1), 0.0)
    score = score[0:1] - similarity_coefficient[0] * top
    score = score + move(score, perm=to_core)
    score_a = move(score, perm=to_near)
    score_b = jnp.where(home, score, move(score, perm=ctx_far))
    return jnp.where(
        parity == 1,
        jnp.concatenate([score_a, score_b], 0),
        jnp.concatenate([score_b, score_a], 0),
    )


def solution(mesh):
    return jax.shard_map(
        on_device,
        mesh=mesh,
        in_specs=(
            P("shard", None),
            P(("shard", "tp"), None),
            P(("shard", "tp"), None),
            P(None, ("shard", "tp"), None),
            P(None, ("shard", "tp")),
            P("shard", None, "tp"),
            P(None, "tp", None),
            P(None, None, "tp"),
            P(None, "tp"),
            P("tp"),
            P(),
        ),
        out_specs=P("shard", None),
        check_vma=False,
    )
```

time: 177 us -> 196 us (1.11)
  Pallas kernels: 23.5 us -> 43 us
  local copies, waits for them, and re-layouts: 20.2 us -> 6.01 us
  starting transfers between devices: 75 us -> 87.3 us
  other arithmetic: 3.72 us -> 6.13 us
    pallas_call x5, Pallas kernels: 23.5 us -> 43 us  [the longest x4 34 us: call(): pl.pallas_call(kernel, in_specs=[SMEM] * len(scalars) + [VMEM] * len(arra...]
    unnamed x64 -> x30, local copies, waits for them, and re-layouts: 14.7 us -> 0.94 us
    ppermute x1, waiting for transfers between devices: 10.4 us -> 0.01 us  [on_device(): ctx_b = jnp.where(home, ctx_own, move(ctx_own, perm=ctx_far))]
    ppermute x3, starting transfers between devices: 5.87 us -> 13.9 us  [the longest x1 5.17 us: on_device(): u_far_y = move(u_far, perm=y_down)]
    ppermute x6, starting transfers between devices: 7.41 us -> 11.8 us  [halve(): return jnp.maximum(best[:half], lax.ppermute(best[half:], 'shard', pairs))]
    ppermute x1, waiting for transfers between devices: 0.01 us -> 4.27 us  [on_device(): u_far = move(u_near, perm=away_swap)]
    ppermute x6, waiting for transfers between devices: 20.7 us -> 24.6 us  [halve(): return jnp.maximum(best[:half], lax.ppermute(best[half:], 'shard', pairs))]
    ppermute x2, starting transfers between devices: 1.28 us -> 4.85 us  [over_x(): lax.ppermute(best, 'tp', [(i, i ^ flip) for i in range(4)])]
  transfers between devices with their start and end apart: 32 -> 32, of which waited for: 14 -> 17; matrix products, arithmetic and copies ran while one was open for 5% -> 4% of each run, Pallas kernels for 13% -> 22%
where the time goes in v4:
time: 196 us; the launch traced here: 195 us
  starting transfers between devices  87.3 us (45%)
  waiting for transfers between devices  49.4 us (25%)
  Pallas kernels  43 us (22%)
  other arithmetic  6.13 us (3%)
  local copies, waits for them, and re-layouts  6.01 us (3%)
    pallas_call x4, Pallas kernels, call(): pl.pallas_call(kernel, in_specs=[SMEM] * len(scalars) + [VMEM] * len(arra...  34 us
    ppermute x6, waiting for transfers between devices, halve(): return jnp.maximum(best[:half], lax.ppermute(best[half:], 'shard', pairs))  24.6 us
    ppermute x6, starting transfers between devices, double(): return jnp.concatenate([users, lax.ppermute(users, 'shard', pairs)], 0)  17.4 us
    all_to_all x1, starting transfers between devices, on_device(): recv = lax.all_to_all(parcel, AXES, split_axis=0, concat_axis=0, tiled=True)  16 us
    ppermute x6, starting transfers between devices, halve(): return jnp.maximum(best[:half], lax.ppermute(best[half:], 'shard', pairs))  11.8 us
    pallas_call x1, Pallas kernels, pick_rows(): pl.pallas_call(pick_kernel, grid=(steps,), in_specs=[VMEM] * 4, out_specs...  9.01 us
    ppermute x6, waiting for transfers between devices, double(): return jnp.concatenate([users, lax.ppermute(users, 'shard', pairs)], 0)  6.06 us
    ppermute x1, waiting for transfers between devices, on_device(): v_far_y = move(v_far, perm=y_down)  5.82 us
  transfers between devices with their start and end apart: 32, of which 17 were waited for; matrix products, arithmetic and copies ran while one was open for 4% of the time, Pallas kernels for 22%

profile of v4, /device:TPU:1, one launch (start us, length us, event | category | flops | bytes accessed | tf_op | source)
XLA Modules:
  0.0 195.3 jit_solution(10023077885385916810)
XLA Ops:
  0.0 3.1 %dynamic-slice_bitcast_fusion = (bf16[1024,512]{1,0:T(8,128)(2,1)}, bf16[1024,512]{1,0:T(8,128)(2,1)}) fusion(bf16[2,1024,512]{2,1,0:T(8,128)(2,1)} %param.16, s32[]{:T(128)S(6)} %select_n.113, s32[]{:T(128)S(6)} %select_n.111), kind=kLoop, calls=%fused_computation.1 | loop fusion | bytes 4194312 | tf_op jit(solution)/shard_map/jit(dynamic_index_in_dim)/squeeze | solution.py:361
  3.1 3.9 %collective-permute-start.1 = (bf16[1024,512]{1,0:T(8,128)(2,1)}, bf16[1024,512]{1,0:T(8,128)(2,1)S(1)}, u32[]{:S(2)}, u32[]{:S(2)}) collective-permute-start(bf16[1024,512]{1,0:T(8,128)(2,1)} %get-tuple-element.78), channel_id=1, source_target_pairs={{0,1},{1,0},{2,5},{3,4},{4,3},{5,2},{6,7},{7,6},{8,9},{9,8},{10,13... | collective-permute-start | bytes 3145736 | tf_op jit(solution)/shard_map/ppermute | solution.py:360
  7.0 1.6 collective-permute-start.2
  8.7 0.4 collective-permute-start
  9.1 0.8 collective-permute-done.2
  9.9 3.1 %collective-permute-start.3 = (bf16[2,2,256]{2,1,0:T(2,128)(2,1)S(1)}, bf16[2,2,256]{2,1,0:T(2,128)(2,1)S(1)}, u32[]{:S(2)}, u32[]{:S(2)}) collective-permute-start(bf16[2,2,256]{2,1,0:T(2,128)(2,1)S(1)} %pad_maximum_fusion.6), channel_id=1, source_target_pairs={{0,64},{4,68},{8,72},{12,76},{16,80},{20,84},{24,88},{28,92},{32,9... | collective-permute-start | bytes 6152 | tf_op jit(solution)/shard_map/ppermute | solution.py:352
  13.0 9.0 %pick_rows.1 = bf16[32,2,32,512]{3,2,1,0:T(8,128)(2,1)} custom-call(s32[8,128]{1,0:T(8,128)} %bitcast.30, s32[1,128]{1,0:T(1,128)} %bitcast.31, bf16[2048,256]{1,0:T(8,128)(2,1)} %emb_ref.1, bf16[2048,768]{1,0:T(8,128)(2,1)} %attr_ref.1), custom_call_target="tpu_custom_call" | custom-call | flops 4294967296 | bytes 6291456 | tf_op jit(solution)/shard_map/pick_rows/pallas_call | solution.py:128
  22.0 4.1 %collective-permute-start.4 = (bf16[4,2,256]{2,1,0:T(2,128)(2,1)S(1)}, bf16[4,2,256]{2,1,0:T(2,128)(2,1)S(1)}, u32[]{:S(2)}, u32[]{:S(2)}) collective-permute-start(bf16[4,2,256]{2,1,0:T(2,128)(2,1)S(1)} %pad_maximum_fusion.5), channel_id=1, source_target_pairs={{0,192},{4,196},{8,200},{12,204},{16,208},{20,212},{24,216},{28,22... | collective-permute-start | bytes 12296 | tf_op jit(solution)/shard_map/ppermute | solution.py:352
  26.1 1.0 collective-permute-done.4
  27.1 1.1 collective-permute-done.v1
  28.2 1.3 collective-permute-start.5
  29.5 1.0 dynamic-slice_bitcast_fusion.2
  30.5 3.0 %collective-permute-start.12 = (bf16[512,768]{1,0:T(8,128)(2,1)}, bf16[512,768]{1,0:T(8,128)(2,1)S(1)}, u32[]{:S(2)}, u32[]{:S(2)}) collective-permute-start(bf16[512,768]{1,0:T(8,128)(2,1)} %dynamic-slice_bitcast_fusion.2), channel_id=1, source_target_pairs={{0,1},{1,0},{2,5},{3,4},{4,3},{5,2},{6,7},{7,6},{8,9},{9,8},{10,13... | collective-permute-start | bytes 2359304 | tf_op jit(solution)/shard_map/ppermute | solution.py:359
  33.4 16.0 %all-to-all-start = ((bf16[256,8,512]{2,1,0:T(8,128)(2,1)}), bf16[256,8,512]{2,1,0:T(8,128)(2,1)}, u32[]{:S(2)}, u32[]{:S(2)}) async-start(bf16[256,8,512]{2,1,0:T(8,128)(2,1)} %bitcast.25), calls=%async_computation | async-start | bytes 4194304 | tf_op jit(solution)/shard_map/all_to_all | solution.py:368
  49.5 0.5 collective-permute-done.5.v2
  49.9 1.3 collective-permute-start.6
  51.3 2.4 %collective-permute-done.6 = bf16[8,2,256]{2,1,0:T(2,128)(2,1)S(1)} collective-permute-done((bf16[8,2,256]{2,1,0:T(2,128)(2,1)S(1)}, bf16[8,2,256]{2,1,0:T(2,128)(2,1)S(1)}, u32[]{:S(2)}, u32[]{:S(2)}) %collective-permute-start.6) | collective-permute-done | bytes 8224 | tf_op jit(solution)/shard_map/ppermute | solution.py:352
  53.7 2.5 %collective-permute-start.7 = (bf16[16,2,256]{2,1,0:T(2,128)(2,1)S(1)}, bf16[16,2,256]{2,1,0:T(2,128)(2,1)S(1)}, u32[]{:S(2)}, u32[]{:S(2)}) collective-permute-start(bf16[16,2,256]{2,1,0:T(2,128)(2,1)S(1)} %pad_maximum_fusion.2), channel_id=1, source_target_pairs={{0,24},{4,28},{8,16},{12,20},{16,8},{20,12},{24,0},{28,4},{32,56},... | collective-permute-start | bytes 49160 | tf_op jit(solution)/shard_map/ppermute | solution.py:352
  56.2 1.8 collective-permute-done.7
  58.1 4.8 %collective-permute-start.8 = (bf16[32,2,256]{2,1,0:T(2,128)(2,1)S(1)}, bf16[32,2,256]{2,1,0:T(2,128)(2,1)S(1)}, u32[]{:S(2)}, u32[]{:S(2)}) collective-permute-start(bf16[32,2,256]{2,1,0:T(2,128)(2,1)S(1)} %pad_maximum_fusion.1), channel_id=1, source_target_pairs={{0,4},{4,0},{8,12},{12,8},{16,20},{20,16},{24,28},{28,24},{32,36},... | collective-permute-start | bytes 98312 | tf_op jit(solution)/shard_map/ppermute | solution.py:352
  62.9 4.0 %collective-permute-start.16 = (f32[3,768]{1,0:T(4,128)S(1)}, f32[3,768]{1,0:T(4,128)S(1)}, u32[]{:S(2)}, u32[]{:S(2)}) collective-permute-start(f32[3,768]{1,0:T(4,128)S(1)} %pad_maximum_fusion.3), channel_id=1, source_target_pairs={{0,1},{1,0},{2,5},{3,4},{4,3},{5,2},{6,7},{7,6},{8,9},{9,8},{10,13... | collective-permute-start | bytes 27656 | tf_op jit(solution)/shard_map/ppermute | solution.py:373
  66.9 1.9 collective-permute-start.17
  68.9 2.5 %collective-permute-start.13 = (bf16[512,768]{1,0:T(8,128)(2,1)S(1)}, bf16[512,768]{1,0:T(8,128)(2,1)S(1)}, u32[]{:S(2)}, u32[]{:S(2)}) collective-permute-start(bf16[512,768]{1,0:T(8,128)(2,1)S(1)} %collective-permute-done.12.u1), channel_id=1, source_target_pairs={{2,3},{3,2},{4,5},{5,4},{10,11},{11,10},{12,13},{13,12},{18,19},{1... | collective-permute-start | bytes 2359304 | tf_op jit(solution)/shard_map/ppermute | solution.py:376
  71.4 2.4 %collective-permute-done.17 = f32[3,768]{1,0:T(4,128)S(1)} collective-permute-done((f32[3,768]{1,0:T(4,128)S(1)}, f32[3,768]{1,0:T(4,128)S(1)}, u32[]{:S(2)}, u32[]{:S(2)}) %collective-permute-start.17) | collective-permute-done | bytes 9248 | tf_op jit(solution)/shard_map/ppermute | solution.py:374
  73.8 2.1 %collective-permute-start.18 = (bf16[1024,512]{1,0:T(8,128)(2,1)S(1)}, bf16[1024,512]{1,0:T(8,128)(2,1)}, u32[]{:S(2)}, u32[]{:S(2)}) collective-permute-start(bf16[1024,512]{1,0:T(8,128)(2,1)S(1)} %copy-done.4), channel_id=1, source_target_pairs={{2,4},{3,5},{4,2},{5,3},{10,12},{11,13},{12,10},{13,11},{18,20},{1... | collective-permute-start | bytes 3145736 | tf_op jit(solution)/shard_map/ppermute | solution.py:381
  76.0 0.1 pad_maximum_fusion
  76.1 1.8 convolution_reduce_fusion
  78.0 0.1 slice.68
  78.1 0.1 collective-permute-start.9
  78.2 0.7 pad_add_fusion.flags
  78.9 0.1 slice.66
  79.0 0.4 collective-permute-done.9
  79.4 3.0 %collective-permute-start.10 = (f32[16,2]{1,0:T(8,128)S(1)}, f32[16,2]{1,0:T(8,128)S(1)}, u32[]{:S(2)}, u32[]{:S(2)}) collective-permute-start(f32[16,2]{1,0:T(8,128)S(1)} %slice.82), channel_id=1, source_target_pairs={{0,24},{4,28},{8,16},{12,20},{16,8},{20,12},{24,0},{28,4},{32,56},... | collective-permute-start | bytes 392 | tf_op jit(solution)/shard_map/ppermute | solution.py:399
  82.3 1.5 collective-permute-done.10
  83.9 4.3 %collective-permute-done.13.u2 = bf16[512,768]{1,0:T(8,128)(2,1)S(1)} collective-permute-done((bf16[512,768]{1,0:T(8,128)(2,1)S(1)}, bf16[512,768]{1,0:T(8,128)(2,1)S(1)}, u32[]{:S(2)}, u32[]{:S(2)}) %collective-permute-start.13) | collective-permute-done | bytes 786464 | tf_op jit(solution)/shard_map/ppermute | solution.py:376
  88.2 5.2 %collective-permute-start.15 = (bf16[512,768]{1,0:T(8,128)(2,1)S(1)}, bf16[512,768]{1,0:T(8,128)(2,1)S(1)}, u32[]{:S(2)}, u32[]{:S(2)}) collective-permute-start(bf16[512,768]{1,0:T(8,128)(2,1)S(1)} %collective-permute-done.13.u2), channel_id=1, source_target_pairs={{2,26},{3,27},{4,28},{5,29},{10,2},{11,3},{12,4},{13,5},{18,10},{1... | collective-permute-start | bytes 2359304 | tf_op jit(solution)/shard_map/ppermute | solution.py:385
  93.3 20.7 %collective-permute-done.11 = f32[8,2]{1,0:T(8,128)S(1)} collective-permute-done((f32[8,2]{1,0:T(8,128)S(1)}, f32[8,2]{1,0:T(8,128)S(1)}, u32[]{:S(2)}, u32[]{:S(2)}) %collective-permute-start.11) | collective-permute-done | bytes 96 | tf_op jit(solution)/shard_map/ppermute | solution.py:399
  114.0 4.9 %collective-permute-start.20 = (bf16[768,512]{1,0:T(8,128)(2,1)}, bf16[768,512]{1,0:T(8,128)(2,1)}, u32[]{:S(2)}, u32[]{:S(2)}) collective-permute-start(bf16[768,512]{1,0:T(8,128)(2,1)} %collective-permute-done.5.v2), channel_id=1, source_target_pairs={{2,26},{3,27},{4,28},{5,29},{10,2},{11,3},{12,4},{13,5},{18,10},{1... | collective-permute-start | bytes 2359304 | tf_op jit(solution)/shard_map/ppermute | solution.py:384
  119.0 2.4 %broadcast_select_fusion.cb_hbm = bf16[1024,512]{1,0:T(8,128)(2,1)} fusion(bf16[1024,512]{1,0:T(8,128)(2,1)S(1)} %copy-done.4, bf16[1024,512]{1,0:T(8,128)(2,1)} %collective-permute-done.18, pred[]{:T(512)} %eq.15), kind=kLoop, calls=%fused_computation.3 | loop fusion | flops 524288 | bytes 3145729 | tf_op jit(solution)/shard_map/jit(_where)/select_n | solution.py:381
  121.5 0.9 copy-done.8
  122.4 5.8 %collective-permute-done.20.v4 = bf16[768,512]{1,0:T(8,128)(2,1)} collective-permute-done((bf16[768,512]{1,0:T(8,128)(2,1)}, bf16[768,512]{1,0:T(8,128)(2,1)}, u32[]{:S(2)}, u32[]{:S(2)}) %collective-permute-start.20) | collective-permute-done | bytes 786464 | tf_op jit(solution)/shard_map/ppermute | solution.py:384
  128.2 5.1 %context_part.1 = (f32[1024,512]{1,0:T(8,128)}, bf16[256,512]{1,0:T(8,128)(2,1)}, bf16[256,512]{1,0:T(8,128)(2,1)}) custom-call(s32[2]{0:T(128)} %pad_add_fusion.flags, bf16[1024,512]{1,0:T(8,128)(2,1)} %copy-done.3, bf16[1024,512]{1,0:T(8,128)(2,1)} %broadcast_select_fusion.cb_hbm, bf16[2,768,512]{2,1,0:T(8,128)(2,1)} %v0.3, ...), custom_call_target="tpu_custom_call" | custom-call | flops 20971520000 | bytes 8388608 | tf_op jit(solution)/shard_map/context_part/pallas_call | solution.py:78
  133.3 0.8 collective-permute-start.21
  134.1 0.6 broadcast_in_dim.15.u_ref
  134.7 9.5 %first_layer.1 = (bf16[1024,512]{1,0:T(8,128)(2,1)}, bf16[1024,512]{1,0:T(8,128)(2,1)}, f32[16,1024]{1,0:T(8,128)}) custom-call(bf16[16,512]{1,0:T(8,128)(2,1)} %broadcast_in_dim.15.u_ref, bf16[2048,512]{1,0:T(8,128)(2,1)} %bitcast.10.recv_hbm, f32[1024,512]{1,0:T(8,128)} %get-tuple-element.52.part_hbm, bf16[256,512]{1,0:T(8,128)(2,1)} %get-tuple-element.53.pa_hbm, ...), custom_call_target="tpu_custom_call" | custom-call | flops 15728640000 | bytes 8388608 | tf_op jit(solution)/shard_map/first_layer/pallas_call | solution.py:78
  144.3 4.0 %collective-permute-start.23 = (f32[8,2]{1,0:T(8,128)S(1)}, f32[8,2]{1,0:T(8,128)S(1)}, u32[]{:S(2)}, u32[]{:S(2)}) collective-permute-start(f32[8,2]{1,0:T(8,128)S(1)} %max.27), channel_id=1, source_target_pairs={{0,3},{1,2},{2,1},{3,0},{4,7},{5,6},{6,5},{7,4},{8,11},{9,10},{10,... | collective-permute-start | bytes 200 | tf_op jit(solution)/shard_map/ppermute | solution.py:402
  148.3 1.0 collective-permute-done.23
  149.3 6.1 %collective-permute-start.24 = (f32[4,2]{1,0:T(4,128)S(1)}, f32[4,2]{1,0:T(4,128)S(1)}, u32[]{:S(2)}, u32[]{:S(2)}) collective-permute-start(f32[4,2]{1,0:T(4,128)S(1)} %slice.74), channel_id=1, source_target_pairs={{0,192},{4,196},{8,200},{12,204},{16,208},{20,212},{24,216},{28,22... | collective-permute-start | bytes 104 | tf_op jit(solution)/shard_map/ppermute | solution.py:399
  155.5 9.8 %second_layer.1 = (bf16[1024,768]{1,0:T(8,128)(2,1)}, bf16[1024,768]{1,0:T(8,128)(2,1)}, bf16[1024,512]{1,0:T(8,128)(2,1)}) custom-call(s32[2]{0:T(128)S(1)} %copy-done.1, bf16[1024,512]{1,0:T(8,128)(2,1)} %get-tuple-element.57.mine_ref, bf16[1024,512]{1,0:T(8,128)(2,1)} %copy-done.10, bf16[1024,512]{1,0:T(8,128)(2,1)} %get-tuple-element.60.pay_ref, ...), custom_call_target="tpu_custom_call" | custom-call | flops 3758096384 | bytes 12582912 | tf_op jit(solution)/shard_map/second_layer/pallas_call | solution.py:78
  165.3 1.2 collective-permute-start.25
  167.1 1.6 collective-permute-start.26
  168.7 2.0 %collective-permute-done.26 = f32[2,2]{1,0:T(2,128)S(1)} collective-permute-done((f32[2,2]{1,0:T(2,128)S(1)}, f32[2,2]{1,0:T(2,128)S(1)}, u32[]{:S(2)}, u32[]{:S(2)}) %collective-permute-start.26) | collective-permute-done | bytes 48 | tf_op jit(solution)/shard_map/ppermute | solution.py:399
  170.7 1.0 collective-permute-start.27
  171.7 9.7 %last_layer.1 = f32[16,1024]{1,0:T(8,128)} custom-call(s32[2]{0:T(128)S(1)} %copy-done.1, f32[1]{0:T(128)} %copy.12.coefficient, bf16[1024,512]{1,0:T(8,128)(2,1)} %get-tuple-element.68.mine_ref, bf16[1024,512]{1,0:T(8,128)(2,1)} %copy-done.9, bf16[1024,512]{1,0:T(8,128)(2,1)} %get-tuple-element.60.pay_ref, bf16[1024,768]{1,0:T(8,128)(2,1)} %get-tuple-element.71.xa_ref, ...), custom_call_target="tpu_custom_call" | custom-call | flops 1879048192 | bytes 10485760 | tf_op jit(solution)/shard_map/last_layer/pallas_call | solution.py:78
  181.5 0.6 fusion.2
  182.7 0.8 slice_subtract_fusion
  183.5 1.0 collective-permute-start.28
  184.4 0.8 collective-permute-done.28
  185.3 0.8 fusion.5
  186.0 4.3 %collective-permute-start.30 = (f32[1,1024]{1,0:T(1,128)S(1)}, f32[1,1024]{1,0:T(1,128)S(1)}, u32[]{:S(2)}, u32[]{:S(2)}) collective-permute-start(f32[1,1024]{1,0:T(1,128)S(1)} %fusion.5), channel_id=1, source_target_pairs={{2,4},{3,5},{4,2},{5,3},{10,12},{11,13},{12,10},{13,11},{18,20},{1... | collective-permute-start | bytes 12296 | tf_op jit(solution)/shard_map/ppermute | solution.py:462
  190.4 1.5 collective-permute-start.29
  191.8 0.6 collective-permute-done.30
  192.5 2.3 %collective-permute-done.29 = f32[1,1024]{1,0:T(1,128)S(1)} collective-permute-done((f32[1,1024]{1,0:T(1,128)S(1)}, f32[1,1024]{1,0:T(1,128)S(1)}, u32[]{:S(2)}, u32[]{:S(2)}) %collective-permute-start.29) | collective-permute-done | bytes 4128 | tf_op jit(solution)/shard_map/ppermute | solution.py:461
  194.7 0.6 maximum_select_fusion
  (76 shorter events, 0.6 us)
Async XLA Ops:
  0.0 7.0 %copy-start.12 = (bf16[2,256]{1,0:T(2,128)(2,1)S(1)}, bf16[2,256]{1,0:T(2,128)(2,1)}, u32[]{:S(2)}) copy-start(bf16[2,256]{1,0:T(2,128)(2,1)} %param.11) | copy-start | bytes 3076
  0.0 8.6 %copy-start.5 = (bf16[2,768,512]{2,1,0:T(8,128)(2,1)S(1)}, bf16[2,768,512]{2,1,0:T(8,128)(2,1)}, u32[]{:S(2)}) copy-start(bf16[2,768,512]{2,1,0:T(8,128)(2,1)} %v0.3) | copy-start | bytes 4718596
  3.1 25.1 %collective-permute-start.1 = (bf16[1024,512]{1,0:T(8,128)(2,1)}, bf16[1024,512]{1,0:T(8,128)(2,1)S(1)}, u32[]{:S(2)}, u32[]{:S(2)}) collective-permute-start(bf16[1024,512]{1,0:T(8,128)(2,1)} %get-tuple-element.78), channel_id=1, source_target_pairs={{0,1},{1,0},{2,5},{3,4},{4,3},{5,2},{6,7},{7,6},{8,9},{9,8},{10,13... | collective-permute-start | bytes 3145736 | tf_op jit(solution)/shard_map/ppermute | solution.py:360
  7.0 2.9 %collective-permute-start.2 = (bf16[1,2,256]{2,1,0:T(2,128)(2,1)S(1)}, bf16[1,2,256]{2,1,0:T(2,128)(2,1)S(1)}, u32[]{:S(2)}, u32[]{:S(2)}) collective-permute-start(bf16[1,2,256]{2,1,0:T(2,128)(2,1)S(1)} %bitcast.26), channel_id=1, source_target_pairs={{0,32},{4,36},{8,40},{12,44},{16,48},{20,52},{24,56},{28,60},{32,0... | collective-permute-start | bytes 3080 | tf_op jit(solution)/shard_map/ppermute | solution.py:352
  8.7 19.5 %collective-permute-start = (bf16[768,512]{1,0:T(8,128)(2,1)S(1)}, bf16[768,512]{1,0:T(8,128)(2,1)}, u32[]{:S(2)}, u32[]{:S(2)}) collective-permute-start(bf16[768,512]{1,0:T(8,128)(2,1)S(1)} %dynamic-slice_bitcast_fusion.3), channel_id=1, source_target_pairs={{0,1},{1,0},{2,5},{3,4},{4,3},{5,2},{6,7},{7,6},{8,9},{9,8},{10,13... | collective-permute-start | bytes 2359304 | tf_op jit(solution)/shard_map/ppermute | solution.py:358
  9.9 12.1 %collective-permute-start.3 = (bf16[2,2,256]{2,1,0:T(2,128)(2,1)S(1)}, bf16[2,2,256]{2,1,0:T(2,128)(2,1)S(1)}, u32[]{:S(2)}, u32[]{:S(2)}) collective-permute-start(bf16[2,2,256]{2,1,0:T(2,128)(2,1)S(1)} %pad_maximum_fusion.6), channel_id=1, source_target_pairs={{0,64},{4,68},{8,72},{12,76},{16,80},{20,84},{24,88},{28,92},{32,9... | collective-permute-start | bytes 6152 | tf_op jit(solution)/shard_map/ppermute | solution.py:352
  13.0 9.0 %copy-start.14 = (bf16[768]{0:T(1024)(128)(2,1)S(1)}, bf16[768]{0:T(1024)(128)(2,1)}, u32[]{:S(2)}) copy-start(bf16[768]{0:T(1024)(128)(2,1)} %param.20) | copy-start | bytes 4612
  13.0 13.2 %copy-start.13 = (f32[2,768]{1,0:T(2,128)S(1)}, f32[2,768]{1,0:T(2,128)}, u32[]{:S(2)}) copy-start(f32[2,768]{1,0:T(2,128)} %param.19) | copy-start | bytes 18436
  13.0 16.5 %copy-start.2 = (bf16[2,512,768]{2,1,0:T(8,128)(2,1)S(1)}, bf16[2,512,768]{2,1,0:T(8,128)(2,1)}, u32[]{:S(2)}) copy-start(bf16[2,512,768]{2,1,0:T(8,128)(2,1)} %u0.3) | copy-start | bytes 4718596
  22.0 5.1 %collective-permute-start.4 = (bf16[4,2,256]{2,1,0:T(2,128)(2,1)S(1)}, bf16[4,2,256]{2,1,0:T(2,128)(2,1)S(1)}, u32[]{:S(2)}, u32[]{:S(2)}) collective-permute-start(bf16[4,2,256]{2,1,0:T(2,128)(2,1)S(1)} %pad_maximum_fusion.5), channel_id=1, source_target_pairs={{0,192},{4,196},{8,200},{12,204},{16,208},{20,212},{24,216},{28,22... | collective-permute-start | bytes 12296 | tf_op jit(solution)/shard_map/ppermute | solution.py:352
  28.2 5.2 %copy-start.3 = (bf16[1024,512]{1,0:T(8,128)(2,1)}, bf16[1024,512]{1,0:T(8,128)(2,1)S(1)}, u32[]{:S(2)}) copy-start(bf16[1024,512]{1,0:T(8,128)(2,1)S(1)} %collective-permute-done.1.ca_hbm) | copy-start | bytes 3145732
  28.2 21.7 %collective-permute-start.5 = (bf16[768,512]{1,0:T(8,128)(2,1)}, bf16[768,512]{1,0:T(8,128)(2,1)}, u32[]{:S(2)}, u32[]{:S(2)}) collective-permute-start(bf16[768,512]{1,0:T(8,128)(2,1)} %collective-permute-done.v1), channel_id=1, source_target_pairs={{0,3},{1,2},{6,5},{7,4},{8,11},{9,10},{14,13},{15,12},{16,19},{17,... | collective-permute-start | bytes 2359304 | tf_op jit(solution)/shard_map/ppermute | solution.py:375
  30.5 43.3 %copy-start.4 = (bf16[1024,512]{1,0:T(8,128)(2,1)S(1)}, bf16[1024,512]{1,0:T(8,128)(2,1)}, u32[]{:S(2)}) copy-start(bf16[1024,512]{1,0:T(8,128)(2,1)} %get-tuple-element.50) | copy-start | bytes 3145732
  30.5 38.4 %collective-permute-start.12 = (bf16[512,768]{1,0:T(8,128)(2,1)}, bf16[512,768]{1,0:T(8,128)(2,1)S(1)}, u32[]{:S(2)}, u32[]{:S(2)}) collective-permute-start(bf16[512,768]{1,0:T(8,128)(2,1)} %dynamic-slice_bitcast_fusion.2), channel_id=1, source_target_pairs={{0,1},{1,0},{2,5},{3,4},{4,3},{5,2},{6,7},{7,6},{8,9},{9,8},{10,13... | collective-permute-start | bytes 2359304 | tf_op jit(solution)/shard_map/ppermute | solution.py:359
  33.4 99.8 %all-to-all-start = ((bf16[256,8,512]{2,1,0:T(8,128)(2,1)}), bf16[256,8,512]{2,1,0:T(8,128)(2,1)}, u32[]{:S(2)}, u32[]{:S(2)}) async-start(bf16[256,8,512]{2,1,0:T(8,128)(2,1)} %bitcast.25), calls=%async_computation | async-start | bytes 4194304 | tf_op jit(solution)/shard_map/all_to_all | solution.py:368
  49.9 3.8 %collective-permute-start.6 = (bf16[8,2,256]{2,1,0:T(2,128)(2,1)S(1)}, bf16[8,2,256]{2,1,0:T(2,128)(2,1)S(1)}, u32[]{:S(2)}, u32[]{:S(2)}) collective-permute-start(bf16[8,2,256]{2,1,0:T(2,128)(2,1)S(1)} %pad_maximum_fusion.4), channel_id=1, source_target_pairs={{0,8},{4,12},{8,0},{12,4},{16,24},{20,28},{24,16},{28,20},{32,40},... | collective-permute-start | bytes 24584 | tf_op jit(solution)/shard_map/ppermute | solution.py:352
  53.7 4.3 %collective-permute-start.7 = (bf16[16,2,256]{2,1,0:T(2,128)(2,1)S(1)}, bf16[16,2,256]{2,1,0:T(2,128)(2,1)S(1)}, u32[]{:S(2)}, u32[]{:S(2)}) collective-permute-start(bf16[16,2,256]{2,1,0:T(2,128)(2,1)S(1)} %pad_maximum_fusion.2), channel_id=1, source_target_pairs={{0,24},{4,28},{8,16},{12,20},{16,8},{20,12},{24,0},{28,4},{32,56},... | collective-permute-start | bytes 49160 | tf_op jit(solution)/shard_map/ppermute | solution.py:352
  58.1 17.9 %collective-permute-start.8 = (bf16[32,2,256]{2,1,0:T(2,128)(2,1)S(1)}, bf16[32,2,256]{2,1,0:T(2,128)(2,1)S(1)}, u32[]{:S(2)}, u32[]{:S(2)}) collective-permute-start(bf16[32,2,256]{2,1,0:T(2,128)(2,1)S(1)} %pad_maximum_fusion.1), channel_id=1, source_target_pairs={{0,4},{4,0},{8,12},{12,8},{16,20},{20,16},{24,28},{28,24},{32,36},... | collective-permute-start | bytes 98312 | tf_op jit(solution)/shard_map/ppermute | solution.py:352
  62.9 8.4 %collective-permute-start.16 = (f32[3,768]{1,0:T(4,128)S(1)}, f32[3,768]{1,0:T(4,128)S(1)}, u32[]{:S(2)}, u32[]{:S(2)}) collective-permute-start(f32[3,768]{1,0:T(4,128)S(1)} %pad_maximum_fusion.3), channel_id=1, source_target_pairs={{0,1},{1,0},{2,5},{3,4},{4,3},{5,2},{6,7},{7,6},{8,9},{9,8},{10,13... | collective-permute-start | bytes 27656 | tf_op jit(solution)/shard_map/ppermute | solution.py:373
  66.9 6.9 %collective-permute-start.17 = (f32[3,768]{1,0:T(4,128)S(1)}, f32[3,768]{1,0:T(4,128)S(1)}, u32[]{:S(2)}, u32[]{:S(2)}) collective-permute-start(f32[3,768]{1,0:T(4,128)S(1)} %pad_maximum_fusion.3), channel_id=1, source_target_pairs={{2,4},{3,5},{4,2},{5,3},{10,12},{11,13},{12,10},{13,11},{18,20},{1... | collective-permute-start | bytes 27656 | tf_op jit(solution)/shard_map/ppermute | solution.py:374
  68.8 86.6 %copy-start = (bf16[512,768]{1,0:T(8,128)(2,1)}, bf16[512,768]{1,0:T(8,128)(2,1)S(1)}, u32[]{:S(2)}) copy-start(bf16[512,768]{1,0:T(8,128)(2,1)S(1)} %collective-permute-done.12.u1) | copy-start | bytes 2359300
  68.9 19.3 %collective-permute-start.13 = (bf16[512,768]{1,0:T(8,128)(2,1)S(1)}, bf16[512,768]{1,0:T(8,128)(2,1)S(1)}, u32[]{:S(2)}, u32[]{:S(2)}) collective-permute-start(bf16[512,768]{1,0:T(8,128)(2,1)S(1)} %collective-permute-done.12.u1), channel_id=1, source_target_pairs={{2,3},{3,2},{4,5},{5,4},{10,11},{11,10},{12,13},{13,12},{18,19},{1... | collective-permute-start | bytes 2359304 | tf_op jit(solution)/shard_map/ppermute | solution.py:376
  73.8 45.2 %collective-permute-start.18 = (bf16[1024,512]{1,0:T(8,128)(2,1)S(1)}, bf16[1024,512]{1,0:T(8,128)(2,1)}, u32[]{:S(2)}, u32[]{:S(2)}) collective-permute-start(bf16[1024,512]{1,0:T(8,128)(2,1)S(1)} %copy-done.4), channel_id=1, source_target_pairs={{2,4},{3,5},{4,2},{5,3},{10,12},{11,13},{12,10},{13,11},{18,20},{1... | collective-permute-start | bytes 3145736 | tf_op jit(solution)/shard_map/ppermute | solution.py:381
  78.1 1.3 collective-permute-start.9
  79.4 4.5 %collective-permute-start.10 = (f32[16,2]{1,0:T(8,128)S(1)}, f32[16,2]{1,0:T(8,128)S(1)}, u32[]{:S(2)}, u32[]{:S(2)}) collective-permute-start(f32[16,2]{1,0:T(8,128)S(1)} %slice.82), channel_id=1, source_target_pairs={{0,24},{4,28},{8,16},{12,20},{16,8},{20,12},{24,0},{28,4},{32,56},... | collective-permute-start | bytes 392 | tf_op jit(solution)/shard_map/ppermute | solution.py:399
  82.3 39.1 %collective-permute-start.14 = (bf16[512,768]{1,0:T(8,128)(2,1)S(1)}, bf16[512,768]{1,0:T(8,128)(2,1)S(1)}, u32[]{:S(2)}, u32[]{:S(2)}) collective-permute-start(bf16[512,768]{1,0:T(8,128)(2,1)S(1)} %collective-permute-done.12.u1), channel_id=1, source_target_pairs={{0,24},{1,25},{2,10},{3,11},{4,12},{5,13},{6,30},{7,31},{8,0},{9,1... | collective-permute-start | bytes 2359304 | tf_op jit(solution)/shard_map/ppermute | solution.py:378
  82.3 40.0 %collective-permute-start.19 = (bf16[768,512]{1,0:T(8,128)(2,1)}, bf16[768,512]{1,0:T(8,128)(2,1)S(1)}, u32[]{:S(2)}, u32[]{:S(2)}) collective-permute-start(bf16[768,512]{1,0:T(8,128)(2,1)} %collective-permute-done.v1), channel_id=1, source_target_pairs={{0,8},{1,9},{2,10},{3,11},{4,12},{5,13},{6,14},{7,15},{8,16},{9,17... | collective-permute-start | bytes 2359304 | tf_op jit(solution)/shard_map/ppermute | solution.py:377
  83.9 30.1 %collective-permute-start.11 = (f32[8,2]{1,0:T(8,128)S(1)}, f32[8,2]{1,0:T(8,128)S(1)}, u32[]{:S(2)}, u32[]{:S(2)}) collective-permute-start(f32[8,2]{1,0:T(8,128)S(1)} %slice.84), channel_id=1, source_target_pairs={{0,8},{4,12},{8,0},{12,4},{16,24},{20,28},{24,16},{28,20},{32,40},... | collective-permute-start | bytes 200 | tf_op jit(solution)/shard_map/ppermute | solution.py:399
  88.2 45.1 %copy-start.6 = (bf16[512,768]{1,0:T(8,128)(2,1)}, bf16[512,768]{1,0:T(8,128)(2,1)S(1)}, u32[]{:S(2)}) copy-start(bf16[512,768]{1,0:T(8,128)(2,1)S(1)} %collective-permute-done.13.u2) | copy-start | bytes 2359300
  88.2 33.3 %collective-permute-start.15 = (bf16[512,768]{1,0:T(8,128)(2,1)S(1)}, bf16[512,768]{1,0:T(8,128)(2,1)S(1)}, u32[]{:S(2)}, u32[]{:S(2)}) collective-permute-start(bf16[512,768]{1,0:T(8,128)(2,1)S(1)} %collective-permute-done.13.u2), channel_id=1, source_target_pairs={{2,26},{3,27},{4,28},{5,29},{10,2},{11,3},{12,4},{13,5},{18,10},{1... | collective-permute-start | bytes 2359304 | tf_op jit(solution)/shard_map/ppermute | solution.py:385
  114.0 14.2 %collective-permute-start.20 = (bf16[768,512]{1,0:T(8,128)(2,1)}, bf16[768,512]{1,0:T(8,128)(2,1)}, u32[]{:S(2)}, u32[]{:S(2)}) collective-permute-start(bf16[768,512]{1,0:T(8,128)(2,1)} %collective-permute-done.5.v2), channel_id=1, source_target_pairs={{2,26},{3,27},{4,28},{5,29},{10,2},{11,3},{12,4},{13,5},{18,10},{1... | collective-permute-start | bytes 2359304 | tf_op jit(solution)/shard_map/ppermute | solution.py:384
  121.5 11.8 %copy-start.7 = (bf16[512,768]{1,0:T(8,128)(2,1)}, bf16[512,768]{1,0:T(8,128)(2,1)S(1)}, u32[]{:S(2)}) copy-start(bf16[512,768]{1,0:T(8,128)(2,1)S(1)} %collective-permute-done.14.u3) | copy-start | bytes 2359300
  121.5 0.9 copy-start.8
  122.4 5.8 %copy-start.11 = (bf16[768,512]{1,0:T(8,128)(2,1)}, bf16[768,512]{1,0:T(8,128)(2,1)S(1)}, u32[]{:S(2)}) copy-start(bf16[768,512]{1,0:T(8,128)(2,1)S(1)} %collective-permute-done.19.v3) | copy-start | bytes 2359300
  133.3 10.9 %collective-permute-start.21 = (f32[8,2]{1,0:T(8,128)S(1)}, f32[8,2]{1,0:T(8,128)S(1)}, u32[]{:S(2)}, u32[]{:S(2)}) collective-permute-start(f32[8,2]{1,0:T(8,128)S(1)} %slice_maximum_fusion.1), channel_id=1, source_target_pairs={{0,1},{1,0},{2,3},{3,2},{4,5},{5,4},{6,7},{7,6},{8,9},{9,8},{10,11... | collective-permute-start | bytes 200 | tf_op jit(solution)/shard_map/ppermute | solution.py:402
  134.7 20.8 %copy-start.1 = (s32[2]{0:T(128)S(1)}, s32[2]{0:T(128)}, u32[]{:S(2)}) copy-start(s32[2]{0:T(128)} %pad_add_fusion.flags) | copy-start | bytes 28
  144.2 5.1 %collective-permute-start.22 = (bf16[1024,512]{1,0:T(8,128)(2,1)}, bf16[1024,512]{1,0:T(8,128)(2,1)S(1)}, u32[]{:S(2)}, u32[]{:S(2)}) collective-permute-start(bf16[1024,512]{1,0:T(8,128)(2,1)} %get-tuple-element.57.mine_ref), channel_id=1, source_target_pairs={{0,4},{1,5},{2,6},{3,7},{4,0},{5,1},{6,2},{7,3},{8,12},{9,13},{10,... | collective-permute-start | bytes 3145736 | tf_op jit(solution)/shard_map/ppermute | solution.py:442
  144.3 5.0 %collective-permute-start.23 = (f32[8,2]{1,0:T(8,128)S(1)}, f32[8,2]{1,0:T(8,128)S(1)}, u32[]{:S(2)}, u32[]{:S(2)}) collective-permute-start(f32[8,2]{1,0:T(8,128)S(1)} %max.27), channel_id=1, source_target_pairs={{0,3},{1,2},{2,1},{3,0},{4,7},{5,6},{6,5},{7,4},{8,11},{9,10},{10,... | collective-permute-start | bytes 200 | tf_op jit(solution)/shard_map/ppermute | solution.py:402
  149.3 6.2 %copy-start.10 = (bf16[1024,512]{1,0:T(8,128)(2,1)}, bf16[1024,512]{1,0:T(8,128)(2,1)S(1)}, u32[]{:S(2)}) copy-start(bf16[1024,512]{1,0:T(8,128)(2,1)S(1)} %collective-permute-done.22.other_ref) | copy-start | bytes 3145732
  149.3 15.9 %collective-permute-start.24 = (f32[4,2]{1,0:T(4,128)S(1)}, f32[4,2]{1,0:T(4,128)S(1)}, u32[]{:S(2)}, u32[]{:S(2)}) collective-permute-start(f32[4,2]{1,0:T(4,128)S(1)} %slice.74), channel_id=1, source_target_pairs={{0,192},{4,196},{8,200},{12,204},{16,208},{20,212},{24,216},{28,22... | collective-permute-start | bytes 104 | tf_op jit(solution)/shard_map/ppermute | solution.py:399
  165.3 5.5 %collective-permute-start.25 = (bf16[1024,512]{1,0:T(8,128)(2,1)}, bf16[1024,512]{1,0:T(8,128)(2,1)S(1)}, u32[]{:S(2)}, u32[]{:S(2)}) collective-permute-start(bf16[1024,512]{1,0:T(8,128)(2,1)} %get-tuple-element.68.mine_ref), channel_id=1, source_target_pairs={{0,4},{1,5},{2,6},{3,7},{4,0},{5,1},{6,2},{7,3},{8,12},{9,13},{10,... | collective-permute-start | bytes 3145736 | tf_op jit(solution)/shard_map/ppermute | solution.py:450
  167.1 3.6 %collective-permute-start.26 = (f32[2,2]{1,0:T(2,128)S(1)}, f32[2,2]{1,0:T(2,128)S(1)}, u32[]{:S(2)}, u32[]{:S(2)}) collective-permute-start(f32[2,2]{1,0:T(2,128)S(1)} %slice.76), channel_id=1, source_target_pairs={{0,64},{4,68},{8,72},{12,76},{16,80},{20,84},{24,88},{28,92},{32,9... | collective-permute-start | bytes 56 | tf_op jit(solution)/shard_map/ppermute | solution.py:399
  170.7 1.0 copy-start.9
  170.7 10.7 %collective-permute-start.27 = (f32[1,2]{1,0:T(1,128)S(1)}, f32[1,2]{1,0:T(1,128)S(1)}, u32[]{:S(2)}, u32[]{:S(2)}) collective-permute-start(f32[1,2]{1,0:T(1,128)S(1)} %slice.78), channel_id=1, source_target_pairs={{0,32},{4,36},{8,40},{12,44},{16,48},{20,52},{24,56},{28,60},{32,0... | collective-permute-start | bytes 32 | tf_op jit(solution)/shard_map/ppermute | solution.py:399
  183.5 1.8 collective-permute-start.28
  186.0 6.4 %collective-permute-start.30 = (f32[1,1024]{1,0:T(1,128)S(1)}, f32[1,1024]{1,0:T(1,128)S(1)}, u32[]{:S(2)}, u32[]{:S(2)}) collective-permute-start(f32[1,1024]{1,0:T(1,128)S(1)} %fusion.5), channel_id=1, source_target_pairs={{2,4},{3,5},{4,2},{5,3},{10,12},{11,13},{12,10},{13,11},{18,20},{1... | collective-permute-start | bytes 12296 | tf_op jit(solution)/shard_map/ppermute | solution.py:462
  190.4 4.3 %collective-permute-start.29 = (f32[1,1024]{1,0:T(1,128)S(1)}, f32[1,1024]{1,0:T(1,128)S(1)}, u32[]{:S(2)}, u32[]{:S(2)}) collective-permute-start(f32[1,1024]{1,0:T(1,128)S(1)} %fusion.5), channel_id=1, source_target_pairs={{0,1},{1,0},{2,5},{3,4},{4,3},{5,2},{6,7},{7,6},{8,9},{9,8},{10,13... | collective-permute-start | bytes 12296 | tf_op jit(solution)/shard_map/ppermute | solution.py:461

commit v5 on v4

v5 whole, which is shorter than its diff:
```python
import functools

import jax
import jax.numpy as jnp
from jax import lax
from jax.experimental import pallas as pl
from jax.experimental.pallas import tpu as pltpu
from jax.sharding import PartitionSpec as P

BF = jnp.bfloat16
F32 = jnp.float32
AXES = ("shard", "tp")
VMEM = pl.BlockSpec(memory_space=pltpu.VMEM)
PICK, CTX, FIRST, SECOND = 4096, 20000, 15000, 15000
SMEM = pl.BlockSpec(memory_space=pltpu.SMEM)
ANY = pl.BlockSpec(memory_space=pl.ANY)


def grant(kbytes):
    return pltpu.CompilerParams(vmem_limit_bytes=kbytes * 1000)


def group_perm(groups, step, member=lambda x, c: True, turn=lambda x, c: 0):
    pairs = []
    for g in range(groups):
        for c in range(2):
            for x in range(4):
                if member(x, c):
                    x2, c2 = step(x, c)
                    g2 = g // 4 * 4 + (g + turn(x, c)) % 4
                    pairs.append((g * 8 + c * 4 + x, g2 * 8 + c2 * 4 + x2))
    return pairs


def is_home(x, c):
    return x // 2 == c


def is_away(x, c):
    return x // 2 != c


def near(x, c):
    return (x ^ 1, x // 2) if is_home(x, c) else (x ^ 3, x // 2)


def partners(shards):
    far_z = (6, 7, 4, 5, 2, 3, 0, 1)
    steps = []
    for of_z, of_y, of_core in (
        (lambda z: z ^ 1, None, None),
        (lambda z: z ^ 2, None, None),
        (lambda z: far_z[z], None, None),
        (None, 1, None),
        (None, 3, None),
        (None, None, 1),
    ):
        pairs = []
        for i in range(shards):
            z, y, c = i // 8, i // 2 % 4, i % 2
            z = of_z(z) if of_z else z
            y = y ^ of_y if of_y else y
            c = c ^ of_core if of_core else c
            pairs.append((i, z * 8 + y * 2 + c))
        steps.append(pairs)
    return steps


def dot(a, b):
    return jnp.dot(a, b, preferred_element_type=F32)


def dot_nt(a, b):
    return lax.dot_general(a, b, (((1,), (1,)), ((), ())), preferred_element_type=F32)


def call(kernel, name, kbytes, outs, scratch, mflops, mbytes, scalars, arrays, far, out_specs=None):
    return pl.pallas_call(
        kernel,
        in_specs=[SMEM] * len(scalars) + [VMEM] * len(arrays) + [ANY] * len(far),
        out_specs=out_specs or [VMEM] * len(outs),
        out_shape=[jax.ShapeDtypeStruct(shape, dtype) for shape, dtype in outs],
        scratch_shapes=scratch,
        compiler_params=grant(kbytes),
        cost_estimate=pl.CostEstimate(
            flops=mflops << 20, bytes_accessed=mbytes << 20, transcendentals=0
        ),
        name=name,
    )(*scalars, *arrays, *far)


def pick_kernel(
    kept_ref, count_ref, emb_hbm, attr_hbm, out_hbm, table, hot_ref, out_ref, in_sems, out_sems
):
    slots, persons = kept_ref.shape
    items = table.shape[1]
    loads = [pltpu.make_async_copy(emb_hbm, table.at[0], in_sems.at[0])]
    for q in range(3):
        columns = attr_hbm.at[:, pl.ds(q * 256, 256)]
        loads.append(pltpu.make_async_copy(columns, table.at[q + 1], in_sems.at[q + 1]))
    for load in loads:
        load.start()
    live = lax.broadcasted_iota(jnp.int32, (slots, persons), 0) < count_ref[...]
    wanted = jnp.where(live, kept_ref[...], 4095)
    digits = jnp.concatenate([wanted >> 6, wanted & 63], 0).astype(F32).astype(BF)
    n = 256
    blocks = persons * slots // n
    lane = lax.broadcasted_iota(jnp.int32, (n, 2 * slots), 1)
    slot = lax.broadcasted_iota(jnp.int32, (n, 2 * slots), 0) % slots
    odd = (lax.broadcasted_iota(jnp.int32, (n, 1), 0) // slots) % 2 == 1
    unused = []
    for b in range(blocks):
        row = lax.broadcasted_iota(jnp.int32, (n, persons), 0) + b * n
        owner = (row // slots == lax.broadcasted_iota(jnp.int32, (n, persons), 1)).astype(BF)
        both = dot_nt(owner, digits)
        high = jnp.where(lane == slot, both * 64.0, 0.0)
        low = jnp.where(lane == slot + slots, both, 0.0)
        rows = jnp.sum(high + low, axis=1, keepdims=True).astype(jnp.int32)
        hot = lax.broadcasted_iota(jnp.int32, (n, items), 1) == rows
        hot_ref[b * n : (b + 1) * n] = hot.astype(BF)
        unused.append(rows >= items)
    stores = []
    for c in range(2):
        loads[2 * c].wait()
        loads[2 * c + 1].wait()
        for b in range(blocks):
            hot = hot_ref[b * n : (b + 1) * n]
            low = jnp.where(unused[b], jnp.inf, dot(hot, table[2 * c]))
            high = jnp.where(unused[b], jnp.inf, dot(hot, table[2 * c + 1]))
            first = jnp.where(odd, low, high).astype(BF)
            second = jnp.where(odd, high, low).astype(BF)
            for g in range(n // 32):
                out_ref[c, b * (n // 32) + g, :, 0:256] = first[g * 32 : (g + 1) * 32]
                out_ref[c, b * (n // 32) + g, :, 256:512] = second[g * 32 : (g + 1) * 32]
        stores.append(pltpu.make_async_copy(out_ref.at[c], out_hbm.at[:, c], out_sems.at[c]))
        stores[-1].start()
    for store in stores:
        store.wait()


def pick_rows(kept, count, emb, attr):
    slots, persons = kept.shape
    out = (persons // 4, 2, 4 * slots, 512)
    return pl.pallas_call(
        pick_kernel,
        in_specs=[VMEM, VMEM, ANY, ANY],
        out_specs=ANY,
        out_shape=jax.ShapeDtypeStruct(out, BF),
        scratch_shapes=[
            pltpu.VMEM((4, emb.shape[0], 256), BF),
            pltpu.VMEM((persons * slots, emb.shape[0]), BF),
            pltpu.VMEM((2, persons // 4, 4 * slots, 512), BF),
            pltpu.SemaphoreType.DMA((4,)),
            pltpu.SemaphoreType.DMA((2,)),
        ],
        compiler_params=grant(62500),
        cost_estimate=pl.CostEstimate(
            flops=PICK << 20, bytes_accessed=6 << 20, transcendentals=0
        ),
        name="pick_rows",
    )(kept, count, emb, attr)


ROWS = 256


def block_copies(src, dst, sems):
    copies = []
    for i in range(dst.shape[0] // ROWS):
        here = pl.ds(i * ROWS, ROWS)
        copies.append(pltpu.make_async_copy(src.at[here], dst.at[here], sems.at[i]))
        copies[-1].start()
    return copies


def context_kernel(ca_ref, cb_ref, va_ref, vb_ref, part_ref, head_ref):
    head_ref[0:256] = va_ref[0:256]
    head_ref[256:512] = vb_ref[0:256]
    for i in range(part_ref.shape[0] // ROWS):
        here = pl.ds(i * ROWS, ROWS)
        part_ref[here] = dot(ca_ref[here], va_ref[256:768]) + dot(cb_ref[here], vb_ref[256:768])


def first_kernel(
    u_ref, part_ref, head_ref, recv_hbm, pay_ref, piece_ref, logit_ref,
    clean, place, recv_ref, recv_sems,
):
    slots = recv_ref.shape[0]
    recv_copies = block_copies(recv_hbm, recv_ref, recv_sems)
    r = lax.broadcasted_iota(jnp.int32, (ROWS, ROWS), 0)
    q = lax.broadcasted_iota(jnp.int32, (ROWS, ROWS), 1)
    upper = (r <= q).astype(BF)
    lane0 = (lax.broadcasted_iota(jnp.int32, (16, 128), 1) == 0).astype(BF)
    before = jnp.zeros((16, 1), F32)
    for i in range(slots // ROWS):
        here = slice(i * ROWS, (i + 1) * ROWS)
        recv_copies[i].wait()
        got = recv_ref[here].astype(F32)
        live = got < jnp.inf
        clean[here] = jnp.where(live, got, 0.0).astype(BF)
        marks = dot_nt(lane0, live[:, 0:128].astype(F32).astype(BF))
        upto = dot(marks.astype(BF), upper) + before
        place[:, here] = jnp.where(marks > 0.5, upto - 1.0, -1.0)
        before = upto[:, ROWS - 1 : ROWS]
    for i in range(pay_ref.shape[0] // ROWS):
        here = pl.ds(i * ROWS, ROWS)
        k = (lax.broadcasted_iota(jnp.int32, (ROWS, slots), 0) + i * ROWS).astype(F32)
        hot = (k == place[0:1, :]).astype(BF)
        pay = dot(hot, clean[...]).astype(BF)
        pay_ref[here] = pay
        piece = part_ref[here] + dot(pay, head_ref[...])
        piece_ref[here] = piece.astype(BF)
        logit_ref[:, here] = dot_nt(u_ref[...], pay)


def cross(x0, hidden, offset, x):
    x0 = x0.astype(F32)
    return (x0 * (hidden + offset) + x.astype(F32)).astype(BF)


def second_kernel(
    mine_ref, other_ref, pay_ref, ba_ref, bb_ref, ca_ref, cb_ref,
    ua_ref, ub_ref, va_ref, vb_ref, xa_ref, xb_ref, piece_ref,
):
    for i in range(pay_ref.shape[0] // ROWS):
        here = pl.ds(i * ROWS, ROWS)
        proj = (mine_ref[here].astype(F32) + other_ref[here].astype(F32)).astype(BF)
        slots = (
            (xa_ref, ua_ref, ba_ref, ca_ref, 0),
            (xb_ref, ub_ref, bb_ref, cb_ref, 256),
        )
        for x_ref, u_ref, b_ref, c_ref, at in slots:
            hidden = dot(proj, u_ref[...])
            pay = pay_ref[here, at : at + 256]
            ctx = c_ref[here]
            x_ref[here, 0:256] = cross(pay, hidden[:, 0:256], b_ref[0:1, 0:256], pay)
            x_ref[here, 256:768] = cross(ctx, hidden[:, 256:768], b_ref[0:1, 256:768], ctx)
        piece = dot(xa_ref[here], va_ref[...]) + dot(xb_ref[here], vb_ref[...])
        piece_ref[here] = piece.astype(BF)


def last_kernel(
    coefficient, mine_ref, other_ref, pay_ref, xa_ref, xb_ref, sa_ref, sb_ref, logit_ref,
    ca_ref, cb_ref, ua_ref, ub_ref, score_ref,
):
    for i in range(pay_ref.shape[0] // ROWS):
        here = pl.ds(i * ROWS, ROWS)
        proj = (mine_ref[here].astype(F32) + other_ref[here].astype(F32)).astype(BF)
        score = coefficient[0] * logit_ref[:, here]
        for x_ref, u_ref, s_ref, c_ref, at in (
            (xa_ref, ua_ref, sa_ref, ca_ref, 0),
            (xb_ref, ub_ref, sb_ref, cb_ref, 256),
        ):
            hidden = dot(proj, u_ref[...])
            low = cross(
                pay_ref[here, at : at + 256], hidden[:, 0:256], s_ref[1:2, 0:256], x_ref[here, 0:256]
            )
            high = cross(
                c_ref[here], hidden[:, 256:768], s_ref[1:2, 256:768], x_ref[here, 256:768]
            )
            out = jnp.broadcast_to(s_ref[2:3, :], (16, 768)).astype(BF)
            score = score + dot_nt(out[:, 0:256], low) + dot_nt(out[:, 256:768], high)
        score_ref[:, here] = score


def on_device(
    person_embedding,
    catalog_embedding,
    catalog_attributes,
    kept_part_entries,
    valid_slot_number,
    pair_attributes,
    lowrank_v_matrix,
    lowrank_u_matrix,
    interaction_offset,
    final_projection,
    similarity_coefficient,
):
    shards = lax.axis_size("shard")
    groups = shards // 2
    x = lax.axis_index("tp")
    core = lax.axis_index("shard") % 2
    home = x // 2 == core
    parity = x % 2
    move = functools.partial(lax.ppermute, axis_name=AXES)
    to_core = group_perm(groups, lambda x, c: (x, 1 - c))
    to_near = group_perm(groups, near)
    home_on = group_perm(groups, lambda x, c: (x ^ 3, c), is_home)
    away_swap = group_perm(groups, lambda x, c: (x ^ 1, c), is_away)
    ctx_near = group_perm(groups, lambda x, c: (x ^ 1, c) if is_home(x, c) else (x ^ 3, 1 - c))
    ctx_far = group_perm(groups, lambda x, c: (x ^ 2, 1 - c), is_away)
    persons, _, kept = kept_part_entries.shape
    hops = partners(shards)
    me = lax.axis_index("shard")
    v0_a = move(lowrank_v_matrix[0], perm=to_near)
    users = jnp.broadcast_to(person_embedding[None], (shards, *person_embedding.shape))
    users = lax.all_to_all(users, "shard", split_axis=0, concat_axis=0, tiled=True)

    parcel = pick_rows(
        kept_part_entries[:, 0, :].T, valid_slot_number.T, catalog_embedding, catalog_attributes
    )
    parcel = parcel.reshape(persons * 2, kept, 512)
    parcel, v0_a, users = lax.optimization_barrier((parcel, v0_a, users))
    recv = lax.all_to_all(parcel, AXES, split_axis=0, concat_axis=0, tiled=True)
    recv = recv.reshape(persons * 2 * kept, 512)

    small = jnp.concatenate([interaction_offset, final_projection[None, :].astype(F32)], 0)
    small, v0_a = lax.optimization_barrier((small, v0_a))
    small_a = move(small, perm=to_near)
    small_b = jnp.where(home, small, move(small, perm=ctx_far))
    v0_b = move(v0_a, perm=home_on)
    u0_a = move(lowrank_u_matrix[0], perm=to_near)
    v1_a = move(lowrank_v_matrix[1], perm=to_near)
    u1_a = move(lowrank_u_matrix[1], perm=to_near)
    v0_b, u0_a, u1_a = lax.optimization_barrier((v0_b, u0_a, u1_a))
    v0_b = jnp.where(home, lowrank_v_matrix[0], v0_b)
    u0_b = jnp.where(home, lowrank_u_matrix[0], move(u0_a, perm=away_swap))
    v1_b = jnp.where(home, lowrank_v_matrix[1], move(v1_a, perm=home_on))
    u1_b = jnp.where(home, lowrank_u_matrix[1], move(u1_a, perm=away_swap))

    ctx_a = move(lax.dynamic_index_in_dim(pair_attributes, 1 - parity, 0, False), perm=ctx_near)
    ctx_own = lax.dynamic_index_in_dim(pair_attributes, parity, 0, False)
    ctx_a, ctx_b = lax.optimization_barrier((ctx_a, move(ctx_own, perm=ctx_far)))
    ctx_b = jnp.where(home, ctx_own, ctx_b)
    ctx_a, u0_b, u1_b = lax.optimization_barrier((ctx_a, u0_b, u1_b))

    all_scores = jnp.einsum(
        "ue,ie->ui", users.reshape(persons, -1), catalog_embedding, preferred_element_type=F32
    )
    best = jnp.max(all_scores, axis=1).reshape(shards, persons // shards)
    order = [[i] for i in range(shards)]
    for pairs in hops:
        order = [order[i] + order[k] for i, k in pairs]
    order = lax.dynamic_index_in_dim(jnp.asarray(order, jnp.int32), me, 0, False)
    chosen = order[:, None] == jnp.arange(shards, dtype=jnp.int32)[None, :]
    best = jnp.sum(jnp.where(chosen[:, :, None], best[None], 0.0), axis=1)

    def halve(best, pairs):
        half = best.shape[0] // 2
        return jnp.maximum(best[:half], lax.ppermute(best[half:], "shard", pairs))

    def over_x(best, flip):
        return jnp.maximum(best, lax.ppermute(best, "tp", [(i, i ^ flip) for i in range(4)]))

    for pairs in hops[:2:-1]:
        best = halve(best, pairs)

    emb_other = lax.dynamic_index_in_dim(users, me ^ 1, 0, False)
    query = lax.dynamic_slice_in_dim(jnp.where(home, person_embedding, emb_other), parity, 1, 0)
    query = jnp.where(core == 0, query, jnp.zeros_like(query))
    zero = jnp.zeros_like(query)
    query = jnp.where(
        parity == 1, jnp.concatenate([query, zero], 1), jnp.concatenate([zero, query], 1)
    )
    query = jnp.broadcast_to(query, (16, 512))

    surv = pair_attributes.shape[1]
    tall, wide, lanes = ((surv, 512), BF), ((surv, 768), BF), ((16, surv), F32)
    part, head = call(
        context_kernel, "context_part", 24000, [((surv, 512), F32), ((512, 512), BF)], [],
        CTX, 8, [], [ctx_a, ctx_b, v0_a, v0_b], [],
    )
    recv, best = lax.optimization_barrier((recv, best))
    step = halve(best, hops[2])
    pay, piece, logit = call(
        first_kernel, "first_layer", 24000, [tall, tall, lanes],
        [pltpu.VMEM(recv.shape, BF), pltpu.VMEM((16, recv.shape[0]), F32)]
        + [pltpu.VMEM(recv.shape, BF), pltpu.SemaphoreType.DMA((recv.shape[0] // ROWS,))],
        FIRST, 8, [], [query, part, head], [recv],
    )
    piece, best = lax.optimization_barrier((piece, step))
    other, best = lax.optimization_barrier((move(piece, perm=to_core), halve(best, hops[1])))
    step = halve(best, hops[0])
    x_a, x_b, piece1 = call(
        second_kernel, "second_layer", 24000, [wide, wide, tall], [],
        SECOND, 12, [],
        [piece, other, pay, small_a, small_b, ctx_a, ctx_b, u0_a, u0_b, v1_a, v1_b], [],
    )
    piece1, best = lax.optimization_barrier((piece1, step))
    other1, best = lax.optimization_barrier((move(piece1, perm=to_core), over_x(best, 1)))
    step = over_x(best, 3)
    (score,) = call(
        last_kernel, "last_layer", 24000, [lanes], [], 1792, 10, [similarity_coefficient],
        [piece1, other1, pay, x_a, x_b, small_a, small_b, logit, ctx_a, ctx_b, u1_a, u1_b], [],
    )
    score, best = lax.optimization_barrier((score, step))
    top = jnp.where(home, lax.dynamic_slice_in_dim(best, parity, 1, 1), 0.0)
    score = score[0:1] - similarity_coefficient[0] * top
    score = score + move(score, perm=to_core)
    score_a = move(score, perm=to_near)
    score_b = jnp.where(home, score, move(score, perm=ctx_far))
    return jnp.where(
        parity == 1,
        jnp.concatenate([score_a, score_b], 0),
        jnp.concatenate([score_b, score_a], 0),
    )


def solution(mesh):
    return jax.shard_map(
        on_device,
        mesh=mesh,
        in_specs=(
            P("shard", None),
            P(("shard", "tp"), None),
            P(("shard", "tp"), None),
            P(None, ("shard", "tp"), None),
            P(None, ("shard", "tp")),
            P("shard", None, "tp"),
            P(None, "tp", None),
            P(None, None, "tp"),
            P(None, "tp"),
            P("tp"),
            P(),
        ),
        out_specs=P("shard", None),
        check_vma=False,
    )
```

time: 196 us -> 185 us (0.944)
  Pallas kernels: 43 us -> 24.4 us
  waiting for transfers between devices: 49.4 us -> 67.4 us
  starting transfers between devices: 87.3 us -> 71.2 us
  local copies, waits for them, and re-layouts: 6.01 us -> 12.4 us
    ppermute x16 -> x10, waiting for transfers between devices: 20.1 us -> 59 us  [the longest x1 29.9 us: on_device(): v1_a = move(lowrank_v_matrix[1], perm=to_near)]
    ppermute x6, waiting for transfers between devices: 24.6 us -> 3.54 us  [halve(): return jnp.maximum(best[:half], lax.ppermute(best[half:], 'shard', pairs))]
    ppermute x16 -> x10, starting transfers between devices: 38.7 us -> 20.3 us  [the longest x1 4.05 us: on_device(): small_b = jnp.where(home, small, move(small, perm=ctx_far))]
    pallas_call x4, Pallas kernels: 34 us -> 16.4 us  [call(): pl.pallas_call(kernel, in_specs=[SMEM] * len(scalars) + [VMEM] * len(arra...]
    all_to_all x0 -> x1, starting transfers between devices: none -> 11.8 us  [on_device(): lax.all_to_all(users, 'shard', split_axis=0, concat_axis=0, tiled=True)]
    all_to_all x1, starting transfers between devices: 16 us -> 12.7 us  [on_device(): recv = lax.all_to_all(parcel, AXES, split_axis=0, concat_axis=0, tiled=True)]
    ppermute x1, starting transfers between devices: 3.97 us -> 0.62 us  [on_device(): small_a = move(small, perm=to_near)]
    squeeze x3, local copies, waits for them, and re-layouts: 1.02 us -> 4.07 us  [the longest x1 2.8 us: on_device(): v1_a = move(lowrank_v_matrix[1], perm=to_near)]
  transfers between devices with their start and end apart: 32 -> 27, of which waited for: 17 -> 11; matrix products, arithmetic and copies ran while one was open for 4% -> 7% of each run, Pallas kernels for 22% -> 13%
where the time goes in v5:
time: 185 us; the launch traced here: 184 us
  starting transfers between devices  71.2 us (38%)
  waiting for transfers between devices  67.4 us (36%)
  Pallas kernels  24.4 us (13%)
  local copies, waits for them, and re-layouts  12.4 us (7%)
  other arithmetic  6.38 us (3%)
    ppermute x1, waiting for transfers between devices, on_device(): v1_a = move(lowrank_v_matrix[1], perm=to_near)  29.9 us
    pallas_call x4, Pallas kernels, call(): pl.pallas_call(kernel, in_specs=[SMEM] * len(scalars) + [VMEM] * len(arra...  16.4 us
    ppermute x1, waiting for transfers between devices, on_device(): u1_a = move(lowrank_u_matrix[1], perm=to_near)  15.3 us
    all_to_all x1, starting transfers between devices, on_device(): recv = lax.all_to_all(parcel, AXES, split_axis=0, concat_axis=0, tiled=True)  12.7 us
    ppermute x6, starting transfers between devices, halve(): return jnp.maximum(best[:half], lax.ppermute(best[half:], 'shard', pairs))  12.2 us
    all_to_all x1, starting transfers between devices, on_device(): lax.all_to_all(users, 'shard', split_axis=0, concat_axis=0, tiled=True)  11.8 us
    ppermute x1, waiting for transfers between devices, on_device(): u1_b = jnp.where(home, lowrank_u_matrix[1], move(u1_a, perm=away_swap))  8.43 us
    pallas_call x1, Pallas kernels, pick_rows(): pl.pallas_call(pick_kernel, in_specs=[VMEM, VMEM, ANY, ANY], out_specs=AN...  8 us
  transfers between devices with their start and end apart: 27, of which 11 were waited for; matrix products, arithmetic and copies ran while one was open for 7% of the time, Pallas kernels for 13%

profile of v5, /device:TPU:1, one launch (start us, length us, event | category | flops | bytes accessed | tf_op | source)
XLA Modules:
  0.0 184.1 jit_solution(13338813023716135935)
XLA Ops:
  0.0 2.8 %slice_bitcast_fusion = (bf16[768,512]{1,0:T(8,128)(2,1)}, bf16[768,512]{1,0:T(8,128)(2,1)}) fusion(bf16[2,768,512]{2,1,0:T(8,128)(2,1)} %param.18), kind=kLoop, calls=%fused_computation.4 | loop fusion | bytes 3145728 | tf_op jit(solution)/shard_map/squeeze | solution.py:313
  2.8 3.9 %collective-permute-start = (bf16[768,512]{1,0:T(8,128)(2,1)}, bf16[768,512]{1,0:T(8,128)(2,1)S(1)}, u32[]{:S(2)}, u32[]{:S(2)}) collective-permute-start(bf16[768,512]{1,0:T(8,128)(2,1)} %get-tuple-element.76), channel_id=1, source_target_pairs={{0,1},{1,0},{2,5},{3,4},{4,3},{5,2},{6,7},{7,6},{8,9},{9,8},{10,13... | collective-permute-start | bytes 2359304 | tf_op jit(solution)/shard_map/ppermute | solution.py:295
  6.7 0.7 broadcast_in_dim.41
  7.3 11.8 %all-to-all-start = ((bf16[64,2,256]{2,1,0:T(2,128)(2,1)}), bf16[64,2,256]{2,1,0:T(2,128)(2,1)S(1)}, u32[]{:S(2)}, u32[]{:S(2)}) async-start(bf16[64,2,256]{2,1,0:T(2,128)(2,1)} %broadcast_in_dim.41), calls=%async_computation | async-start | bytes 131072 | tf_op jit(solution)/shard_map/all_to_all | solution.py:297
  19.1 1.3 slice_bitcast_fusion.1
  20.4 0.4 collective-permute-start.4
  20.7 3.1 %dynamic-slice_bitcast_fusion = (bf16[1024,512]{1,0:T(8,128)(2,1)}, bf16[1024,512]{1,0:T(8,128)(2,1)}) fusion(bf16[2,1024,512]{2,1,0:T(8,128)(2,1)} %param.17, s32[]{:T(128)S(6)} %select_n.133, s32[]{:T(128)S(6)} %select_n.136), kind=kLoop, calls=%fused_computation.1 | loop fusion | bytes 4194312 | tf_op jit(solution)/shard_map/jit(dynamic_index_in_dim)/squeeze | solution.py:322
  23.8 2.6 %collective-permute-start.1 = (bf16[1024,512]{1,0:T(8,128)(2,1)}, bf16[1024,512]{1,0:T(8,128)(2,1)S(1)}, u32[]{:S(2)}, u32[]{:S(2)}) collective-permute-start(bf16[1024,512]{1,0:T(8,128)(2,1)} %get-tuple-element.72), channel_id=1, source_target_pairs={{0,1},{1,0},{2,5},{3,4},{4,3},{5,2},{6,7},{7,6},{8,9},{9,8},{10,13... | collective-permute-start | bytes 3145736 | tf_op jit(solution)/shard_map/ppermute | solution.py:321
  26.4 1.9 %collective-permute-start.2 = (bf16[1024,512]{1,0:T(8,128)(2,1)}, bf16[1024,512]{1,0:T(8,128)(2,1)}, u32[]{:S(2)}, u32[]{:S(2)}) collective-permute-start(bf16[1024,512]{1,0:T(8,128)(2,1)} %get-tuple-element.71), channel_id=1, source_target_pairs={{2,4},{3,5},{4,2},{5,3},{10,12},{11,13},{12,10},{13,11},{18,20},{1... | collective-permute-start | bytes 3145736 | tf_op jit(solution)/shard_map/ppermute | solution.py:323
  28.3 1.5 collective-permute-start.16
  29.8 8.0 %pick_rows.1 = bf16[32,2,32,512]{3,2,1,0:T(8,128)(2,1)} custom-call(s32[8,128]{1,0:T(8,128)} %bitcast.37, s32[1,128]{1,0:T(1,128)} %bitcast.38, bf16[2048,256]{1,0:T(8,128)(2,1)} %emb_hbm.1, bf16[2048,768]{1,0:T(8,128)(2,1)} %attr_hbm.1), custom_call_target="tpu_custom_call" | custom-call | flops 4294967296 | bytes 6291456 | tf_op jit(solution)/shard_map/pick_rows/pallas_call | solution.py:144
  37.8 0.7 fusion.2
  38.5 0.1 iota_compare_fusion
  38.7 12.7 %all-to-all-start.1 = ((bf16[256,8,512]{2,1,0:T(8,128)(2,1)}), bf16[256,8,512]{2,1,0:T(8,128)(2,1)}, u32[]{:S(2)}, u32[]{:S(2)}) async-start(bf16[256,8,512]{2,1,0:T(8,128)(2,1)} %bitcast.36), calls=%async_computation.1 | async-start | bytes 4194304 | tf_op jit(solution)/shard_map/all_to_all | solution.py:304
  51.4 0.6 convolution_reduce_fusion
  52.0 0.1 broadcast_in_dim.45
  52.2 0.1 select_reduce_fusion
  52.3 0.1 slice.59
  52.4 2.2 %collective-permute-start.8 = (f32[32,2]{0,1:T(2,128)S(1)}, f32[32,2]{0,1:T(2,128)S(1)}, u32[]{:S(2)}, u32[]{:S(2)}) collective-permute-start(f32[32,2]{0,1:T(2,128)S(1)} %slice.59), channel_id=1, source_target_pairs={{0,4},{4,0},{8,12},{12,8},{16,20},{20,16},{24,28},{28,24},{32,36},... | collective-permute-start | bytes 776 | tf_op jit(solution)/shard_map/ppermute | solution.py:340
  54.6 0.8 collective-permute-start.5
  55.4 1.3 collective-permute-start.3
  56.8 0.1 slice.61
  56.8 29.9 %collective-permute-done.16.va_ref = bf16[768,512]{1,0:T(8,128)(2,1)} collective-permute-done((bf16[768,512]{1,0:T(8,128)(2,1)}, bf16[768,512]{1,0:T(8,128)(2,1)}, u32[]{:S(2)}, u32[]{:S(2)}) %collective-permute-start.16) | collective-permute-done | bytes 786464 | tf_op jit(solution)/shard_map/ppermute | solution.py:313
  86.7 3.2 %collective-permute-start.9 = (f32[16,2]{0,1:T(2,128)S(1)}, f32[16,2]{0,1:T(2,128)S(1)}, u32[]{:S(2)}, u32[]{:S(2)}) collective-permute-start(f32[16,2]{0,1:T(2,128)S(1)} %slice.61), channel_id=1, source_target_pairs={{0,24},{4,28},{8,16},{12,20},{16,8},{20,12},{24,0},{28,4},{32,56},... | collective-permute-start | bytes 392 | tf_op jit(solution)/shard_map/ppermute | solution.py:340
  89.9 1.4 collective-permute-done.9
  91.3 1.3 collective-permute-start.17
  92.6 0.1 slice.63
  92.7 15.3 %collective-permute-done.5.ua_ref = bf16[512,768]{1,0:T(8,128)(2,1)S(1)} collective-permute-done((bf16[512,768]{1,0:T(8,128)(2,1)}, bf16[512,768]{1,0:T(8,128)(2,1)S(1)}, u32[]{:S(2)}, u32[]{:S(2)}) %collective-permute-start.5) | collective-permute-done | bytes 786464 | tf_op jit(solution)/shard_map/ppermute | solution.py:314
  108.0 1.9 %collective-permute-start.10 = (f32[8,2]{0,1:T(2,128)S(1)}, f32[8,2]{0,1:T(2,128)S(1)}, u32[]{:S(2)}, u32[]{:S(2)}) collective-permute-start(f32[8,2]{0,1:T(2,128)S(1)} %slice.63), channel_id=1, source_target_pairs={{0,8},{4,12},{8,0},{12,4},{16,24},{20,28},{24,16},{28,20},{32,40},... | collective-permute-start | bytes 200 | tf_op jit(solution)/shard_map/ppermute | solution.py:340
  109.9 2.0 %collective-permute-start.6 = (bf16[512,768]{1,0:T(8,128)(2,1)}, bf16[512,768]{1,0:T(8,128)(2,1)S(1)}, u32[]{:S(2)}, u32[]{:S(2)}) collective-permute-start(bf16[512,768]{1,0:T(8,128)(2,1)} %collective-permute-done.4.ua_ref), channel_id=1, source_target_pairs={{2,3},{3,2},{4,5},{5,4},{10,11},{11,10},{12,13},{13,12},{18,19},{1... | collective-permute-start | bytes 2359304 | tf_op jit(solution)/shard_map/ppermute | solution.py:317
  111.9 3.3 %collective-permute-start.7 = (bf16[512,768]{1,0:T(8,128)(2,1)S(1)}, bf16[512,768]{1,0:T(8,128)(2,1)S(1)}, u32[]{:S(2)}, u32[]{:S(2)}) collective-permute-start(bf16[512,768]{1,0:T(8,128)(2,1)S(1)} %collective-permute-done.5.ua_ref), channel_id=1, source_target_pairs={{2,3},{3,2},{4,5},{5,4},{10,11},{11,10},{12,13},{13,12},{18,19},{1... | collective-permute-start | bytes 2359304 | tf_op jit(solution)/shard_map/ppermute | solution.py:319
  115.2 1.5 broadcast_select_fusion.cb_ref
  116.7 0.2 copy-done.8
  116.9 2.3 %broadcast_select_fusion.1 = (bf16[768,512]{1,0:T(8,128)(2,1)}, bf16[768,512]{1,0:T(8,128)(2,1)S(1)}) fusion(bf16[768,512]{1,0:T(8,128)(2,1)S(1)} %collective-permute-done.17, pred[]{:T(512)} %eq.34, bf16[2,768,512]{2,1,0:T(8,128)(2,1)S(1)} %copy-done.8, bf16[768,512]{1,0:T(8,128)(2,1)} %collective-permute-done.3), kind=kLoop, calls=%fused_computation.8 | loop fusion | flops 786432 | bytes 4718593 | tf_op jit(solution)/shard_map/jit(_where)/select_n | solution.py:318
  119.3 3.6 %collective-permute-done.6 = bf16[512,768]{1,0:T(8,128)(2,1)S(1)} collective-permute-done((bf16[512,768]{1,0:T(8,128)(2,1)}, bf16[512,768]{1,0:T(8,128)(2,1)S(1)}, u32[]{:S(2)}, u32[]{:S(2)}) %collective-permute-start.6) | collective-permute-done | bytes 786464 | tf_op jit(solution)/shard_map/ppermute | solution.py:317
  122.8 8.4 %collective-permute-done.7 = bf16[512,768]{1,0:T(8,128)(2,1)S(1)} collective-permute-done((bf16[512,768]{1,0:T(8,128)(2,1)S(1)}, bf16[512,768]{1,0:T(8,128)(2,1)S(1)}, u32[]{:S(2)}, u32[]{:S(2)}) %collective-permute-start.7) | collective-permute-done | bytes 786464 | tf_op jit(solution)/shard_map/ppermute | solution.py:319
  131.2 1.1 broadcast_select_fusion.3
  132.3 1.3 context_part.1
  133.6 1.4 copy-done.6
  135.0 0.1 slice.65
  135.1 3.7 %collective-permute-start.11 = (f32[4,2]{0,1:T(2,128)S(1)}, f32[4,2]{0,1:T(2,128)S(1)}, u32[]{:S(2)}, u32[]{:S(2)}) collective-permute-start(f32[4,2]{0,1:T(2,128)S(1)} %slice.65), channel_id=1, source_target_pairs={{0,192},{4,196},{8,200},{12,204},{16,208},{20,212},{24,216},{28,22... | collective-permute-start | bytes 104 | tf_op jit(solution)/shard_map/ppermute | solution.py:340
  138.8 1.6 copy-done.7
  140.4 6.8 %first_layer.1 = (bf16[1024,512]{1,0:T(8,128)(2,1)S(1)}, bf16[1024,512]{1,0:T(8,128)(2,1)S(1)}, f32[16,1024]{1,0:T(8,128)S(1)}) custom-call(bf16[16,512]{1,0:T(8,128)(2,1)S(1)} %broadcast_in_dim.43.u_ref, f32[1024,512]{1,0:T(8,128)S(1)} %copy-done.7, bf16[512,512]{1,0:T(8,128)(2,1)S(1)} %get-tuple-element.48.head_ref, bf16[2048,512]{1,0:T(8,128)(2,1)} %bitcast.10.recv_hbm), custom_call_target="tpu_custom_call" | custom-call | flops 15728640000 | bytes 8388608 | tf_op jit(solution)/shard_map/first_layer/pallas_call | solution.py:78
  147.1 0.1 collective-permute-start.12
  147.2 4.1 %collective-permute-start.15 = (f32[3,768]{1,0:T(4,128)S(1)}, f32[3,768]{1,0:T(4,128)S(1)}, u32[]{:S(2)}, u32[]{:S(2)}) collective-permute-start(f32[3,768]{1,0:T(4,128)S(1)} %pad_maximum_fusion), channel_id=1, source_target_pairs={{2,4},{3,5},{4,2},{5,3},{10,12},{11,13},{12,10},{13,11},{18,20},{1... | collective-permute-start | bytes 27656 | tf_op jit(solution)/shard_map/ppermute | solution.py:310
  151.3 0.6 collective-permute-start.14
  151.9 1.8 collective-permute-done.15
  153.8 0.1 slice.67
  153.8 1.2 collective-permute-start.13
  155.0 2.1 %collective-permute-done.13 = f32[2,2]{0,1:T(2,128)S(1)} collective-permute-done((f32[2,2]{0,1:T(2,128)S(1)}, f32[2,2]{0,1:T(2,128)S(1)}, u32[]{:S(2)}, u32[]{:S(2)}) %collective-permute-start.13) | collective-permute-done | bytes 48 | tf_op jit(solution)/shard_map/ppermute | solution.py:340
  157.3 5.2 %second_layer.1 = (bf16[1024,768]{1,0:T(8,128)(2,1)S(1)}, bf16[1024,768]{1,0:T(8,128)(2,1)S(1)}, bf16[1024,512]{1,0:T(8,128)(2,1)S(1)}) custom-call(bf16[1024,512]{1,0:T(8,128)(2,1)S(1)} %get-tuple-element.53.mine_ref, bf16[1024,512]{1,0:T(8,128)(2,1)S(1)} %collective-permute-done.12.other_ref, bf16[1024,512]{1,0:T(8,128)(2,1)S(1)} %get-tuple-element.56.pay_ref, ...), custom_call_target="tpu_custom_call" | custom-call | flops 15728640000 | bytes 12582912 | tf_op jit(solution)/shard_map/second_layer/pallas_call | solution.py:78
  162.6 0.3 collective-permute-start.19
  163.6 0.7 collective-permute-start.20
  164.3 1.8 collective-permute-done.20
  166.1 3.1 %collective-permute-start.21 = (f32[1,2]{0,1:T(2,128)S(1)}, f32[1,2]{0,1:T(2,128)S(1)}, u32[]{:S(2)}, u32[]{:S(2)}) collective-permute-start(f32[1,2]{0,1:T(2,128)S(1)} %max.30), channel_id=1, source_target_pairs={{0,3},{1,2},{2,1},{3,0},{4,7},{5,6},{6,5},{7,4},{8,11},{9,10},{10,... | collective-permute-start | bytes 32 | tf_op jit(solution)/shard_map/ppermute | solution.py:343
  169.2 3.2 %last_layer.1 = f32[16,1024]{1,0:T(8,128)S(1)} custom-call(f32[1]{0:T(128)} %copy.14.coefficient, bf16[1024,512]{1,0:T(8,128)(2,1)S(1)} %get-tuple-element.61.mine_ref, bf16[1024,512]{1,0:T(8,128)(2,1)S(1)} %collective-permute-done.19.other_ref, bf16[1024,512]{1,0:T(8,128)(2,1)S(1)} %get-tuple-element.56.pay_ref, ...), custom_call_target="tpu_custom_call" | custom-call | flops 1879048192 | bytes 10485760 | tf_op jit(solution)/shard_map/last_layer/pallas_call | solution.py:78
  172.4 0.6 fusion.3
  173.7 1.5 collective-permute-start.22
  175.2 0.8 collective-permute-done.22
  176.0 3.1 %collective-permute-start.24 = (f32[1,1024]{1,0:T(1,128)S(1)}, f32[1,1024]{1,0:T(1,128)S(1)}, u32[]{:S(2)}, u32[]{:S(2)}) collective-permute-start(f32[1,1024]{1,0:T(1,128)S(1)} %fusion.6), channel_id=1, source_target_pairs={{2,4},{3,5},{4,2},{5,3},{10,12},{11,13},{12,10},{13,11},{18,20},{1... | collective-permute-start | bytes 12296 | tf_op jit(solution)/shard_map/ppermute | solution.py:391
  179.2 2.1 %collective-permute-start.23 = (f32[1,1024]{1,0:T(1,128)S(1)}, f32[1,1024]{1,0:T(1,128)S(1)}, u32[]{:S(2)}, u32[]{:S(2)}) collective-permute-start(f32[1,1024]{1,0:T(1,128)S(1)} %fusion.6), channel_id=1, source_target_pairs={{0,1},{1,0},{2,5},{3,4},{4,3},{5,2},{6,7},{7,6},{8,9},{9,8},{10,13... | collective-permute-start | bytes 12296 | tf_op jit(solution)/shard_map/ppermute | solution.py:390
  181.3 1.1 collective-permute-done.24
  182.4 1.1 collective-permute-done.23
  183.5 0.6 maximum_select_fusion
  (65 shorter events, 0.5 us)
Async XLA Ops:
  0.0 6.7 %copy-start.13 = (bf16[2,256]{1,0:T(2,128)(2,1)S(1)}, bf16[2,256]{1,0:T(2,128)(2,1)}, u32[]{:S(2)}) copy-start(bf16[2,256]{1,0:T(2,128)(2,1)} %param.12) | copy-start | bytes 3076
  0.0 19.1 %copy-start.9 = (bf16[2,512,768]{2,1,0:T(8,128)(2,1)S(1)}, bf16[2,512,768]{2,1,0:T(8,128)(2,1)}, u32[]{:S(2)}) copy-start(bf16[2,512,768]{2,1,0:T(8,128)(2,1)} %param.19) | copy-start | bytes 4718596
  2.8 35.8 %collective-permute-start = (bf16[768,512]{1,0:T(8,128)(2,1)}, bf16[768,512]{1,0:T(8,128)(2,1)S(1)}, u32[]{:S(2)}, u32[]{:S(2)}) collective-permute-start(bf16[768,512]{1,0:T(8,128)(2,1)} %get-tuple-element.76), channel_id=1, source_target_pairs={{0,1},{1,0},{2,5},{3,4},{4,3},{5,2},{6,7},{7,6},{8,9},{9,8},{10,13... | collective-permute-start | bytes 2359304 | tf_op jit(solution)/shard_map/ppermute | solution.py:295
  7.3 31.3 %all-to-all-start = ((bf16[64,2,256]{2,1,0:T(2,128)(2,1)}), bf16[64,2,256]{2,1,0:T(2,128)(2,1)S(1)}, u32[]{:S(2)}, u32[]{:S(2)}) async-start(bf16[64,2,256]{2,1,0:T(2,128)(2,1)} %broadcast_in_dim.41), calls=%async_computation | async-start | bytes 131072 | tf_op jit(solution)/shard_map/all_to_all | solution.py:297
  20.4 34.2 %collective-permute-start.4 = (bf16[512,768]{1,0:T(8,128)(2,1)}, bf16[512,768]{1,0:T(8,128)(2,1)}, u32[]{:S(2)}, u32[]{:S(2)}) collective-permute-start(bf16[512,768]{1,0:T(8,128)(2,1)} %get-tuple-element.80), channel_id=1, source_target_pairs={{0,1},{1,0},{2,5},{3,4},{4,3},{5,2},{6,7},{7,6},{8,9},{9,8},{10,13... | collective-permute-start | bytes 2359304 | tf_op jit(solution)/shard_map/ppermute | solution.py:312
  23.8 91.4 %collective-permute-start.1 = (bf16[1024,512]{1,0:T(8,128)(2,1)}, bf16[1024,512]{1,0:T(8,128)(2,1)S(1)}, u32[]{:S(2)}, u32[]{:S(2)}) collective-permute-start(bf16[1024,512]{1,0:T(8,128)(2,1)} %get-tuple-element.72), channel_id=1, source_target_pairs={{0,1},{1,0},{2,5},{3,4},{4,3},{5,2},{6,7},{7,6},{8,9},{9,8},{10,13... | collective-permute-start | bytes 3145736 | tf_op jit(solution)/shard_map/ppermute | solution.py:321
  26.4 88.8 %collective-permute-start.2 = (bf16[1024,512]{1,0:T(8,128)(2,1)}, bf16[1024,512]{1,0:T(8,128)(2,1)}, u32[]{:S(2)}, u32[]{:S(2)}) collective-permute-start(bf16[1024,512]{1,0:T(8,128)(2,1)} %get-tuple-element.71), channel_id=1, source_target_pairs={{2,4},{3,5},{4,2},{5,3},{10,12},{11,13},{12,10},{13,11},{18,20},{1... | collective-permute-start | bytes 3145736 | tf_op jit(solution)/shard_map/ppermute | solution.py:323
  28.3 58.4 %collective-permute-start.16 = (bf16[768,512]{1,0:T(8,128)(2,1)}, bf16[768,512]{1,0:T(8,128)(2,1)}, u32[]{:S(2)}, u32[]{:S(2)}) collective-permute-start(bf16[768,512]{1,0:T(8,128)(2,1)} %get-tuple-element.75), channel_id=1, source_target_pairs={{0,1},{1,0},{2,5},{3,4},{4,3},{5,2},{6,7},{7,6},{8,9},{9,8},{10,13... | collective-permute-start | bytes 2359304 | tf_op jit(solution)/shard_map/ppermute | solution.py:313
  29.8 8.8 %copy-start.14 = (bf16[768]{0:T(1024)(128)(2,1)S(1)}, bf16[768]{0:T(1024)(128)(2,1)}, u32[]{:S(2)}) copy-start(bf16[768]{0:T(1024)(128)(2,1)} %param.21) | copy-start | bytes 4612
  29.8 8.8 %copy-start.12 = (f32[2,768]{1,0:T(2,128)S(1)}, f32[2,768]{1,0:T(2,128)}, u32[]{:S(2)}) copy-start(f32[2,768]{1,0:T(2,128)} %param.20) | copy-start | bytes 18436
  38.7 16.8 %copy-start.4 = (bf16[768,512]{1,0:T(8,128)(2,1)}, bf16[768,512]{1,0:T(8,128)(2,1)S(1)}, u32[]{:S(2)}) copy-start(bf16[768,512]{1,0:T(8,128)(2,1)S(1)} %collective-permute-done.va_ref) | copy-start | bytes 2359300
  38.7 12.7 %copy-start.11 = (bf16[2048,256]{1,0:T(8,128)(2,1)S(1)}, bf16[2048,256]{1,0:T(8,128)(2,1)}, u32[]{:S(2)}) copy-start(bf16[2048,256]{1,0:T(8,128)(2,1)} %emb_hbm.1) | copy-start | bytes 3145732
  38.7 96.3 %all-to-all-start.1 = ((bf16[256,8,512]{2,1,0:T(8,128)(2,1)}), bf16[256,8,512]{2,1,0:T(8,128)(2,1)}, u32[]{:S(2)}, u32[]{:S(2)}) async-start(bf16[256,8,512]{2,1,0:T(8,128)(2,1)} %bitcast.36), calls=%async_computation.1 | async-start | bytes 4194304 | tf_op jit(solution)/shard_map/all_to_all | solution.py:304
  52.4 3.1 %collective-permute-start.8 = (f32[32,2]{0,1:T(2,128)S(1)}, f32[32,2]{0,1:T(2,128)S(1)}, u32[]{:S(2)}, u32[]{:S(2)}) collective-permute-start(f32[32,2]{0,1:T(2,128)S(1)} %slice.59), channel_id=1, source_target_pairs={{0,4},{4,0},{8,12},{12,8},{16,20},{20,16},{24,28},{28,24},{32,36},... | collective-permute-start | bytes 776 | tf_op jit(solution)/shard_map/ppermute | solution.py:340
  54.6 53.4 %collective-permute-start.5 = (bf16[512,768]{1,0:T(8,128)(2,1)}, bf16[512,768]{1,0:T(8,128)(2,1)S(1)}, u32[]{:S(2)}, u32[]{:S(2)}) collective-permute-start(bf16[512,768]{1,0:T(8,128)(2,1)} %get-tuple-element.79), channel_id=1, source_target_pairs={{0,1},{1,0},{2,5},{3,4},{4,3},{5,2},{6,7},{7,6},{8,9},{9,8},{10,13... | collective-permute-start | bytes 2359304 | tf_op jit(solution)/shard_map/ppermute | solution.py:314
  55.4 54.4 %collective-permute-start.3 = (bf16[768,512]{1,0:T(8,128)(2,1)S(1)}, bf16[768,512]{1,0:T(8,128)(2,1)}, u32[]{:S(2)}, u32[]{:S(2)}) collective-permute-start(bf16[768,512]{1,0:T(8,128)(2,1)S(1)} %collective-permute-done.va_ref), channel_id=1, source_target_pairs={{0,3},{1,2},{6,5},{7,4},{8,11},{9,10},{14,13},{15,12},{16,19},{17,... | collective-permute-start | bytes 2359304 | tf_op jit(solution)/shard_map/ppermute | solution.py:311
  86.7 4.6 %collective-permute-start.9 = (f32[16,2]{0,1:T(2,128)S(1)}, f32[16,2]{0,1:T(2,128)S(1)}, u32[]{:S(2)}, u32[]{:S(2)}) collective-permute-start(f32[16,2]{0,1:T(2,128)S(1)} %slice.61), channel_id=1, source_target_pairs={{0,24},{4,28},{8,16},{12,20},{16,8},{20,12},{24,0},{28,4},{32,56},... | collective-permute-start | bytes 392 | tf_op jit(solution)/shard_map/ppermute | solution.py:340
  91.3 25.4 %collective-permute-start.17 = (bf16[768,512]{1,0:T(8,128)(2,1)}, bf16[768,512]{1,0:T(8,128)(2,1)S(1)}, u32[]{:S(2)}, u32[]{:S(2)}) collective-permute-start(bf16[768,512]{1,0:T(8,128)(2,1)} %collective-permute-done.16.va_ref), channel_id=1, source_target_pairs={{0,3},{1,2},{6,5},{7,4},{8,11},{9,10},{14,13},{15,12},{16,19},{17,... | collective-permute-start | bytes 2359304 | tf_op jit(solution)/shard_map/ppermute | solution.py:318
  108.0 8.7 %copy-start = (bf16[512,768]{1,0:T(8,128)(2,1)}, bf16[512,768]{1,0:T(8,128)(2,1)S(1)}, u32[]{:S(2)}) copy-start(bf16[512,768]{1,0:T(8,128)(2,1)S(1)} %collective-permute-done.5.ua_ref) | copy-start | bytes 2359300
  108.0 3.8 %collective-permute-start.10 = (f32[8,2]{0,1:T(2,128)S(1)}, f32[8,2]{0,1:T(2,128)S(1)}, u32[]{:S(2)}, u32[]{:S(2)}) collective-permute-start(f32[8,2]{0,1:T(2,128)S(1)} %slice.63), channel_id=1, source_target_pairs={{0,8},{4,12},{8,0},{12,4},{16,24},{20,28},{24,16},{28,20},{32,40},... | collective-permute-start | bytes 200 | tf_op jit(solution)/shard_map/ppermute | solution.py:340
  109.9 12.9 %collective-permute-start.6 = (bf16[512,768]{1,0:T(8,128)(2,1)}, bf16[512,768]{1,0:T(8,128)(2,1)S(1)}, u32[]{:S(2)}, u32[]{:S(2)}) collective-permute-start(bf16[512,768]{1,0:T(8,128)(2,1)} %collective-permute-done.4.ua_ref), channel_id=1, source_target_pairs={{2,3},{3,2},{4,5},{5,4},{10,11},{11,10},{12,13},{13,12},{18,19},{1... | collective-permute-start | bytes 2359304 | tf_op jit(solution)/shard_map/ppermute | solution.py:317
  111.9 19.4 %collective-permute-start.7 = (bf16[512,768]{1,0:T(8,128)(2,1)S(1)}, bf16[512,768]{1,0:T(8,128)(2,1)S(1)}, u32[]{:S(2)}, u32[]{:S(2)}) collective-permute-start(bf16[512,768]{1,0:T(8,128)(2,1)S(1)} %collective-permute-done.5.ua_ref), channel_id=1, source_target_pairs={{2,3},{3,2},{4,5},{5,4},{10,11},{11,10},{12,13},{13,12},{18,19},{1... | collective-permute-start | bytes 2359304 | tf_op jit(solution)/shard_map/ppermute | solution.py:319
  115.2 1.7 copy-start.8
  116.7 14.5 %copy-start.10 = (bf16[2,512,768]{2,1,0:T(8,128)(2,1)S(1)}, bf16[2,512,768]{2,1,0:T(8,128)(2,1)}, u32[]{:S(2)}) copy-start(bf16[2,512,768]{2,1,0:T(8,128)(2,1)} %param.19) | copy-start | bytes 4718596
  119.3 13.1 %copy-start.5 = (bf16[768,512]{1,0:T(8,128)(2,1)S(1)}, bf16[768,512]{1,0:T(8,128)(2,1)}, u32[]{:S(2)}) copy-start(bf16[768,512]{1,0:T(8,128)(2,1)} %copy-done.4) | copy-start | bytes 2359300
  133.6 1.4 copy-start.6
  135.1 12.1 %collective-permute-start.11 = (f32[4,2]{0,1:T(2,128)S(1)}, f32[4,2]{0,1:T(2,128)S(1)}, u32[]{:S(2)}, u32[]{:S(2)}) collective-permute-start(f32[4,2]{0,1:T(2,128)S(1)} %slice.65), channel_id=1, source_target_pairs={{0,192},{4,196},{8,200},{12,204},{16,208},{20,212},{24,216},{28,22... | collective-permute-start | bytes 104 | tf_op jit(solution)/shard_map/ppermute | solution.py:340
  138.8 1.6 copy-start.7
  140.4 17.0 %copy-start.2 = (bf16[768,512]{1,0:T(8,128)(2,1)S(1)}, bf16[768,512]{1,0:T(8,128)(2,1)}, u32[]{:S(2)}) copy-start(bf16[768,512]{1,0:T(8,128)(2,1)} %get-tuple-element.73.vb_ref) | copy-start | bytes 2359300
  140.4 17.0 %copy-start.3 = (bf16[512,768]{1,0:T(8,128)(2,1)S(1)}, bf16[512,768]{1,0:T(8,128)(2,1)}, u32[]{:S(2)}) copy-start(bf16[512,768]{1,0:T(8,128)(2,1)} %get-tuple-element.58.ub_ref) | copy-start | bytes 2359300
  147.1 10.0 %collective-permute-start.12 = (bf16[1024,512]{1,0:T(8,128)(2,1)S(1)}, bf16[1024,512]{1,0:T(8,128)(2,1)S(1)}, u32[]{:S(2)}, u32[]{:S(2)}) collective-permute-start(bf16[1024,512]{1,0:T(8,128)(2,1)S(1)} %get-tuple-element.53.mine_ref), channel_id=1, source_target_pairs={{0,4},{1,5},{2,6},{3,7},{4,0},{5,1},{6,2},{7,3},{8,12},{9,13},{10,... | collective-permute-start | bytes 3145736 | tf_op jit(solution)/shard_map/ppermute | solution.py:372
  147.2 6.5 %collective-permute-start.15 = (f32[3,768]{1,0:T(4,128)S(1)}, f32[3,768]{1,0:T(4,128)S(1)}, u32[]{:S(2)}, u32[]{:S(2)}) collective-permute-start(f32[3,768]{1,0:T(4,128)S(1)} %pad_maximum_fusion), channel_id=1, source_target_pairs={{2,4},{3,5},{4,2},{5,3},{10,12},{11,13},{12,10},{13,11},{18,20},{1... | collective-permute-start | bytes 27656 | tf_op jit(solution)/shard_map/ppermute | solution.py:310
  151.3 6.0 %collective-permute-start.14 = (f32[3,768]{1,0:T(4,128)S(1)}, f32[3,768]{1,0:T(4,128)S(1)}, u32[]{:S(2)}, u32[]{:S(2)}) collective-permute-start(f32[3,768]{1,0:T(4,128)S(1)} %pad_maximum_fusion), channel_id=1, source_target_pairs={{0,1},{1,0},{2,5},{3,4},{4,3},{5,2},{6,7},{7,6},{8,9},{9,8},{10,13... | collective-permute-start | bytes 27656 | tf_op jit(solution)/shard_map/ppermute | solution.py:309
  153.8 3.3 %collective-permute-start.13 = (f32[2,2]{0,1:T(2,128)S(1)}, f32[2,2]{0,1:T(2,128)S(1)}, u32[]{:S(2)}, u32[]{:S(2)}) collective-permute-start(f32[2,2]{0,1:T(2,128)S(1)} %slice.67), channel_id=1, source_target_pairs={{0,64},{4,68},{8,72},{12,76},{16,80},{20,84},{24,88},{28,92},{32,9... | collective-permute-start | bytes 56 | tf_op jit(solution)/shard_map/ppermute | solution.py:340
  157.3 5.3 %collective-permute-start.18 = (f32[1,2]{0,1:T(2,128)S(1)}, f32[1,2]{0,1:T(2,128)S(1)}, u32[]{:S(2)}, u32[]{:S(2)}) collective-permute-start(f32[1,2]{0,1:T(2,128)S(1)} %slice.70), channel_id=1, source_target_pairs={{0,32},{4,36},{8,40},{12,44},{16,48},{20,52},{24,56},{28,60},{32,0... | collective-permute-start | bytes 32 | tf_op jit(solution)/shard_map/ppermute | solution.py:340
  157.3 11.9 %copy-start.1 = (bf16[512,768]{1,0:T(8,128)(2,1)S(1)}, bf16[512,768]{1,0:T(8,128)(2,1)}, u32[]{:S(2)}) copy-start(bf16[512,768]{1,0:T(8,128)(2,1)} %copy-done) | copy-start | bytes 2359300
  162.6 3.5 %collective-permute-start.19 = (bf16[1024,512]{1,0:T(8,128)(2,1)S(1)}, bf16[1024,512]{1,0:T(8,128)(2,1)S(1)}, u32[]{:S(2)}, u32[]{:S(2)}) collective-permute-start(bf16[1024,512]{1,0:T(8,128)(2,1)S(1)} %get-tuple-element.61.mine_ref), channel_id=1, source_target_pairs={{0,4},{1,5},{2,6},{3,7},{4,0},{5,1},{6,2},{7,3},{8,12},{9,13},{10,... | collective-permute-start | bytes 3145736 | tf_op jit(solution)/shard_map/ppermute | solution.py:380
  163.6 2.5 %collective-permute-start.20 = (f32[1,2]{0,1:T(2,128)S(1)}, f32[1,2]{0,1:T(2,128)S(1)}, u32[]{:S(2)}, u32[]{:S(2)}) collective-permute-start(f32[1,2]{0,1:T(2,128)S(1)} %slice_maximum_fusion), channel_id=1, source_target_pairs={{0,1},{1,0},{2,3},{3,2},{4,5},{5,4},{6,7},{7,6},{8,9},{9,8},{10,11... | collective-permute-start | bytes 32 | tf_op jit(solution)/shard_map/ppermute | solution.py:343
  166.1 6.3 %collective-permute-start.21 = (f32[1,2]{0,1:T(2,128)S(1)}, f32[1,2]{0,1:T(2,128)S(1)}, u32[]{:S(2)}, u32[]{:S(2)}) collective-permute-start(f32[1,2]{0,1:T(2,128)S(1)} %max.30), channel_id=1, source_target_pairs={{0,3},{1,2},{2,1},{3,0},{4,7},{5,6},{6,5},{7,4},{8,11},{9,10},{10,... | collective-permute-start | bytes 32 | tf_op jit(solution)/shard_map/ppermute | solution.py:343
  173.7 2.4 %collective-permute-start.22 = (f32[1,1024]{1,0:T(1,128)S(1)}, f32[1,1024]{1,0:T(1,128)S(1)}, u32[]{:S(2)}, u32[]{:S(2)}) collective-permute-start(f32[1,1024]{1,0:T(1,128)S(1)} %slice_subtract_fusion), channel_id=1, source_target_pairs={{0,4},{1,5},{2,6},{3,7},{4,0},{5,1},{6,2},{7,3},{8,12},{9,13},{10,... | collective-permute-start | bytes 12296 | tf_op jit(solution)/shard_map/ppermute | solution.py:389
  176.0 6.4 %collective-permute-start.24 = (f32[1,1024]{1,0:T(1,128)S(1)}, f32[1,1024]{1,0:T(1,128)S(1)}, u32[]{:S(2)}, u32[]{:S(2)}) collective-permute-start(f32[1,1024]{1,0:T(1,128)S(1)} %fusion.6), channel_id=1, source_target_pairs={{2,4},{3,5},{4,2},{5,3},{10,12},{11,13},{12,10},{13,11},{18,20},{1... | collective-permute-start | bytes 12296 | tf_op jit(solution)/shard_map/ppermute | solution.py:391
  179.2 4.3 %collective-permute-start.23 = (f32[1,1024]{1,0:T(1,128)S(1)}, f32[1,1024]{1,0:T(1,128)S(1)}, u32[]{:S(2)}, u32[]{:S(2)}) collective-permute-start(f32[1,1024]{1,0:T(1,128)S(1)} %fusion.6), channel_id=1, source_target_pairs={{0,1},{1,0},{2,5},{3,4},{4,3},{5,2},{6,7},{7,6},{8,9},{9,8},{10,13... | collective-permute-start | bytes 12296 | tf_op jit(solution)/shard_map/ppermute | solution.py:390

commit v6 on v5

--- a/solution.py
+++ b/solution.py
@@ -11,7 +11,7 @@
 F32 = jnp.float32
 AXES = ("shard", "tp")
 VMEM = pl.BlockSpec(memory_space=pltpu.VMEM)
-PICK, CTX, FIRST, SECOND = 4096, 20000, 15000, 15000
+PICK, CTX, FIRST, SECOND = 4096, 6000, 15000, 15000
 SMEM = pl.BlockSpec(memory_space=pltpu.SMEM)
 ANY = pl.BlockSpec(memory_space=pl.ANY)
 
@@ -87,6 +87,34 @@
         ),
         name=name,
     )(*scalars, *arrays, *far)
+
+
+def cut_kernel(where, v_ref, u_ref, ctx_ref, v_out, u_out, own_out, away_out, sems):
+    layer, parity = where[0], where[1]
+    copies = [
+        pltpu.make_async_copy(v_ref.at[layer], v_out, sems.at[0]),
+        pltpu.make_async_copy(u_ref.at[layer], u_out, sems.at[1]),
+        pltpu.make_async_copy(ctx_ref.at[1 - parity], away_out, sems.at[2]),
+        pltpu.make_async_copy(ctx_ref.at[parity], own_out, sems.at[3]),
+    ]
+    for copy in copies:
+        copy.start()
+    for copy in copies:
+        copy.wait()
+
+
+def cut_blocks(where, v, u, ctx):
+    shapes = [v.shape[1:], u.shape[1:], ctx.shape[1:], ctx.shape[1:]]
+    return pl.pallas_call(
+        cut_kernel,
+        in_specs=[SMEM, ANY, ANY, ANY],
+        out_specs=[ANY] * 4,
+        out_shape=[jax.ShapeDtypeStruct(shape, BF) for shape in shapes],
+        scratch_shapes=[pltpu.SemaphoreType.DMA((4,))],
+        compiler_params=grant(63000),
+        cost_estimate=pl.CostEstimate(flops=0, bytes_accessed=7 << 20, transcendentals=0),
+        name="cut_blocks",
+    )(where, v, u, ctx)
 
 
 def pick_kernel(
@@ -289,10 +317,24 @@
     away_swap = group_perm(groups, lambda x, c: (x ^ 1, c), is_away)
     ctx_near = group_perm(groups, lambda x, c: (x ^ 1, c) if is_home(x, c) else (x ^ 3, 1 - c))
     ctx_far = group_perm(groups, lambda x, c: (x ^ 2, 1 - c), is_away)
+
+    def stay(x, c):
+        return x, c
+
+    y_up = group_perm(groups, stay, turn=lambda x, c: 1)
+    y_mixed = group_perm(groups, stay, turn=lambda x, c: -1 if is_home(x, c) else 1)
+    y_down = group_perm(groups, stay, is_away, lambda x, c: -1)
+    odd_y = lax.axis_index("shard") // 2 % 2
     persons, _, kept = kept_part_entries.shape
     hops = partners(shards)
     me = lax.axis_index("shard")
-    v0_a = move(lowrank_v_matrix[0], perm=to_near)
+    v_mine, u_mine, ctx_own, ctx_away = cut_blocks(
+        jnp.stack([odd_y, parity]), lowrank_v_matrix, lowrank_u_matrix, pair_attributes
+    )
+    v_near = move(v_mine, perm=to_near)
+    u_near = move(u_mine, perm=to_near)
+    ctx_a = move(ctx_away, perm=ctx_near)
+    ctx_b = move(ctx_own, perm=ctx_far)
     users = jnp.broadcast_to(person_embedding[None], (shards, *person_embedding.shape))
     users = lax.all_to_all(users, "shard", split_axis=0, concat_axis=0, tiled=True)
 
@@ -300,29 +342,9 @@
         kept_part_entries[:, 0, :].T, valid_slot_number.T, catalog_embedding, catalog_attributes
     )
     parcel = parcel.reshape(persons * 2, kept, 512)
-    parcel, v0_a, users = lax.optimization_barrier((parcel, v0_a, users))
+    parcel, v_near, u_near, users = lax.optimization_barrier((parcel, v_near, u_near, users))
     recv = lax.all_to_all(parcel, AXES, split_axis=0, concat_axis=0, tiled=True)
     recv = recv.reshape(persons * 2 * kept, 512)
-
-    small = jnp.concatenate([interaction_offset, final_projection[None, :].astype(F32)], 0)
-    small, v0_a = lax.optimization_barrier((small, v0_a))
-    small_a = move(small, perm=to_near)
-    small_b = jnp.where(home, small, move(small, perm=ctx_far))
-    v0_b = move(v0_a, perm=home_on)
-    u0_a = move(lowrank_u_matrix[0], perm=to_near)
-    v1_a = move(lowrank_v_matrix[1], perm=to_near)
-    u1_a = move(lowrank_u_matrix[1], perm=to_near)
-    v0_b, u0_a, u1_a = lax.optimization_barrier((v0_b, u0_a, u1_a))
-    v0_b = jnp.where(home, lowrank_v_matrix[0], v0_b)
-    u0_b = jnp.where(home, lowrank_u_matrix[0], move(u0_a, perm=away_swap))
-    v1_b = jnp.where(home, lowrank_v_matrix[1], move(v1_a, perm=home_on))
-    u1_b = jnp.where(home, lowrank_u_matrix[1], move(u1_a, perm=away_swap))
-
-    ctx_a = move(lax.dynamic_index_in_dim(pair_attributes, 1 - parity, 0, False), perm=ctx_near)
-    ctx_own = lax.dynamic_index_in_dim(pair_attributes, parity, 0, False)
-    ctx_a, ctx_b = lax.optimization_barrier((ctx_a, move(ctx_own, perm=ctx_far)))
-    ctx_b = jnp.where(home, ctx_own, ctx_b)
-    ctx_a, u0_b, u1_b = lax.optimization_barrier((ctx_a, u0_b, u1_b))
 
     all_scores = jnp.einsum(
         "ue,ie->ui", users.reshape(persons, -1), catalog_embedding, preferred_element_type=F32
@@ -339,11 +361,44 @@
         half = best.shape[0] // 2
         return jnp.maximum(best[:half], lax.ppermute(best[half:], "shard", pairs))
 
-    def over_x(best, flip):
-        return jnp.maximum(best, lax.ppermute(best, "tp", [(i, i ^ flip) for i in range(4)]))
-
-    for pairs in hops[:2:-1]:
-        best = halve(best, pairs)
+    def over_x(best):
+        out = best
+        for flip in (1, 3, 2):
+            out = jnp.maximum(out, lax.ppermute(best, "tp", [(i, i ^ flip) for i in range(4)]))
+        return out
+
+    def over_y(best):
+        n = best.shape[0] // 4
+        out = best[:n]
+        for block, flip in ((1, 1), (2, 3), (3, 2)):
+            pairs = [(i, i ^ (2 * flip)) for i in range(shards)]
+            got = lax.ppermute(best[block * n : (block + 1) * n], "shard", pairs)
+            out = jnp.maximum(out, got)
+        return out
+
+    best = halve(best, hops[5])
+
+    v_far = move(v_near, perm=home_on)
+    u_far = move(u_near, perm=away_swap)
+    v_near_y = move(v_near, perm=y_up)
+    v_far_y = move(v_far, perm=y_down)
+    u_near_y = move(u_near, perm=y_mixed)
+    u_far_y = move(u_far, perm=y_down)
+    even = odd_y == 0
+    v0_a = jnp.where(even, v_near, v_near_y)
+    v1_a = jnp.where(even, v_near_y, v_near)
+    u0_a = jnp.where(even, u_near, u_near_y)
+    u1_a = jnp.where(even, u_near_y, u_near)
+    v0_b = jnp.where(home, lowrank_v_matrix[0], jnp.where(even, v_far, v_far_y))
+    v1_b = jnp.where(home, lowrank_v_matrix[1], jnp.where(even, v_far_y, v_far))
+    u0_b = jnp.where(home, lowrank_u_matrix[0], jnp.where(even, u_far, u_far_y))
+    u1_b = jnp.where(home, lowrank_u_matrix[1], jnp.where(even, u_far_y, u_far))
+    ctx_b = jnp.where(home, ctx_own, ctx_b)
+    small = jnp.concatenate([interaction_offset, final_projection[None, :].astype(F32)], 0)
+    small, _ = lax.optimization_barrier((small, u_far))
+    small_a = move(small, perm=to_near)
+    small_b = jnp.where(home, small, move(small, perm=ctx_far))
+    ctx_a, u0_a, u0_b, u1_a, u1_b = lax.optimization_barrier((ctx_a, u0_a, u0_b, u1_a, u1_b))
 
     emb_other = lax.dynamic_index_in_dim(users, me ^ 1, 0, False)
     query = lax.dynamic_slice_in_dim(jnp.where(home, person_embedding, emb_other), parity, 1, 0)
@@ -361,7 +416,7 @@
         CTX, 8, [], [ctx_a, ctx_b, v0_a, v0_b], [],
     )
     recv, best = lax.optimization_barrier((recv, best))
-    step = halve(best, hops[2])
+    step = over_y(best)
     pay, piece, logit = call(
         first_kernel, "first_layer", 24000, [tall, tall, lanes],
         [pltpu.VMEM(recv.shape, BF), pltpu.VMEM((16, recv.shape[0]), F32)]
@@ -369,16 +424,16 @@
         FIRST, 8, [], [query, part, head], [recv],
     )
     piece, best = lax.optimization_barrier((piece, step))
-    other, best = lax.optimization_barrier((move(piece, perm=to_core), halve(best, hops[1])))
-    step = halve(best, hops[0])
+    other, best = lax.optimization_barrier((move(piece, perm=to_core), halve(best, hops[2])))
+    step = halve(best, hops[1])
     x_a, x_b, piece1 = call(
         second_kernel, "second_layer", 24000, [wide, wide, tall], [],
         SECOND, 12, [],
         [piece, other, pay, small_a, small_b, ctx_a, ctx_b, u0_a, u0_b, v1_a, v1_b], [],
     )
     piece1, best = lax.optimization_barrier((piece1, step))
-    other1, best = lax.optimization_barrier((move(piece1, perm=to_core), over_x(best, 1)))
-    step = over_x(best, 3)
+    other1, best = lax.optimization_barrier((move(piece1, perm=to_core), halve(best, hops[0])))
+    step = over_x(best)
     (score,) = call(
         last_kernel, "last_layer", 24000, [lanes], [], 1792, 10, [similarity_coefficient],
         [piece1, other1, pay, x_a, x_b, small_a, small_b, logit, ctx_a, ctx_b, u1_a, u1_b], [],

time: 185 us -> 295 us (1.59)
  Pallas kernels: 24.4 us -> 136 us
  starting transfers between devices: 71.2 us -> 80.4 us
  waiting for transfers between devices: 67.4 us -> 59.4 us
  local copies, waits for them, and re-layouts: 12.4 us -> 8.66 us
    pallas_call x0 -> x1, Pallas kernels: none -> 113 us  [cut_blocks(): pl.pallas_call(cut_kernel, in_specs=[SMEM, ANY, ANY, ANY], out_specs=[ANY...]
    ppermute x10 -> x13, starting transfers between devices: 18.8 us -> 29 us  [the longest x1 5.05 us: on_device(): ctx_b = move(ctx_own, perm=ctx_far)]
    ppermute x10 -> x13, waiting for transfers between devices: 57.2 us -> 47.4 us  [the longest x1 18.7 us: on_device(): u_far = move(u_near, perm=away_swap)]
    squeeze x3 -> x0, local copies, waits for them, and re-layouts: 7.12 us -> none  [the longest x1 3.06 us: on_device(): ctx_own = lax.dynamic_index_in_dim(pair_attributes, parity, 0, False)]
    ppermute x6 -> x4, starting transfers between devices: 12.2 us -> 8.66 us  [halve(): return jnp.maximum(best[:half], lax.ppermute(best[half:], 'shard', pairs))]
    unnamed x30 -> x40, local copies, waits for them, and re-layouts: 3.22 us -> 6.69 us
  transfers between devices with their start and end apart: 27 -> 29, of which waited for: 11 -> 13; matrix products, arithmetic and copies ran while one was open for 7% -> 3% of each run, Pallas kernels for 13% -> 8%
where the time goes in v6:
time: 295 us
  Pallas kernels  136 us (46%)
  starting transfers between devices  80.4 us (27%)
  waiting for transfers between devices  59.4 us (20%)
  local copies, waits for them, and re-layouts  8.66 us (3%)
  other arithmetic  7.75 us (3%)
    pallas_call x1, Pallas kernels, cut_blocks(): pl.pallas_call(cut_kernel, in_specs=[SMEM, ANY, ANY, ANY], out_specs=[ANY...  113 us
    ppermute x1, waiting for transfers between devices, on_device(): u_far = move(u_near, perm=away_swap)  18.7 us
    ppermute x1, waiting for transfers between devices, on_device(): ctx_b = move(ctx_own, perm=ctx_far)  18.4 us
    pallas_call x4, Pallas kernels, call(): pl.pallas_call(kernel, in_specs=[SMEM] * len(scalars) + [VMEM] * len(arra...  14.9 us
    all_to_all x1, starting transfers between devices, on_device(): recv = lax.all_to_all(parcel, AXES, split_axis=0, concat_axis=0, tiled=True)  11.8 us
    all_to_all x1, starting transfers between devices, on_device(): lax.all_to_all(users, 'shard', split_axis=0, concat_axis=0, tiled=True)  11.8 us
    ppermute x4, starting transfers between devices, halve(): return jnp.maximum(best[:half], lax.ppermute(best[half:], 'shard', pairs))  8.66 us
    pallas_call x1, Pallas kernels, pick_rows(): pl.pallas_call(pick_kernel, in_specs=[VMEM, VMEM, ANY, ANY], out_specs=AN...  7.97 us
  transfers between devices with their start and end apart: 29, of which 13 were waited for; matrix products, arithmetic and copies ran while one was open for 3% of the time, Pallas kernels for 8%

profile of v6, /device:TPU:1, one launch (start us, length us, event | category | flops | bytes accessed | tf_op | source)
XLA Modules:
  0.0 294.5 jit_solution(13850014362188793471)
XLA Ops:
  0.0 0.6 pad_add_fusion.where
  0.6 113.1 %cut_blocks.1 = (bf16[768,512]{1,0:T(8,128)(2,1)}, bf16[512,768]{1,0:T(8,128)(2,1)}, bf16[1024,512]{1,0:T(8,128)(2,1)}, bf16[1024,512]{1,0:T(8,128)(2,1)}) custom-call(s32[2]{0:T(128)} %pad_add_fusion.where, bf16[2,768,512]{2,1,0:T(8,128)(2,1)} %v_ref.1, bf16[2,512,768]{2,1,0:T(8,128)(2,1)} %u_ref.1, bf16[2,1024,512]{2,1,0:T(8,128)(2,1)} %ctx_ref.1), custom_call_target="tpu_custom_call" | custom-call | bytes 7340032 | tf_op jit(solution)/shard_map/cut_blocks/pallas_call | solution.py:108
  113.7 4.0 %collective-permute-start = (bf16[768,512]{1,0:T(8,128)(2,1)}, bf16[768,512]{1,0:T(8,128)(2,1)S(1)}, u32[]{:S(2)}, u32[]{:S(2)}) collective-permute-start(bf16[768,512]{1,0:T(8,128)(2,1)} %get-tuple-element.39), channel_id=1, source_target_pairs={{0,1},{1,0},{2,5},{3,4},{4,3},{5,2},{6,7},{7,6},{8,9},{9,8},{10,13... | collective-permute-start | bytes 2359304 | tf_op jit(solution)/shard_map/ppermute | solution.py:334
  117.7 0.1 collective-permute-start.1
  117.8 0.7 broadcast_in_dim.41
  118.4 11.8 %all-to-all-start = ((bf16[64,2,256]{2,1,0:T(2,128)(2,1)}), bf16[64,2,256]{2,1,0:T(2,128)(2,1)S(1)}, u32[]{:S(2)}, u32[]{:S(2)}) async-start(bf16[64,2,256]{2,1,0:T(2,128)(2,1)} %broadcast_in_dim.41), calls=%async_computation | async-start | bytes 131072 | tf_op jit(solution)/shard_map/all_to_all | solution.py:339
  130.2 8.0 %pick_rows.1 = bf16[32,2,32,512]{3,2,1,0:T(8,128)(2,1)} custom-call(s32[8,128]{1,0:T(8,128)} %bitcast.27, s32[1,128]{1,0:T(1,128)} %bitcast.28, bf16[2048,256]{1,0:T(8,128)(2,1)} %emb_hbm.1, bf16[2048,768]{1,0:T(8,128)(2,1)} %attr_hbm.1), custom_call_target="tpu_custom_call" | custom-call | flops 4294967296 | bytes 6291456 | tf_op jit(solution)/shard_map/pick_rows/pallas_call | solution.py:172
  138.2 2.1 all-to-all-done
  140.3 0.9 copy-done.13
  141.2 1.0 copy-done.15
  142.2 11.8 %all-to-all-start.1 = ((bf16[256,8,512]{2,1,0:T(8,128)(2,1)}), bf16[256,8,512]{2,1,0:T(8,128)(2,1)}, u32[]{:S(2)}, u32[]{:S(2)}) async-start(bf16[256,8,512]{2,1,0:T(8,128)(2,1)} %bitcast.26), calls=%async_computation.1 | async-start | bytes 4194304 | tf_op jit(solution)/shard_map/all_to_all | solution.py:346
  154.0 5.0 %collective-permute-start.6 = (bf16[1024,512]{1,0:T(8,128)(2,1)S(1)}, bf16[1024,512]{1,0:T(8,128)(2,1)S(1)}, u32[]{:S(2)}, u32[]{:S(2)}) collective-permute-start(bf16[1024,512]{1,0:T(8,128)(2,1)S(1)} %copy-done.12), channel_id=1, source_target_pairs={{2,4},{3,5},{4,2},{5,3},{10,12},{11,13},{12,10},{13,11},{18,20},{1... | collective-permute-start | bytes 3145736 | tf_op jit(solution)/shard_map/ppermute | solution.py:337
  159.0 0.7 fusion.2
  159.7 2.2 collective-permute-start.4
  162.0 1.3 collective-permute-start.3
  163.3 0.6 convolution_reduce_fusion
  163.9 0.1 broadcast_in_dim.45
  164.1 1.3 collective-permute-start.8
  165.4 0.1 select_reduce_fusion
  165.6 2.0 collective-permute-start.10
  167.6 0.8 collective-permute-done.10
  168.4 1.2 collective-permute-start.7
  169.6 18.4 %collective-permute-done.6 = bf16[1024,512]{1,0:T(8,128)(2,1)S(1)} collective-permute-done((bf16[1024,512]{1,0:T(8,128)(2,1)S(1)}, bf16[1024,512]{1,0:T(8,128)(2,1)S(1)}, u32[]{:S(2)}, u32[]{:S(2)}) %collective-permute-start.6) | collective-permute-done | bytes 1048608 | tf_op jit(solution)/shard_map/ppermute | solution.py:337
  188.0 2.8 collective-permute-start.2
  190.8 18.7 %collective-permute-done.4 = bf16[512,768]{1,0:T(8,128)(2,1)} collective-permute-done((bf16[512,768]{1,0:T(8,128)(2,1)}, bf16[512,768]{1,0:T(8,128)(2,1)}, u32[]{:S(2)}, u32[]{:S(2)}) %collective-permute-start.4) | collective-permute-done | bytes 786464 | tf_op jit(solution)/shard_map/ppermute | solution.py:382
  209.4 4.3 %collective-permute-start.5 = (bf16[512,768]{1,0:T(8,128)(2,1)}, bf16[512,768]{1,0:T(8,128)(2,1)S(1)}, u32[]{:S(2)}, u32[]{:S(2)}) collective-permute-start(bf16[512,768]{1,0:T(8,128)(2,1)} %collective-permute-done.4), channel_id=1, source_target_pairs={{2,26},{3,27},{4,28},{5,29},{10,2},{11,3},{12,4},{13,5},{18,10},{1... | collective-permute-start | bytes 2359304 | tf_op jit(solution)/shard_map/ppermute | solution.py:386
  213.8 0.1 broadcast_select_fusion.cb_ref
  213.9 2.5 collective-permute-start.9
  216.4 2.2 broadcast_select_fusion.3
  218.6 1.0 broadcast_select_fusion.1
  219.7 3.4 %collective-permute-done.5 = bf16[512,768]{1,0:T(8,128)(2,1)S(1)} collective-permute-done((bf16[512,768]{1,0:T(8,128)(2,1)}, bf16[512,768]{1,0:T(8,128)(2,1)S(1)}, u32[]{:S(2)}, u32[]{:S(2)}) %collective-permute-start.5) | collective-permute-done | bytes 786464 | tf_op jit(solution)/shard_map/ppermute | solution.py:386
  223.0 1.3 bitcast_select_fusion.2
  224.4 7.0 %collective-permute-done.9 = bf16[768,512]{1,0:T(8,128)(2,1)S(1)} collective-permute-done((bf16[768,512]{1,0:T(8,128)(2,1)S(1)}, bf16[768,512]{1,0:T(8,128)(2,1)S(1)}, u32[]{:S(2)}, u32[]{:S(2)}) %collective-permute-start.9) | collective-permute-done | bytes 786464 | tf_op jit(solution)/shard_map/ppermute | solution.py:384
  231.4 1.1 bitcast_select_fusion
  232.4 1.3 context_part.1
  233.7 1.4 copy-done.5
  235.0 0.8 copy-done.7
  235.9 0.4 collective-permute-start.11
  236.4 3.9 %collective-permute-start.13 = (f32[8,2]{0,1:T(2,128)S(1)}, f32[8,2]{0,1:T(2,128)S(1)}, u32[]{:S(2)}, u32[]{:S(2)}) collective-permute-start(f32[8,2]{0,1:T(2,128)S(1)} %get-tuple-element.82), channel_id=1, source_target_pairs={{0,16},{4,20},{8,24},{12,28},{16,0},{20,4},{24,8},{28,12},{32,48},... | collective-permute-start | bytes 200 | tf_op jit(solution)/shard_map/ppermute | solution.py:375
  240.3 1.6 copy-done.6
  241.9 1.0 copy-done.8
  242.9 6.8 %first_layer.1 = (bf16[1024,512]{1,0:T(8,128)(2,1)S(1)}, bf16[1024,512]{1,0:T(8,128)(2,1)S(1)}, f32[16,1024]{1,0:T(8,128)S(1)}) custom-call(bf16[16,512]{1,0:T(8,128)(2,1)S(1)} %broadcast_in_dim.43.u_ref, f32[1024,512]{1,0:T(8,128)S(1)} %copy-done.6, bf16[512,512]{1,0:T(8,128)(2,1)S(1)} %copy-done.8, bf16[2048,512]{1,0:T(8,128)(2,1)} %bitcast.10.recv_hbm), custom_call_target="tpu_custom_call" | custom-call | flops 15728640000 | bytes 8388608 | tf_op jit(solution)/shard_map/first_layer/pallas_call | solution.py:78
  249.8 0.1 collective-permute-start.14
  249.9 6.5 %collective-permute-start.17 = (f32[3,768]{1,0:T(4,128)S(1)}, f32[3,768]{1,0:T(4,128)S(1)}, u32[]{:S(2)}, u32[]{:S(2)}) collective-permute-start(f32[3,768]{1,0:T(4,128)S(1)} %pad_maximum_fusion), channel_id=1, source_target_pairs={{2,4},{3,5},{4,2},{5,3},{10,12},{11,13},{12,10},{13,11},{18,20},{1... | collective-permute-start | bytes 27656 | tf_op jit(solution)/shard_map/ppermute | solution.py:400
  256.5 0.1 collective-permute-start.16
  256.6 1.3 collective-permute-done.17
  257.9 3.4 %collective-permute-start.15 = (f32[4,2]{0,1:T(2,128)S(1)}, f32[4,2]{0,1:T(2,128)S(1)}, u32[]{:S(2)}, u32[]{:S(2)}) collective-permute-start(f32[4,2]{0,1:T(2,128)S(1)} %slice.61), channel_id=1, source_target_pairs={{0,192},{4,196},{8,200},{12,204},{16,208},{20,212},{24,216},{28,22... | collective-permute-start | bytes 104 | tf_op jit(solution)/shard_map/ppermute | solution.py:362
  261.3 1.1 collective-permute-done.15
  262.5 2.0 collective-permute-start.18
  264.6 3.7 %second_layer.1 = (bf16[1024,768]{1,0:T(8,128)(2,1)S(1)}, bf16[1024,768]{1,0:T(8,128)(2,1)S(1)}, bf16[1024,512]{1,0:T(8,128)(2,1)S(1)}) custom-call(bf16[1024,512]{1,0:T(8,128)(2,1)S(1)} %get-tuple-element.53.mine_ref, bf16[1024,512]{1,0:T(8,128)(2,1)S(1)} %collective-permute-done.14.other_ref, bf16[1024,512]{1,0:T(8,128)(2,1)S(1)} %get-tuple-element.56.pay_ref, ...), custom_call_target="tpu_custom_call" | custom-call | flops 15728640000 | bytes 12582912 | tf_op jit(solution)/shard_map/second_layer/pallas_call | solution.py:78
  268.3 0.1 collective-permute-start.19
  269.1 1.2 collective-permute-start.20
  270.4 1.2 collective-permute-done.20
  271.6 4.7 %collective-permute-start.23 = (f32[1,2]{0,1:T(2,128)S(1)}, f32[1,2]{0,1:T(2,128)S(1)}, u32[]{:S(2)}, u32[]{:S(2)}) collective-permute-start(f32[1,2]{0,1:T(2,128)S(1)} %slice_maximum_fusion), channel_id=1, source_target_pairs={{0,2},{1,3},{2,0},{3,1},{4,6},{5,7},{6,4},{7,5},{8,10},{9,11},{10,... | collective-permute-start | bytes 32 | tf_op jit(solution)/shard_map/ppermute | solution.py:367
  276.3 3.1 %last_layer.1 = f32[16,1024]{1,0:T(8,128)S(1)} custom-call(f32[1]{0:T(128)} %copy.14.coefficient, bf16[1024,512]{1,0:T(8,128)(2,1)S(1)} %get-tuple-element.62.mine_ref, bf16[1024,512]{1,0:T(8,128)(2,1)S(1)} %collective-permute-done.19.other_ref, bf16[1024,512]{1,0:T(8,128)(2,1)S(1)} %get-tuple-element.56.pay_ref, ...), custom_call_target="tpu_custom_call" | custom-call | flops 1879048192 | bytes 10485760 | tf_op jit(solution)/shard_map/last_layer/pallas_call | solution.py:78
  279.4 0.5 collective-permute-done.22
  279.9 0.5 fusion.4
  281.1 2.7 collective-permute-start.24
  283.8 0.8 collective-permute-done.24
  284.6 5.0 %collective-permute-start.26 = (f32[1,1024]{1,0:T(1,128)S(1)}, f32[1,1024]{1,0:T(1,128)S(1)}, u32[]{:S(2)}, u32[]{:S(2)}) collective-permute-start(f32[1,1024]{1,0:T(1,128)S(1)} %fusion.7), channel_id=1, source_target_pairs={{2,4},{3,5},{4,2},{5,3},{10,12},{11,13},{12,10},{13,11},{18,20},{1... | collective-permute-start | bytes 12296 | tf_op jit(solution)/shard_map/ppermute | solution.py:446
  289.6 0.1 collective-permute-start.25
  289.7 1.3 collective-permute-done.26
  291.1 2.9 collective-permute-done.25
  293.9 0.6 maximum_select_fusion
  (77 shorter events, 0.8 us)
Async XLA Ops:
  0.6 117.2 %copy-start.18 = (bf16[2,256]{1,0:T(2,128)(2,1)S(1)}, bf16[2,256]{1,0:T(2,128)(2,1)}, u32[]{:S(2)}) copy-start(bf16[2,256]{1,0:T(2,128)(2,1)} %param.12) | copy-start | bytes 3076
  113.7 26.6 %collective-permute-start = (bf16[768,512]{1,0:T(8,128)(2,1)}, bf16[768,512]{1,0:T(8,128)(2,1)S(1)}, u32[]{:S(2)}, u32[]{:S(2)}) collective-permute-start(bf16[768,512]{1,0:T(8,128)(2,1)} %get-tuple-element.39), channel_id=1, source_target_pairs={{0,1},{1,0},{2,5},{3,4},{4,3},{5,2},{6,7},{7,6},{8,9},{9,8},{10,13... | collective-permute-start | bytes 2359304 | tf_op jit(solution)/shard_map/ppermute | solution.py:334
  117.7 22.6 %collective-permute-start.1 = (bf16[512,768]{1,0:T(8,128)(2,1)}, bf16[512,768]{1,0:T(8,128)(2,1)S(1)}, u32[]{:S(2)}, u32[]{:S(2)}) collective-permute-start(bf16[512,768]{1,0:T(8,128)(2,1)} %get-tuple-element.40), channel_id=1, source_target_pairs={{0,1},{1,0},{2,5},{3,4},{4,3},{5,2},{6,7},{7,6},{8,9},{9,8},{10,13... | collective-permute-start | bytes 2359304 | tf_op jit(solution)/shard_map/ppermute | solution.py:335
  118.4 21.9 %all-to-all-start = ((bf16[64,2,256]{2,1,0:T(2,128)(2,1)}), bf16[64,2,256]{2,1,0:T(2,128)(2,1)S(1)}, u32[]{:S(2)}, u32[]{:S(2)}) async-start(bf16[64,2,256]{2,1,0:T(2,128)(2,1)} %broadcast_in_dim.41), calls=%async_computation | async-start | bytes 131072 | tf_op jit(solution)/shard_map/all_to_all | solution.py:339
  140.3 0.9 copy-start.13
  141.2 1.0 copy-start.15
  142.1 11.8 %copy-start.12 = (bf16[1024,512]{1,0:T(8,128)(2,1)S(1)}, bf16[1024,512]{1,0:T(8,128)(2,1)}, u32[]{:S(2)}) copy-start(bf16[1024,512]{1,0:T(8,128)(2,1)} %get-tuple-element.45) | copy-start | bytes 3145732
  142.2 21.2 %copy-start.11 = (bf16[2048,256]{1,0:T(8,128)(2,1)S(1)}, bf16[2048,256]{1,0:T(8,128)(2,1)}, u32[]{:S(2)}) copy-start(bf16[2048,256]{1,0:T(8,128)(2,1)} %emb_hbm.1) | copy-start | bytes 3145732
  142.2 93.7 %all-to-all-start.1 = ((bf16[256,8,512]{2,1,0:T(8,128)(2,1)}), bf16[256,8,512]{2,1,0:T(8,128)(2,1)}, u32[]{:S(2)}, u32[]{:S(2)}) async-start(bf16[256,8,512]{2,1,0:T(8,128)(2,1)} %bitcast.26), calls=%async_computation.1 | async-start | bytes 4194304 | tf_op jit(solution)/shard_map/all_to_all | solution.py:346
  154.0 34.0 %collective-permute-start.6 = (bf16[1024,512]{1,0:T(8,128)(2,1)S(1)}, bf16[1024,512]{1,0:T(8,128)(2,1)S(1)}, u32[]{:S(2)}, u32[]{:S(2)}) collective-permute-start(bf16[1024,512]{1,0:T(8,128)(2,1)S(1)} %copy-done.12), channel_id=1, source_target_pairs={{2,4},{3,5},{4,2},{5,3},{10,12},{11,13},{12,10},{13,11},{18,20},{1... | collective-permute-start | bytes 3145736 | tf_op jit(solution)/shard_map/ppermute | solution.py:337
  159.7 49.7 %collective-permute-start.4 = (bf16[512,768]{1,0:T(8,128)(2,1)}, bf16[512,768]{1,0:T(8,128)(2,1)}, u32[]{:S(2)}, u32[]{:S(2)}) collective-permute-start(bf16[512,768]{1,0:T(8,128)(2,1)} %copy-done.15), channel_id=1, source_target_pairs={{2,3},{3,2},{4,5},{5,4},{10,11},{11,10},{12,13},{13,12},{18,19},{1... | collective-permute-start | bytes 2359304 | tf_op jit(solution)/shard_map/ppermute | solution.py:382
  162.0 54.4 %collective-permute-start.3 = (bf16[512,768]{1,0:T(8,128)(2,1)}, bf16[512,768]{1,0:T(8,128)(2,1)}, u32[]{:S(2)}, u32[]{:S(2)}) collective-permute-start(bf16[512,768]{1,0:T(8,128)(2,1)} %copy-done.15), channel_id=1, source_target_pairs={{0,24},{1,25},{2,10},{3,11},{4,12},{5,13},{6,30},{7,31},{8,0},{9,1... | collective-permute-start | bytes 2359304 | tf_op jit(solution)/shard_map/ppermute | solution.py:385
  164.1 49.8 %collective-permute-start.8 = (bf16[768,512]{1,0:T(8,128)(2,1)}, bf16[768,512]{1,0:T(8,128)(2,1)S(1)}, u32[]{:S(2)}, u32[]{:S(2)}) collective-permute-start(bf16[768,512]{1,0:T(8,128)(2,1)} %copy-done.13), channel_id=1, source_target_pairs={{0,3},{1,2},{6,5},{7,4},{8,11},{9,10},{14,13},{15,12},{16,19},{17,... | collective-permute-start | bytes 2359304 | tf_op jit(solution)/shard_map/ppermute | solution.py:381
  165.6 2.8 collective-permute-start.10
  168.4 50.2 %collective-permute-start.7 = (bf16[768,512]{1,0:T(8,128)(2,1)}, bf16[768,512]{1,0:T(8,128)(2,1)S(1)}, u32[]{:S(2)}, u32[]{:S(2)}) collective-permute-start(bf16[768,512]{1,0:T(8,128)(2,1)} %copy-done.13), channel_id=1, source_target_pairs={{0,8},{1,9},{2,10},{3,11},{4,12},{5,13},{6,14},{7,15},{8,16},{9,17... | collective-permute-start | bytes 2359304 | tf_op jit(solution)/shard_map/ppermute | solution.py:383
  188.0 28.4 %copy-start.16 = (bf16[512,768]{1,0:T(8,128)(2,1)S(1)}, bf16[512,768]{1,0:T(8,128)(2,1)}, u32[]{:S(2)}) copy-start(bf16[512,768]{1,0:T(8,128)(2,1)} %copy-done.15) | copy-start | bytes 2359300
  188.0 36.4 %collective-permute-start.2 = (bf16[1024,512]{1,0:T(8,128)(2,1)}, bf16[1024,512]{1,0:T(8,128)(2,1)S(1)}, u32[]{:S(2)}, u32[]{:S(2)}) collective-permute-start(bf16[1024,512]{1,0:T(8,128)(2,1)} %get-tuple-element.42), channel_id=1, source_target_pairs={{0,1},{1,0},{2,5},{3,4},{4,3},{5,2},{6,7},{7,6},{8,9},{9,8},{10,13... | collective-permute-start | bytes 3145736 | tf_op jit(solution)/shard_map/ppermute | solution.py:336
  209.4 13.6 %collective-permute-start.5 = (bf16[512,768]{1,0:T(8,128)(2,1)}, bf16[512,768]{1,0:T(8,128)(2,1)S(1)}, u32[]{:S(2)}, u32[]{:S(2)}) collective-permute-start(bf16[512,768]{1,0:T(8,128)(2,1)} %collective-permute-done.4), channel_id=1, source_target_pairs={{2,26},{3,27},{4,28},{5,29},{10,2},{11,3},{12,4},{13,5},{18,10},{1... | collective-permute-start | bytes 2359304 | tf_op jit(solution)/shard_map/ppermute | solution.py:386
  213.9 4.7 %copy-start.14 = (bf16[768,512]{1,0:T(8,128)(2,1)S(1)}, bf16[768,512]{1,0:T(8,128)(2,1)}, u32[]{:S(2)}) copy-start(bf16[768,512]{1,0:T(8,128)(2,1)} %copy-done.13) | copy-start | bytes 2359300
  213.9 17.4 %collective-permute-start.9 = (bf16[768,512]{1,0:T(8,128)(2,1)S(1)}, bf16[768,512]{1,0:T(8,128)(2,1)S(1)}, u32[]{:S(2)}, u32[]{:S(2)}) collective-permute-start(bf16[768,512]{1,0:T(8,128)(2,1)S(1)} %collective-permute-done.8), channel_id=1, source_target_pairs={{2,26},{3,27},{4,28},{5,29},{10,2},{11,3},{12,4},{13,5},{18,10},{1... | collective-permute-start | bytes 2359304 | tf_op jit(solution)/shard_map/ppermute | solution.py:384
  218.6 4.4 %copy-start.9 = (bf16[2,512,768]{2,1,0:T(8,128)(2,1)S(1)}, bf16[2,512,768]{2,1,0:T(8,128)(2,1)}, u32[]{:S(2)}) copy-start(bf16[2,512,768]{2,1,0:T(8,128)(2,1)} %u_ref.1) | copy-start | bytes 4718596
  219.7 11.7 %copy-start.10 = (bf16[2,768,512]{2,1,0:T(8,128)(2,1)S(1)}, bf16[2,768,512]{2,1,0:T(8,128)(2,1)}, u32[]{:S(2)}) copy-start(bf16[2,768,512]{2,1,0:T(8,128)(2,1)} %v_ref.1) | copy-start | bytes 4718596
  224.4 8.0 %copy-start = (bf16[1024,512]{1,0:T(8,128)(2,1)}, bf16[1024,512]{1,0:T(8,128)(2,1)S(1)}, u32[]{:S(2)}) copy-start(bf16[1024,512]{1,0:T(8,128)(2,1)S(1)} %collective-permute-done.2.ca_ref) | copy-start | bytes 3145732
  233.7 1.4 copy-start.5
  235.0 0.8 copy-start.7
  235.9 13.8 %collective-permute-start.11 = (f32[8,2]{0,1:T(2,128)S(1)}, f32[8,2]{0,1:T(2,128)S(1)}, u32[]{:S(2)}, u32[]{:S(2)}) collective-permute-start(f32[8,2]{0,1:T(2,128)S(1)} %get-tuple-element.81), channel_id=1, source_target_pairs={{0,8},{4,12},{8,0},{12,4},{16,24},{20,28},{24,16},{28,20},{32,40},... | collective-permute-start | bytes 200 | tf_op jit(solution)/shard_map/ppermute | solution.py:375
  236.4 13.4 %collective-permute-start.13 = (f32[8,2]{0,1:T(2,128)S(1)}, f32[8,2]{0,1:T(2,128)S(1)}, u32[]{:S(2)}, u32[]{:S(2)}) collective-permute-start(f32[8,2]{0,1:T(2,128)S(1)} %get-tuple-element.82), channel_id=1, source_target_pairs={{0,16},{4,20},{8,24},{12,28},{16,0},{20,4},{24,8},{28,12},{32,48},... | collective-permute-start | bytes 200 | tf_op jit(solution)/shard_map/ppermute | solution.py:375
  240.3 9.5 %collective-permute-start.12 = (f32[8,2]{0,1:T(2,128)S(1)}, f32[8,2]{0,1:T(2,128)S(1)}, u32[]{:S(2)}, u32[]{:S(2)}) collective-permute-start(f32[8,2]{0,1:T(2,128)S(1)} %get-tuple-element.83), channel_id=1, source_target_pairs={{0,24},{4,28},{8,16},{12,20},{16,8},{20,12},{24,0},{28,4},{32,56},... | collective-permute-start | bytes 200 | tf_op jit(solution)/shard_map/ppermute | solution.py:375
  240.3 1.6 copy-start.6
  241.9 1.0 copy-start.8
  242.9 7.0 %copy-start.19 = (bf16[768]{0:T(1024)(128)(2,1)S(1)}, bf16[768]{0:T(1024)(128)(2,1)}, u32[]{:S(2)}) copy-start(bf16[768]{0:T(1024)(128)(2,1)} %param.21) | copy-start | bytes 4612
  242.9 7.0 %copy-start.17 = (f32[2,768]{1,0:T(2,128)S(1)}, f32[2,768]{1,0:T(2,128)}, u32[]{:S(2)}) copy-start(f32[2,768]{1,0:T(2,128)} %param.20) | copy-start | bytes 18436
  242.9 21.6 %copy-start.1 = (bf16[1024,512]{1,0:T(8,128)(2,1)S(1)}, bf16[1024,512]{1,0:T(8,128)(2,1)}, u32[]{:S(2)}) copy-start(bf16[1024,512]{1,0:T(8,128)(2,1)} %copy-done) | copy-start | bytes 3145732
  242.9 21.6 %copy-start.2 = (bf16[768,512]{1,0:T(8,128)(2,1)S(1)}, bf16[768,512]{1,0:T(8,128)(2,1)}, u32[]{:S(2)}) copy-start(bf16[768,512]{1,0:T(8,128)(2,1)} %get-tuple-element.73.vb_ref) | copy-start | bytes 2359300
  242.9 21.6 %copy-start.3 = (bf16[512,768]{1,0:T(8,128)(2,1)S(1)}, bf16[512,768]{1,0:T(8,128)(2,1)}, u32[]{:S(2)}) copy-start(bf16[512,768]{1,0:T(8,128)(2,1)} %get-tuple-element.58.ua_ref) | copy-start | bytes 2359300
  242.9 21.6 %copy-start.4 = (bf16[768,512]{1,0:T(8,128)(2,1)S(1)}, bf16[768,512]{1,0:T(8,128)(2,1)}, u32[]{:S(2)}) copy-start(bf16[768,512]{1,0:T(8,128)(2,1)} %get-tuple-element.77.va_ref) | copy-start | bytes 2359300
  249.8 12.7 %collective-permute-start.14 = (bf16[1024,512]{1,0:T(8,128)(2,1)S(1)}, bf16[1024,512]{1,0:T(8,128)(2,1)S(1)}, u32[]{:S(2)}, u32[]{:S(2)}) collective-permute-start(bf16[1024,512]{1,0:T(8,128)(2,1)S(1)} %get-tuple-element.53.mine_ref), channel_id=1, source_target_pairs={{0,4},{1,5},{2,6},{3,7},{4,0},{5,1},{6,2},{7,3},{8,12},{9,13},{10,... | collective-permute-start | bytes 3145736 | tf_op jit(solution)/shard_map/ppermute | solution.py:427
  249.9 7.9 %collective-permute-start.17 = (f32[3,768]{1,0:T(4,128)S(1)}, f32[3,768]{1,0:T(4,128)S(1)}, u32[]{:S(2)}, u32[]{:S(2)}) collective-permute-start(f32[3,768]{1,0:T(4,128)S(1)} %pad_maximum_fusion), channel_id=1, source_target_pairs={{2,4},{3,5},{4,2},{5,3},{10,12},{11,13},{12,10},{13,11},{18,20},{1... | collective-permute-start | bytes 27656 | tf_op jit(solution)/shard_map/ppermute | solution.py:400
  256.5 8.1 %collective-permute-start.16 = (f32[3,768]{1,0:T(4,128)S(1)}, f32[3,768]{1,0:T(4,128)S(1)}, u32[]{:S(2)}, u32[]{:S(2)}) collective-permute-start(f32[3,768]{1,0:T(4,128)S(1)} %pad_maximum_fusion), channel_id=1, source_target_pairs={{0,1},{1,0},{2,5},{3,4},{4,3},{5,2},{6,7},{7,6},{8,9},{9,8},{10,13... | collective-permute-start | bytes 27656 | tf_op jit(solution)/shard_map/ppermute | solution.py:399
  257.9 4.6 %collective-permute-start.15 = (f32[4,2]{0,1:T(2,128)S(1)}, f32[4,2]{0,1:T(2,128)S(1)}, u32[]{:S(2)}, u32[]{:S(2)}) collective-permute-start(f32[4,2]{0,1:T(2,128)S(1)} %slice.61), channel_id=1, source_target_pairs={{0,192},{4,196},{8,200},{12,204},{16,208},{20,212},{24,216},{28,22... | collective-permute-start | bytes 104 | tf_op jit(solution)/shard_map/ppermute | solution.py:362
  262.5 5.8 %collective-permute-start.18 = (f32[2,2]{0,1:T(2,128)S(1)}, f32[2,2]{0,1:T(2,128)S(1)}, u32[]{:S(2)}, u32[]{:S(2)}) collective-permute-start(f32[2,2]{0,1:T(2,128)S(1)} %slice.64), channel_id=1, source_target_pairs={{0,64},{4,68},{8,72},{12,76},{16,80},{20,84},{24,88},{28,92},{32,9... | collective-permute-start | bytes 56 | tf_op jit(solution)/shard_map/ppermute | solution.py:362
  268.3 3.3 %collective-permute-start.19 = (bf16[1024,512]{1,0:T(8,128)(2,1)S(1)}, bf16[1024,512]{1,0:T(8,128)(2,1)S(1)}, u32[]{:S(2)}, u32[]{:S(2)}) collective-permute-start(bf16[1024,512]{1,0:T(8,128)(2,1)S(1)} %get-tuple-element.62.mine_ref), channel_id=1, source_target_pairs={{0,4},{1,5},{2,6},{3,7},{4,0},{5,1},{6,2},{7,3},{8,12},{9,13},{10,... | collective-permute-start | bytes 3145736 | tf_op jit(solution)/shard_map/ppermute | solution.py:435
  269.1 2.4 collective-permute-start.20
  271.6 7.8 %collective-permute-start.23 = (f32[1,2]{0,1:T(2,128)S(1)}, f32[1,2]{0,1:T(2,128)S(1)}, u32[]{:S(2)}, u32[]{:S(2)}) collective-permute-start(f32[1,2]{0,1:T(2,128)S(1)} %slice_maximum_fusion), channel_id=1, source_target_pairs={{0,2},{1,3},{2,0},{3,1},{4,6},{5,7},{6,4},{7,5},{8,10},{9,11},{10,... | collective-permute-start | bytes 32 | tf_op jit(solution)/shard_map/ppermute | solution.py:367
  276.3 3.6 %collective-permute-start.22 = (f32[1,2]{0,1:T(2,128)S(1)}, f32[1,2]{0,1:T(2,128)S(1)}, u32[]{:S(2)}, u32[]{:S(2)}) collective-permute-start(f32[1,2]{0,1:T(2,128)S(1)} %slice_maximum_fusion), channel_id=1, source_target_pairs={{0,3},{1,2},{2,1},{3,0},{4,7},{5,6},{6,5},{7,4},{8,11},{9,10},{10,... | collective-permute-start | bytes 32 | tf_op jit(solution)/shard_map/ppermute | solution.py:367
  276.3 3.6 %collective-permute-start.21 = (f32[1,2]{0,1:T(2,128)S(1)}, f32[1,2]{0,1:T(2,128)S(1)}, u32[]{:S(2)}, u32[]{:S(2)}) collective-permute-start(f32[1,2]{0,1:T(2,128)S(1)} %slice_maximum_fusion), channel_id=1, source_target_pairs={{0,1},{1,0},{2,3},{3,2},{4,5},{5,4},{6,7},{7,6},{8,9},{9,8},{10,11... | collective-permute-start | bytes 32 | tf_op jit(solution)/shard_map/ppermute | solution.py:367
  281.1 3.5 %collective-permute-start.24 = (f32[1,1024]{1,0:T(1,128)S(1)}, f32[1,1024]{1,0:T(1,128)S(1)}, u32[]{:S(2)}, u32[]{:S(2)}) collective-permute-start(f32[1,1024]{1,0:T(1,128)S(1)} %slice_subtract_fusion), channel_id=1, source_target_pairs={{0,4},{1,5},{2,6},{3,7},{4,0},{5,1},{6,2},{7,3},{8,12},{9,13},{10,... | collective-permute-start | bytes 12296 | tf_op jit(solution)/shard_map/ppermute | solution.py:444
  284.6 6.4 %collective-permute-start.26 = (f32[1,1024]{1,0:T(1,128)S(1)}, f32[1,1024]{1,0:T(1,128)S(1)}, u32[]{:S(2)}, u32[]{:S(2)}) collective-permute-start(f32[1,1024]{1,0:T(1,128)S(1)} %fusion.7), channel_id=1, source_target_pairs={{2,4},{3,5},{4,2},{5,3},{10,12},{11,13},{12,10},{13,11},{18,20},{1... | collective-permute-start | bytes 12296 | tf_op jit(solution)/shard_map/ppermute | solution.py:446
  289.6 4.3 %collective-permute-start.25 = (f32[1,1024]{1,0:T(1,128)S(1)}, f32[1,1024]{1,0:T(1,128)S(1)}, u32[]{:S(2)}, u32[]{:S(2)}) collective-permute-start(f32[1,1024]{1,0:T(1,128)S(1)} %fusion.7), channel_id=1, source_target_pairs={{0,1},{1,0},{2,5},{3,4},{4,3},{5,2},{6,7},{7,6},{8,9},{9,8},{10,13... | collective-permute-start | bytes 12296 | tf_op jit(solution)/shard_map/ppermute | solution.py:445

commit v7 on v6

--- a/solution.py
+++ b/solution.py
@@ -87,34 +87,6 @@
         ),
         name=name,
     )(*scalars, *arrays, *far)
-
-
-def cut_kernel(where, v_ref, u_ref, ctx_ref, v_out, u_out, own_out, away_out, sems):
-    layer, parity = where[0], where[1]
-    copies = [
-        pltpu.make_async_copy(v_ref.at[layer], v_out, sems.at[0]),
-        pltpu.make_async_copy(u_ref.at[layer], u_out, sems.at[1]),
-        pltpu.make_async_copy(ctx_ref.at[1 - parity], away_out, sems.at[2]),
-        pltpu.make_async_copy(ctx_ref.at[parity], own_out, sems.at[3]),
-    ]
-    for copy in copies:
-        copy.start()
-    for copy in copies:
-        copy.wait()
-
-
-def cut_blocks(where, v, u, ctx):
-    shapes = [v.shape[1:], u.shape[1:], ctx.shape[1:], ctx.shape[1:]]
-    return pl.pallas_call(
-        cut_kernel,
-        in_specs=[SMEM, ANY, ANY, ANY],
-        out_specs=[ANY] * 4,
-        out_shape=[jax.ShapeDtypeStruct(shape, BF) for shape in shapes],
-        scratch_shapes=[pltpu.SemaphoreType.DMA((4,))],
-        compiler_params=grant(63000),
-        cost_estimate=pl.CostEstimate(flops=0, bytes_accessed=7 << 20, transcendentals=0),
-        name="cut_blocks",
-    )(where, v, u, ctx)
 
 
 def pick_kernel(
@@ -328,13 +300,10 @@
     persons, _, kept = kept_part_entries.shape
     hops = partners(shards)
     me = lax.axis_index("shard")
-    v_mine, u_mine, ctx_own, ctx_away = cut_blocks(
-        jnp.stack([odd_y, parity]), lowrank_v_matrix, lowrank_u_matrix, pair_attributes
-    )
-    v_near = move(v_mine, perm=to_near)
-    u_near = move(u_mine, perm=to_near)
-    ctx_a = move(ctx_away, perm=ctx_near)
-    ctx_b = move(ctx_own, perm=ctx_far)
+    v_near = move(lax.dynamic_index_in_dim(lowrank_v_matrix, odd_y, 0, False), perm=to_near)
+    u_near = move(lax.dynamic_index_in_dim(lowrank_u_matrix, odd_y, 0, False), perm=to_near)
+    ctx_own = lax.dynamic_index_in_dim(pair_attributes, parity, 0, False)
+    ctx_away = lax.dynamic_index_in_dim(pair_attributes, 1 - parity, 0, False)
     users = jnp.broadcast_to(person_embedding[None], (shards, *person_embedding.shape))
     users = lax.all_to_all(users, "shard", split_axis=0, concat_axis=0, tiled=True)
 
@@ -345,6 +314,19 @@
     parcel, v_near, u_near, users = lax.optimization_barrier((parcel, v_near, u_near, users))
     recv = lax.all_to_all(parcel, AXES, split_axis=0, concat_axis=0, tiled=True)
     recv = recv.reshape(persons * 2 * kept, 512)
+
+    v_far = move(v_near, perm=home_on)
+    u_far = move(u_near, perm=away_swap)
+    v_near_y = move(v_near, perm=y_up)
+    v_far, u_near_on, ctx_out, ctx_away = lax.optimization_barrier(
+        (v_far, u_near, ctx_own, ctx_away)
+    )
+    ctx_a = move(ctx_away, perm=ctx_near)
+    ctx_b = move(ctx_out, perm=ctx_far)
+    ctx_a, ctx_b = lax.optimization_barrier((ctx_a, ctx_b))
+    v_far_y = move(v_far, perm=y_down)
+    u_near_y = move(u_near_on, perm=y_mixed)
+    u_far_y = move(u_far, perm=y_down)
 
     all_scores = jnp.einsum(
         "ue,ie->ui", users.reshape(persons, -1), catalog_embedding, preferred_element_type=F32
@@ -378,12 +360,6 @@
 
     best = halve(best, hops[5])
 
-    v_far = move(v_near, perm=home_on)
-    u_far = move(u_near, perm=away_swap)
-    v_near_y = move(v_near, perm=y_up)
-    v_far_y = move(v_far, perm=y_down)
-    u_near_y = move(u_near, perm=y_mixed)
-    u_far_y = move(u_far, perm=y_down)
     even = odd_y == 0
     v0_a = jnp.where(even, v_near, v_near_y)
     v1_a = jnp.where(even, v_near_y, v_near)

time: 295 us -> 164 us (0.56)
  Pallas kernels: 136 us -> 22.9 us
  waiting for transfers between devices: 59.4 us -> 34.3 us
    pallas_call x1 -> x0, Pallas kernels: 113 us -> none  [cut_blocks(): pl.pallas_call(cut_kernel, in_specs=[SMEM, ANY, ANY, ANY], out_specs=[ANY...]
    ppermute x1, waiting for transfers between devices: 18.7 us -> 0.01 us  [on_device(): u_far = move(u_near, perm=away_swap)]
    ppermute x4, waiting for transfers between devices: 18.4 us -> 4.2 us  [the longest x1 4.19 us: on_device(): u_near_y = move(u_near_on, perm=y_mixed)]
    ppermute x1, waiting for transfers between devices: 0.01 us -> 11.2 us  [on_device(): v_far = move(v_near, perm=home_on)]
    ppermute x1, waiting for transfers between devices: 6.97 us -> 0.01 us  [on_device(): v_far_y = move(v_far, perm=y_down)]
    ppermute x4, starting transfers between devices: 10.4 us -> 16.4 us  [the longest x1 11.1 us: on_device(): ctx_b = move(ctx_out, perm=ctx_far)]
    ppermute x1, starting transfers between devices: 6.5 us -> 2.81 us  [on_device(): small_b = jnp.where(home, small, move(small, perm=ctx_far))]
    ppermute x1, waiting for transfers between devices: 3.36 us -> 6.59 us  [on_device(): u_far_y = move(u_far, perm=y_down)]
  transfers between devices with their start and end apart: 29 -> 29, of which waited for: 13 -> 10; matrix products, arithmetic and copies ran while one was open for 3% -> 9% of each run, Pallas kernels for 8% -> 14%
where the time goes in v7:
time: 164 us; the launch traced here: 163 us
  starting transfers between devices  81.7 us (50%)
  waiting for transfers between devices  34.3 us (21%)
  Pallas kernels  22.9 us (14%)
  local copies, waits for them, and re-layouts  10.2 us (6%)
  other arithmetic  9.79 us (6%)
  matrix products  2.14 us (1%)
  between operations  1.7 us (1%)
    pallas_call x4, Pallas kernels, call(): pl.pallas_call(kernel, in_specs=[SMEM] * len(scalars) + [VMEM] * len(arra...  15 us
    all_to_all x1, starting transfers between devices, on_device(): lax.all_to_all(users, 'shard', split_axis=0, concat_axis=0, tiled=True)  11.8 us
    all_to_all x1, starting transfers between devices, on_device(): recv = lax.all_to_all(parcel, AXES, split_axis=0, concat_axis=0, tiled=True)  11.7 us
    ppermute x1, waiting for transfers between devices, on_device(): v_far = move(v_near, perm=home_on)  11.2 us
    ppermute x1, starting transfers between devices, on_device(): ctx_b = move(ctx_out, perm=ctx_far)  11.1 us
    pallas_call x1, Pallas kernels, pick_rows(): pl.pallas_call(pick_kernel, in_specs=[VMEM, VMEM, ANY, ANY], out_specs=AN...  7.98 us
    ppermute x4, starting transfers between devices, halve(): return jnp.maximum(best[:half], lax.ppermute(best[half:], 'shard', pairs))  7.36 us
    ppermute x1, waiting for transfers between devices, on_device(): u_far_y = move(u_far, perm=y_down)  6.59 us
  transfers between devices with their start and end apart: 29, of which 10 were waited for; matrix products, arithmetic and copies ran while one was open for 9% of the time, Pallas kernels for 14%

profile of v7, /device:TPU:1, one launch (start us, length us, event | category | flops | bytes accessed | tf_op | source)
XLA Modules:
  0.0 162.8 jit_solution(5902087886711920180)
XLA Ops:
  0.0 1.3 dynamic-slice_bitcast_fusion.2
  1.3 4.0 %collective-permute-start.1 = (bf16[512,768]{1,0:T(8,128)(2,1)S(1)}, bf16[512,768]{1,0:T(8,128)(2,1)}, u32[]{:S(2)}, u32[]{:S(2)}) collective-permute-start(bf16[512,768]{1,0:T(8,128)(2,1)S(1)} %dynamic-slice_bitcast_fusion.2), channel_id=1, source_target_pairs={{0,1},{1,0},{2,5},{3,4},{4,3},{5,2},{6,7},{7,6},{8,9},{9,8},{10,13... | collective-permute-start | bytes 2359304 | tf_op jit(solution)/shard_map/ppermute | solution.py:304
  5.3 0.3 collective-permute-start
  5.7 0.7 broadcast_in_dim.41
  6.3 11.8 %all-to-all-start = ((bf16[64,2,256]{2,1,0:T(2,128)(2,1)}), bf16[64,2,256]{2,1,0:T(2,128)(2,1)S(1)}, u32[]{:S(2)}, u32[]{:S(2)}) async-start(bf16[64,2,256]{2,1,0:T(2,128)(2,1)} %broadcast_in_dim.41), calls=%async_computation | async-start | bytes 131072 | tf_op jit(solution)/shard_map/all_to_all | solution.py:308
  18.1 8.0 %pick_rows.1 = bf16[32,2,32,512]{3,2,1,0:T(8,128)(2,1)} custom-call(s32[8,128]{1,0:T(8,128)} %bitcast.33, s32[1,128]{1,0:T(1,128)} %bitcast.34, bf16[2048,256]{1,0:T(8,128)(2,1)} %emb_hbm.1, bf16[2048,768]{1,0:T(8,128)(2,1)} %attr_hbm.1), custom_call_target="tpu_custom_call" | custom-call | flops 4294967296 | bytes 6291456 | tf_op jit(solution)/shard_map/pick_rows/pallas_call | solution.py:144
  26.1 2.1 %all-to-all-done = bf16[64,2,256]{2,1,0:T(2,128)(2,1)S(1)} async-done(((bf16[64,2,256]{2,1,0:T(2,128)(2,1)}), bf16[64,2,256]{2,1,0:T(2,128)(2,1)S(1)}, u32[]{:S(2)}, u32[]{:S(2)}) %all-to-all-start) | async-done | bytes 65568 | tf_op jit(solution)/shard_map/all_to_all | solution.py:308
  28.2 11.7 %all-to-all-start.1 = ((bf16[256,8,512]{2,1,0:T(8,128)(2,1)}), bf16[256,8,512]{2,1,0:T(8,128)(2,1)}, u32[]{:S(2)}, u32[]{:S(2)}) async-start(bf16[256,8,512]{2,1,0:T(8,128)(2,1)} %bitcast.32), calls=%async_computation.1 | async-start | bytes 4194304 | tf_op jit(solution)/shard_map/all_to_all | solution.py:315
  39.9 1.3 collective-permute-start.2
  41.2 0.7 fusion.2
  41.9 0.1 iota_compare_fusion
  42.0 1.5 collective-permute-start.8
  43.5 3.1 %collective-permute-start.6 = (bf16[512,768]{1,0:T(8,128)(2,1)}, bf16[512,768]{1,0:T(8,128)(2,1)}, u32[]{:S(2)}, u32[]{:S(2)}) collective-permute-start(bf16[512,768]{1,0:T(8,128)(2,1)} %collective-permute-done.1), channel_id=1, source_target_pairs={{2,3},{3,2},{4,5},{5,4},{10,11},{11,10},{12,13},{13,12},{18,19},{1... | collective-permute-start | bytes 2359304 | tf_op jit(solution)/shard_map/ppermute | solution.py:319
  46.6 1.2 dynamic-slice_bitcast_fusion
  47.8 2.1 %convolution_reduce_fusion = f32[128]{0:T(128)S(1)} fusion(bf16[128,256]{1,0:T(8,128)(2,1)S(1)} %reshape.43, bf16[2048,256]{1,0:T(8,128)(2,1)} %emb_hbm.1), kind=kOutput, calls=%fused_computation | convolution fusion | flops 134479744 | bytes 1114624 | tf_op jit(solution)/shard_map/ue,ie->ui/dot_general | solution.py:331
  50.0 0.1 broadcast_in_dim.45
  50.2 11.2 %collective-permute-done.2 = bf16[768,512]{1,0:T(8,128)(2,1)} collective-permute-done((bf16[768,512]{1,0:T(8,128)(2,1)}, bf16[768,512]{1,0:T(8,128)(2,1)}, u32[]{:S(2)}, u32[]{:S(2)}) %collective-permute-start.2) | collective-permute-done | bytes 786464 | tf_op jit(solution)/shard_map/ppermute | solution.py:318
  61.4 1.0 collective-permute-start.5
  62.4 0.1 select_reduce_fusion
  62.5 0.1 slice.55
  62.6 2.0 %collective-permute-start.10 = (f32[32,2]{0,1:T(2,128)S(1)}, f32[32,2]{0,1:T(2,128)S(1)}, u32[]{:S(2)}, u32[]{:S(2)}) collective-permute-start(f32[32,2]{0,1:T(2,128)S(1)} %slice.55), channel_id=1, source_target_pairs={{0,4},{4,0},{8,12},{12,8},{16,20},{20,16},{24,28},{28,24},{32,36},... | collective-permute-start | bytes 776 | tf_op jit(solution)/shard_map/ppermute | solution.py:344
  64.6 1.9 %collective-permute-start.9 = (bf16[768,512]{1,0:T(8,128)(2,1)}, bf16[768,512]{1,0:T(8,128)(2,1)S(1)}, u32[]{:S(2)}, u32[]{:S(2)}) collective-permute-start(bf16[768,512]{1,0:T(8,128)(2,1)} %collective-permute-done.2), channel_id=1, source_target_pairs={{2,26},{3,27},{4,28},{5,29},{10,2},{11,3},{12,4},{13,5},{18,10},{1... | collective-permute-start | bytes 2359304 | tf_op jit(solution)/shard_map/ppermute | solution.py:327
  66.5 3.9 %collective-permute-start.3 = (bf16[1024,512]{1,0:T(8,128)(2,1)}, bf16[1024,512]{1,0:T(8,128)(2,1)S(1)}, u32[]{:S(2)}, u32[]{:S(2)}) collective-permute-start(bf16[1024,512]{1,0:T(8,128)(2,1)} %get-tuple-element.44), channel_id=1, source_target_pairs={{0,1},{1,0},{2,5},{3,4},{4,3},{5,2},{6,7},{7,6},{8,9},{9,8},{10,13... | collective-permute-start | bytes 3145736 | tf_op jit(solution)/shard_map/ppermute | solution.py:324
  70.5 11.1 %collective-permute-start.4 = (bf16[1024,512]{1,0:T(8,128)(2,1)S(1)}, bf16[1024,512]{1,0:T(8,128)(2,1)S(1)}, u32[]{:S(2)}, u32[]{:S(2)}) collective-permute-start(bf16[1024,512]{1,0:T(8,128)(2,1)S(1)} %get-tuple-element.45), channel_id=1, source_target_pairs={{2,4},{3,5},{4,2},{5,3},{10,12},{11,13},{12,10},{13,11},{18,20},{1... | collective-permute-start | bytes 3145736 | tf_op jit(solution)/shard_map/ppermute | solution.py:325
  81.6 2.6 %collective-permute-start.7 = (bf16[512,768]{1,0:T(8,128)(2,1)}, bf16[512,768]{1,0:T(8,128)(2,1)S(1)}, u32[]{:S(2)}, u32[]{:S(2)}) collective-permute-start(bf16[512,768]{1,0:T(8,128)(2,1)} %collective-permute-done.6), channel_id=1, source_target_pairs={{2,26},{3,27},{4,28},{5,29},{10,2},{11,3},{12,4},{13,5},{18,10},{1... | collective-permute-start | bytes 2359304 | tf_op jit(solution)/shard_map/ppermute | solution.py:329
  84.1 2.4 %broadcast_select_fusion.1 = (bf16[768,512]{1,0:T(8,128)(2,1)}, bf16[768,512]{1,0:T(8,128)(2,1)S(1)}) fusion(bf16[768,512]{1,0:T(8,128)(2,1)} %collective-permute-done.8, bf16[768,512]{1,0:T(8,128)(2,1)} %collective-permute-done, pred[]{:T(512)S(6)} %eq.39), kind=kLoop, calls=%fused_computation.10 | loop fusion | flops 786432 | bytes 3145729 | tf_op jit(solution)/shard_map/jit(_where)/select_n | solution.py:365
  86.5 4.2 %collective-permute-done.5 = bf16[512,768]{1,0:T(8,128)(2,1)S(1)} collective-permute-done((bf16[512,768]{1,0:T(8,128)(2,1)}, bf16[512,768]{1,0:T(8,128)(2,1)S(1)}, u32[]{:S(2)}, u32[]{:S(2)}) %collective-permute-start.5) | collective-permute-done | bytes 786464 | tf_op jit(solution)/shard_map/ppermute | solution.py:328
  90.7 2.1 %broadcast_select_fusion.3 = (bf16[512,768]{1,0:T(8,128)(2,1)S(1)}, bf16[512,768]{1,0:T(8,128)(2,1)}) fusion(bf16[512,768]{1,0:T(8,128)(2,1)S(1)} %collective-permute-done.5, bf16[512,768]{1,0:T(8,128)(2,1)} %collective-permute-done.1, pred[]{:T(512)S(6)} %eq.39), kind=kLoop, calls=%fused_computation.12 | loop fusion | flops 786432 | bytes 3145729 | tf_op jit(solution)/shard_map/jit(_where)/select_n | solution.py:367
  92.9 1.4 bitcast_select_fusion
  94.3 6.6 %collective-permute-done.7 = bf16[512,768]{1,0:T(8,128)(2,1)S(1)} collective-permute-done((bf16[512,768]{1,0:T(8,128)(2,1)}, bf16[512,768]{1,0:T(8,128)(2,1)S(1)}, u32[]{:S(2)}, u32[]{:S(2)}) %collective-permute-start.7) | collective-permute-done | bytes 786464 | tf_op jit(solution)/shard_map/ppermute | solution.py:329
  100.9 2.2 %bitcast_select_fusion.2 = (bf16[512,768]{1,0:T(8,128)(2,1)S(1)}, bf16[512,768]{1,0:T(8,128)(2,1)}) fusion(bf16[512,768]{1,0:T(8,128)(2,1)S(1)} %collective-permute-done.7, bf16[512,768]{1,0:T(8,128)(2,1)} %collective-permute-done.6, bf16[2,512,768]{2,1,0:T(8,128)(2,1)S(1)} %copy-done.13, pred[]{:T(512)} %eq.38, pred[]{:T(512)S(6)} %eq.39), kind=kLoop, calls=%fused_computation.6 | loop fusion | flops 1572864 | bytes 4718594 | tf_op jit(solution)/shard_map/jit(_where)/select_n | solution.py:371
  103.2 0.1 broadcast_select_fusion.cb_ref
  103.3 0.9 copy-done
  104.2 1.3 context_part.1
  105.5 1.3 copy-done.5
  106.8 0.8 copy-done.7
  107.7 0.9 collective-permute-start.11
  108.6 3.3 %collective-permute-start.13 = (f32[8,2]{0,1:T(2,128)S(1)}, f32[8,2]{0,1:T(2,128)S(1)}, u32[]{:S(2)}, u32[]{:S(2)}) collective-permute-start(f32[8,2]{0,1:T(2,128)S(1)} %get-tuple-element.88), channel_id=1, source_target_pairs={{0,16},{4,20},{8,24},{12,28},{16,0},{20,4},{24,8},{28,12},{32,48},... | collective-permute-start | bytes 200 | tf_op jit(solution)/shard_map/ppermute | solution.py:357
  111.9 1.6 copy-done.6
  113.5 1.0 copy-done.8
  114.6 6.8 %first_layer.1 = (bf16[1024,512]{1,0:T(8,128)(2,1)S(1)}, bf16[1024,512]{1,0:T(8,128)(2,1)S(1)}, f32[16,1024]{1,0:T(8,128)S(1)}) custom-call(bf16[16,512]{1,0:T(8,128)(2,1)S(1)} %broadcast_in_dim.43.u_ref, f32[1024,512]{1,0:T(8,128)S(1)} %copy-done.6, bf16[512,512]{1,0:T(8,128)(2,1)S(1)} %copy-done.8, bf16[2048,512]{1,0:T(8,128)(2,1)} %bitcast.12.recv_hbm), custom_call_target="tpu_custom_call" | custom-call | flops 15728640000 | bytes 8388608 | tf_op jit(solution)/shard_map/first_layer/pallas_call | solution.py:78
  121.4 0.1 collective-permute-start.14
  121.6 2.8 %collective-permute-start.17 = (f32[3,768]{1,0:T(4,128)S(1)}, f32[3,768]{1,0:T(4,128)S(1)}, u32[]{:S(2)}, u32[]{:S(2)}) collective-permute-start(f32[3,768]{1,0:T(4,128)S(1)} %pad_maximum_fusion), channel_id=1, source_target_pairs={{2,4},{3,5},{4,2},{5,3},{10,12},{11,13},{12,10},{13,11},{18,20},{1... | collective-permute-start | bytes 27656 | tf_op jit(solution)/shard_map/ppermute | solution.py:376
  124.4 1.7 %collective-permute-start.16 = (f32[3,768]{1,0:T(4,128)S(1)}, f32[3,768]{1,0:T(4,128)S(1)}, u32[]{:S(2)}, u32[]{:S(2)}) collective-permute-start(f32[3,768]{1,0:T(4,128)S(1)} %pad_maximum_fusion), channel_id=1, source_target_pairs={{0,1},{1,0},{2,5},{3,4},{4,3},{5,2},{6,7},{7,6},{8,9},{9,8},{10,13... | collective-permute-start | bytes 27656 | tf_op jit(solution)/shard_map/ppermute | solution.py:375
  126.1 2.2 %collective-permute-done.17 = f32[3,768]{1,0:T(4,128)S(1)} collective-permute-done((f32[3,768]{1,0:T(4,128)S(1)}, f32[3,768]{1,0:T(4,128)S(1)}, u32[]{:S(2)}, u32[]{:S(2)}) %collective-permute-start.17) | collective-permute-done | bytes 9248 | tf_op jit(solution)/shard_map/ppermute | solution.py:376
  128.4 2.6 %collective-permute-start.15 = (f32[4,2]{0,1:T(2,128)S(1)}, f32[4,2]{0,1:T(2,128)S(1)}, u32[]{:S(2)}, u32[]{:S(2)}) collective-permute-start(f32[4,2]{0,1:T(2,128)S(1)} %slice.61), channel_id=1, source_target_pairs={{0,192},{4,196},{8,200},{12,204},{16,208},{20,212},{24,216},{28,22... | collective-permute-start | bytes 104 | tf_op jit(solution)/shard_map/ppermute | solution.py:344
  131.0 1.9 %collective-permute-done.15 = f32[4,2]{0,1:T(2,128)S(1)} collective-permute-done((f32[4,2]{0,1:T(2,128)S(1)}, f32[4,2]{0,1:T(2,128)S(1)}, u32[]{:S(2)}, u32[]{:S(2)}) %collective-permute-start.15) | collective-permute-done | bytes 64 | tf_op jit(solution)/shard_map/ppermute | solution.py:344
  133.0 1.5 collective-permute-start.18
  134.5 3.8 %second_layer.1 = (bf16[1024,768]{1,0:T(8,128)(2,1)S(1)}, bf16[1024,768]{1,0:T(8,128)(2,1)S(1)}, bf16[1024,512]{1,0:T(8,128)(2,1)S(1)}) custom-call(bf16[1024,512]{1,0:T(8,128)(2,1)S(1)} %get-tuple-element.57.mine_ref, bf16[1024,512]{1,0:T(8,128)(2,1)S(1)} %collective-permute-done.14.other_ref, bf16[1024,512]{1,0:T(8,128)(2,1)S(1)} %get-tuple-element.60.pay_ref, ...), custom_call_target="tpu_custom_call" | custom-call | flops 15728640000 | bytes 12582912 | tf_op jit(solution)/shard_map/second_layer/pallas_call | solution.py:78
  138.3 0.1 collective-permute-start.19
  139.1 1.3 collective-permute-start.20
  140.5 1.1 collective-permute-done.20
  141.6 3.0 %collective-permute-start.23 = (f32[1,2]{0,1:T(2,128)S(1)}, f32[1,2]{0,1:T(2,128)S(1)}, u32[]{:S(2)}, u32[]{:S(2)}) collective-permute-start(f32[1,2]{0,1:T(2,128)S(1)} %slice_maximum_fusion), channel_id=1, source_target_pairs={{0,2},{1,3},{2,0},{3,1},{4,6},{5,7},{6,4},{7,5},{8,10},{9,11},{10,... | collective-permute-start | bytes 32 | tf_op jit(solution)/shard_map/ppermute | solution.py:349
  144.6 0.2 collective-permute-start.22
  144.9 0.5 collective-permute-start.21
  145.3 3.2 %last_layer.1 = f32[16,1024]{1,0:T(8,128)S(1)} custom-call(f32[1]{0:T(128)} %copy.14.coefficient, bf16[1024,512]{1,0:T(8,128)(2,1)S(1)} %get-tuple-element.66.mine_ref, bf16[1024,512]{1,0:T(8,128)(2,1)S(1)} %collective-permute-done.19.other_ref, bf16[1024,512]{1,0:T(8,128)(2,1)S(1)} %get-tuple-element.60.pay_ref, ...), custom_call_target="tpu_custom_call" | custom-call | flops 1879048192 | bytes 10485760 | tf_op jit(solution)/shard_map/last_layer/pallas_call | solution.py:78
  148.6 0.6 fusion.4
  149.8 2.2 %collective-permute-start.24 = (f32[1,1024]{1,0:T(1,128)S(1)}, f32[1,1024]{1,0:T(1,128)S(1)}, u32[]{:S(2)}, u32[]{:S(2)}) collective-permute-start(f32[1,1024]{1,0:T(1,128)S(1)} %slice_subtract_fusion), channel_id=1, source_target_pairs={{0,4},{1,5},{2,6},{3,7},{4,0},{5,1},{6,2},{7,3},{8,12},{9,13},{10,... | collective-permute-start | bytes 12296 | tf_op jit(solution)/shard_map/ppermute | solution.py:420
  152.0 0.8 collective-permute-done.24
  152.9 5.0 %collective-permute-start.26 = (f32[1,1024]{1,0:T(1,128)S(1)}, f32[1,1024]{1,0:T(1,128)S(1)}, u32[]{:S(2)}, u32[]{:S(2)}) collective-permute-start(f32[1,1024]{1,0:T(1,128)S(1)} %fusion.7), channel_id=1, source_target_pairs={{2,4},{3,5},{4,2},{5,3},{10,12},{11,13},{12,10},{13,11},{18,20},{1... | collective-permute-start | bytes 12296 | tf_op jit(solution)/shard_map/ppermute | solution.py:422
  157.8 0.4 collective-permute-start.25
  158.2 1.0 collective-permute-done.26
  159.3 2.9 %collective-permute-done.25 = f32[1,1024]{1,0:T(1,128)S(1)} collective-permute-done((f32[1,1024]{1,0:T(1,128)S(1)}, f32[1,1024]{1,0:T(1,128)S(1)}, u32[]{:S(2)}, u32[]{:S(2)}) %collective-permute-start.25) | collective-permute-done | bytes 4128 | tf_op jit(solution)/shard_map/ppermute | solution.py:421
  162.2 0.6 maximum_select_fusion
  (74 shorter events, 0.7 us)
Async XLA Ops:
  0.0 5.3 %copy-start.11 = (bf16[2,768,512]{2,1,0:T(8,128)(2,1)S(1)}, bf16[2,768,512]{2,1,0:T(8,128)(2,1)}, u32[]{:S(2)}) copy-start(bf16[2,768,512]{2,1,0:T(8,128)(2,1)} %param.18) | copy-start | bytes 4718596
  0.0 5.7 %copy-start.16 = (bf16[2,256]{1,0:T(2,128)(2,1)S(1)}, bf16[2,256]{1,0:T(2,128)(2,1)}, u32[]{:S(2)}) copy-start(bf16[2,256]{1,0:T(2,128)(2,1)} %param.12) | copy-start | bytes 3076
  1.3 26.9 %collective-permute-start.1 = (bf16[512,768]{1,0:T(8,128)(2,1)S(1)}, bf16[512,768]{1,0:T(8,128)(2,1)}, u32[]{:S(2)}, u32[]{:S(2)}) collective-permute-start(bf16[512,768]{1,0:T(8,128)(2,1)S(1)} %dynamic-slice_bitcast_fusion.2), channel_id=1, source_target_pairs={{0,1},{1,0},{2,5},{3,4},{4,3},{5,2},{6,7},{7,6},{8,9},{9,8},{10,13... | collective-permute-start | bytes 2359304 | tf_op jit(solution)/shard_map/ppermute | solution.py:304
  5.3 22.9 %collective-permute-start = (bf16[768,512]{1,0:T(8,128)(2,1)S(1)}, bf16[768,512]{1,0:T(8,128)(2,1)}, u32[]{:S(2)}, u32[]{:S(2)}) collective-permute-start(bf16[768,512]{1,0:T(8,128)(2,1)S(1)} %dynamic-slice_bitcast_fusion.3), channel_id=1, source_target_pairs={{0,1},{1,0},{2,5},{3,4},{4,3},{5,2},{6,7},{7,6},{8,9},{9,8},{10,13... | collective-permute-start | bytes 2359304 | tf_op jit(solution)/shard_map/ppermute | solution.py:303
  6.3 21.9 %all-to-all-start = ((bf16[64,2,256]{2,1,0:T(2,128)(2,1)}), bf16[64,2,256]{2,1,0:T(2,128)(2,1)S(1)}, u32[]{:S(2)}, u32[]{:S(2)}) async-start(bf16[64,2,256]{2,1,0:T(2,128)(2,1)} %broadcast_in_dim.41), calls=%async_computation | async-start | bytes 131072 | tf_op jit(solution)/shard_map/all_to_all | solution.py:308
  28.2 18.4 %copy-start.14 = (bf16[2,1024,512]{2,1,0:T(8,128)(2,1)S(1)}, bf16[2,1024,512]{2,1,0:T(8,128)(2,1)}, u32[]{:S(2)}) copy-start(bf16[2,1024,512]{2,1,0:T(8,128)(2,1)} %param.17) | copy-start | bytes 6291460
  28.2 79.4 %all-to-all-start.1 = ((bf16[256,8,512]{2,1,0:T(8,128)(2,1)}), bf16[256,8,512]{2,1,0:T(8,128)(2,1)}, u32[]{:S(2)}, u32[]{:S(2)}) async-start(bf16[256,8,512]{2,1,0:T(8,128)(2,1)} %bitcast.32), calls=%async_computation.1 | async-start | bytes 4194304 | tf_op jit(solution)/shard_map/all_to_all | solution.py:315
  39.9 21.5 %collective-permute-start.2 = (bf16[768,512]{1,0:T(8,128)(2,1)}, bf16[768,512]{1,0:T(8,128)(2,1)}, u32[]{:S(2)}, u32[]{:S(2)}) collective-permute-start(bf16[768,512]{1,0:T(8,128)(2,1)} %collective-permute-done), channel_id=1, source_target_pairs={{0,3},{1,2},{6,5},{7,4},{8,11},{9,10},{14,13},{15,12},{16,19},{17,... | collective-permute-start | bytes 2359304 | tf_op jit(solution)/shard_map/ppermute | solution.py:318
  42.0 28.5 %collective-permute-start.8 = (bf16[768,512]{1,0:T(8,128)(2,1)}, bf16[768,512]{1,0:T(8,128)(2,1)}, u32[]{:S(2)}, u32[]{:S(2)}) collective-permute-start(bf16[768,512]{1,0:T(8,128)(2,1)} %collective-permute-done), channel_id=1, source_target_pairs={{0,8},{1,9},{2,10},{3,11},{4,12},{5,13},{6,14},{7,15},{8,16},{9,17... | collective-permute-start | bytes 2359304 | tf_op jit(solution)/shard_map/ppermute | solution.py:320
  43.5 38.1 %collective-permute-start.6 = (bf16[512,768]{1,0:T(8,128)(2,1)}, bf16[512,768]{1,0:T(8,128)(2,1)}, u32[]{:S(2)}, u32[]{:S(2)}) collective-permute-start(bf16[512,768]{1,0:T(8,128)(2,1)} %collective-permute-done.1), channel_id=1, source_target_pairs={{2,3},{3,2},{4,5},{5,4},{10,11},{11,10},{12,13},{13,12},{18,19},{1... | collective-permute-start | bytes 2359304 | tf_op jit(solution)/shard_map/ppermute | solution.py:319
  47.8 38.8 %copy-start.9 = (bf16[1024,512]{1,0:T(8,128)(2,1)}, bf16[1024,512]{1,0:T(8,128)(2,1)S(1)}, u32[]{:S(2)}) copy-start(bf16[1024,512]{1,0:T(8,128)(2,1)S(1)} %get-tuple-element.45) | copy-start | bytes 3145732
  61.4 29.3 %collective-permute-start.5 = (bf16[512,768]{1,0:T(8,128)(2,1)}, bf16[512,768]{1,0:T(8,128)(2,1)S(1)}, u32[]{:S(2)}, u32[]{:S(2)}) collective-permute-start(bf16[512,768]{1,0:T(8,128)(2,1)} %collective-permute-done.1), channel_id=1, source_target_pairs={{0,24},{1,25},{2,10},{3,11},{4,12},{5,13},{6,30},{7,31},{8,0},{9,1... | collective-permute-start | bytes 2359304 | tf_op jit(solution)/shard_map/ppermute | solution.py:328
  62.6 3.9 %collective-permute-start.10 = (f32[32,2]{0,1:T(2,128)S(1)}, f32[32,2]{0,1:T(2,128)S(1)}, u32[]{:S(2)}, u32[]{:S(2)}) collective-permute-start(f32[32,2]{0,1:T(2,128)S(1)} %slice.55), channel_id=1, source_target_pairs={{0,4},{4,0},{8,12},{12,8},{16,20},{20,16},{24,28},{28,24},{32,36},... | collective-permute-start | bytes 776 | tf_op jit(solution)/shard_map/ppermute | solution.py:344
  64.6 28.3 %collective-permute-start.9 = (bf16[768,512]{1,0:T(8,128)(2,1)}, bf16[768,512]{1,0:T(8,128)(2,1)S(1)}, u32[]{:S(2)}, u32[]{:S(2)}) collective-permute-start(bf16[768,512]{1,0:T(8,128)(2,1)} %collective-permute-done.2), channel_id=1, source_target_pairs={{2,26},{3,27},{4,28},{5,29},{10,2},{11,3},{12,4},{13,5},{18,10},{1... | collective-permute-start | bytes 2359304 | tf_op jit(solution)/shard_map/ppermute | solution.py:327
  66.5 36.6 %collective-permute-start.3 = (bf16[1024,512]{1,0:T(8,128)(2,1)}, bf16[1024,512]{1,0:T(8,128)(2,1)S(1)}, u32[]{:S(2)}, u32[]{:S(2)}) collective-permute-start(bf16[1024,512]{1,0:T(8,128)(2,1)} %get-tuple-element.44), channel_id=1, source_target_pairs={{0,1},{1,0},{2,5},{3,4},{4,3},{5,2},{6,7},{7,6},{8,9},{9,8},{10,13... | collective-permute-start | bytes 3145736 | tf_op jit(solution)/shard_map/ppermute | solution.py:324
  70.5 32.7 %collective-permute-start.4 = (bf16[1024,512]{1,0:T(8,128)(2,1)S(1)}, bf16[1024,512]{1,0:T(8,128)(2,1)S(1)}, u32[]{:S(2)}, u32[]{:S(2)}) collective-permute-start(bf16[1024,512]{1,0:T(8,128)(2,1)S(1)} %get-tuple-element.45), channel_id=1, source_target_pairs={{2,4},{3,5},{4,2},{5,3},{10,12},{11,13},{12,10},{13,11},{18,20},{1... | collective-permute-start | bytes 3145736 | tf_op jit(solution)/shard_map/ppermute | solution.py:325
  81.6 19.4 %collective-permute-start.7 = (bf16[512,768]{1,0:T(8,128)(2,1)}, bf16[512,768]{1,0:T(8,128)(2,1)S(1)}, u32[]{:S(2)}, u32[]{:S(2)}) collective-permute-start(bf16[512,768]{1,0:T(8,128)(2,1)} %collective-permute-done.6), channel_id=1, source_target_pairs={{2,26},{3,27},{4,28},{5,29},{10,2},{11,3},{12,4},{13,5},{18,10},{1... | collective-permute-start | bytes 2359304 | tf_op jit(solution)/shard_map/ppermute | solution.py:329
  86.5 6.3 %copy-start.12 = (bf16[2,768,512]{2,1,0:T(8,128)(2,1)S(1)}, bf16[2,768,512]{2,1,0:T(8,128)(2,1)}, u32[]{:S(2)}) copy-start(bf16[2,768,512]{2,1,0:T(8,128)(2,1)} %param.18) | copy-start | bytes 4718596
  92.9 8.1 %copy-start.13 = (bf16[2,512,768]{2,1,0:T(8,128)(2,1)S(1)}, bf16[2,512,768]{2,1,0:T(8,128)(2,1)}, u32[]{:S(2)}) copy-start(bf16[2,512,768]{2,1,0:T(8,128)(2,1)} %param.19) | copy-start | bytes 4718596
  94.3 8.9 %copy-start.10 = (bf16[1024,512]{1,0:T(8,128)(2,1)S(1)}, bf16[1024,512]{1,0:T(8,128)(2,1)}, u32[]{:S(2)}) copy-start(bf16[1024,512]{1,0:T(8,128)(2,1)} %copy-done.9) | copy-start | bytes 3145732
  103.2 1.1 copy-start
  105.5 1.3 copy-start.5
  106.8 0.8 copy-start.7
  107.7 13.7 %collective-permute-start.11 = (f32[8,2]{0,1:T(2,128)S(1)}, f32[8,2]{0,1:T(2,128)S(1)}, u32[]{:S(2)}, u32[]{:S(2)}) collective-permute-start(f32[8,2]{0,1:T(2,128)S(1)} %get-tuple-element.87), channel_id=1, source_target_pairs={{0,8},{4,12},{8,0},{12,4},{16,24},{20,28},{24,16},{28,20},{32,40},... | collective-permute-start | bytes 200 | tf_op jit(solution)/shard_map/ppermute | solution.py:357
  108.6 12.8 %collective-permute-start.13 = (f32[8,2]{0,1:T(2,128)S(1)}, f32[8,2]{0,1:T(2,128)S(1)}, u32[]{:S(2)}, u32[]{:S(2)}) collective-permute-start(f32[8,2]{0,1:T(2,128)S(1)} %get-tuple-element.88), channel_id=1, source_target_pairs={{0,16},{4,20},{8,24},{12,28},{16,0},{20,4},{24,8},{28,12},{32,48},... | collective-permute-start | bytes 200 | tf_op jit(solution)/shard_map/ppermute | solution.py:357
  111.9 9.5 %collective-permute-start.12 = (f32[8,2]{0,1:T(2,128)S(1)}, f32[8,2]{0,1:T(2,128)S(1)}, u32[]{:S(2)}, u32[]{:S(2)}) collective-permute-start(f32[8,2]{0,1:T(2,128)S(1)} %get-tuple-element.89), channel_id=1, source_target_pairs={{0,24},{4,28},{8,16},{12,20},{16,8},{20,12},{24,0},{28,4},{32,56},... | collective-permute-start | bytes 200 | tf_op jit(solution)/shard_map/ppermute | solution.py:357
  111.9 1.6 copy-start.6
  113.5 1.0 copy-start.8
  114.5 7.0 %copy-start.17 = (bf16[768]{0:T(1024)(128)(2,1)S(1)}, bf16[768]{0:T(1024)(128)(2,1)}, u32[]{:S(2)}) copy-start(bf16[768]{0:T(1024)(128)(2,1)} %param.21) | copy-start | bytes 4612
  114.5 7.0 %copy-start.15 = (f32[2,768]{1,0:T(2,128)S(1)}, f32[2,768]{1,0:T(2,128)}, u32[]{:S(2)}) copy-start(f32[2,768]{1,0:T(2,128)} %param.20) | copy-start | bytes 18436
  114.5 19.9 %copy-start.1 = (bf16[1024,512]{1,0:T(8,128)(2,1)S(1)}, bf16[1024,512]{1,0:T(8,128)(2,1)}, u32[]{:S(2)}) copy-start(bf16[1024,512]{1,0:T(8,128)(2,1)} %copy-done) | copy-start | bytes 3145732
  114.5 19.9 %copy-start.2 = (bf16[512,768]{1,0:T(8,128)(2,1)S(1)}, bf16[512,768]{1,0:T(8,128)(2,1)}, u32[]{:S(2)}) copy-start(bf16[512,768]{1,0:T(8,128)(2,1)} %get-tuple-element.63.ub_ref) | copy-start | bytes 2359300
  114.5 19.9 %copy-start.3 = (bf16[768,512]{1,0:T(8,128)(2,1)S(1)}, bf16[768,512]{1,0:T(8,128)(2,1)}, u32[]{:S(2)}) copy-start(bf16[768,512]{1,0:T(8,128)(2,1)} %get-tuple-element.83.va_ref) | copy-start | bytes 2359300
  114.6 19.9 %copy-start.4 = (bf16[512,768]{1,0:T(8,128)(2,1)S(1)}, bf16[512,768]{1,0:T(8,128)(2,1)}, u32[]{:S(2)}) copy-start(bf16[512,768]{1,0:T(8,128)(2,1)} %get-tuple-element.62.ua_ref) | copy-start | bytes 2359300
  121.4 11.5 %collective-permute-start.14 = (bf16[1024,512]{1,0:T(8,128)(2,1)S(1)}, bf16[1024,512]{1,0:T(8,128)(2,1)S(1)}, u32[]{:S(2)}, u32[]{:S(2)}) collective-permute-start(bf16[1024,512]{1,0:T(8,128)(2,1)S(1)} %get-tuple-element.57.mine_ref), channel_id=1, source_target_pairs={{0,4},{1,5},{2,6},{3,7},{4,0},{5,1},{6,2},{7,3},{8,12},{9,13},{10,... | collective-permute-start | bytes 3145736 | tf_op jit(solution)/shard_map/ppermute | solution.py:403
  121.6 6.8 %collective-permute-start.17 = (f32[3,768]{1,0:T(4,128)S(1)}, f32[3,768]{1,0:T(4,128)S(1)}, u32[]{:S(2)}, u32[]{:S(2)}) collective-permute-start(f32[3,768]{1,0:T(4,128)S(1)} %pad_maximum_fusion), channel_id=1, source_target_pairs={{2,4},{3,5},{4,2},{5,3},{10,12},{11,13},{12,10},{13,11},{18,20},{1... | collective-permute-start | bytes 27656 | tf_op jit(solution)/shard_map/ppermute | solution.py:376
  124.4 10.1 %collective-permute-start.16 = (f32[3,768]{1,0:T(4,128)S(1)}, f32[3,768]{1,0:T(4,128)S(1)}, u32[]{:S(2)}, u32[]{:S(2)}) collective-permute-start(f32[3,768]{1,0:T(4,128)S(1)} %pad_maximum_fusion), channel_id=1, source_target_pairs={{0,1},{1,0},{2,5},{3,4},{4,3},{5,2},{6,7},{7,6},{8,9},{9,8},{10,13... | collective-permute-start | bytes 27656 | tf_op jit(solution)/shard_map/ppermute | solution.py:375
  128.4 4.6 %collective-permute-start.15 = (f32[4,2]{0,1:T(2,128)S(1)}, f32[4,2]{0,1:T(2,128)S(1)}, u32[]{:S(2)}, u32[]{:S(2)}) collective-permute-start(f32[4,2]{0,1:T(2,128)S(1)} %slice.61), channel_id=1, source_target_pairs={{0,192},{4,196},{8,200},{12,204},{16,208},{20,212},{24,216},{28,22... | collective-permute-start | bytes 104 | tf_op jit(solution)/shard_map/ppermute | solution.py:344
  133.0 5.3 %collective-permute-start.18 = (f32[2,2]{0,1:T(2,128)S(1)}, f32[2,2]{0,1:T(2,128)S(1)}, u32[]{:S(2)}, u32[]{:S(2)}) collective-permute-start(f32[2,2]{0,1:T(2,128)S(1)} %slice.64), channel_id=1, source_target_pairs={{0,64},{4,68},{8,72},{12,76},{16,80},{20,84},{24,88},{28,92},{32,9... | collective-permute-start | bytes 56 | tf_op jit(solution)/shard_map/ppermute | solution.py:344
  138.3 3.3 %collective-permute-start.19 = (bf16[1024,512]{1,0:T(8,128)(2,1)S(1)}, bf16[1024,512]{1,0:T(8,128)(2,1)S(1)}, u32[]{:S(2)}, u32[]{:S(2)}) collective-permute-start(bf16[1024,512]{1,0:T(8,128)(2,1)S(1)} %get-tuple-element.66.mine_ref), channel_id=1, source_target_pairs={{0,4},{1,5},{2,6},{3,7},{4,0},{5,1},{6,2},{7,3},{8,12},{9,13},{10,... | collective-permute-start | bytes 3145736 | tf_op jit(solution)/shard_map/ppermute | solution.py:411
  139.1 2.4 %collective-permute-start.20 = (f32[1,2]{0,1:T(2,128)S(1)}, f32[1,2]{0,1:T(2,128)S(1)}, u32[]{:S(2)}, u32[]{:S(2)}) collective-permute-start(f32[1,2]{0,1:T(2,128)S(1)} %slice.66), channel_id=1, source_target_pairs={{0,32},{4,36},{8,40},{12,44},{16,48},{20,52},{24,56},{28,60},{32,0... | collective-permute-start | bytes 32 | tf_op jit(solution)/shard_map/ppermute | solution.py:344
  141.6 6.9 %collective-permute-start.23 = (f32[1,2]{0,1:T(2,128)S(1)}, f32[1,2]{0,1:T(2,128)S(1)}, u32[]{:S(2)}, u32[]{:S(2)}) collective-permute-start(f32[1,2]{0,1:T(2,128)S(1)} %slice_maximum_fusion), channel_id=1, source_target_pairs={{0,2},{1,3},{2,0},{3,1},{4,6},{5,7},{6,4},{7,5},{8,10},{9,11},{10,... | collective-permute-start | bytes 32 | tf_op jit(solution)/shard_map/ppermute | solution.py:349
  144.6 3.9 %collective-permute-start.22 = (f32[1,2]{0,1:T(2,128)S(1)}, f32[1,2]{0,1:T(2,128)S(1)}, u32[]{:S(2)}, u32[]{:S(2)}) collective-permute-start(f32[1,2]{0,1:T(2,128)S(1)} %slice_maximum_fusion), channel_id=1, source_target_pairs={{0,3},{1,2},{2,1},{3,0},{4,7},{5,6},{6,5},{7,4},{8,11},{9,10},{10,... | collective-permute-start | bytes 32 | tf_op jit(solution)/shard_map/ppermute | solution.py:349
  144.9 3.7 %collective-permute-start.21 = (f32[1,2]{0,1:T(2,128)S(1)}, f32[1,2]{0,1:T(2,128)S(1)}, u32[]{:S(2)}, u32[]{:S(2)}) collective-permute-start(f32[1,2]{0,1:T(2,128)S(1)} %slice_maximum_fusion), channel_id=1, source_target_pairs={{0,1},{1,0},{2,3},{3,2},{4,5},{5,4},{6,7},{7,6},{8,9},{9,8},{10,11... | collective-permute-start | bytes 32 | tf_op jit(solution)/shard_map/ppermute | solution.py:349
  149.8 3.1 %collective-permute-start.24 = (f32[1,1024]{1,0:T(1,128)S(1)}, f32[1,1024]{1,0:T(1,128)S(1)}, u32[]{:S(2)}, u32[]{:S(2)}) collective-permute-start(f32[1,1024]{1,0:T(1,128)S(1)} %slice_subtract_fusion), channel_id=1, source_target_pairs={{0,4},{1,5},{2,6},{3,7},{4,0},{5,1},{6,2},{7,3},{8,12},{9,13},{10,... | collective-permute-start | bytes 12296 | tf_op jit(solution)/shard_map/ppermute | solution.py:420
  152.9 6.4 %collective-permute-start.26 = (f32[1,1024]{1,0:T(1,128)S(1)}, f32[1,1024]{1,0:T(1,128)S(1)}, u32[]{:S(2)}, u32[]{:S(2)}) collective-permute-start(f32[1,1024]{1,0:T(1,128)S(1)} %fusion.7), channel_id=1, source_target_pairs={{2,4},{3,5},{4,2},{5,3},{10,12},{11,13},{12,10},{13,11},{18,20},{1... | collective-permute-start | bytes 12296 | tf_op jit(solution)/shard_map/ppermute | solution.py:422
  157.8 4.3 %collective-permute-start.25 = (f32[1,1024]{1,0:T(1,128)S(1)}, f32[1,1024]{1,0:T(1,128)S(1)}, u32[]{:S(2)}, u32[]{:S(2)}) collective-permute-start(f32[1,1024]{1,0:T(1,128)S(1)} %fusion.7), channel_id=1, source_target_pairs={{0,1},{1,0},{2,5},{3,4},{4,3},{5,2},{6,7},{7,6},{8,9},{9,8},{10,13... | collective-permute-start | bytes 12296 | tf_op jit(solution)/shard_map/ppermute | solution.py:421

commit v8 on v7

--- a/solution.py
+++ b/solution.py
@@ -317,16 +317,10 @@
 
     v_far = move(v_near, perm=home_on)
     u_far = move(u_near, perm=away_swap)
-    v_near_y = move(v_near, perm=y_up)
-    v_far, u_near_on, ctx_out, ctx_away = lax.optimization_barrier(
-        (v_far, u_near, ctx_own, ctx_away)
-    )
+    v_far, ctx_out, ctx_away = lax.optimization_barrier((v_far, ctx_own, ctx_away))
     ctx_a = move(ctx_away, perm=ctx_near)
     ctx_b = move(ctx_out, perm=ctx_far)
     ctx_a, ctx_b = lax.optimization_barrier((ctx_a, ctx_b))
-    v_far_y = move(v_far, perm=y_down)
-    u_near_y = move(u_near_on, perm=y_mixed)
-    u_far_y = move(u_far, perm=y_down)
 
     all_scores = jnp.einsum(
         "ue,ie->ui", users.reshape(persons, -1), catalog_embedding, preferred_element_type=F32
@@ -358,8 +352,19 @@
             out = jnp.maximum(out, got)
         return out
 
-    best = halve(best, hops[5])
-
+    best = over_y(halve(best, hops[5]))
+
+    small = jnp.concatenate([interaction_offset, final_projection[None, :].astype(F32)], 0)
+    best, v_near_on = lax.optimization_barrier((best, v_near))
+    v_near_y = move(v_near_on, perm=y_up)
+    v_far_y = move(v_far, perm=y_down)
+    v_near_y, u_near_on = lax.optimization_barrier((v_near_y, u_near))
+    u_near_y = move(u_near_on, perm=y_mixed)
+    u_far_y = move(u_far, perm=y_down)
+    ctx_a, best, small = lax.optimization_barrier((ctx_a, best, small))
+    best = halve(best, hops[2])
+    small_a = move(small, perm=to_near)
+    small_b = move(small, perm=ctx_far)
     even = odd_y == 0
     v0_a = jnp.where(even, v_near, v_near_y)
     v1_a = jnp.where(even, v_near_y, v_near)
@@ -370,10 +375,6 @@
     u0_b = jnp.where(home, lowrank_u_matrix[0], jnp.where(even, u_far, u_far_y))
     u1_b = jnp.where(home, lowrank_u_matrix[1], jnp.where(even, u_far_y, u_far))
     ctx_b = jnp.where(home, ctx_own, ctx_b)
-    small = jnp.concatenate([interaction_offset, final_projection[None, :].astype(F32)], 0)
-    small, _ = lax.optimization_barrier((small, u_far))
-    small_a = move(small, perm=to_near)
-    small_b = jnp.where(home, small, move(small, perm=ctx_far))
     ctx_a, u0_a, u0_b, u1_a, u1_b = lax.optimization_barrier((ctx_a, u0_a, u0_b, u1_a, u1_b))
 
     emb_other = lax.dynamic_index_in_dim(users, me ^ 1, 0, False)
@@ -392,29 +393,28 @@
         CTX, 8, [], [ctx_a, ctx_b, v0_a, v0_b], [],
     )
     recv, best = lax.optimization_barrier((recv, best))
-    step = over_y(best)
+    step = halve(best, hops[1])
     pay, piece, logit = call(
         first_kernel, "first_layer", 24000, [tall, tall, lanes],
         [pltpu.VMEM(recv.shape, BF), pltpu.VMEM((16, recv.shape[0]), F32)]
         + [pltpu.VMEM(recv.shape, BF), pltpu.SemaphoreType.DMA((recv.shape[0] // ROWS,))],
         FIRST, 8, [], [query, part, head], [recv],
     )
-    piece, best = lax.optimization_barrier((piece, step))
-    other, best = lax.optimization_barrier((move(piece, perm=to_core), halve(best, hops[2])))
-    step = halve(best, hops[1])
+    piece, best, small_a, small_b = lax.optimization_barrier((piece, step, small_a, small_b))
+    small_b = jnp.where(home, small, small_b)
+    other, best = lax.optimization_barrier((move(piece, perm=to_core), halve(best, hops[0])))
+    step = over_x(best)
     x_a, x_b, piece1 = call(
         second_kernel, "second_layer", 24000, [wide, wide, tall], [],
         SECOND, 12, [],
         [piece, other, pay, small_a, small_b, ctx_a, ctx_b, u0_a, u0_b, v1_a, v1_b], [],
     )
     piece1, best = lax.optimization_barrier((piece1, step))
-    other1, best = lax.optimization_barrier((move(piece1, perm=to_core), halve(best, hops[0])))
-    step = over_x(best)
+    other1 = move(piece1, perm=to_core)
     (score,) = call(
         last_kernel, "last_layer", 24000, [lanes], [], 1792, 10, [similarity_coefficient],
         [piece1, other1, pay, x_a, x_b, small_a, small_b, logit, ctx_a, ctx_b, u1_a, u1_b], [],
     )
-    score, best = lax.optimization_barrier((score, step))
     top = jnp.where(home, lax.dynamic_slice_in_dim(best, parity, 1, 1), 0.0)
     score = score[0:1] - similarity_coefficient[0] * top
     score = score + move(score, perm=to_core)

time: 164 us -> 157 us (0.957)
  starting transfers between devices: 81.7 us -> 72.1 us
  waiting for transfers between devices: 34.3 us -> 40.1 us
    ppermute x1, starting transfers between devices: 11.1 us -> 1.91 us  [on_device(): ctx_b = move(ctx_out, perm=ctx_far)]
    ppermute x1, waiting for transfers between devices: 4.19 us -> 0.01 us  [on_device(): u_near_y = move(u_near_on, perm=y_mixed)]
    ppermute x3, waiting for transfers between devices: 2.28 us -> 6.38 us  [the longest x1 5.93 us: on_device(): v_near_y = move(v_near_on, perm=y_up)]
    ppermute x1, starting transfers between devices: 3.96 us -> 0.33 us  [on_device(): move(lax.dynamic_index_in_dim(lowrank_u_matrix, odd_y, 0, False), perm=to...]
    ppermute x1, starting transfers between devices: 0.33 us -> 3.96 us  [on_device(): move(lax.dynamic_index_in_dim(lowrank_v_matrix, odd_y, 0, False), perm=to...]
    ppermute x3, waiting for transfers between devices: 0.01 us -> 3.63 us  [over_y(): got = lax.ppermute(best[block * n:(block + 1) * n], 'shard', pairs)]
    ppermute x1, waiting for transfers between devices: 6.59 us -> 9.81 us  [on_device(): u_far_y = move(u_far, perm=y_down)]
    ppermute x1, waiting for transfers between devices: 0.01 us -> 3.17 us  [on_device(): ctx_a = move(ctx_away, perm=ctx_near)]
  transfers between devices with their start and end apart: 29 -> 29, of which waited for: 10 -> 13; matrix products, arithmetic and copies ran while one was open for 9% -> 8% of each run, Pallas kernels for 14% -> 13%
where the time goes in v8:
time: 157 us
  starting transfers between devices  72.1 us (46%)
  waiting for transfers between devices  40.1 us (26%)
  Pallas kernels  22.9 us (15%)
  other arithmetic  10.1 us (6%)
  local copies, waits for them, and re-layouts  9.2 us (6%)
  between operations  1.74 us (1%)
    pallas_call x4, Pallas kernels, call(): pl.pallas_call(kernel, in_specs=[SMEM] * len(scalars) + [VMEM] * len(arra...  15 us
    all_to_all x1, starting transfers between devices, on_device(): recv = lax.all_to_all(parcel, AXES, split_axis=0, concat_axis=0, tiled=True)  12.3 us
    all_to_all x1, starting transfers between devices, on_device(): lax.all_to_all(users, 'shard', split_axis=0, concat_axis=0, tiled=True)  11.8 us
    ppermute x1, waiting for transfers between devices, on_device(): u_far_y = move(u_far, perm=y_down)  9.81 us
    ppermute x1, waiting for transfers between devices, on_device(): v_far = move(v_near, perm=home_on)  9.62 us
    ppermute x4, starting transfers between devices, halve(): return jnp.maximum(best[:half], lax.ppermute(best[half:], 'shard', pairs))  8.26 us
    pallas_call x1, Pallas kernels, pick_rows(): pl.pallas_call(pick_kernel, in_specs=[VMEM, VMEM, ANY, ANY], out_specs=AN...  7.94 us
    ppermute x1, waiting for transfers between devices, on_device(): v_near_y = move(v_near_on, perm=y_up)  5.93 us
  transfers between devices with their start and end apart: 29, of which 13 were waited for; matrix products, arithmetic and copies ran while one was open for 8% of the time, Pallas kernels for 13%

profile of v8, /device:TPU:1, one launch (start us, length us, event | category | flops | bytes accessed | tf_op | source)
XLA Modules:
  0.0 156.8 jit_solution(14489811017625403980)
XLA Ops:
  0.0 1.3 dynamic-slice_bitcast_fusion.3
  1.3 4.0 %collective-permute-start = (bf16[768,512]{1,0:T(8,128)(2,1)S(1)}, bf16[768,512]{1,0:T(8,128)(2,1)}, u32[]{:S(2)}, u32[]{:S(2)}) collective-permute-start(bf16[768,512]{1,0:T(8,128)(2,1)S(1)} %dynamic-slice_bitcast_fusion.3), channel_id=1, source_target_pairs={{0,1},{1,0},{2,5},{3,4},{4,3},{5,2},{6,7},{7,6},{8,9},{9,8},{10,13... | collective-permute-start | bytes 2359304 | tf_op jit(solution)/shard_map/ppermute | solution.py:303
  5.3 0.3 collective-permute-start.1
  5.7 0.7 broadcast_in_dim.41
  6.3 11.8 %all-to-all-start = ((bf16[64,2,256]{2,1,0:T(2,128)(2,1)}), bf16[64,2,256]{2,1,0:T(2,128)(2,1)S(1)}, u32[]{:S(2)}, u32[]{:S(2)}) async-start(bf16[64,2,256]{2,1,0:T(2,128)(2,1)} %broadcast_in_dim.41), calls=%async_computation | async-start | bytes 131072 | tf_op jit(solution)/shard_map/all_to_all | solution.py:308
  18.1 7.9 %pick_rows.1 = bf16[32,2,32,512]{3,2,1,0:T(8,128)(2,1)} custom-call(s32[8,128]{1,0:T(8,128)} %bitcast.33, s32[1,128]{1,0:T(1,128)} %bitcast.34, bf16[2048,256]{1,0:T(8,128)(2,1)} %emb_hbm.1, bf16[2048,768]{1,0:T(8,128)(2,1)} %attr_hbm.1), custom_call_target="tpu_custom_call" | custom-call | flops 4294967296 | bytes 6291456 | tf_op jit(solution)/shard_map/pick_rows/pallas_call | solution.py:144
  26.0 0.7 fusion.2
  26.7 1.4 all-to-all-done
  28.2 12.3 %all-to-all-start.1 = ((bf16[256,8,512]{2,1,0:T(8,128)(2,1)}), bf16[256,8,512]{2,1,0:T(8,128)(2,1)}, u32[]{:S(2)}, u32[]{:S(2)}) async-start(bf16[256,8,512]{2,1,0:T(8,128)(2,1)} %bitcast.32), calls=%async_computation.1 | async-start | bytes 4194304 | tf_op jit(solution)/shard_map/all_to_all | solution.py:315
  40.7 0.6 convolution_reduce_fusion
  41.2 0.1 broadcast_in_dim.45
  41.5 0.1 select_reduce_fusion
  41.6 2.2 %collective-permute-start.5 = (f32[32,2]{0,1:T(2,128)S(1)}, f32[32,2]{0,1:T(2,128)S(1)}, u32[]{:S(2)}, u32[]{:S(2)}) collective-permute-start(f32[32,2]{0,1:T(2,128)S(1)} %slice.52), channel_id=1, source_target_pairs={{0,4},{4,0},{8,12},{12,8},{16,20},{20,16},{24,28},{28,24},{32,36},... | collective-permute-start | bytes 776 | tf_op jit(solution)/shard_map/ppermute | solution.py:338
  43.9 1.3 collective-permute-start.2
  45.2 1.9 %collective-permute-start.11 = (bf16[512,768]{1,0:T(8,128)(2,1)}, bf16[512,768]{1,0:T(8,128)(2,1)}, u32[]{:S(2)}, u32[]{:S(2)}) collective-permute-start(bf16[512,768]{1,0:T(8,128)(2,1)} %collective-permute-done.1), channel_id=1, source_target_pairs={{2,3},{3,2},{4,5},{5,4},{10,11},{11,10},{12,13},{13,12},{18,19},{1... | collective-permute-start | bytes 2359304 | tf_op jit(solution)/shard_map/ppermute | solution.py:319
  47.2 0.7 collective-permute-start.6
  47.9 1.8 %collective-permute-start.7 = (f32[8,2]{0,1:T(2,128)S(1)}, f32[8,2]{0,1:T(2,128)S(1)}, u32[]{:S(2)}, u32[]{:S(2)}) collective-permute-start(f32[8,2]{0,1:T(2,128)S(1)} %get-tuple-element.95), channel_id=1, source_target_pairs={{0,24},{4,28},{8,16},{12,20},{16,8},{20,12},{24,0},{28,4},{32,56},... | collective-permute-start | bytes 200 | tf_op jit(solution)/shard_map/ppermute | solution.py:351
  49.7 0.8 collective-permute-start.8
  50.5 1.5 collective-permute-done.7
  52.0 2.1 %collective-permute-done.8 = f32[8,2]{0,1:T(2,128)S(1)} collective-permute-done((f32[8,2]{0,1:T(2,128)S(1)}, f32[8,2]{0,1:T(2,128)S(1)}, u32[]{:S(2)}, u32[]{:S(2)}) %collective-permute-start.8) | collective-permute-done | bytes 96 | tf_op jit(solution)/shard_map/ppermute | solution.py:351
  54.1 0.3 collective-permute-start.9
  54.4 1.1 dynamic-slice_bitcast_fusion
  55.5 9.6 %collective-permute-done.2 = bf16[768,512]{1,0:T(8,128)(2,1)} collective-permute-done((bf16[768,512]{1,0:T(8,128)(2,1)}, bf16[768,512]{1,0:T(8,128)(2,1)}, u32[]{:S(2)}, u32[]{:S(2)}) %collective-permute-start.2) | collective-permute-done | bytes 786464 | tf_op jit(solution)/shard_map/ppermute | solution.py:318
  65.1 2.7 %collective-permute-start.13 = (bf16[768,512]{1,0:T(8,128)(2,1)}, bf16[768,512]{1,0:T(8,128)(2,1)}, u32[]{:S(2)}, u32[]{:S(2)}) collective-permute-start(bf16[768,512]{1,0:T(8,128)(2,1)} %collective-permute-done.2), channel_id=1, source_target_pairs={{2,26},{3,27},{4,28},{5,29},{10,2},{11,3},{12,4},{13,5},{18,10},{1... | collective-permute-start | bytes 2359304 | tf_op jit(solution)/shard_map/ppermute | solution.py:360
  68.0 2.2 %collective-permute-start.12 = (bf16[512,768]{1,0:T(8,128)(2,1)}, bf16[512,768]{1,0:T(8,128)(2,1)S(1)}, u32[]{:S(2)}, u32[]{:S(2)}) collective-permute-start(bf16[512,768]{1,0:T(8,128)(2,1)} %collective-permute-done.11), channel_id=1, source_target_pairs={{2,26},{3,27},{4,28},{5,29},{10,2},{11,3},{12,4},{13,5},{18,10},{1... | collective-permute-start | bytes 2359304 | tf_op jit(solution)/shard_map/ppermute | solution.py:363
  70.2 4.1 %collective-permute-start.3 = (bf16[1024,512]{1,0:T(8,128)(2,1)}, bf16[1024,512]{1,0:T(8,128)(2,1)S(1)}, u32[]{:S(2)}, u32[]{:S(2)}) collective-permute-start(bf16[1024,512]{1,0:T(8,128)(2,1)} %get-tuple-element.46), channel_id=1, source_target_pairs={{0,1},{1,0},{2,5},{3,4},{4,3},{5,2},{6,7},{7,6},{8,9},{9,8},{10,13... | collective-permute-start | bytes 3145736 | tf_op jit(solution)/shard_map/ppermute | solution.py:321
  74.3 1.9 %collective-permute-start.4 = (bf16[1024,512]{1,0:T(8,128)(2,1)S(1)}, bf16[1024,512]{1,0:T(8,128)(2,1)S(1)}, u32[]{:S(2)}, u32[]{:S(2)}) collective-permute-start(bf16[1024,512]{1,0:T(8,128)(2,1)S(1)} %get-tuple-element.47), channel_id=1, source_target_pairs={{2,4},{3,5},{4,2},{5,3},{10,12},{11,13},{12,10},{13,11},{18,20},{1... | collective-permute-start | bytes 3145736 | tf_op jit(solution)/shard_map/ppermute | solution.py:322
  76.3 5.9 %collective-permute-done.9 = bf16[768,512]{1,0:T(8,128)(2,1)} collective-permute-done((bf16[768,512]{1,0:T(8,128)(2,1)}, bf16[768,512]{1,0:T(8,128)(2,1)}, u32[]{:S(2)}, u32[]{:S(2)}) %collective-permute-start.9) | collective-permute-done | bytes 786464 | tf_op jit(solution)/shard_map/ppermute | solution.py:359
  82.2 0.6 collective-permute-start.10
  82.8 2.4 %broadcast_select_fusion.1 = (bf16[768,512]{1,0:T(8,128)(2,1)}, bf16[768,512]{1,0:T(8,128)(2,1)S(1)}) fusion(bf16[768,512]{1,0:T(8,128)(2,1)} %collective-permute-done.9, bf16[768,512]{1,0:T(8,128)(2,1)} %collective-permute-done, pred[]{:T(512)S(6)} %eq.43), kind=kLoop, calls=%fused_computation.10 | loop fusion | flops 786432 | bytes 3145729 | tf_op jit(solution)/shard_map/jit(_where)/select_n | solution.py:370
  85.2 1.7 %bitcast_select_fusion = (bf16[768,512]{1,0:T(8,128)(2,1)S(1)}, bf16[768,512]{1,0:T(8,128)(2,1)S(1)}) fusion(bf16[768,512]{1,0:T(8,128)(2,1)} %collective-permute-done.13, bf16[768,512]{1,0:T(8,128)(2,1)} %collective-permute-done.2, bf16[2,768,512]{2,1,0:T(8,128)(2,1)S(1)} %copy-done.11, pred[]{:T(512)} %eq.38, pred[]{:T(512)S(6)} %eq.43), kind=kLoop, calls=%fused_computation.4 | loop fusion | flops 1572864 | bytes 4718594 | tf_op jit(solution)/shard_map/jit(_where)/select_n | solution.py:374
  86.9 9.8 %collective-permute-done.12 = bf16[512,768]{1,0:T(8,128)(2,1)S(1)} collective-permute-done((bf16[512,768]{1,0:T(8,128)(2,1)}, bf16[512,768]{1,0:T(8,128)(2,1)S(1)}, u32[]{:S(2)}, u32[]{:S(2)}) %collective-permute-start.12) | collective-permute-done | bytes 786464 | tf_op jit(solution)/shard_map/ppermute | solution.py:363
  96.7 2.2 %bitcast_select_fusion.2 = (bf16[512,768]{1,0:T(8,128)(2,1)S(1)}, bf16[512,768]{1,0:T(8,128)(2,1)}) fusion(bf16[512,768]{1,0:T(8,128)(2,1)S(1)} %collective-permute-done.12, bf16[512,768]{1,0:T(8,128)(2,1)} %collective-permute-done.11, bf16[2,512,768]{2,1,0:T(8,128)(2,1)S(1)} %copy-done.13, pred[]{:T(512)} %eq.38, pred[]{:T(512)S(6)} %eq.43), kind=kLoop, calls=%fused_computation.6 | loop fusion | flops 1572864 | bytes 4718594 | tf_op jit(solution)/shard_map/jit(_where)/select_n | solution.py:376
  98.9 2.3 %broadcast_select_fusion.3 = (bf16[512,768]{1,0:T(8,128)(2,1)S(1)}, bf16[512,768]{1,0:T(8,128)(2,1)}) fusion(bf16[512,768]{1,0:T(8,128)(2,1)S(1)} %collective-permute-done.10, bf16[512,768]{1,0:T(8,128)(2,1)} %collective-permute-done.1, pred[]{:T(512)S(6)} %eq.43), kind=kLoop, calls=%fused_computation.12 | loop fusion | flops 786432 | bytes 3145729 | tf_op jit(solution)/shard_map/jit(_where)/select_n | solution.py:372
  101.2 3.2 %collective-permute-done.3.ca_ref = bf16[1024,512]{1,0:T(8,128)(2,1)S(1)} collective-permute-done((bf16[1024,512]{1,0:T(8,128)(2,1)}, bf16[1024,512]{1,0:T(8,128)(2,1)S(1)}, u32[]{:S(2)}, u32[]{:S(2)}) %collective-permute-start.3) | collective-permute-done | bytes 1048608 | tf_op jit(solution)/shard_map/ppermute | solution.py:321
  104.3 3.4 %collective-permute-start.16 = (f32[3,768]{1,0:T(4,128)S(1)}, f32[3,768]{1,0:T(4,128)S(1)}, u32[]{:S(2)}, u32[]{:S(2)}) collective-permute-start(f32[3,768]{1,0:T(4,128)S(1)} %pad_maximum_fusion), channel_id=1, source_target_pairs={{0,1},{1,0},{2,5},{3,4},{4,3},{5,2},{6,7},{7,6},{8,9},{9,8},{10,13... | collective-permute-start | bytes 27656 | tf_op jit(solution)/shard_map/ppermute | solution.py:366
  107.8 1.9 %collective-permute-start.17 = (f32[3,768]{1,0:T(4,128)S(1)}, f32[3,768]{1,0:T(4,128)S(1)}, u32[]{:S(2)}, u32[]{:S(2)}) collective-permute-start(f32[3,768]{1,0:T(4,128)S(1)} %pad_maximum_fusion), channel_id=1, source_target_pairs={{2,4},{3,5},{4,2},{5,3},{10,12},{11,13},{12,10},{13,11},{18,20},{1... | collective-permute-start | bytes 27656 | tf_op jit(solution)/shard_map/ppermute | solution.py:367
  109.7 4.0 %collective-permute-start.14 = (f32[4,2]{0,1:T(2,128)S(1)}, f32[4,2]{0,1:T(2,128)S(1)}, u32[]{:S(2)}, u32[]{:S(2)}) collective-permute-start(f32[4,2]{0,1:T(2,128)S(1)} %slice.61), channel_id=1, source_target_pairs={{0,192},{4,196},{8,200},{12,204},{16,208},{20,212},{24,216},{28,22... | collective-permute-start | bytes 104 | tf_op jit(solution)/shard_map/ppermute | solution.py:338
  113.8 0.1 broadcast_select_fusion.cb_ref
  113.9 1.3 context_part.1
  115.2 1.3 copy-done.5
  116.5 0.8 copy-done.7
  117.3 0.7 collective-permute-start.15
  118.0 1.6 %copy-done.6 = f32[1024,512]{1,0:T(8,128)S(1)} copy-done((f32[1024,512]{1,0:T(8,128)S(1)}, f32[1024,512]{1,0:T(8,128)}, u32[]{:S(2)}) %copy-start.6) | copy-done | bytes 2097176
  119.6 1.0 copy-done.8
  120.7 6.8 %first_layer.1 = (bf16[1024,512]{1,0:T(8,128)(2,1)S(1)}, bf16[1024,512]{1,0:T(8,128)(2,1)S(1)}, f32[16,1024]{1,0:T(8,128)S(1)}) custom-call(bf16[16,512]{1,0:T(8,128)(2,1)S(1)} %broadcast_in_dim.43.u_ref, f32[1024,512]{1,0:T(8,128)S(1)} %copy-done.6, bf16[512,512]{1,0:T(8,128)(2,1)S(1)} %copy-done.8, bf16[2048,512]{1,0:T(8,128)(2,1)} %bitcast.13.recv_hbm), custom_call_target="tpu_custom_call" | custom-call | flops 15728640000 | bytes 8388608 | tf_op jit(solution)/shard_map/first_layer/pallas_call | solution.py:78
  127.7 1.3 collective-permute-start.19
  129.0 1.1 collective-permute-done.19
  130.1 0.1 collective-permute-done.18.other_ref
  130.2 0.4 collective-permute-start.20
  130.6 3.4 %collective-permute-start.21 = (f32[1,2]{0,1:T(2,128)S(1)}, f32[1,2]{0,1:T(2,128)S(1)}, u32[]{:S(2)}, u32[]{:S(2)}) collective-permute-start(f32[1,2]{0,1:T(2,128)S(1)} %slice_maximum_fusion), channel_id=1, source_target_pairs={{0,3},{1,2},{2,1},{3,0},{4,7},{5,6},{6,5},{7,4},{8,11},{9,10},{10,... | collective-permute-start | bytes 32 | tf_op jit(solution)/shard_map/ppermute | solution.py:343
  134.1 0.2 collective-permute-start.22
  134.3 3.8 %second_layer.1 = (bf16[1024,768]{1,0:T(8,128)(2,1)S(1)}, bf16[1024,768]{1,0:T(8,128)(2,1)S(1)}, bf16[1024,512]{1,0:T(8,128)(2,1)S(1)}) custom-call(bf16[1024,512]{1,0:T(8,128)(2,1)S(1)} %get-tuple-element.66.mine_ref, bf16[1024,512]{1,0:T(8,128)(2,1)S(1)} %collective-permute-done.18.other_ref, bf16[1024,512]{1,0:T(8,128)(2,1)S(1)} %get-tuple-element.69.pay_ref, ...), custom_call_target="tpu_custom_call" | custom-call | flops 15728640000 | bytes 12582912 | tf_op jit(solution)/shard_map/second_layer/pallas_call | solution.py:78
  138.1 2.8 %collective-permute-start.23 = (bf16[1024,512]{1,0:T(8,128)(2,1)S(1)}, bf16[1024,512]{1,0:T(8,128)(2,1)S(1)}, u32[]{:S(2)}, u32[]{:S(2)}) collective-permute-start(bf16[1024,512]{1,0:T(8,128)(2,1)S(1)} %get-tuple-element.76.mine_ref), channel_id=1, source_target_pairs={{0,4},{1,5},{2,6},{3,7},{4,0},{5,1},{6,2},{7,3},{8,12},{9,13},{10,... | collective-permute-start | bytes 3145736 | tf_op jit(solution)/shard_map/ppermute | solution.py:413
  141.5 0.5 fusion.4
  142.7 0.4 collective-permute-done.23.other_ref
  143.2 3.2 %last_layer.1 = f32[16,1024]{1,0:T(8,128)S(1)} custom-call(f32[1]{0:T(128)} %copy.14.coefficient, bf16[1024,512]{1,0:T(8,128)(2,1)S(1)} %get-tuple-element.76.mine_ref, bf16[1024,512]{1,0:T(8,128)(2,1)S(1)} %collective-permute-done.23.other_ref, bf16[1024,512]{1,0:T(8,128)(2,1)S(1)} %get-tuple-element.69.pay_ref, ...), custom_call_target="tpu_custom_call" | custom-call | flops 1879048192 | bytes 10485760 | tf_op jit(solution)/shard_map/last_layer/pallas_call | solution.py:78
  146.3 0.4 collective-permute-start.24
  146.8 0.8 collective-permute-done.24
  147.6 4.2 %collective-permute-start.26 = (f32[1,1024]{1,0:T(1,128)S(1)}, f32[1,1024]{1,0:T(1,128)S(1)}, u32[]{:S(2)}, u32[]{:S(2)}) collective-permute-start(f32[1,1024]{1,0:T(1,128)S(1)} %fusion.7), channel_id=1, source_target_pairs={{2,4},{3,5},{4,2},{5,3},{10,12},{11,13},{12,10},{13,11},{18,20},{1... | collective-permute-start | bytes 12296 | tf_op jit(solution)/shard_map/ppermute | solution.py:422
  151.8 0.3 collective-permute-start.25
  152.1 1.9 %collective-permute-done.26 = f32[1,1024]{1,0:T(1,128)S(1)} collective-permute-done((f32[1,1024]{1,0:T(1,128)S(1)}, f32[1,1024]{1,0:T(1,128)S(1)}, u32[]{:S(2)}, u32[]{:S(2)}) %collective-permute-start.26) | collective-permute-done | bytes 4128 | tf_op jit(solution)/shard_map/ppermute | solution.py:422
  154.0 2.1 %collective-permute-done.25 = f32[1,1024]{1,0:T(1,128)S(1)} collective-permute-done((f32[1,1024]{1,0:T(1,128)S(1)}, f32[1,1024]{1,0:T(1,128)S(1)}, u32[]{:S(2)}, u32[]{:S(2)}) %collective-permute-start.25) | collective-permute-done | bytes 4128 | tf_op jit(solution)/shard_map/ppermute | solution.py:421
  156.2 0.6 maximum_select_fusion
  (76 shorter events, 0.9 us)
Async XLA Ops:
  0.0 5.3 %copy-start.12 = (bf16[2,512,768]{2,1,0:T(8,128)(2,1)S(1)}, bf16[2,512,768]{2,1,0:T(8,128)(2,1)}, u32[]{:S(2)}) copy-start(bf16[2,512,768]{2,1,0:T(8,128)(2,1)} %param.19) | copy-start | bytes 4718596
  0.0 5.7 %copy-start.17 = (bf16[2,256]{1,0:T(2,128)(2,1)S(1)}, bf16[2,256]{1,0:T(2,128)(2,1)}, u32[]{:S(2)}) copy-start(bf16[2,256]{1,0:T(2,128)(2,1)} %param.12) | copy-start | bytes 3076
  1.3 26.9 %collective-permute-start = (bf16[768,512]{1,0:T(8,128)(2,1)S(1)}, bf16[768,512]{1,0:T(8,128)(2,1)}, u32[]{:S(2)}, u32[]{:S(2)}) collective-permute-start(bf16[768,512]{1,0:T(8,128)(2,1)S(1)} %dynamic-slice_bitcast_fusion.3), channel_id=1, source_target_pairs={{0,1},{1,0},{2,5},{3,4},{4,3},{5,2},{6,7},{7,6},{8,9},{9,8},{10,13... | collective-permute-start | bytes 2359304 | tf_op jit(solution)/shard_map/ppermute | solution.py:303
  5.3 22.9 %collective-permute-start.1 = (bf16[512,768]{1,0:T(8,128)(2,1)S(1)}, bf16[512,768]{1,0:T(8,128)(2,1)}, u32[]{:S(2)}, u32[]{:S(2)}) collective-permute-start(bf16[512,768]{1,0:T(8,128)(2,1)S(1)} %dynamic-slice_bitcast_fusion.2), channel_id=1, source_target_pairs={{0,1},{1,0},{2,5},{3,4},{4,3},{5,2},{6,7},{7,6},{8,9},{9,8},{10,13... | collective-permute-start | bytes 2359304 | tf_op jit(solution)/shard_map/ppermute | solution.py:304
  6.3 21.9 %all-to-all-start = ((bf16[64,2,256]{2,1,0:T(2,128)(2,1)}), bf16[64,2,256]{2,1,0:T(2,128)(2,1)S(1)}, u32[]{:S(2)}, u32[]{:S(2)}) async-start(bf16[64,2,256]{2,1,0:T(2,128)(2,1)} %broadcast_in_dim.41), calls=%async_computation | async-start | bytes 131072 | tf_op jit(solution)/shard_map/all_to_all | solution.py:308
  28.2 12.5 %copy-start.15 = (bf16[2048,256]{1,0:T(8,128)(2,1)S(1)}, bf16[2048,256]{1,0:T(8,128)(2,1)}, u32[]{:S(2)}) copy-start(bf16[2048,256]{1,0:T(8,128)(2,1)} %emb_hbm.1) | copy-start | bytes 3145732
  28.2 26.2 %copy-start.14 = (bf16[2,1024,512]{2,1,0:T(8,128)(2,1)S(1)}, bf16[2,1024,512]{2,1,0:T(8,128)(2,1)}, u32[]{:S(2)}) copy-start(bf16[2,1024,512]{2,1,0:T(8,128)(2,1)} %param.17) | copy-start | bytes 6291460
  28.2 89.1 %all-to-all-start.1 = ((bf16[256,8,512]{2,1,0:T(8,128)(2,1)}), bf16[256,8,512]{2,1,0:T(8,128)(2,1)}, u32[]{:S(2)}, u32[]{:S(2)}) async-start(bf16[256,8,512]{2,1,0:T(8,128)(2,1)} %bitcast.32), calls=%async_computation.1 | async-start | bytes 4194304 | tf_op jit(solution)/shard_map/all_to_all | solution.py:315
  41.6 5.5 %collective-permute-start.5 = (f32[32,2]{0,1:T(2,128)S(1)}, f32[32,2]{0,1:T(2,128)S(1)}, u32[]{:S(2)}, u32[]{:S(2)}) collective-permute-start(f32[32,2]{0,1:T(2,128)S(1)} %slice.52), channel_id=1, source_target_pairs={{0,4},{4,0},{8,12},{12,8},{16,20},{20,16},{24,28},{28,24},{32,36},... | collective-permute-start | bytes 776 | tf_op jit(solution)/shard_map/ppermute | solution.py:338
  43.9 21.2 %collective-permute-start.2 = (bf16[768,512]{1,0:T(8,128)(2,1)}, bf16[768,512]{1,0:T(8,128)(2,1)}, u32[]{:S(2)}, u32[]{:S(2)}) collective-permute-start(bf16[768,512]{1,0:T(8,128)(2,1)} %collective-permute-done), channel_id=1, source_target_pairs={{0,3},{1,2},{6,5},{7,4},{8,11},{9,10},{14,13},{15,12},{16,19},{17,... | collective-permute-start | bytes 2359304 | tf_op jit(solution)/shard_map/ppermute | solution.py:318
  45.2 22.8 %collective-permute-start.11 = (bf16[512,768]{1,0:T(8,128)(2,1)}, bf16[512,768]{1,0:T(8,128)(2,1)}, u32[]{:S(2)}, u32[]{:S(2)}) collective-permute-start(bf16[512,768]{1,0:T(8,128)(2,1)} %collective-permute-done.1), channel_id=1, source_target_pairs={{2,3},{3,2},{4,5},{5,4},{10,11},{11,10},{12,13},{13,12},{18,19},{1... | collective-permute-start | bytes 2359304 | tf_op jit(solution)/shard_map/ppermute | solution.py:319
  47.2 3.3 %collective-permute-start.6 = (f32[8,2]{0,1:T(2,128)S(1)}, f32[8,2]{0,1:T(2,128)S(1)}, u32[]{:S(2)}, u32[]{:S(2)}) collective-permute-start(f32[8,2]{0,1:T(2,128)S(1)} %get-tuple-element.93), channel_id=1, source_target_pairs={{0,8},{4,12},{8,0},{12,4},{16,24},{20,28},{24,16},{28,20},{32,40},... | collective-permute-start | bytes 200 | tf_op jit(solution)/shard_map/ppermute | solution.py:351
  47.9 4.0 %collective-permute-start.7 = (f32[8,2]{0,1:T(2,128)S(1)}, f32[8,2]{0,1:T(2,128)S(1)}, u32[]{:S(2)}, u32[]{:S(2)}) collective-permute-start(f32[8,2]{0,1:T(2,128)S(1)} %get-tuple-element.95), channel_id=1, source_target_pairs={{0,24},{4,28},{8,16},{12,20},{16,8},{20,12},{24,0},{28,4},{32,56},... | collective-permute-start | bytes 200 | tf_op jit(solution)/shard_map/ppermute | solution.py:351
  49.7 4.4 %collective-permute-start.8 = (f32[8,2]{0,1:T(2,128)S(1)}, f32[8,2]{0,1:T(2,128)S(1)}, u32[]{:S(2)}, u32[]{:S(2)}) collective-permute-start(f32[8,2]{0,1:T(2,128)S(1)} %get-tuple-element.94), channel_id=1, source_target_pairs={{0,16},{4,20},{8,24},{12,28},{16,0},{20,4},{24,8},{28,12},{32,48},... | collective-permute-start | bytes 200 | tf_op jit(solution)/shard_map/ppermute | solution.py:351
  54.1 28.1 %collective-permute-start.9 = (bf16[768,512]{1,0:T(8,128)(2,1)}, bf16[768,512]{1,0:T(8,128)(2,1)}, u32[]{:S(2)}, u32[]{:S(2)}) collective-permute-start(bf16[768,512]{1,0:T(8,128)(2,1)} %collective-permute-done), channel_id=1, source_target_pairs={{0,8},{1,9},{2,10},{3,11},{4,12},{5,13},{6,14},{7,15},{8,16},{9,17... | collective-permute-start | bytes 2359304 | tf_op jit(solution)/shard_map/ppermute | solution.py:359
  54.4 13.5 %copy-start.18 = (bf16[768]{0:T(1024)(128)(2,1)S(1)}, bf16[768]{0:T(1024)(128)(2,1)}, u32[]{:S(2)}) copy-start(bf16[768]{0:T(1024)(128)(2,1)} %param.21) | copy-start | bytes 4612
  54.4 13.5 %copy-start.16 = (f32[2,768]{1,0:T(2,128)S(1)}, f32[2,768]{1,0:T(2,128)}, u32[]{:S(2)}) copy-start(f32[2,768]{1,0:T(2,128)} %param.20) | copy-start | bytes 18436
  55.5 29.7 %copy-start.9 = (bf16[1024,512]{1,0:T(8,128)(2,1)}, bf16[1024,512]{1,0:T(8,128)(2,1)S(1)}, u32[]{:S(2)}) copy-start(bf16[1024,512]{1,0:T(8,128)(2,1)S(1)} %get-tuple-element.47) | copy-start | bytes 3145732
  65.1 20.1 %collective-permute-start.13 = (bf16[768,512]{1,0:T(8,128)(2,1)}, bf16[768,512]{1,0:T(8,128)(2,1)}, u32[]{:S(2)}, u32[]{:S(2)}) collective-permute-start(bf16[768,512]{1,0:T(8,128)(2,1)} %collective-permute-done.2), channel_id=1, source_target_pairs={{2,26},{3,27},{4,28},{5,29},{10,2},{11,3},{12,4},{13,5},{18,10},{1... | collective-permute-start | bytes 2359304 | tf_op jit(solution)/shard_map/ppermute | solution.py:360
  68.0 28.7 %collective-permute-start.12 = (bf16[512,768]{1,0:T(8,128)(2,1)}, bf16[512,768]{1,0:T(8,128)(2,1)S(1)}, u32[]{:S(2)}, u32[]{:S(2)}) collective-permute-start(bf16[512,768]{1,0:T(8,128)(2,1)} %collective-permute-done.11), channel_id=1, source_target_pairs={{2,26},{3,27},{4,28},{5,29},{10,2},{11,3},{12,4},{13,5},{18,10},{1... | collective-permute-start | bytes 2359304 | tf_op jit(solution)/shard_map/ppermute | solution.py:363
  70.2 15.0 %copy-start.11 = (bf16[2,768,512]{2,1,0:T(8,128)(2,1)S(1)}, bf16[2,768,512]{2,1,0:T(8,128)(2,1)}, u32[]{:S(2)}) copy-start(bf16[2,768,512]{2,1,0:T(8,128)(2,1)} %param.18) | copy-start | bytes 4718596
  70.2 34.1 %collective-permute-start.3 = (bf16[1024,512]{1,0:T(8,128)(2,1)}, bf16[1024,512]{1,0:T(8,128)(2,1)S(1)}, u32[]{:S(2)}, u32[]{:S(2)}) collective-permute-start(bf16[1024,512]{1,0:T(8,128)(2,1)} %get-tuple-element.46), channel_id=1, source_target_pairs={{0,1},{1,0},{2,5},{3,4},{4,3},{5,2},{6,7},{7,6},{8,9},{9,8},{10,13... | collective-permute-start | bytes 3145736 | tf_op jit(solution)/shard_map/ppermute | solution.py:321
  74.3 30.0 %collective-permute-start.4 = (bf16[1024,512]{1,0:T(8,128)(2,1)S(1)}, bf16[1024,512]{1,0:T(8,128)(2,1)S(1)}, u32[]{:S(2)}, u32[]{:S(2)}) collective-permute-start(bf16[1024,512]{1,0:T(8,128)(2,1)S(1)} %get-tuple-element.47), channel_id=1, source_target_pairs={{2,4},{3,5},{4,2},{5,3},{10,12},{11,13},{12,10},{13,11},{18,20},{1... | collective-permute-start | bytes 3145736 | tf_op jit(solution)/shard_map/ppermute | solution.py:322
  82.2 16.7 %collective-permute-start.10 = (bf16[512,768]{1,0:T(8,128)(2,1)}, bf16[512,768]{1,0:T(8,128)(2,1)S(1)}, u32[]{:S(2)}, u32[]{:S(2)}) collective-permute-start(bf16[512,768]{1,0:T(8,128)(2,1)} %collective-permute-done.1), channel_id=1, source_target_pairs={{0,24},{1,25},{2,10},{3,11},{4,12},{5,13},{6,30},{7,31},{8,0},{9,1... | collective-permute-start | bytes 2359304 | tf_op jit(solution)/shard_map/ppermute | solution.py:362
  85.2 11.5 %copy-start.13 = (bf16[2,512,768]{2,1,0:T(8,128)(2,1)S(1)}, bf16[2,512,768]{2,1,0:T(8,128)(2,1)}, u32[]{:S(2)}) copy-start(bf16[2,512,768]{2,1,0:T(8,128)(2,1)} %param.19) | copy-start | bytes 4718596
  98.9 14.9 %copy-start.10 = (bf16[1024,512]{1,0:T(8,128)(2,1)S(1)}, bf16[1024,512]{1,0:T(8,128)(2,1)}, u32[]{:S(2)}) copy-start(bf16[1024,512]{1,0:T(8,128)(2,1)} %copy-done.9) | copy-start | bytes 3145732
  104.3 9.6 %copy-start = (bf16[1024,512]{1,0:T(8,128)(2,1)}, bf16[1024,512]{1,0:T(8,128)(2,1)S(1)}, u32[]{:S(2)}) copy-start(bf16[1024,512]{1,0:T(8,128)(2,1)S(1)} %collective-permute-done.3.ca_ref) | copy-start | bytes 3145732
  104.3 23.1 %collective-permute-start.16 = (f32[3,768]{1,0:T(4,128)S(1)}, f32[3,768]{1,0:T(4,128)S(1)}, u32[]{:S(2)}, u32[]{:S(2)}) collective-permute-start(f32[3,768]{1,0:T(4,128)S(1)} %pad_maximum_fusion), channel_id=1, source_target_pairs={{0,1},{1,0},{2,5},{3,4},{4,3},{5,2},{6,7},{7,6},{8,9},{9,8},{10,13... | collective-permute-start | bytes 27656 | tf_op jit(solution)/shard_map/ppermute | solution.py:366
  107.8 19.7 %collective-permute-start.17 = (f32[3,768]{1,0:T(4,128)S(1)}, f32[3,768]{1,0:T(4,128)S(1)}, u32[]{:S(2)}, u32[]{:S(2)}) collective-permute-start(f32[3,768]{1,0:T(4,128)S(1)} %pad_maximum_fusion), channel_id=1, source_target_pairs={{2,4},{3,5},{4,2},{5,3},{10,12},{11,13},{12,10},{13,11},{18,20},{1... | collective-permute-start | bytes 27656 | tf_op jit(solution)/shard_map/ppermute | solution.py:367
  109.7 7.5 %collective-permute-start.14 = (f32[4,2]{0,1:T(2,128)S(1)}, f32[4,2]{0,1:T(2,128)S(1)}, u32[]{:S(2)}, u32[]{:S(2)}) collective-permute-start(f32[4,2]{0,1:T(2,128)S(1)} %slice.61), channel_id=1, source_target_pairs={{0,192},{4,196},{8,200},{12,204},{16,208},{20,212},{24,216},{28,22... | collective-permute-start | bytes 104 | tf_op jit(solution)/shard_map/ppermute | solution.py:338
  115.2 1.3 copy-start.5
  116.5 0.8 copy-start.7
  117.3 10.1 %collective-permute-start.15 = (f32[2,2]{0,1:T(2,128)S(1)}, f32[2,2]{0,1:T(2,128)S(1)}, u32[]{:S(2)}, u32[]{:S(2)}) collective-permute-start(f32[2,2]{0,1:T(2,128)S(1)} %slice.63), channel_id=1, source_target_pairs={{0,64},{4,68},{8,72},{12,76},{16,80},{20,84},{24,88},{28,92},{32,9... | collective-permute-start | bytes 56 | tf_op jit(solution)/shard_map/ppermute | solution.py:338
  118.0 1.6 %copy-start.6 = (f32[1024,512]{1,0:T(8,128)S(1)}, f32[1024,512]{1,0:T(8,128)}, u32[]{:S(2)}) copy-start(f32[1024,512]{1,0:T(8,128)} %copy-done.5) | copy-start | bytes 6291460
  119.6 1.0 copy-start.8
  120.6 13.6 %copy-start.1 = (bf16[1024,512]{1,0:T(8,128)(2,1)S(1)}, bf16[1024,512]{1,0:T(8,128)(2,1)}, u32[]{:S(2)}) copy-start(bf16[1024,512]{1,0:T(8,128)(2,1)} %copy-done) | copy-start | bytes 3145732
  120.6 13.6 %copy-start.2 = (bf16[512,768]{1,0:T(8,128)(2,1)S(1)}, bf16[512,768]{1,0:T(8,128)(2,1)}, u32[]{:S(2)}) copy-start(bf16[512,768]{1,0:T(8,128)(2,1)} %get-tuple-element.73.ub_ref) | copy-start | bytes 2359300
  120.6 13.6 %copy-start.3 = (bf16[768,512]{1,0:T(8,128)(2,1)S(1)}, bf16[768,512]{1,0:T(8,128)(2,1)}, u32[]{:S(2)}) copy-start(bf16[768,512]{1,0:T(8,128)(2,1)} %get-tuple-element.89.va_ref) | copy-start | bytes 2359300
  120.6 13.6 %copy-start.4 = (bf16[512,768]{1,0:T(8,128)(2,1)S(1)}, bf16[512,768]{1,0:T(8,128)(2,1)}, u32[]{:S(2)}) copy-start(bf16[512,768]{1,0:T(8,128)(2,1)} %get-tuple-element.72.ua_ref) | copy-start | bytes 2359300
  127.5 2.7 %collective-permute-start.18 = (bf16[1024,512]{1,0:T(8,128)(2,1)S(1)}, bf16[1024,512]{1,0:T(8,128)(2,1)S(1)}, u32[]{:S(2)}, u32[]{:S(2)}) collective-permute-start(bf16[1024,512]{1,0:T(8,128)(2,1)S(1)} %get-tuple-element.66.mine_ref), channel_id=1, source_target_pairs={{0,4},{1,5},{2,6},{3,7},{4,0},{5,1},{6,2},{7,3},{8,12},{9,13},{10,... | collective-permute-start | bytes 3145736 | tf_op jit(solution)/shard_map/ppermute | solution.py:405
  127.7 2.4 %collective-permute-start.19 = (f32[1,2]{0,1:T(2,128)S(1)}, f32[1,2]{0,1:T(2,128)S(1)}, u32[]{:S(2)}, u32[]{:S(2)}) collective-permute-start(f32[1,2]{0,1:T(2,128)S(1)} %slice.65), channel_id=1, source_target_pairs={{0,32},{4,36},{8,40},{12,44},{16,48},{20,52},{24,56},{28,60},{32,0... | collective-permute-start | bytes 32 | tf_op jit(solution)/shard_map/ppermute | solution.py:338
  130.2 7.8 %collective-permute-start.20 = (f32[1,2]{0,1:T(2,128)S(1)}, f32[1,2]{0,1:T(2,128)S(1)}, u32[]{:S(2)}, u32[]{:S(2)}) collective-permute-start(f32[1,2]{0,1:T(2,128)S(1)} %slice_maximum_fusion), channel_id=1, source_target_pairs={{0,1},{1,0},{2,3},{3,2},{4,5},{5,4},{6,7},{7,6},{8,9},{9,8},{10,11... | collective-permute-start | bytes 32 | tf_op jit(solution)/shard_map/ppermute | solution.py:343
  130.6 7.5 %collective-permute-start.21 = (f32[1,2]{0,1:T(2,128)S(1)}, f32[1,2]{0,1:T(2,128)S(1)}, u32[]{:S(2)}, u32[]{:S(2)}) collective-permute-start(f32[1,2]{0,1:T(2,128)S(1)} %slice_maximum_fusion), channel_id=1, source_target_pairs={{0,3},{1,2},{2,1},{3,0},{4,7},{5,6},{6,5},{7,4},{8,11},{9,10},{10,... | collective-permute-start | bytes 32 | tf_op jit(solution)/shard_map/ppermute | solution.py:343
  134.1 4.0 %collective-permute-start.22 = (f32[1,2]{0,1:T(2,128)S(1)}, f32[1,2]{0,1:T(2,128)S(1)}, u32[]{:S(2)}, u32[]{:S(2)}) collective-permute-start(f32[1,2]{0,1:T(2,128)S(1)} %slice_maximum_fusion), channel_id=1, source_target_pairs={{0,2},{1,3},{2,0},{3,1},{4,6},{5,7},{6,4},{7,5},{8,10},{9,11},{10,... | collective-permute-start | bytes 32 | tf_op jit(solution)/shard_map/ppermute | solution.py:343
  138.1 5.1 %collective-permute-start.23 = (bf16[1024,512]{1,0:T(8,128)(2,1)S(1)}, bf16[1024,512]{1,0:T(8,128)(2,1)S(1)}, u32[]{:S(2)}, u32[]{:S(2)}) collective-permute-start(bf16[1024,512]{1,0:T(8,128)(2,1)S(1)} %get-tuple-element.76.mine_ref), channel_id=1, source_target_pairs={{0,4},{1,5},{2,6},{3,7},{4,0},{5,1},{6,2},{7,3},{8,12},{9,13},{10,... | collective-permute-start | bytes 3145736 | tf_op jit(solution)/shard_map/ppermute | solution.py:413
  146.3 1.3 collective-permute-start.24
  147.6 6.4 %collective-permute-start.26 = (f32[1,1024]{1,0:T(1,128)S(1)}, f32[1,1024]{1,0:T(1,128)S(1)}, u32[]{:S(2)}, u32[]{:S(2)}) collective-permute-start(f32[1,1024]{1,0:T(1,128)S(1)} %fusion.7), channel_id=1, source_target_pairs={{2,4},{3,5},{4,2},{5,3},{10,12},{11,13},{12,10},{13,11},{18,20},{1... | collective-permute-start | bytes 12296 | tf_op jit(solution)/shard_map/ppermute | solution.py:422
  151.8 4.3 %collective-permute-start.25 = (f32[1,1024]{1,0:T(1,128)S(1)}, f32[1,1024]{1,0:T(1,128)S(1)}, u32[]{:S(2)}, u32[]{:S(2)}) collective-permute-start(f32[1,1024]{1,0:T(1,128)S(1)} %fusion.7), channel_id=1, source_target_pairs={{0,1},{1,0},{2,5},{3,4},{4,3},{5,2},{6,7},{7,6},{8,9},{9,8},{10,13... | collective-permute-start | bytes 12296 | tf_op jit(solution)/shard_map/ppermute | solution.py:421

commit v9 on v8

--- a/solution.py
+++ b/solution.py
@@ -293,8 +293,9 @@
     def stay(x, c):
         return x, c
 
-    y_up = group_perm(groups, stay, turn=lambda x, c: 1)
-    y_mixed = group_perm(groups, stay, turn=lambda x, c: -1 if is_home(x, c) else 1)
+    y_split = group_perm(groups, stay, turn=lambda x, c: -1 if is_home(x, c) else 1)
+    y_mirror = group_perm(groups, stay, turn=lambda x, c: 1 if is_home(x, c) else -1)
+    y_up = group_perm(groups, stay, is_away, lambda x, c: 1)
     y_down = group_perm(groups, stay, is_away, lambda x, c: -1)
     odd_y = lax.axis_index("shard") // 2 % 2
     persons, _, kept = kept_part_entries.shape
@@ -317,10 +318,6 @@
 
     v_far = move(v_near, perm=home_on)
     u_far = move(u_near, perm=away_swap)
-    v_far, ctx_out, ctx_away = lax.optimization_barrier((v_far, ctx_own, ctx_away))
-    ctx_a = move(ctx_away, perm=ctx_near)
-    ctx_b = move(ctx_out, perm=ctx_far)
-    ctx_a, ctx_b = lax.optimization_barrier((ctx_a, ctx_b))
 
     all_scores = jnp.einsum(
         "ue,ie->ui", users.reshape(persons, -1), catalog_embedding, preferred_element_type=F32
@@ -355,16 +352,18 @@
     best = over_y(halve(best, hops[5]))
 
     small = jnp.concatenate([interaction_offset, final_projection[None, :].astype(F32)], 0)
-    best, v_near_on = lax.optimization_barrier((best, v_near))
-    v_near_y = move(v_near_on, perm=y_up)
+    best, v_near_on, ctx_out, ctx_away = lax.optimization_barrier(
+        (best, v_near, ctx_own, ctx_away)
+    )
+    ctx_a = move(ctx_away, perm=ctx_near)
+    ctx_b = move(ctx_out, perm=ctx_far)
+    ctx_a, ctx_b = lax.optimization_barrier((ctx_a, ctx_b))
+    v_near_y = move(v_near_on, perm=y_split)
     v_far_y = move(v_far, perm=y_down)
     v_near_y, u_near_on = lax.optimization_barrier((v_near_y, u_near))
-    u_near_y = move(u_near_on, perm=y_mixed)
-    u_far_y = move(u_far, perm=y_down)
-    ctx_a, best, small = lax.optimization_barrier((ctx_a, best, small))
-    best = halve(best, hops[2])
-    small_a = move(small, perm=to_near)
-    small_b = move(small, perm=ctx_far)
+    u_near_y = move(u_near_on, perm=y_mirror)
+    u_far_y = move(u_far, perm=y_up)
+    ctx_b = jnp.where(home, ctx_own, ctx_b)
     even = odd_y == 0
     v0_a = jnp.where(even, v_near, v_near_y)
     v1_a = jnp.where(even, v_near_y, v_near)
@@ -374,8 +373,12 @@
     v1_b = jnp.where(home, lowrank_v_matrix[1], jnp.where(even, v_far_y, v_far))
     u0_b = jnp.where(home, lowrank_u_matrix[0], jnp.where(even, u_far, u_far_y))
     u1_b = jnp.where(home, lowrank_u_matrix[1], jnp.where(even, u_far_y, u_far))
-    ctx_b = jnp.where(home, ctx_own, ctx_b)
-    ctx_a, u0_a, u0_b, u1_a, u1_b = lax.optimization_barrier((ctx_a, u0_a, u0_b, u1_a, u1_b))
+    ctx_a, u0_a, u0_b, u1_a, u1_b, best, small = lax.optimization_barrier(
+        (ctx_a, u0_a, u0_b, u1_a, u1_b, best, small)
+    )
+    best = halve(best, hops[2])
+    small_a = move(small, perm=to_near)
+    small_b = move(small, perm=ctx_far)
 
     emb_other = lax.dynamic_index_in_dim(users, me ^ 1, 0, False)
     query = lax.dynamic_slice_in_dim(jnp.where(home, person_embedding, emb_other), parity, 1, 0)

time: 157 us -> 168 us (1.070)
  waiting for transfers between devices: 40.1 us -> 44.6 us
  starting transfers between devices: 72.1 us -> 75.7 us
  local copies, waits for them, and re-layouts: 9.2 us -> 11 us
    ppermute x3, waiting for transfers between devices: 15.7 us -> 0.01 us  [the longest x1 0.01 us: on_device(): u_far_y = move(u_far, perm=y_up)]
    ppermute x1, waiting for transfers between devices: 3.17 us -> 12.2 us  [on_device(): ctx_a = move(ctx_away, perm=ctx_near)]
    ppermute x1, waiting for transfers between devices: 9.62 us -> 16.5 us  [on_device(): v_far = move(v_near, perm=home_on)]
    ppermute x1, starting transfers between devices: 3.41 us -> 7.86 us  [on_device(): small_a = move(small, perm=to_near)]
    ppermute x1, waiting for transfers between devices: 0.01 us -> 2.84 us  [on_device(): u_far = move(u_near, perm=away_swap)]
    unnamed x38 -> x34, local copies, waits for them, and re-layouts: 4.77 us -> 6 us
  transfers between devices with their start and end apart: 29 -> 29, of which waited for: 13 -> 12; matrix products, arithmetic and copies ran while one was open for 8% -> 9% of each run, Pallas kernels for 13% -> 12%
where the time goes in v9:
time: 168 us
  starting transfers between devices  75.7 us (45%)
  waiting for transfers between devices  44.6 us (27%)
  Pallas kernels  23 us (14%)
  other arithmetic  11.1 us (7%)
  local copies, waits for them, and re-layouts  11 us (7%)
  between operations  1.69 us (1%)
    ppermute x1, waiting for transfers between devices, on_device(): v_far = move(v_near, perm=home_on)  16.5 us
    pallas_call x4, Pallas kernels, call(): pl.pallas_call(kernel, in_specs=[SMEM] * len(scalars) + [VMEM] * len(arra...  15 us
    all_to_all x1, starting transfers between devices, on_device(): recv = lax.all_to_all(parcel, AXES, split_axis=0, concat_axis=0, tiled=True)  12.5 us
    ppermute x1, waiting for transfers between devices, on_device(): ctx_a = move(ctx_away, perm=ctx_near)  12.2 us
    all_to_all x1, starting transfers between devices, on_device(): lax.all_to_all(users, 'shard', split_axis=0, concat_axis=0, tiled=True)  11.8 us
    ppermute x4, starting transfers between devices, halve(): return jnp.maximum(best[:half], lax.ppermute(best[half:], 'shard', pairs))  8.46 us
    pallas_call x1, Pallas kernels, pick_rows(): pl.pallas_call(pick_kernel, in_specs=[VMEM, VMEM, ANY, ANY], out_specs=AN...  8.01 us
    ppermute x1, starting transfers between devices, on_device(): small_a = move(small, perm=to_near)  7.86 us
  transfers between devices with their start and end apart: 29, of which 12 were waited for; matrix products, arithmetic and copies ran while one was open for 9% of the time, Pallas kernels for 12%

profile of v9, /device:TPU:1, one launch (start us, length us, event | category | flops | bytes accessed | tf_op | source)
XLA Modules:
  0.0 167.6 jit_solution(7948388609612143561)
XLA Ops:
  0.0 1.3 dynamic-slice_bitcast_fusion.3
  1.3 4.0 %collective-permute-start = (bf16[768,512]{1,0:T(8,128)(2,1)S(1)}, bf16[768,512]{1,0:T(8,128)(2,1)}, u32[]{:S(2)}, u32[]{:S(2)}) collective-permute-start(bf16[768,512]{1,0:T(8,128)(2,1)S(1)} %dynamic-slice_bitcast_fusion.3), channel_id=1, source_target_pairs={{0,1},{1,0},{2,5},{3,4},{4,3},{5,2},{6,7},{7,6},{8,9},{9,8},{10,13... | collective-permute-start | bytes 2359304 | tf_op jit(solution)/shard_map/ppermute | solution.py:304
  5.3 0.3 collective-permute-start.1
  5.7 0.7 broadcast_in_dim.41
  6.3 11.8 %all-to-all-start = ((bf16[64,2,256]{2,1,0:T(2,128)(2,1)}), bf16[64,2,256]{2,1,0:T(2,128)(2,1)S(1)}, u32[]{:S(2)}, u32[]{:S(2)}) async-start(bf16[64,2,256]{2,1,0:T(2,128)(2,1)} %broadcast_in_dim.41), calls=%async_computation | async-start | bytes 131072 | tf_op jit(solution)/shard_map/all_to_all | solution.py:309
  18.1 0.7 fusion.2
  18.8 8.0 %pick_rows.1 = bf16[32,2,32,512]{3,2,1,0:T(8,128)(2,1)} custom-call(s32[8,128]{1,0:T(8,128)} %bitcast.33, s32[1,128]{1,0:T(1,128)} %bitcast.34, bf16[2048,256]{1,0:T(8,128)(2,1)} %emb_hbm.1, bf16[2048,768]{1,0:T(8,128)(2,1)} %attr_hbm.1), custom_call_target="tpu_custom_call" | custom-call | flops 4294967296 | bytes 6291456 | tf_op jit(solution)/shard_map/pick_rows/pallas_call | solution.py:144
  26.9 1.3 all-to-all-done
  28.2 12.5 %all-to-all-start.1 = ((bf16[256,8,512]{2,1,0:T(8,128)(2,1)}), bf16[256,8,512]{2,1,0:T(8,128)(2,1)}, u32[]{:S(2)}, u32[]{:S(2)}) async-start(bf16[256,8,512]{2,1,0:T(8,128)(2,1)} %bitcast.32), calls=%async_computation.1 | async-start | bytes 4194304 | tf_op jit(solution)/shard_map/all_to_all | solution.py:316
  40.8 0.6 convolution_reduce_fusion
  41.3 0.1 broadcast_in_dim.45
  41.6 0.1 select_reduce_fusion
  41.7 2.3 %collective-permute-start.2 = (f32[32,2]{0,1:T(2,128)S(1)}, f32[32,2]{0,1:T(2,128)S(1)}, u32[]{:S(2)}, u32[]{:S(2)}) collective-permute-start(f32[32,2]{0,1:T(2,128)S(1)} %slice.52), channel_id=1, source_target_pairs={{0,4},{4,0},{8,12},{12,8},{16,20},{20,16},{24,28},{28,24},{32,36},... | collective-permute-start | bytes 776 | tf_op jit(solution)/shard_map/ppermute | solution.py:335
  44.0 1.7 %dynamic-slice_bitcast_fusion = (bf16[1024,512]{1,0:T(8,128)(2,1)S(1)}, bf16[1024,512]{1,0:T(8,128)(2,1)S(1)}) fusion(bf16[2,1024,512]{2,1,0:T(8,128)(2,1)} %param.17, s32[]{:T(128)S(6)} %select_n.190, s32[]{:T(128)S(6)} %select_n.185), kind=kLoop, calls=%fused_computation.1 | loop fusion | bytes 4194312 | tf_op jit(solution)/shard_map/jit(dynamic_index_in_dim)/squeeze | solution.py:307
  45.7 1.9 %collective-permute-start.10 = (bf16[512,768]{1,0:T(8,128)(2,1)}, bf16[512,768]{1,0:T(8,128)(2,1)}, u32[]{:S(2)}, u32[]{:S(2)}) collective-permute-start(bf16[512,768]{1,0:T(8,128)(2,1)} %collective-permute-done.1), channel_id=1, source_target_pairs={{2,3},{3,2},{4,5},{5,4},{10,11},{11,10},{12,13},{13,12},{18,19},{1... | collective-permute-start | bytes 2359304 | tf_op jit(solution)/shard_map/ppermute | solution.py:320
  47.6 1.3 collective-permute-start.12
  49.0 0.7 collective-permute-start.3
  49.8 1.8 %collective-permute-start.4 = (f32[8,2]{0,1:T(2,128)S(1)}, f32[8,2]{0,1:T(2,128)S(1)}, u32[]{:S(2)}, u32[]{:S(2)}) collective-permute-start(f32[8,2]{0,1:T(2,128)S(1)} %get-tuple-element.91), channel_id=1, source_target_pairs={{0,24},{4,28},{8,16},{12,20},{16,8},{20,12},{24,0},{28,4},{32,56},... | collective-permute-start | bytes 200 | tf_op jit(solution)/shard_map/ppermute | solution.py:348
  51.5 0.8 collective-permute-start.5
  52.3 1.5 collective-permute-done.4
  53.8 2.1 %collective-permute-done.5 = f32[8,2]{0,1:T(2,128)S(1)} collective-permute-done((f32[8,2]{0,1:T(2,128)S(1)}, f32[8,2]{0,1:T(2,128)S(1)}, u32[]{:S(2)}, u32[]{:S(2)}) %collective-permute-start.5) | collective-permute-done | bytes 96 | tf_op jit(solution)/shard_map/ppermute | solution.py:348
  55.9 0.4 collective-permute-start.8
  56.2 3.7 %collective-permute-start.6 = (bf16[1024,512]{1,0:T(8,128)(2,1)S(1)}, bf16[1024,512]{1,0:T(8,128)(2,1)S(1)}, u32[]{:S(2)}, u32[]{:S(2)}) collective-permute-start(bf16[1024,512]{1,0:T(8,128)(2,1)S(1)} %get-tuple-element.44), channel_id=1, source_target_pairs={{0,1},{1,0},{2,5},{3,4},{4,3},{5,2},{6,7},{7,6},{8,9},{9,8},{10,13... | collective-permute-start | bytes 3145736 | tf_op jit(solution)/shard_map/ppermute | solution.py:358
  59.9 2.5 %collective-permute-start.7 = (bf16[1024,512]{1,0:T(8,128)(2,1)S(1)}, bf16[1024,512]{1,0:T(8,128)(2,1)}, u32[]{:S(2)}, u32[]{:S(2)}) collective-permute-start(bf16[1024,512]{1,0:T(8,128)(2,1)S(1)} %get-tuple-element.45), channel_id=1, source_target_pairs={{2,4},{3,5},{4,2},{5,3},{10,12},{11,13},{12,10},{13,11},{18,20},{1... | collective-permute-start | bytes 3145736 | tf_op jit(solution)/shard_map/ppermute | solution.py:359
  62.6 2.8 %collective-permute-done.10 = bf16[512,768]{1,0:T(8,128)(2,1)} collective-permute-done((bf16[512,768]{1,0:T(8,128)(2,1)}, bf16[512,768]{1,0:T(8,128)(2,1)}, u32[]{:S(2)}, u32[]{:S(2)}) %collective-permute-start.10) | collective-permute-done | bytes 786464 | tf_op jit(solution)/shard_map/ppermute | solution.py:320
  65.4 1.9 %collective-permute-start.11 = (bf16[512,768]{1,0:T(8,128)(2,1)}, bf16[512,768]{1,0:T(8,128)(2,1)S(1)}, u32[]{:S(2)}, u32[]{:S(2)}) collective-permute-start(bf16[512,768]{1,0:T(8,128)(2,1)} %collective-permute-done.10), channel_id=1, source_target_pairs={{2,10},{3,11},{4,12},{5,13},{10,18},{11,19},{12,20},{13,21},{18,26... | collective-permute-start | bytes 2359304 | tf_op jit(solution)/shard_map/ppermute | solution.py:365
  67.4 16.5 %collective-permute-done.12 = bf16[768,512]{1,0:T(8,128)(2,1)} collective-permute-done((bf16[768,512]{1,0:T(8,128)(2,1)}, bf16[768,512]{1,0:T(8,128)(2,1)}, u32[]{:S(2)}, u32[]{:S(2)}) %collective-permute-start.12) | collective-permute-done | bytes 786464 | tf_op jit(solution)/shard_map/ppermute | solution.py:319
  83.9 1.9 %collective-permute-start.13 = (bf16[768,512]{1,0:T(8,128)(2,1)}, bf16[768,512]{1,0:T(8,128)(2,1)S(1)}, u32[]{:S(2)}, u32[]{:S(2)}) collective-permute-start(bf16[768,512]{1,0:T(8,128)(2,1)} %collective-permute-done.12), channel_id=1, source_target_pairs={{2,26},{3,27},{4,28},{5,29},{10,2},{11,3},{12,4},{13,5},{18,10},{1... | collective-permute-start | bytes 2359304 | tf_op jit(solution)/shard_map/ppermute | solution.py:362
  85.9 2.4 %broadcast_select_fusion.1 = (bf16[768,512]{1,0:T(8,128)(2,1)}, bf16[768,512]{1,0:T(8,128)(2,1)S(1)}) fusion(bf16[768,512]{1,0:T(8,128)(2,1)} %collective-permute-done.8, bf16[768,512]{1,0:T(8,128)(2,1)} %collective-permute-done, pred[]{:T(512)S(6)} %eq.43), kind=kLoop, calls=%fused_computation.10 | loop fusion | flops 786432 | bytes 3145729 | tf_op jit(solution)/shard_map/jit(_where)/select_n | solution.py:369
  88.4 12.2 %collective-permute-done.6.ca_ref = bf16[1024,512]{1,0:T(8,128)(2,1)S(1)} collective-permute-done((bf16[1024,512]{1,0:T(8,128)(2,1)S(1)}, bf16[1024,512]{1,0:T(8,128)(2,1)S(1)}, u32[]{:S(2)}, u32[]{:S(2)}) %collective-permute-start.6) | collective-permute-done | bytes 1048608 | tf_op jit(solution)/shard_map/ppermute | solution.py:358
  100.6 1.0 copy-done
  101.6 1.3 broadcast_select_fusion.cb_ref
  102.9 1.4 bitcast_select_fusion.2
  104.4 0.2 copy-done.12
  104.5 2.2 %bitcast_select_fusion = (bf16[768,512]{1,0:T(8,128)(2,1)}, bf16[768,512]{1,0:T(8,128)(2,1)S(1)}) fusion(bf16[768,512]{1,0:T(8,128)(2,1)S(1)} %collective-permute-done.13, bf16[768,512]{1,0:T(8,128)(2,1)} %collective-permute-done.12, bf16[2,768,512]{2,1,0:T(8,128)(2,1)S(1)} %copy-done.12, pred[]{:T(512)} %eq.38, pred[]{:T(512)S(6)} %eq.43), kind=kLoop, calls=%fused_computation.4 | loop fusion | flops 1572864 | bytes 4718594 | tf_op jit(solution)/shard_map/jit(_where)/select_n | solution.py:373
  106.8 2.3 %broadcast_select_fusion.3 = (bf16[512,768]{1,0:T(8,128)(2,1)S(1)}, bf16[512,768]{1,0:T(8,128)(2,1)}) fusion(bf16[512,768]{1,0:T(8,128)(2,1)S(1)} %collective-permute-done.9, bf16[512,768]{1,0:T(8,128)(2,1)} %collective-permute-done.1, pred[]{:T(512)S(6)} %eq.43), kind=kLoop, calls=%fused_computation.12 | loop fusion | flops 786432 | bytes 3145729 | tf_op jit(solution)/shard_map/jit(_where)/select_n | solution.py:371
  109.0 7.9 %collective-permute-start.16 = (f32[3,768]{1,0:T(4,128)S(1)}, f32[3,768]{1,0:T(4,128)S(1)}, u32[]{:S(2)}, u32[]{:S(2)}) collective-permute-start(f32[3,768]{1,0:T(4,128)S(1)} %pad_maximum_fusion), channel_id=1, source_target_pairs={{0,1},{1,0},{2,5},{3,4},{4,3},{5,2},{6,7},{7,6},{8,9},{9,8},{10,13... | collective-permute-start | bytes 27656 | tf_op jit(solution)/shard_map/ppermute | solution.py:380
  116.9 1.9 %collective-permute-start.17 = (f32[3,768]{1,0:T(4,128)S(1)}, f32[3,768]{1,0:T(4,128)S(1)}, u32[]{:S(2)}, u32[]{:S(2)}) collective-permute-start(f32[3,768]{1,0:T(4,128)S(1)} %pad_maximum_fusion), channel_id=1, source_target_pairs={{2,4},{3,5},{4,2},{5,3},{10,12},{11,13},{12,10},{13,11},{18,20},{1... | collective-permute-start | bytes 27656 | tf_op jit(solution)/shard_map/ppermute | solution.py:381
  118.9 2.9 %collective-permute-start.14 = (f32[4,2]{0,1:T(2,128)S(1)}, f32[4,2]{0,1:T(2,128)S(1)}, u32[]{:S(2)}, u32[]{:S(2)}) collective-permute-start(f32[4,2]{0,1:T(2,128)S(1)} %slice.61), channel_id=1, source_target_pairs={{0,192},{4,196},{8,200},{12,204},{16,208},{20,212},{24,216},{28,22... | collective-permute-start | bytes 104 | tf_op jit(solution)/shard_map/ppermute | solution.py:335
  121.8 1.3 context_part.1
  123.1 1.4 copy-done.6
  124.4 0.8 copy-done.8
  125.3 3.3 %collective-permute-start.15 = (f32[2,2]{0,1:T(2,128)S(1)}, f32[2,2]{0,1:T(2,128)S(1)}, u32[]{:S(2)}, u32[]{:S(2)}) collective-permute-start(f32[2,2]{0,1:T(2,128)S(1)} %slice.63), channel_id=1, source_target_pairs={{0,64},{4,68},{8,72},{12,76},{16,80},{20,84},{24,88},{28,92},{32,9... | collective-permute-start | bytes 56 | tf_op jit(solution)/shard_map/ppermute | solution.py:335
  128.6 1.6 copy-done.7
  130.2 1.0 copy-done.9
  131.2 6.8 %first_layer.1 = (bf16[1024,512]{1,0:T(8,128)(2,1)S(1)}, bf16[1024,512]{1,0:T(8,128)(2,1)S(1)}, f32[16,1024]{1,0:T(8,128)S(1)}) custom-call(bf16[16,512]{1,0:T(8,128)(2,1)S(1)} %broadcast_in_dim.43.u_ref, f32[1024,512]{1,0:T(8,128)S(1)} %copy-done.7, bf16[512,512]{1,0:T(8,128)(2,1)S(1)} %copy-done.9, bf16[2048,512]{1,0:T(8,128)(2,1)} %bitcast.13.recv_hbm), custom_call_target="tpu_custom_call" | custom-call | flops 15728640000 | bytes 8388608 | tf_op jit(solution)/shard_map/first_layer/pallas_call | solution.py:78
  138.1 0.1 collective-permute-start.18
  138.4 2.4 %collective-permute-done.19 = f32[1,2]{0,1:T(2,128)S(1)} collective-permute-done((f32[1,2]{0,1:T(2,128)S(1)}, f32[1,2]{0,1:T(2,128)S(1)}, u32[]{:S(2)}, u32[]{:S(2)}) %collective-permute-start.19) | collective-permute-done | bytes 40 | tf_op jit(solution)/shard_map/ppermute | solution.py:335
  140.8 0.1 collective-permute-done.18.other_ref
  140.9 0.6 collective-permute-start.20
  141.5 3.5 %collective-permute-start.21 = (f32[1,2]{0,1:T(2,128)S(1)}, f32[1,2]{0,1:T(2,128)S(1)}, u32[]{:S(2)}, u32[]{:S(2)}) collective-permute-start(f32[1,2]{0,1:T(2,128)S(1)} %slice_maximum_fusion), channel_id=1, source_target_pairs={{0,3},{1,2},{2,1},{3,0},{4,7},{5,6},{6,5},{7,4},{8,11},{9,10},{10,... | collective-permute-start | bytes 32 | tf_op jit(solution)/shard_map/ppermute | solution.py:340
  144.9 0.1 collective-permute-start.22
  145.1 3.8 %second_layer.1 = (bf16[1024,768]{1,0:T(8,128)(2,1)S(1)}, bf16[1024,768]{1,0:T(8,128)(2,1)S(1)}, bf16[1024,512]{1,0:T(8,128)(2,1)S(1)}) custom-call(bf16[1024,512]{1,0:T(8,128)(2,1)S(1)} %get-tuple-element.62.mine_ref, bf16[1024,512]{1,0:T(8,128)(2,1)S(1)} %collective-permute-done.18.other_ref, bf16[1024,512]{1,0:T(8,128)(2,1)S(1)} %get-tuple-element.65.pay_ref, ...), custom_call_target="tpu_custom_call" | custom-call | flops 15728640000 | bytes 12582912 | tf_op jit(solution)/shard_map/second_layer/pallas_call | solution.py:78
  148.9 2.9 %collective-permute-start.23 = (bf16[1024,512]{1,0:T(8,128)(2,1)S(1)}, bf16[1024,512]{1,0:T(8,128)(2,1)S(1)}, u32[]{:S(2)}, u32[]{:S(2)}) collective-permute-start(bf16[1024,512]{1,0:T(8,128)(2,1)S(1)} %get-tuple-element.72.mine_ref), channel_id=1, source_target_pairs={{0,4},{1,5},{2,6},{3,7},{4,0},{5,1},{6,2},{7,3},{8,12},{9,13},{10,... | collective-permute-start | bytes 3145736 | tf_op jit(solution)/shard_map/ppermute | solution.py:416
  152.4 0.5 fusion.4
  153.5 0.6 collective-permute-done.23.other_ref
  154.1 3.1 %last_layer.1 = f32[16,1024]{1,0:T(8,128)S(1)} custom-call(f32[1]{0:T(128)} %copy.14.coefficient, bf16[1024,512]{1,0:T(8,128)(2,1)S(1)} %get-tuple-element.72.mine_ref, bf16[1024,512]{1,0:T(8,128)(2,1)S(1)} %collective-permute-done.23.other_ref, bf16[1024,512]{1,0:T(8,128)(2,1)S(1)} %get-tuple-element.65.pay_ref, ...), custom_call_target="tpu_custom_call" | custom-call | flops 1879048192 | bytes 10485760 | tf_op jit(solution)/shard_map/last_layer/pallas_call | solution.py:78
  157.2 0.4 collective-permute-start.24
  157.6 0.8 collective-permute-done.24
  158.4 4.2 %collective-permute-start.26 = (f32[1,1024]{1,0:T(1,128)S(1)}, f32[1,1024]{1,0:T(1,128)S(1)}, u32[]{:S(2)}, u32[]{:S(2)}) collective-permute-start(f32[1,1024]{1,0:T(1,128)S(1)} %fusion.7), channel_id=1, source_target_pairs={{2,4},{3,5},{4,2},{5,3},{10,12},{11,13},{12,10},{13,11},{18,20},{1... | collective-permute-start | bytes 12296 | tf_op jit(solution)/shard_map/ppermute | solution.py:425
  162.6 0.1 collective-permute-start.25
  162.7 2.1 %collective-permute-done.26 = f32[1,1024]{1,0:T(1,128)S(1)} collective-permute-done((f32[1,1024]{1,0:T(1,128)S(1)}, f32[1,1024]{1,0:T(1,128)S(1)}, u32[]{:S(2)}, u32[]{:S(2)}) %collective-permute-start.26) | collective-permute-done | bytes 4128 | tf_op jit(solution)/shard_map/ppermute | solution.py:425
  164.8 2.1 %collective-permute-done.25 = f32[1,1024]{1,0:T(1,128)S(1)} collective-permute-done((f32[1,1024]{1,0:T(1,128)S(1)}, f32[1,1024]{1,0:T(1,128)S(1)}, u32[]{:S(2)}, u32[]{:S(2)}) %collective-permute-start.25) | collective-permute-done | bytes 4128 | tf_op jit(solution)/shard_map/ppermute | solution.py:424
  167.0 0.6 maximum_select_fusion
  (72 shorter events, 0.9 us)
Async XLA Ops:
  0.0 5.3 %copy-start.10 = (bf16[2,512,768]{2,1,0:T(8,128)(2,1)S(1)}, bf16[2,512,768]{2,1,0:T(8,128)(2,1)}, u32[]{:S(2)}) copy-start(bf16[2,512,768]{2,1,0:T(8,128)(2,1)} %param.19) | copy-start | bytes 4718596
  0.0 5.7 %copy-start.15 = (bf16[2,256]{1,0:T(2,128)(2,1)S(1)}, bf16[2,256]{1,0:T(2,128)(2,1)}, u32[]{:S(2)}) copy-start(bf16[2,256]{1,0:T(2,128)(2,1)} %param.12) | copy-start | bytes 3076
  1.3 26.9 %collective-permute-start = (bf16[768,512]{1,0:T(8,128)(2,1)S(1)}, bf16[768,512]{1,0:T(8,128)(2,1)}, u32[]{:S(2)}, u32[]{:S(2)}) collective-permute-start(bf16[768,512]{1,0:T(8,128)(2,1)S(1)} %dynamic-slice_bitcast_fusion.3), channel_id=1, source_target_pairs={{0,1},{1,0},{2,5},{3,4},{4,3},{5,2},{6,7},{7,6},{8,9},{9,8},{10,13... | collective-permute-start | bytes 2359304 | tf_op jit(solution)/shard_map/ppermute | solution.py:304
  5.3 22.9 %collective-permute-start.1 = (bf16[512,768]{1,0:T(8,128)(2,1)S(1)}, bf16[512,768]{1,0:T(8,128)(2,1)}, u32[]{:S(2)}, u32[]{:S(2)}) collective-permute-start(bf16[512,768]{1,0:T(8,128)(2,1)S(1)} %dynamic-slice_bitcast_fusion.2), channel_id=1, source_target_pairs={{0,1},{1,0},{2,5},{3,4},{4,3},{5,2},{6,7},{7,6},{8,9},{9,8},{10,13... | collective-permute-start | bytes 2359304 | tf_op jit(solution)/shard_map/ppermute | solution.py:305
  6.3 21.9 %all-to-all-start = ((bf16[64,2,256]{2,1,0:T(2,128)(2,1)}), bf16[64,2,256]{2,1,0:T(2,128)(2,1)S(1)}, u32[]{:S(2)}, u32[]{:S(2)}) async-start(bf16[64,2,256]{2,1,0:T(2,128)(2,1)} %broadcast_in_dim.41), calls=%async_computation | async-start | bytes 131072 | tf_op jit(solution)/shard_map/all_to_all | solution.py:309
  28.2 12.5 %copy-start.13 = (bf16[2048,256]{1,0:T(8,128)(2,1)S(1)}, bf16[2048,256]{1,0:T(8,128)(2,1)}, u32[]{:S(2)}) copy-start(bf16[2048,256]{1,0:T(8,128)(2,1)} %emb_hbm.1) | copy-start | bytes 3145732
  28.2 97.0 %all-to-all-start.1 = ((bf16[256,8,512]{2,1,0:T(8,128)(2,1)}), bf16[256,8,512]{2,1,0:T(8,128)(2,1)}, u32[]{:S(2)}, u32[]{:S(2)}) async-start(bf16[256,8,512]{2,1,0:T(8,128)(2,1)} %bitcast.32), calls=%async_computation.1 | async-start | bytes 4194304 | tf_op jit(solution)/shard_map/all_to_all | solution.py:316
  41.7 20.8 %copy-start.16 = (bf16[768]{0:T(1024)(128)(2,1)S(1)}, bf16[768]{0:T(1024)(128)(2,1)}, u32[]{:S(2)}) copy-start(bf16[768]{0:T(1024)(128)(2,1)} %param.21) | copy-start | bytes 4612
  41.7 20.8 %copy-start.14 = (f32[2,768]{1,0:T(2,128)S(1)}, f32[2,768]{1,0:T(2,128)}, u32[]{:S(2)}) copy-start(f32[2,768]{1,0:T(2,128)} %param.20) | copy-start | bytes 18436
  41.7 7.2 %collective-permute-start.2 = (f32[32,2]{0,1:T(2,128)S(1)}, f32[32,2]{0,1:T(2,128)S(1)}, u32[]{:S(2)}, u32[]{:S(2)}) collective-permute-start(f32[32,2]{0,1:T(2,128)S(1)} %slice.52), channel_id=1, source_target_pairs={{0,4},{4,0},{8,12},{12,8},{16,20},{20,16},{24,28},{28,24},{32,36},... | collective-permute-start | bytes 776 | tf_op jit(solution)/shard_map/ppermute | solution.py:335
  45.7 19.7 %collective-permute-start.10 = (bf16[512,768]{1,0:T(8,128)(2,1)}, bf16[512,768]{1,0:T(8,128)(2,1)}, u32[]{:S(2)}, u32[]{:S(2)}) collective-permute-start(bf16[512,768]{1,0:T(8,128)(2,1)} %collective-permute-done.1), channel_id=1, source_target_pairs={{2,3},{3,2},{4,5},{5,4},{10,11},{11,10},{12,13},{13,12},{18,19},{1... | collective-permute-start | bytes 2359304 | tf_op jit(solution)/shard_map/ppermute | solution.py:320
  47.6 36.3 %collective-permute-start.12 = (bf16[768,512]{1,0:T(8,128)(2,1)}, bf16[768,512]{1,0:T(8,128)(2,1)}, u32[]{:S(2)}, u32[]{:S(2)}) collective-permute-start(bf16[768,512]{1,0:T(8,128)(2,1)} %collective-permute-done), channel_id=1, source_target_pairs={{0,3},{1,2},{6,5},{7,4},{8,11},{9,10},{14,13},{15,12},{16,19},{17,... | collective-permute-start | bytes 2359304 | tf_op jit(solution)/shard_map/ppermute | solution.py:319
  49.0 3.3 %collective-permute-start.3 = (f32[8,2]{0,1:T(2,128)S(1)}, f32[8,2]{0,1:T(2,128)S(1)}, u32[]{:S(2)}, u32[]{:S(2)}) collective-permute-start(f32[8,2]{0,1:T(2,128)S(1)} %get-tuple-element.89), channel_id=1, source_target_pairs={{0,8},{4,12},{8,0},{12,4},{16,24},{20,28},{24,16},{28,20},{32,40},... | collective-permute-start | bytes 200 | tf_op jit(solution)/shard_map/ppermute | solution.py:348
  49.8 4.0 %collective-permute-start.4 = (f32[8,2]{0,1:T(2,128)S(1)}, f32[8,2]{0,1:T(2,128)S(1)}, u32[]{:S(2)}, u32[]{:S(2)}) collective-permute-start(f32[8,2]{0,1:T(2,128)S(1)} %get-tuple-element.91), channel_id=1, source_target_pairs={{0,24},{4,28},{8,16},{12,20},{16,8},{20,12},{24,0},{28,4},{32,56},... | collective-permute-start | bytes 200 | tf_op jit(solution)/shard_map/ppermute | solution.py:348
  51.5 4.3 %collective-permute-start.5 = (f32[8,2]{0,1:T(2,128)S(1)}, f32[8,2]{0,1:T(2,128)S(1)}, u32[]{:S(2)}, u32[]{:S(2)}) collective-permute-start(f32[8,2]{0,1:T(2,128)S(1)} %get-tuple-element.90), channel_id=1, source_target_pairs={{0,16},{4,20},{8,24},{12,28},{16,0},{20,4},{24,8},{28,12},{32,48},... | collective-permute-start | bytes 200 | tf_op jit(solution)/shard_map/ppermute | solution.py:348
  55.9 30.0 %collective-permute-start.8 = (bf16[768,512]{1,0:T(8,128)(2,1)}, bf16[768,512]{1,0:T(8,128)(2,1)}, u32[]{:S(2)}, u32[]{:S(2)}) collective-permute-start(bf16[768,512]{1,0:T(8,128)(2,1)} %collective-permute-done), channel_id=1, source_target_pairs={{0,24},{1,25},{2,10},{3,11},{4,12},{5,13},{6,30},{7,31},{8,0},{9,1... | collective-permute-start | bytes 2359304 | tf_op jit(solution)/shard_map/ppermute | solution.py:361
  56.2 44.3 %collective-permute-start.6 = (bf16[1024,512]{1,0:T(8,128)(2,1)S(1)}, bf16[1024,512]{1,0:T(8,128)(2,1)S(1)}, u32[]{:S(2)}, u32[]{:S(2)}) collective-permute-start(bf16[1024,512]{1,0:T(8,128)(2,1)S(1)} %get-tuple-element.44), channel_id=1, source_target_pairs={{0,1},{1,0},{2,5},{3,4},{4,3},{5,2},{6,7},{7,6},{8,9},{9,8},{10,13... | collective-permute-start | bytes 3145736 | tf_op jit(solution)/shard_map/ppermute | solution.py:358
  59.9 41.6 %collective-permute-start.7 = (bf16[1024,512]{1,0:T(8,128)(2,1)S(1)}, bf16[1024,512]{1,0:T(8,128)(2,1)}, u32[]{:S(2)}, u32[]{:S(2)}) collective-permute-start(bf16[1024,512]{1,0:T(8,128)(2,1)S(1)} %get-tuple-element.45), channel_id=1, source_target_pairs={{2,4},{3,5},{4,2},{5,3},{10,12},{11,13},{12,10},{13,11},{18,20},{1... | collective-permute-start | bytes 3145736 | tf_op jit(solution)/shard_map/ppermute | solution.py:359
  65.4 37.5 %collective-permute-start.11 = (bf16[512,768]{1,0:T(8,128)(2,1)}, bf16[512,768]{1,0:T(8,128)(2,1)S(1)}, u32[]{:S(2)}, u32[]{:S(2)}) collective-permute-start(bf16[512,768]{1,0:T(8,128)(2,1)} %collective-permute-done.10), channel_id=1, source_target_pairs={{2,10},{3,11},{4,12},{5,13},{10,18},{11,19},{12,20},{13,21},{18,26... | collective-permute-start | bytes 2359304 | tf_op jit(solution)/shard_map/ppermute | solution.py:365
  83.9 20.4 %collective-permute-start.13 = (bf16[768,512]{1,0:T(8,128)(2,1)}, bf16[768,512]{1,0:T(8,128)(2,1)S(1)}, u32[]{:S(2)}, u32[]{:S(2)}) collective-permute-start(bf16[768,512]{1,0:T(8,128)(2,1)} %collective-permute-done.12), channel_id=1, source_target_pairs={{2,26},{3,27},{4,28},{5,29},{10,2},{11,3},{12,4},{13,5},{18,10},{1... | collective-permute-start | bytes 2359304 | tf_op jit(solution)/shard_map/ppermute | solution.py:362
  85.9 20.9 %collective-permute-start.9 = (bf16[512,768]{1,0:T(8,128)(2,1)}, bf16[512,768]{1,0:T(8,128)(2,1)S(1)}, u32[]{:S(2)}, u32[]{:S(2)}) collective-permute-start(bf16[512,768]{1,0:T(8,128)(2,1)} %collective-permute-done.1), channel_id=1, source_target_pairs={{0,8},{1,9},{2,26},{3,27},{4,28},{5,29},{6,14},{7,15},{8,16},{9,17... | collective-permute-start | bytes 2359304 | tf_op jit(solution)/shard_map/ppermute | solution.py:364
  88.4 14.5 %copy-start.11 = (bf16[2,512,768]{2,1,0:T(8,128)(2,1)S(1)}, bf16[2,512,768]{2,1,0:T(8,128)(2,1)}, u32[]{:S(2)}) copy-start(bf16[2,512,768]{2,1,0:T(8,128)(2,1)} %param.19) | copy-start | bytes 4718596
  100.6 1.0 copy-start
  102.9 1.6 copy-start.12
  106.7 15.0 %copy-start.1 = (bf16[1024,512]{1,0:T(8,128)(2,1)S(1)}, bf16[1024,512]{1,0:T(8,128)(2,1)}, u32[]{:S(2)}) copy-start(bf16[1024,512]{1,0:T(8,128)(2,1)} %copy-done) | copy-start | bytes 3145732
  109.0 29.1 %collective-permute-start.16 = (f32[3,768]{1,0:T(4,128)S(1)}, f32[3,768]{1,0:T(4,128)S(1)}, u32[]{:S(2)}, u32[]{:S(2)}) collective-permute-start(f32[3,768]{1,0:T(4,128)S(1)} %pad_maximum_fusion), channel_id=1, source_target_pairs={{0,1},{1,0},{2,5},{3,4},{4,3},{5,2},{6,7},{7,6},{8,9},{9,8},{10,13... | collective-permute-start | bytes 27656 | tf_op jit(solution)/shard_map/ppermute | solution.py:380
  116.9 21.2 %collective-permute-start.17 = (f32[3,768]{1,0:T(4,128)S(1)}, f32[3,768]{1,0:T(4,128)S(1)}, u32[]{:S(2)}, u32[]{:S(2)}) collective-permute-start(f32[3,768]{1,0:T(4,128)S(1)} %pad_maximum_fusion), channel_id=1, source_target_pairs={{2,4},{3,5},{4,2},{5,3},{10,12},{11,13},{12,10},{13,11},{18,20},{1... | collective-permute-start | bytes 27656 | tf_op jit(solution)/shard_map/ppermute | solution.py:381
  118.9 6.4 %collective-permute-start.14 = (f32[4,2]{0,1:T(2,128)S(1)}, f32[4,2]{0,1:T(2,128)S(1)}, u32[]{:S(2)}, u32[]{:S(2)}) collective-permute-start(f32[4,2]{0,1:T(2,128)S(1)} %slice.61), channel_id=1, source_target_pairs={{0,192},{4,196},{8,200},{12,204},{16,208},{20,212},{24,216},{28,22... | collective-permute-start | bytes 104 | tf_op jit(solution)/shard_map/ppermute | solution.py:335
  123.1 1.4 copy-start.6
  124.4 0.8 copy-start.8
  125.3 12.8 %collective-permute-start.15 = (f32[2,2]{0,1:T(2,128)S(1)}, f32[2,2]{0,1:T(2,128)S(1)}, u32[]{:S(2)}, u32[]{:S(2)}) collective-permute-start(f32[2,2]{0,1:T(2,128)S(1)} %slice.63), channel_id=1, source_target_pairs={{0,64},{4,68},{8,72},{12,76},{16,80},{20,84},{24,88},{28,92},{32,9... | collective-permute-start | bytes 56 | tf_op jit(solution)/shard_map/ppermute | solution.py:335
  128.6 1.6 copy-start.7
  130.2 1.0 copy-start.9
  131.2 13.8 %copy-start.2 = (bf16[1024,512]{1,0:T(8,128)(2,1)S(1)}, bf16[1024,512]{1,0:T(8,128)(2,1)}, u32[]{:S(2)}) copy-start(bf16[1024,512]{1,0:T(8,128)(2,1)} %copy-done) | copy-start | bytes 3145732
  131.2 13.8 %copy-start.3 = (bf16[768,512]{1,0:T(8,128)(2,1)S(1)}, bf16[768,512]{1,0:T(8,128)(2,1)}, u32[]{:S(2)}) copy-start(bf16[768,512]{1,0:T(8,128)(2,1)} %get-tuple-element.79.vb_ref) | copy-start | bytes 2359300
  131.2 13.8 %copy-start.4 = (bf16[768,512]{1,0:T(8,128)(2,1)S(1)}, bf16[768,512]{1,0:T(8,128)(2,1)}, u32[]{:S(2)}) copy-start(bf16[768,512]{1,0:T(8,128)(2,1)} %get-tuple-element.85.va_ref) | copy-start | bytes 2359300
  131.2 13.8 %copy-start.5 = (bf16[512,768]{1,0:T(8,128)(2,1)S(1)}, bf16[512,768]{1,0:T(8,128)(2,1)}, u32[]{:S(2)}) copy-start(bf16[512,768]{1,0:T(8,128)(2,1)} %get-tuple-element.68.ua_ref) | copy-start | bytes 2359300
  138.1 2.7 %collective-permute-start.18 = (bf16[1024,512]{1,0:T(8,128)(2,1)S(1)}, bf16[1024,512]{1,0:T(8,128)(2,1)S(1)}, u32[]{:S(2)}, u32[]{:S(2)}) collective-permute-start(bf16[1024,512]{1,0:T(8,128)(2,1)S(1)} %get-tuple-element.62.mine_ref), channel_id=1, source_target_pairs={{0,4},{1,5},{2,6},{3,7},{4,0},{5,1},{6,2},{7,3},{8,12},{9,13},{10,... | collective-permute-start | bytes 3145736 | tf_op jit(solution)/shard_map/ppermute | solution.py:408
  138.3 2.4 %collective-permute-start.19 = (f32[1,2]{0,1:T(2,128)S(1)}, f32[1,2]{0,1:T(2,128)S(1)}, u32[]{:S(2)}, u32[]{:S(2)}) collective-permute-start(f32[1,2]{0,1:T(2,128)S(1)} %slice.65), channel_id=1, source_target_pairs={{0,32},{4,36},{8,40},{12,44},{16,48},{20,52},{24,56},{28,60},{32,0... | collective-permute-start | bytes 32 | tf_op jit(solution)/shard_map/ppermute | solution.py:335
  140.9 7.9 %collective-permute-start.20 = (f32[1,2]{0,1:T(2,128)S(1)}, f32[1,2]{0,1:T(2,128)S(1)}, u32[]{:S(2)}, u32[]{:S(2)}) collective-permute-start(f32[1,2]{0,1:T(2,128)S(1)} %slice_maximum_fusion), channel_id=1, source_target_pairs={{0,1},{1,0},{2,3},{3,2},{4,5},{5,4},{6,7},{7,6},{8,9},{9,8},{10,11... | collective-permute-start | bytes 32 | tf_op jit(solution)/shard_map/ppermute | solution.py:340
  141.5 7.4 %collective-permute-start.21 = (f32[1,2]{0,1:T(2,128)S(1)}, f32[1,2]{0,1:T(2,128)S(1)}, u32[]{:S(2)}, u32[]{:S(2)}) collective-permute-start(f32[1,2]{0,1:T(2,128)S(1)} %slice_maximum_fusion), channel_id=1, source_target_pairs={{0,3},{1,2},{2,1},{3,0},{4,7},{5,6},{6,5},{7,4},{8,11},{9,10},{10,... | collective-permute-start | bytes 32 | tf_op jit(solution)/shard_map/ppermute | solution.py:340
  144.9 3.9 %collective-permute-start.22 = (f32[1,2]{0,1:T(2,128)S(1)}, f32[1,2]{0,1:T(2,128)S(1)}, u32[]{:S(2)}, u32[]{:S(2)}) collective-permute-start(f32[1,2]{0,1:T(2,128)S(1)} %slice_maximum_fusion), channel_id=1, source_target_pairs={{0,2},{1,3},{2,0},{3,1},{4,6},{5,7},{6,4},{7,5},{8,10},{9,11},{10,... | collective-permute-start | bytes 32 | tf_op jit(solution)/shard_map/ppermute | solution.py:340
  148.9 5.2 %collective-permute-start.23 = (bf16[1024,512]{1,0:T(8,128)(2,1)S(1)}, bf16[1024,512]{1,0:T(8,128)(2,1)S(1)}, u32[]{:S(2)}, u32[]{:S(2)}) collective-permute-start(bf16[1024,512]{1,0:T(8,128)(2,1)S(1)} %get-tuple-element.72.mine_ref), channel_id=1, source_target_pairs={{0,4},{1,5},{2,6},{3,7},{4,0},{5,1},{6,2},{7,3},{8,12},{9,13},{10,... | collective-permute-start | bytes 3145736 | tf_op jit(solution)/shard_map/ppermute | solution.py:416
  157.2 1.3 collective-permute-start.24
  158.4 6.4 %collective-permute-start.26 = (f32[1,1024]{1,0:T(1,128)S(1)}, f32[1,1024]{1,0:T(1,128)S(1)}, u32[]{:S(2)}, u32[]{:S(2)}) collective-permute-start(f32[1,1024]{1,0:T(1,128)S(1)} %fusion.7), channel_id=1, source_target_pairs={{2,4},{3,5},{4,2},{5,3},{10,12},{11,13},{12,10},{13,11},{18,20},{1... | collective-permute-start | bytes 12296 | tf_op jit(solution)/shard_map/ppermute | solution.py:425
  162.6 4.3 %collective-permute-start.25 = (f32[1,1024]{1,0:T(1,128)S(1)}, f32[1,1024]{1,0:T(1,128)S(1)}, u32[]{:S(2)}, u32[]{:S(2)}) collective-permute-start(f32[1,1024]{1,0:T(1,128)S(1)} %fusion.7), channel_id=1, source_target_pairs={{0,1},{1,0},{2,5},{3,4},{4,3},{5,2},{6,7},{7,6},{8,9},{9,8},{10,13... | collective-permute-start | bytes 12296 | tf_op jit(solution)/shard_map/ppermute | solution.py:424

commit v10 on v8

--- a/solution.py
+++ b/solution.py
@@ -11,7 +11,7 @@
 F32 = jnp.float32
 AXES = ("shard", "tp")
 VMEM = pl.BlockSpec(memory_space=pltpu.VMEM)
-PICK, CTX, FIRST, SECOND = 4096, 6000, 15000, 15000
+PICK, CTX, FIRST, SECOND = 4096, 11000, 15000, 15000
 SMEM = pl.BlockSpec(memory_space=pltpu.SMEM)
 ANY = pl.BlockSpec(memory_space=pl.ANY)
 
@@ -293,8 +293,9 @@
     def stay(x, c):
         return x, c
 
-    y_up = group_perm(groups, stay, turn=lambda x, c: 1)
-    y_mixed = group_perm(groups, stay, turn=lambda x, c: -1 if is_home(x, c) else 1)
+    y_split = group_perm(groups, stay, turn=lambda x, c: -1 if is_home(x, c) else 1)
+    y_mirror = group_perm(groups, stay, turn=lambda x, c: 1 if is_home(x, c) else -1)
+    y_up = group_perm(groups, stay, is_away, lambda x, c: 1)
     y_down = group_perm(groups, stay, is_away, lambda x, c: -1)
     odd_y = lax.axis_index("shard") // 2 % 2
     persons, _, kept = kept_part_entries.shape
@@ -302,8 +303,6 @@
     me = lax.axis_index("shard")
     v_near = move(lax.dynamic_index_in_dim(lowrank_v_matrix, odd_y, 0, False), perm=to_near)
     u_near = move(lax.dynamic_index_in_dim(lowrank_u_matrix, odd_y, 0, False), perm=to_near)
-    ctx_own = lax.dynamic_index_in_dim(pair_attributes, parity, 0, False)
-    ctx_away = lax.dynamic_index_in_dim(pair_attributes, 1 - parity, 0, False)
     users = jnp.broadcast_to(person_embedding[None], (shards, *person_embedding.shape))
     users = lax.all_to_all(users, "shard", split_axis=0, concat_axis=0, tiled=True)
 
@@ -317,9 +316,11 @@
 
     v_far = move(v_near, perm=home_on)
     u_far = move(u_near, perm=away_swap)
-    v_far, ctx_out, ctx_away = lax.optimization_barrier((v_far, ctx_own, ctx_away))
+    v_far, pair_attributes = lax.optimization_barrier((v_far, pair_attributes))
+    ctx_own = lax.dynamic_index_in_dim(pair_attributes, parity, 0, False)
+    ctx_away = lax.dynamic_index_in_dim(pair_attributes, 1 - parity, 0, False)
     ctx_a = move(ctx_away, perm=ctx_near)
-    ctx_b = move(ctx_out, perm=ctx_far)
+    ctx_b = move(ctx_own, perm=ctx_far)
     ctx_a, ctx_b = lax.optimization_barrier((ctx_a, ctx_b))
 
     all_scores = jnp.einsum(
@@ -355,12 +356,11 @@
     best = over_y(halve(best, hops[5]))
 
     small = jnp.concatenate([interaction_offset, final_projection[None, :].astype(F32)], 0)
-    best, v_near_on = lax.optimization_barrier((best, v_near))
-    v_near_y = move(v_near_on, perm=y_up)
+    v_near_y = move(v_near, perm=y_split)
     v_far_y = move(v_far, perm=y_down)
     v_near_y, u_near_on = lax.optimization_barrier((v_near_y, u_near))
-    u_near_y = move(u_near_on, perm=y_mixed)
-    u_far_y = move(u_far, perm=y_down)
+    u_near_y = move(u_near_on, perm=y_mirror)
+    u_far_y = move(u_far, perm=y_up)
     ctx_a, best, small = lax.optimization_barrier((ctx_a, best, small))
     best = halve(best, hops[2])
     small_a = move(small, perm=to_near)

time: 157 us -> 161 us (1.025)
  starting transfers between devices: 72.1 us -> 76.8 us
    ppermute x4, waiting for transfers between devices: 15.7 us -> 3.73 us  [the longest x1 3.73 us: on_device(): u_far_y = move(u_far, perm=y_up)]
    ppermute x3, waiting for transfers between devices: 3.63 us -> 14.8 us  [over_y(): got = lax.ppermute(best[block * n:(block + 1) * n], 'shard', pairs)]
    ppermute x1, waiting for transfers between devices: 9.62 us -> 0.01 us  [on_device(): v_far = move(v_near, perm=home_on)]
    ppermute x1, waiting for transfers between devices: 0.01 us -> 5.09 us  [on_device(): v_far_y = move(v_far, perm=y_down)]
    ppermute x1, waiting for transfers between devices: 3.17 us -> 7.94 us  [on_device(): ctx_a = move(ctx_away, perm=ctx_near)]
    all_to_all x1, starting transfers between devices: 12.3 us -> 15.7 us  [on_device(): recv = lax.all_to_all(parcel, AXES, split_axis=0, concat_axis=0, tiled=True)]
    ppermute x4, starting transfers between devices: 5 us -> 8.16 us  [the longest x1 3.46 us: on_device(): ctx_b = move(ctx_own, perm=ctx_far)]
    ppermute x4, starting transfers between devices: 8.26 us -> 5.42 us  [halve(): return jnp.maximum(best[:half], lax.ppermute(best[half:], 'shard', pairs))]
  transfers between devices with their start and end apart: 29 -> 29, of which waited for: 13 -> 12; matrix products, arithmetic and copies ran while one was open for 8% -> 7% of each run, Pallas kernels for 13% -> 12%
where the time goes in v10:
time: 161 us; the launch traced here: 160 us
  starting transfers between devices  76.8 us (48%)
  waiting for transfers between devices  40.9 us (25%)
  Pallas kernels  23 us (14%)
  other arithmetic  8.63 us (5%)
  local copies, waits for them, and re-layouts  8.35 us (5%)
  between operations  1.67 us (1%)
    all_to_all x1, starting transfers between devices, on_device(): recv = lax.all_to_all(parcel, AXES, split_axis=0, concat_axis=0, tiled=True)  15.7 us
    pallas_call x4, Pallas kernels, call(): pl.pallas_call(kernel, in_specs=[SMEM] * len(scalars) + [VMEM] * len(arra...  14.9 us
    ppermute x3, waiting for transfers between devices, over_y(): got = lax.ppermute(best[block * n:(block + 1) * n], 'shard', pairs)  14.8 us
    all_to_all x1, starting transfers between devices, on_device(): lax.all_to_all(users, 'shard', split_axis=0, concat_axis=0, tiled=True)  11.8 us
    pallas_call x1, Pallas kernels, pick_rows(): pl.pallas_call(pick_kernel, in_specs=[VMEM, VMEM, ANY, ANY], out_specs=AN...  8.03 us
    ppermute x1, waiting for transfers between devices, on_device(): ctx_a = move(ctx_away, perm=ctx_near)  7.94 us
    ppermute x4, starting transfers between devices, halve(): return jnp.maximum(best[:half], lax.ppermute(best[half:], 'shard', pairs))  5.42 us
    ppermute x1, waiting for transfers between devices, on_device(): v_far_y = move(v_far, perm=y_down)  5.09 us
  transfers between devices with their start and end apart: 29, of which 12 were waited for; matrix products, arithmetic and copies ran while one was open for 7% of the time, Pallas kernels for 12%

profile of v10, /device:TPU:1, one launch (start us, length us, event | category | flops | bytes accessed | tf_op | source)
XLA Modules:
  0.0 159.9 jit_solution(4412427100032264146)
XLA Ops:
  0.0 1.3 dynamic-slice_bitcast_fusion.3
  1.3 4.0 %collective-permute-start = (bf16[768,512]{1,0:T(8,128)(2,1)S(1)}, bf16[768,512]{1,0:T(8,128)(2,1)}, u32[]{:S(2)}, u32[]{:S(2)}) collective-permute-start(bf16[768,512]{1,0:T(8,128)(2,1)S(1)} %dynamic-slice_bitcast_fusion.3), channel_id=1, source_target_pairs={{0,1},{1,0},{2,5},{3,4},{4,3},{5,2},{6,7},{7,6},{8,9},{9,8},{10,13... | collective-permute-start | bytes 2359304 | tf_op jit(solution)/shard_map/ppermute | solution.py:304
  5.3 0.3 collective-permute-start.1
  5.7 0.7 broadcast_in_dim.41
  6.3 11.8 %all-to-all-start = ((bf16[64,2,256]{2,1,0:T(2,128)(2,1)}), bf16[64,2,256]{2,1,0:T(2,128)(2,1)S(1)}, u32[]{:S(2)}, u32[]{:S(2)}) async-start(bf16[64,2,256]{2,1,0:T(2,128)(2,1)} %broadcast_in_dim.41), calls=%async_computation | async-start | bytes 131072 | tf_op jit(solution)/shard_map/all_to_all | solution.py:307
  18.2 0.7 fusion.2
  18.9 8.0 %pick_rows.1 = bf16[32,2,32,512]{3,2,1,0:T(8,128)(2,1)} custom-call(s32[8,128]{1,0:T(8,128)} %bitcast.33, s32[1,128]{1,0:T(1,128)} %bitcast.34, bf16[2048,256]{1,0:T(8,128)(2,1)} %emb_hbm.1, bf16[2048,768]{1,0:T(8,128)(2,1)} %attr_hbm.1), custom_call_target="tpu_custom_call" | custom-call | flops 4294967296 | bytes 6291456 | tf_op jit(solution)/shard_map/pick_rows/pallas_call | solution.py:144
  26.9 0.1 iota_compare_fusion
  27.0 1.2 all-to-all-done
  28.2 0.3 collective-permute-start.9
  28.5 1.3 collective-permute-start.2
  29.9 15.7 %all-to-all-start.1 = ((bf16[256,8,512]{2,1,0:T(8,128)(2,1)}), bf16[256,8,512]{2,1,0:T(8,128)(2,1)}, u32[]{:S(2)}, u32[]{:S(2)}) async-start(bf16[256,8,512]{2,1,0:T(8,128)(2,1)} %bitcast.32), calls=%async_computation.1 | async-start | bytes 4194304 | tf_op jit(solution)/shard_map/all_to_all | solution.py:314
  45.6 0.6 convolution_reduce_fusion
  46.1 0.1 broadcast_in_dim.45
  46.3 3.3 %collective-permute-start.11 = (bf16[512,768]{1,0:T(8,128)(2,1)}, bf16[512,768]{1,0:T(8,128)(2,1)S(1)}, u32[]{:S(2)}, u32[]{:S(2)}) collective-permute-start(bf16[512,768]{1,0:T(8,128)(2,1)} %collective-permute-done.1), channel_id=1, source_target_pairs={{2,3},{3,2},{4,5},{5,4},{10,11},{11,10},{12,13},{13,12},{18,19},{1... | collective-permute-start | bytes 2359304 | tf_op jit(solution)/shard_map/ppermute | solution.py:318
  49.6 0.1 select_reduce_fusion
  49.7 0.1 slice.52
  49.9 1.1 collective-permute-done.5
  51.0 2.5 %collective-permute-start.10 = (bf16[512,768]{1,0:T(8,128)(2,1)}, bf16[512,768]{1,0:T(8,128)(2,1)S(1)}, u32[]{:S(2)}, u32[]{:S(2)}) collective-permute-start(bf16[512,768]{1,0:T(8,128)(2,1)} %collective-permute-done.1), channel_id=1, source_target_pairs={{0,8},{1,9},{2,26},{3,27},{4,28},{5,29},{6,14},{7,15},{8,16},{9,17... | collective-permute-start | bytes 2359304 | tf_op jit(solution)/shard_map/ppermute | solution.py:362
  53.5 0.8 collective-permute-start.7
  54.3 14.8 %collective-permute-done.6 = f32[8,2]{0,1:T(2,128)S(1)} collective-permute-done((f32[8,2]{0,1:T(2,128)S(1)}, f32[8,2]{0,1:T(2,128)S(1)}, u32[]{:S(2)}, u32[]{:S(2)}) %collective-permute-start.6) | collective-permute-done | bytes 96 | tf_op jit(solution)/shard_map/ppermute | solution.py:352
  69.1 2.8 %collective-permute-start.8 = (f32[8,2]{0,1:T(2,128)S(1)}, f32[8,2]{0,1:T(2,128)S(1)}, u32[]{:S(2)}, u32[]{:S(2)}) collective-permute-start(f32[8,2]{0,1:T(2,128)S(1)} %get-tuple-element.88), channel_id=1, source_target_pairs={{0,16},{4,20},{8,24},{12,28},{16,0},{20,4},{24,8},{28,12},{32,48},... | collective-permute-start | bytes 200 | tf_op jit(solution)/shard_map/ppermute | solution.py:352
  71.9 1.9 %collective-permute-start.12 = (bf16[512,768]{1,0:T(8,128)(2,1)S(1)}, bf16[512,768]{1,0:T(8,128)(2,1)S(1)}, u32[]{:S(2)}, u32[]{:S(2)}) collective-permute-start(bf16[512,768]{1,0:T(8,128)(2,1)S(1)} %collective-permute-done.11), channel_id=1, source_target_pairs={{2,10},{3,11},{4,12},{5,13},{10,18},{11,19},{12,20},{13,21},{18,26... | collective-permute-start | bytes 2359304 | tf_op jit(solution)/shard_map/ppermute | solution.py:363
  73.9 0.1 dynamic-slice_bitcast_fusion
  74.1 3.4 %collective-permute-start.3 = (bf16[1024,512]{1,0:T(8,128)(2,1)S(1)}, bf16[1024,512]{1,0:T(8,128)(2,1)S(1)}, u32[]{:S(2)}, u32[]{:S(2)}) collective-permute-start(bf16[1024,512]{1,0:T(8,128)(2,1)S(1)} %get-tuple-element.82), channel_id=1, source_target_pairs={{0,1},{1,0},{2,5},{3,4},{4,3},{5,2},{6,7},{7,6},{8,9},{9,8},{10,13... | collective-permute-start | bytes 3145736 | tf_op jit(solution)/shard_map/ppermute | solution.py:322
  77.5 3.5 %collective-permute-start.4 = (bf16[1024,512]{1,0:T(8,128)(2,1)S(1)}, bf16[1024,512]{1,0:T(8,128)(2,1)S(1)}, u32[]{:S(2)}, u32[]{:S(2)}) collective-permute-start(bf16[1024,512]{1,0:T(8,128)(2,1)S(1)} %get-tuple-element.81), channel_id=1, source_target_pairs={{2,4},{3,5},{4,2},{5,3},{10,12},{11,13},{12,10},{13,11},{18,20},{1... | collective-permute-start | bytes 3145736 | tf_op jit(solution)/shard_map/ppermute | solution.py:323
  81.0 3.5 %collective-permute-start.13 = (bf16[768,512]{1,0:T(8,128)(2,1)}, bf16[768,512]{1,0:T(8,128)(2,1)S(1)}, u32[]{:S(2)}, u32[]{:S(2)}) collective-permute-start(bf16[768,512]{1,0:T(8,128)(2,1)} %collective-permute-done.2), channel_id=1, source_target_pairs={{2,26},{3,27},{4,28},{5,29},{10,2},{11,3},{12,4},{13,5},{18,10},{1... | collective-permute-start | bytes 2359304 | tf_op jit(solution)/shard_map/ppermute | solution.py:360
  84.4 2.4 %broadcast_select_fusion.1 = (bf16[768,512]{1,0:T(8,128)(2,1)}, bf16[768,512]{1,0:T(8,128)(2,1)S(1)}) fusion(bf16[768,512]{1,0:T(8,128)(2,1)} %collective-permute-done.9, bf16[768,512]{1,0:T(8,128)(2,1)} %collective-permute-done, pred[]{:T(512)S(6)} %eq.43), kind=kLoop, calls=%fused_computation.10 | loop fusion | flops 786432 | bytes 3145729 | tf_op jit(solution)/shard_map/jit(_where)/select_n | solution.py:370
  86.9 2.3 %broadcast_select_fusion.3 = (bf16[512,768]{1,0:T(8,128)(2,1)S(1)}, bf16[512,768]{1,0:T(8,128)(2,1)}) fusion(bf16[512,768]{1,0:T(8,128)(2,1)S(1)} %collective-permute-done.10, bf16[512,768]{1,0:T(8,128)(2,1)} %collective-permute-done.1, pred[]{:T(512)S(6)} %eq.43), kind=kLoop, calls=%fused_computation.12 | loop fusion | flops 786432 | bytes 3145729 | tf_op jit(solution)/shard_map/jit(_where)/select_n | solution.py:372
  89.2 3.7 %collective-permute-done.12 = bf16[512,768]{1,0:T(8,128)(2,1)S(1)} collective-permute-done((bf16[512,768]{1,0:T(8,128)(2,1)S(1)}, bf16[512,768]{1,0:T(8,128)(2,1)S(1)}, u32[]{:S(2)}, u32[]{:S(2)}) %collective-permute-start.12) | collective-permute-done | bytes 786464 | tf_op jit(solution)/shard_map/ppermute | solution.py:363
  92.9 0.2 bitcast_select_fusion.2
  93.1 5.1 %collective-permute-done.13 = bf16[768,512]{1,0:T(8,128)(2,1)S(1)} collective-permute-done((bf16[768,512]{1,0:T(8,128)(2,1)}, bf16[768,512]{1,0:T(8,128)(2,1)S(1)}, u32[]{:S(2)}, u32[]{:S(2)}) %collective-permute-start.13) | collective-permute-done | bytes 786464 | tf_op jit(solution)/shard_map/ppermute | solution.py:360
  98.2 2.2 %bitcast_select_fusion = (bf16[768,512]{1,0:T(8,128)(2,1)}, bf16[768,512]{1,0:T(8,128)(2,1)S(1)}) fusion(bf16[768,512]{1,0:T(8,128)(2,1)S(1)} %collective-permute-done.13, bf16[768,512]{1,0:T(8,128)(2,1)} %collective-permute-done.2, bf16[2,768,512]{2,1,0:T(8,128)(2,1)S(1)} %copy-done.11, pred[]{:T(512)} %eq.38, pred[]{:T(512)S(6)} %eq.43), kind=kLoop, calls=%fused_computation.4 | loop fusion | flops 1572864 | bytes 4718594 | tf_op jit(solution)/shard_map/jit(_where)/select_n | solution.py:374
  100.4 7.9 %collective-permute-done.3.ca_ref = bf16[1024,512]{1,0:T(8,128)(2,1)S(1)} collective-permute-done((bf16[1024,512]{1,0:T(8,128)(2,1)S(1)}, bf16[1024,512]{1,0:T(8,128)(2,1)S(1)}, u32[]{:S(2)}, u32[]{:S(2)}) %collective-permute-start.3) | collective-permute-done | bytes 1048608 | tf_op jit(solution)/shard_map/ppermute | solution.py:322
  108.3 1.9 %collective-permute-start.16 = (f32[3,768]{1,0:T(4,128)S(1)}, f32[3,768]{1,0:T(4,128)S(1)}, u32[]{:S(2)}, u32[]{:S(2)}) collective-permute-start(f32[3,768]{1,0:T(4,128)S(1)} %pad_maximum_fusion), channel_id=1, source_target_pairs={{0,1},{1,0},{2,5},{3,4},{4,3},{5,2},{6,7},{7,6},{8,9},{9,8},{10,13... | collective-permute-start | bytes 27656 | tf_op jit(solution)/shard_map/ppermute | solution.py:366
  110.2 2.4 %collective-permute-start.17 = (f32[3,768]{1,0:T(4,128)S(1)}, f32[3,768]{1,0:T(4,128)S(1)}, u32[]{:S(2)}, u32[]{:S(2)}) collective-permute-start(f32[3,768]{1,0:T(4,128)S(1)} %pad_maximum_fusion), channel_id=1, source_target_pairs={{2,4},{3,5},{4,2},{5,3},{10,12},{11,13},{12,10},{13,11},{18,20},{1... | collective-permute-start | bytes 27656 | tf_op jit(solution)/shard_map/ppermute | solution.py:367
  112.8 3.3 %collective-permute-start.14 = (f32[4,2]{0,1:T(2,128)S(1)}, f32[4,2]{0,1:T(2,128)S(1)}, u32[]{:S(2)}, u32[]{:S(2)}) collective-permute-start(f32[4,2]{0,1:T(2,128)S(1)} %slice.61), channel_id=1, source_target_pairs={{0,192},{4,196},{8,200},{12,204},{16,208},{20,212},{24,216},{28,22... | collective-permute-start | bytes 104 | tf_op jit(solution)/shard_map/ppermute | solution.py:339
  116.1 0.1 broadcast_select_fusion.cb_ref
  116.2 1.3 context_part.1
  117.5 1.4 copy-done.5
  118.9 0.8 copy-done.7
  119.8 1.4 collective-permute-start.15
  121.2 1.6 copy-done.6
  122.8 1.0 copy-done.8
  123.8 6.8 %first_layer.1 = (bf16[1024,512]{1,0:T(8,128)(2,1)S(1)}, bf16[1024,512]{1,0:T(8,128)(2,1)S(1)}, f32[16,1024]{1,0:T(8,128)S(1)}) custom-call(bf16[16,512]{1,0:T(8,128)(2,1)S(1)} %broadcast_in_dim.43.u_ref, f32[1024,512]{1,0:T(8,128)S(1)} %copy-done.6, bf16[512,512]{1,0:T(8,128)(2,1)S(1)} %copy-done.8, bf16[2048,512]{1,0:T(8,128)(2,1)} %bitcast.13.recv_hbm), custom_call_target="tpu_custom_call" | custom-call | flops 15728640000 | bytes 8388608 | tf_op jit(solution)/shard_map/first_layer/pallas_call | solution.py:78
  130.7 0.1 collective-permute-start.18
  130.9 0.7 collective-permute-start.19
  131.6 1.8 %collective-permute-done.19 = f32[1,2]{0,1:T(2,128)S(1)} collective-permute-done((f32[1,2]{0,1:T(2,128)S(1)}, f32[1,2]{0,1:T(2,128)S(1)}, u32[]{:S(2)}, u32[]{:S(2)}) %collective-permute-start.19) | collective-permute-done | bytes 40 | tf_op jit(solution)/shard_map/ppermute | solution.py:339
  133.4 0.1 collective-permute-done.18.other_ref
  133.5 1.3 collective-permute-start.20
  134.8 2.6 %collective-permute-start.21 = (f32[1,2]{0,1:T(2,128)S(1)}, f32[1,2]{0,1:T(2,128)S(1)}, u32[]{:S(2)}, u32[]{:S(2)}) collective-permute-start(f32[1,2]{0,1:T(2,128)S(1)} %slice_maximum_fusion), channel_id=1, source_target_pairs={{0,3},{1,2},{2,1},{3,0},{4,7},{5,6},{6,5},{7,4},{8,11},{9,10},{10,... | collective-permute-start | bytes 32 | tf_op jit(solution)/shard_map/ppermute | solution.py:344
  137.3 0.1 collective-permute-start.22
  137.5 3.7 %second_layer.1 = (bf16[1024,768]{1,0:T(8,128)(2,1)S(1)}, bf16[1024,768]{1,0:T(8,128)(2,1)S(1)}, bf16[1024,512]{1,0:T(8,128)(2,1)S(1)}) custom-call(bf16[1024,512]{1,0:T(8,128)(2,1)S(1)} %get-tuple-element.60.mine_ref, bf16[1024,512]{1,0:T(8,128)(2,1)S(1)} %collective-permute-done.18.other_ref, bf16[1024,512]{1,0:T(8,128)(2,1)S(1)} %get-tuple-element.63.pay_ref, ...), custom_call_target="tpu_custom_call" | custom-call | flops 15728640000 | bytes 12582912 | tf_op jit(solution)/shard_map/second_layer/pallas_call | solution.py:78
  141.2 2.9 %collective-permute-start.23 = (bf16[1024,512]{1,0:T(8,128)(2,1)S(1)}, bf16[1024,512]{1,0:T(8,128)(2,1)S(1)}, u32[]{:S(2)}, u32[]{:S(2)}) collective-permute-start(bf16[1024,512]{1,0:T(8,128)(2,1)S(1)} %get-tuple-element.70.mine_ref), channel_id=1, source_target_pairs={{0,4},{1,5},{2,6},{3,7},{4,0},{5,1},{6,2},{7,3},{8,12},{9,13},{10,... | collective-permute-start | bytes 3145736 | tf_op jit(solution)/shard_map/ppermute | solution.py:413
  144.8 0.5 fusion.4
  145.8 0.6 collective-permute-done.23.other_ref
  146.4 3.1 %last_layer.1 = f32[16,1024]{1,0:T(8,128)S(1)} custom-call(f32[1]{0:T(128)} %copy.14.coefficient, bf16[1024,512]{1,0:T(8,128)(2,1)S(1)} %get-tuple-element.70.mine_ref, bf16[1024,512]{1,0:T(8,128)(2,1)S(1)} %collective-permute-done.23.other_ref, bf16[1024,512]{1,0:T(8,128)(2,1)S(1)} %get-tuple-element.63.pay_ref, ...), custom_call_target="tpu_custom_call" | custom-call | flops 1879048192 | bytes 10485760 | tf_op jit(solution)/shard_map/last_layer/pallas_call | solution.py:78
  149.5 0.4 collective-permute-start.24
  150.0 0.8 collective-permute-done.24
  150.8 4.2 %collective-permute-start.26 = (f32[1,1024]{1,0:T(1,128)S(1)}, f32[1,1024]{1,0:T(1,128)S(1)}, u32[]{:S(2)}, u32[]{:S(2)}) collective-permute-start(f32[1,1024]{1,0:T(1,128)S(1)} %fusion.7), channel_id=1, source_target_pairs={{2,4},{3,5},{4,2},{5,3},{10,12},{11,13},{12,10},{13,11},{18,20},{1... | collective-permute-start | bytes 12296 | tf_op jit(solution)/shard_map/ppermute | solution.py:422
  155.0 0.6 collective-permute-start.25
  155.6 1.7 %collective-permute-done.26 = f32[1,1024]{1,0:T(1,128)S(1)} collective-permute-done((f32[1,1024]{1,0:T(1,128)S(1)}, f32[1,1024]{1,0:T(1,128)S(1)}, u32[]{:S(2)}, u32[]{:S(2)}) %collective-permute-start.26) | collective-permute-done | bytes 4128 | tf_op jit(solution)/shard_map/ppermute | solution.py:422
  157.2 2.1 %collective-permute-done.25 = f32[1,1024]{1,0:T(1,128)S(1)} collective-permute-done((f32[1,1024]{1,0:T(1,128)S(1)}, f32[1,1024]{1,0:T(1,128)S(1)}, u32[]{:S(2)}, u32[]{:S(2)}) %collective-permute-start.25) | collective-permute-done | bytes 4128 | tf_op jit(solution)/shard_map/ppermute | solution.py:421
  159.3 0.6 maximum_select_fusion
  (72 shorter events, 0.7 us)
Async XLA Ops:
  0.0 5.3 %copy-start.9 = (bf16[2,512,768]{2,1,0:T(8,128)(2,1)S(1)}, bf16[2,512,768]{2,1,0:T(8,128)(2,1)}, u32[]{:S(2)}) copy-start(bf16[2,512,768]{2,1,0:T(8,128)(2,1)} %param.19) | copy-start | bytes 4718596
  0.0 5.7 %copy-start.15 = (bf16[2,256]{1,0:T(2,128)(2,1)S(1)}, bf16[2,256]{1,0:T(2,128)(2,1)}, u32[]{:S(2)}) copy-start(bf16[2,256]{1,0:T(2,128)(2,1)} %param.12) | copy-start | bytes 3076
  0.0 18.1 %copy-start.16 = (bf16[768]{0:T(1024)(128)(2,1)S(1)}, bf16[768]{0:T(1024)(128)(2,1)}, u32[]{:S(2)}) copy-start(bf16[768]{0:T(1024)(128)(2,1)} %param.21) | copy-start | bytes 4612
  1.3 26.9 %collective-permute-start = (bf16[768,512]{1,0:T(8,128)(2,1)S(1)}, bf16[768,512]{1,0:T(8,128)(2,1)}, u32[]{:S(2)}, u32[]{:S(2)}) collective-permute-start(bf16[768,512]{1,0:T(8,128)(2,1)S(1)} %dynamic-slice_bitcast_fusion.3), channel_id=1, source_target_pairs={{0,1},{1,0},{2,5},{3,4},{4,3},{5,2},{6,7},{7,6},{8,9},{9,8},{10,13... | collective-permute-start | bytes 2359304 | tf_op jit(solution)/shard_map/ppermute | solution.py:304
  5.3 22.8 %collective-permute-start.1 = (bf16[512,768]{1,0:T(8,128)(2,1)S(1)}, bf16[512,768]{1,0:T(8,128)(2,1)}, u32[]{:S(2)}, u32[]{:S(2)}) collective-permute-start(bf16[512,768]{1,0:T(8,128)(2,1)S(1)} %dynamic-slice_bitcast_fusion.2), channel_id=1, source_target_pairs={{0,1},{1,0},{2,5},{3,4},{4,3},{5,2},{6,7},{7,6},{8,9},{9,8},{10,13... | collective-permute-start | bytes 2359304 | tf_op jit(solution)/shard_map/ppermute | solution.py:305
  6.3 21.9 %all-to-all-start = ((bf16[64,2,256]{2,1,0:T(2,128)(2,1)}), bf16[64,2,256]{2,1,0:T(2,128)(2,1)S(1)}, u32[]{:S(2)}, u32[]{:S(2)}) async-start(bf16[64,2,256]{2,1,0:T(2,128)(2,1)} %broadcast_in_dim.41), calls=%async_computation | async-start | bytes 131072 | tf_op jit(solution)/shard_map/all_to_all | solution.py:307
  18.9 9.6 %copy-start.14 = (f32[2,768]{1,0:T(2,128)S(1)}, f32[2,768]{1,0:T(2,128)}, u32[]{:S(2)}) copy-start(f32[2,768]{1,0:T(2,128)} %param.20) | copy-start | bytes 18436
  28.2 22.8 %collective-permute-start.9 = (bf16[768,512]{1,0:T(8,128)(2,1)}, bf16[768,512]{1,0:T(8,128)(2,1)}, u32[]{:S(2)}, u32[]{:S(2)}) collective-permute-start(bf16[768,512]{1,0:T(8,128)(2,1)} %collective-permute-done), channel_id=1, source_target_pairs={{0,24},{1,25},{2,10},{3,11},{4,12},{5,13},{6,30},{7,31},{8,0},{9,1... | collective-permute-start | bytes 2359304 | tf_op jit(solution)/shard_map/ppermute | solution.py:359
  28.5 45.4 %collective-permute-start.2 = (bf16[768,512]{1,0:T(8,128)(2,1)}, bf16[768,512]{1,0:T(8,128)(2,1)}, u32[]{:S(2)}, u32[]{:S(2)}) collective-permute-start(bf16[768,512]{1,0:T(8,128)(2,1)} %collective-permute-done), channel_id=1, source_target_pairs={{0,3},{1,2},{6,5},{7,4},{8,11},{9,10},{14,13},{15,12},{16,19},{17,... | collective-permute-start | bytes 2359304 | tf_op jit(solution)/shard_map/ppermute | solution.py:317
  29.9 15.7 %copy-start.13 = (bf16[2048,256]{1,0:T(8,128)(2,1)S(1)}, bf16[2048,256]{1,0:T(8,128)(2,1)}, u32[]{:S(2)}) copy-start(bf16[2048,256]{1,0:T(8,128)(2,1)} %emb_hbm.1) | copy-start | bytes 3145732
  29.9 44.0 %copy-start.12 = (bf16[2,1024,512]{2,1,0:T(8,128)(2,1)S(1)}, bf16[2,1024,512]{2,1,0:T(8,128)(2,1)}, u32[]{:S(2)}) copy-start(bf16[2,1024,512]{2,1,0:T(8,128)(2,1)} %param.17) | copy-start | bytes 6291460
  29.9 89.8 %all-to-all-start.1 = ((bf16[256,8,512]{2,1,0:T(8,128)(2,1)}), bf16[256,8,512]{2,1,0:T(8,128)(2,1)}, u32[]{:S(2)}, u32[]{:S(2)}) async-start(bf16[256,8,512]{2,1,0:T(8,128)(2,1)} %bitcast.32), calls=%async_computation.1 | async-start | bytes 4194304 | tf_op jit(solution)/shard_map/all_to_all | solution.py:314
  46.3 25.6 %collective-permute-start.11 = (bf16[512,768]{1,0:T(8,128)(2,1)}, bf16[512,768]{1,0:T(8,128)(2,1)S(1)}, u32[]{:S(2)}, u32[]{:S(2)}) collective-permute-start(bf16[512,768]{1,0:T(8,128)(2,1)} %collective-permute-done.1), channel_id=1, source_target_pairs={{2,3},{3,2},{4,5},{5,4},{10,11},{11,10},{12,13},{13,12},{18,19},{1... | collective-permute-start | bytes 2359304 | tf_op jit(solution)/shard_map/ppermute | solution.py:318
  49.8 1.2 collective-permute-start.5
  51.0 35.9 %collective-permute-start.10 = (bf16[512,768]{1,0:T(8,128)(2,1)}, bf16[512,768]{1,0:T(8,128)(2,1)S(1)}, u32[]{:S(2)}, u32[]{:S(2)}) collective-permute-start(bf16[512,768]{1,0:T(8,128)(2,1)} %collective-permute-done.1), channel_id=1, source_target_pairs={{0,8},{1,9},{2,26},{3,27},{4,28},{5,29},{6,14},{7,15},{8,16},{9,17... | collective-permute-start | bytes 2359304 | tf_op jit(solution)/shard_map/ppermute | solution.py:362
  53.5 15.6 %collective-permute-start.6 = (f32[8,2]{0,1:T(2,128)S(1)}, f32[8,2]{0,1:T(2,128)S(1)}, u32[]{:S(2)}, u32[]{:S(2)}) collective-permute-start(f32[8,2]{0,1:T(2,128)S(1)} %get-tuple-element.87), channel_id=1, source_target_pairs={{0,8},{4,12},{8,0},{12,4},{16,24},{20,28},{24,16},{28,20},{32,40},... | collective-permute-start | bytes 200 | tf_op jit(solution)/shard_map/ppermute | solution.py:352
  53.5 20.3 %collective-permute-start.7 = (f32[8,2]{0,1:T(2,128)S(1)}, f32[8,2]{0,1:T(2,128)S(1)}, u32[]{:S(2)}, u32[]{:S(2)}) collective-permute-start(f32[8,2]{0,1:T(2,128)S(1)} %get-tuple-element.89), channel_id=1, source_target_pairs={{0,24},{4,28},{8,16},{12,20},{16,8},{20,12},{24,0},{28,4},{32,56},... | collective-permute-start | bytes 200 | tf_op jit(solution)/shard_map/ppermute | solution.py:352
  69.1 4.7 %collective-permute-start.8 = (f32[8,2]{0,1:T(2,128)S(1)}, f32[8,2]{0,1:T(2,128)S(1)}, u32[]{:S(2)}, u32[]{:S(2)}) collective-permute-start(f32[8,2]{0,1:T(2,128)S(1)} %get-tuple-element.88), channel_id=1, source_target_pairs={{0,16},{4,20},{8,24},{12,28},{16,0},{20,4},{24,8},{28,12},{32,48},... | collective-permute-start | bytes 200 | tf_op jit(solution)/shard_map/ppermute | solution.py:352
  71.9 21.0 %collective-permute-start.12 = (bf16[512,768]{1,0:T(8,128)(2,1)S(1)}, bf16[512,768]{1,0:T(8,128)(2,1)S(1)}, u32[]{:S(2)}, u32[]{:S(2)}) collective-permute-start(bf16[512,768]{1,0:T(8,128)(2,1)S(1)} %collective-permute-done.11), channel_id=1, source_target_pairs={{2,10},{3,11},{4,12},{5,13},{10,18},{11,19},{12,20},{13,21},{18,26... | collective-permute-start | bytes 2359304 | tf_op jit(solution)/shard_map/ppermute | solution.py:363
  74.1 34.3 %collective-permute-start.3 = (bf16[1024,512]{1,0:T(8,128)(2,1)S(1)}, bf16[1024,512]{1,0:T(8,128)(2,1)S(1)}, u32[]{:S(2)}, u32[]{:S(2)}) collective-permute-start(bf16[1024,512]{1,0:T(8,128)(2,1)S(1)} %get-tuple-element.82), channel_id=1, source_target_pairs={{0,1},{1,0},{2,5},{3,4},{4,3},{5,2},{6,7},{7,6},{8,9},{9,8},{10,13... | collective-permute-start | bytes 3145736 | tf_op jit(solution)/shard_map/ppermute | solution.py:322
  77.5 30.8 %collective-permute-start.4 = (bf16[1024,512]{1,0:T(8,128)(2,1)S(1)}, bf16[1024,512]{1,0:T(8,128)(2,1)S(1)}, u32[]{:S(2)}, u32[]{:S(2)}) collective-permute-start(bf16[1024,512]{1,0:T(8,128)(2,1)S(1)} %get-tuple-element.81), channel_id=1, source_target_pairs={{2,4},{3,5},{4,2},{5,3},{10,12},{11,13},{12,10},{13,11},{18,20},{1... | collective-permute-start | bytes 3145736 | tf_op jit(solution)/shard_map/ppermute | solution.py:323
  81.0 17.2 %collective-permute-start.13 = (bf16[768,512]{1,0:T(8,128)(2,1)}, bf16[768,512]{1,0:T(8,128)(2,1)S(1)}, u32[]{:S(2)}, u32[]{:S(2)}) collective-permute-start(bf16[768,512]{1,0:T(8,128)(2,1)} %collective-permute-done.2), channel_id=1, source_target_pairs={{2,26},{3,27},{4,28},{5,29},{10,2},{11,3},{12,4},{13,5},{18,10},{1... | collective-permute-start | bytes 2359304 | tf_op jit(solution)/shard_map/ppermute | solution.py:360
  86.9 6.1 %copy-start.10 = (bf16[2,512,768]{2,1,0:T(8,128)(2,1)S(1)}, bf16[2,512,768]{2,1,0:T(8,128)(2,1)}, u32[]{:S(2)}) copy-start(bf16[2,512,768]{2,1,0:T(8,128)(2,1)} %param.19) | copy-start | bytes 4718596
  89.2 9.0 %copy-start.11 = (bf16[2,768,512]{2,1,0:T(8,128)(2,1)S(1)}, bf16[2,768,512]{2,1,0:T(8,128)(2,1)}, u32[]{:S(2)}) copy-start(bf16[2,768,512]{2,1,0:T(8,128)(2,1)} %param.18) | copy-start | bytes 4718596
  108.3 7.9 %copy-start = (bf16[1024,512]{1,0:T(8,128)(2,1)}, bf16[1024,512]{1,0:T(8,128)(2,1)S(1)}, u32[]{:S(2)}) copy-start(bf16[1024,512]{1,0:T(8,128)(2,1)S(1)} %collective-permute-done.3.ca_ref) | copy-start | bytes 3145732
  108.3 22.4 %collective-permute-start.16 = (f32[3,768]{1,0:T(4,128)S(1)}, f32[3,768]{1,0:T(4,128)S(1)}, u32[]{:S(2)}, u32[]{:S(2)}) collective-permute-start(f32[3,768]{1,0:T(4,128)S(1)} %pad_maximum_fusion), channel_id=1, source_target_pairs={{0,1},{1,0},{2,5},{3,4},{4,3},{5,2},{6,7},{7,6},{8,9},{9,8},{10,13... | collective-permute-start | bytes 27656 | tf_op jit(solution)/shard_map/ppermute | solution.py:366
  110.2 20.5 %collective-permute-start.17 = (f32[3,768]{1,0:T(4,128)S(1)}, f32[3,768]{1,0:T(4,128)S(1)}, u32[]{:S(2)}, u32[]{:S(2)}) collective-permute-start(f32[3,768]{1,0:T(4,128)S(1)} %pad_maximum_fusion), channel_id=1, source_target_pairs={{2,4},{3,5},{4,2},{5,3},{10,12},{11,13},{12,10},{13,11},{18,20},{1... | collective-permute-start | bytes 27656 | tf_op jit(solution)/shard_map/ppermute | solution.py:367
  112.8 7.0 %collective-permute-start.14 = (f32[4,2]{0,1:T(2,128)S(1)}, f32[4,2]{0,1:T(2,128)S(1)}, u32[]{:S(2)}, u32[]{:S(2)}) collective-permute-start(f32[4,2]{0,1:T(2,128)S(1)} %slice.61), channel_id=1, source_target_pairs={{0,192},{4,196},{8,200},{12,204},{16,208},{20,212},{24,216},{28,22... | collective-permute-start | bytes 104 | tf_op jit(solution)/shard_map/ppermute | solution.py:339
  117.5 1.4 copy-start.5
  118.9 0.8 copy-start.7
  119.8 10.9 %collective-permute-start.15 = (f32[2,2]{0,1:T(2,128)S(1)}, f32[2,2]{0,1:T(2,128)S(1)}, u32[]{:S(2)}, u32[]{:S(2)}) collective-permute-start(f32[2,2]{0,1:T(2,128)S(1)} %slice.63), channel_id=1, source_target_pairs={{0,64},{4,68},{8,72},{12,76},{16,80},{20,84},{24,88},{28,92},{32,9... | collective-permute-start | bytes 56 | tf_op jit(solution)/shard_map/ppermute | solution.py:339
  121.2 1.6 copy-start.6
  122.8 1.0 copy-start.8
  123.8 13.6 %copy-start.1 = (bf16[1024,512]{1,0:T(8,128)(2,1)S(1)}, bf16[1024,512]{1,0:T(8,128)(2,1)}, u32[]{:S(2)}) copy-start(bf16[1024,512]{1,0:T(8,128)(2,1)} %copy-done) | copy-start | bytes 3145732
  123.8 13.6 %copy-start.2 = (bf16[768,512]{1,0:T(8,128)(2,1)S(1)}, bf16[768,512]{1,0:T(8,128)(2,1)}, u32[]{:S(2)}) copy-start(bf16[768,512]{1,0:T(8,128)(2,1)} %get-tuple-element.77.vb_ref) | copy-start | bytes 2359300
  123.8 13.6 %copy-start.3 = (bf16[768,512]{1,0:T(8,128)(2,1)S(1)}, bf16[768,512]{1,0:T(8,128)(2,1)}, u32[]{:S(2)}) copy-start(bf16[768,512]{1,0:T(8,128)(2,1)} %get-tuple-element.83.va_ref) | copy-start | bytes 2359300
  123.8 13.6 %copy-start.4 = (bf16[512,768]{1,0:T(8,128)(2,1)S(1)}, bf16[512,768]{1,0:T(8,128)(2,1)}, u32[]{:S(2)}) copy-start(bf16[512,768]{1,0:T(8,128)(2,1)} %get-tuple-element.66.ua_ref) | copy-start | bytes 2359300
  130.7 2.7 %collective-permute-start.18 = (bf16[1024,512]{1,0:T(8,128)(2,1)S(1)}, bf16[1024,512]{1,0:T(8,128)(2,1)S(1)}, u32[]{:S(2)}, u32[]{:S(2)}) collective-permute-start(bf16[1024,512]{1,0:T(8,128)(2,1)S(1)} %get-tuple-element.60.mine_ref), channel_id=1, source_target_pairs={{0,4},{1,5},{2,6},{3,7},{4,0},{5,1},{6,2},{7,3},{8,12},{9,13},{10,... | collective-permute-start | bytes 3145736 | tf_op jit(solution)/shard_map/ppermute | solution.py:405
  130.9 2.4 %collective-permute-start.19 = (f32[1,2]{0,1:T(2,128)S(1)}, f32[1,2]{0,1:T(2,128)S(1)}, u32[]{:S(2)}, u32[]{:S(2)}) collective-permute-start(f32[1,2]{0,1:T(2,128)S(1)} %slice.65), channel_id=1, source_target_pairs={{0,32},{4,36},{8,40},{12,44},{16,48},{20,52},{24,56},{28,60},{32,0... | collective-permute-start | bytes 32 | tf_op jit(solution)/shard_map/ppermute | solution.py:339
  133.5 7.7 %collective-permute-start.20 = (f32[1,2]{0,1:T(2,128)S(1)}, f32[1,2]{0,1:T(2,128)S(1)}, u32[]{:S(2)}, u32[]{:S(2)}) collective-permute-start(f32[1,2]{0,1:T(2,128)S(1)} %slice_maximum_fusion), channel_id=1, source_target_pairs={{0,1},{1,0},{2,3},{3,2},{4,5},{5,4},{6,7},{7,6},{8,9},{9,8},{10,11... | collective-permute-start | bytes 32 | tf_op jit(solution)/shard_map/ppermute | solution.py:344
  134.8 6.5 %collective-permute-start.21 = (f32[1,2]{0,1:T(2,128)S(1)}, f32[1,2]{0,1:T(2,128)S(1)}, u32[]{:S(2)}, u32[]{:S(2)}) collective-permute-start(f32[1,2]{0,1:T(2,128)S(1)} %slice_maximum_fusion), channel_id=1, source_target_pairs={{0,3},{1,2},{2,1},{3,0},{4,7},{5,6},{6,5},{7,4},{8,11},{9,10},{10,... | collective-permute-start | bytes 32 | tf_op jit(solution)/shard_map/ppermute | solution.py:344
  137.3 3.9 %collective-permute-start.22 = (f32[1,2]{0,1:T(2,128)S(1)}, f32[1,2]{0,1:T(2,128)S(1)}, u32[]{:S(2)}, u32[]{:S(2)}) collective-permute-start(f32[1,2]{0,1:T(2,128)S(1)} %slice_maximum_fusion), channel_id=1, source_target_pairs={{0,2},{1,3},{2,0},{3,1},{4,6},{5,7},{6,4},{7,5},{8,10},{9,11},{10,... | collective-permute-start | bytes 32 | tf_op jit(solution)/shard_map/ppermute | solution.py:344
  141.2 5.2 %collective-permute-start.23 = (bf16[1024,512]{1,0:T(8,128)(2,1)S(1)}, bf16[1024,512]{1,0:T(8,128)(2,1)S(1)}, u32[]{:S(2)}, u32[]{:S(2)}) collective-permute-start(bf16[1024,512]{1,0:T(8,128)(2,1)S(1)} %get-tuple-element.70.mine_ref), channel_id=1, source_target_pairs={{0,4},{1,5},{2,6},{3,7},{4,0},{5,1},{6,2},{7,3},{8,12},{9,13},{10,... | collective-permute-start | bytes 3145736 | tf_op jit(solution)/shard_map/ppermute | solution.py:413
  149.5 1.3 collective-permute-start.24
  150.8 6.4 %collective-permute-start.26 = (f32[1,1024]{1,0:T(1,128)S(1)}, f32[1,1024]{1,0:T(1,128)S(1)}, u32[]{:S(2)}, u32[]{:S(2)}) collective-permute-start(f32[1,1024]{1,0:T(1,128)S(1)} %fusion.7), channel_id=1, source_target_pairs={{2,4},{3,5},{4,2},{5,3},{10,12},{11,13},{12,10},{13,11},{18,20},{1... | collective-permute-start | bytes 12296 | tf_op jit(solution)/shard_map/ppermute | solution.py:422
  155.0 4.3 %collective-permute-start.25 = (f32[1,1024]{1,0:T(1,128)S(1)}, f32[1,1024]{1,0:T(1,128)S(1)}, u32[]{:S(2)}, u32[]{:S(2)}) collective-permute-start(f32[1,1024]{1,0:T(1,128)S(1)} %fusion.7), channel_id=1, source_target_pairs={{0,1},{1,0},{2,5},{3,4},{4,3},{5,2},{6,7},{7,6},{8,9},{9,8},{10,13... | collective-permute-start | bytes 12296 | tf_op jit(solution)/shard_map/ppermute | solution.py:421

commit v11 on v10

--- a/solution.py
+++ b/solution.py
@@ -11,7 +11,7 @@
 F32 = jnp.float32
 AXES = ("shard", "tp")
 VMEM = pl.BlockSpec(memory_space=pltpu.VMEM)
-PICK, CTX, FIRST, SECOND = 4096, 11000, 15000, 15000
+PICK, CTX, FIRST, SECOND = 4096, 13500, 15000, 15000
 SMEM = pl.BlockSpec(memory_space=pltpu.SMEM)
 ANY = pl.BlockSpec(memory_space=pl.ANY)
 
@@ -48,9 +48,9 @@
     far_z = (6, 7, 4, 5, 2, 3, 0, 1)
     steps = []
     for of_z, of_y, of_core in (
+        (lambda z: far_z[z], None, None),
+        (lambda z: z ^ 2, None, None),
         (lambda z: z ^ 1, None, None),
-        (lambda z: z ^ 2, None, None),
-        (lambda z: far_z[z], None, None),
         (None, 1, None),
         (None, 3, None),
         (None, None, 1),
@@ -358,7 +358,7 @@
     small = jnp.concatenate([interaction_offset, final_projection[None, :].astype(F32)], 0)
     v_near_y = move(v_near, perm=y_split)
     v_far_y = move(v_far, perm=y_down)
-    v_near_y, u_near_on = lax.optimization_barrier((v_near_y, u_near))
+    best, u_near_on = lax.optimization_barrier((best, u_near))
     u_near_y = move(u_near_on, perm=y_mirror)
     u_far_y = move(u_far, perm=y_up)
     ctx_a, best, small = lax.optimization_barrier((ctx_a, best, small))

time: 161 us -> 155 us (0.963)
  waiting for transfers between devices: 40.9 us -> 28.4 us
  starting transfers between devices: 76.8 us -> 84.5 us
    ppermute x3, waiting for transfers between devices: 14.8 us -> 1.79 us  [over_y(): got = lax.ppermute(best[block * n:(block + 1) * n], 'shard', pairs)]
    ppermute x1, waiting for transfers between devices: 7.94 us -> 0.01 us  [on_device(): ctx_a = move(ctx_away, perm=ctx_near)]
    ppermute x1, waiting for transfers between devices: 3.73 us -> 9.95 us  [on_device(): u_far_y = move(u_far, perm=y_up)]
    ppermute x1, starting transfers between devices: 3.46 us -> 9.23 us  [on_device(): ctx_b = move(ctx_own, perm=ctx_far)]
    ppermute x1, waiting for transfers between devices: 0.01 us -> 2.93 us  [on_device(): u_far = move(u_near, perm=away_swap)]
    select_n x1, other arithmetic: 2.19 us -> 0.17 us  [on_device(): v1_b = jnp.where(home, lowrank_v_matrix[1], jnp.where(even, v_far_y, v_far))]
    ppermute x3, starting transfers between devices: 3.61 us -> 5.55 us  [over_y(): got = lax.ppermute(best[block * n:(block + 1) * n], 'shard', pairs)]
    ppermute x1, waiting for transfers between devices: 0.01 us -> 1.93 us  [on_device(): ctx_b = move(ctx_own, perm=ctx_far)]
  transfers between devices with their start and end apart: 29 -> 29, of which waited for: 12 -> 11; matrix products, arithmetic and copies ran while one was open for 7% -> 6% of each run, Pallas kernels for 12% -> 13%
where the time goes in v11:
time: 155 us; the launch traced here: 154 us
  starting transfers between devices  84.5 us (55%)
  waiting for transfers between devices  28.4 us (18%)
  Pallas kernels  23 us (15%)
  local copies, waits for them, and re-layouts  8.35 us (5%)
  other arithmetic  7.59 us (5%)
  between operations  1.74 us (1%)
    pallas_call x4, Pallas kernels, call(): pl.pallas_call(kernel, in_specs=[SMEM] * len(scalars) + [VMEM] * len(arra...  14.9 us
    all_to_all x1, starting transfers between devices, on_device(): recv = lax.all_to_all(parcel, AXES, split_axis=0, concat_axis=0, tiled=True)  14 us
    all_to_all x1, starting transfers between devices, on_device(): lax.all_to_all(users, 'shard', split_axis=0, concat_axis=0, tiled=True)  11.8 us
    ppermute x1, waiting for transfers between devices, on_device(): u_far_y = move(u_far, perm=y_up)  9.95 us
    ppermute x1, starting transfers between devices, on_device(): ctx_b = move(ctx_own, perm=ctx_far)  9.23 us
    pallas_call x1, Pallas kernels, pick_rows(): pl.pallas_call(pick_kernel, in_specs=[VMEM, VMEM, ANY, ANY], out_specs=AN...  8.07 us
    ppermute x4, starting transfers between devices, halve(): return jnp.maximum(best[:half], lax.ppermute(best[half:], 'shard', pairs))  5.97 us
    ppermute x3, starting transfers between devices, over_y(): got = lax.ppermute(best[block * n:(block + 1) * n], 'shard', pairs)  5.55 us
  transfers between devices with their start and end apart: 29, of which 11 were waited for; matrix products, arithmetic and copies ran while one was open for 6% of the time, Pallas kernels for 13%

profile of v11, /device:TPU:1, one launch (start us, length us, event | category | flops | bytes accessed | tf_op | source)
XLA Modules:
  0.0 154.1 jit_solution(15633895036542651240)
XLA Ops:
  0.0 1.3 dynamic-slice_bitcast_fusion.3
  1.3 4.0 %collective-permute-start = (bf16[768,512]{1,0:T(8,128)(2,1)S(1)}, bf16[768,512]{1,0:T(8,128)(2,1)}, u32[]{:S(2)}, u32[]{:S(2)}) collective-permute-start(bf16[768,512]{1,0:T(8,128)(2,1)S(1)} %dynamic-slice_bitcast_fusion.3), channel_id=1, source_target_pairs={{0,1},{1,0},{2,5},{3,4},{4,3},{5,2},{6,7},{7,6},{8,9},{9,8},{10,13... | collective-permute-start | bytes 2359304 | tf_op jit(solution)/shard_map/ppermute | solution.py:304
  5.3 0.3 collective-permute-start.1
  5.7 0.7 broadcast_in_dim.41
  6.3 11.8 %all-to-all-start = ((bf16[64,2,256]{2,1,0:T(2,128)(2,1)}), bf16[64,2,256]{2,1,0:T(2,128)(2,1)S(1)}, u32[]{:S(2)}, u32[]{:S(2)}) async-start(bf16[64,2,256]{2,1,0:T(2,128)(2,1)} %broadcast_in_dim.41), calls=%async_computation | async-start | bytes 131072 | tf_op jit(solution)/shard_map/all_to_all | solution.py:307
  18.2 0.7 fusion.2
  18.9 8.1 %pick_rows.1 = bf16[32,2,32,512]{3,2,1,0:T(8,128)(2,1)} custom-call(s32[8,128]{1,0:T(8,128)} %bitcast.33, s32[1,128]{1,0:T(1,128)} %bitcast.34, bf16[2048,256]{1,0:T(8,128)(2,1)} %emb_hbm.1, bf16[2048,768]{1,0:T(8,128)(2,1)} %attr_hbm.1), custom_call_target="tpu_custom_call" | custom-call | flops 4294967296 | bytes 6291456 | tf_op jit(solution)/shard_map/pick_rows/pallas_call | solution.py:144
  27.0 0.1 iota_compare_fusion
  27.1 1.1 all-to-all-done
  28.2 0.6 convolution_reduce_fusion
  28.8 0.1 broadcast_in_dim.45
  29.0 0.1 select_reduce_fusion
  29.2 0.4 collective-permute-start.5
  29.7 1.4 collective-permute-start.2
  31.1 0.3 collective-permute-start.12
  31.4 14.0 %all-to-all-start.1 = ((bf16[256,8,512]{2,1,0:T(8,128)(2,1)}), bf16[256,8,512]{2,1,0:T(8,128)(2,1)}, u32[]{:S(2)}, u32[]{:S(2)}) async-start(bf16[256,8,512]{2,1,0:T(8,128)(2,1)} %bitcast.32), calls=%async_computation.1 | async-start | bytes 4194304 | tf_op jit(solution)/shard_map/all_to_all | solution.py:314
  45.4 3.3 %collective-permute-start.10 = (bf16[512,768]{1,0:T(8,128)(2,1)}, bf16[512,768]{1,0:T(8,128)(2,1)S(1)}, u32[]{:S(2)}, u32[]{:S(2)}) collective-permute-start(bf16[512,768]{1,0:T(8,128)(2,1)} %collective-permute-done.1), channel_id=1, source_target_pairs={{2,3},{3,2},{4,5},{5,4},{10,11},{11,10},{12,13},{13,12},{18,19},{1... | collective-permute-start | bytes 2359304 | tf_op jit(solution)/shard_map/ppermute | solution.py:318
  48.8 1.2 collective-permute-start.6
  50.0 1.8 %collective-permute-start.7 = (f32[8,2]{0,1:T(2,128)S(1)}, f32[8,2]{0,1:T(2,128)S(1)}, u32[]{:S(2)}, u32[]{:S(2)}) collective-permute-start(f32[8,2]{0,1:T(2,128)S(1)} %get-tuple-element.89), channel_id=1, source_target_pairs={{0,24},{4,28},{8,16},{12,20},{16,8},{20,12},{24,0},{28,4},{32,56},... | collective-permute-start | bytes 200 | tf_op jit(solution)/shard_map/ppermute | solution.py:352
  51.8 2.5 %collective-permute-start.8 = (f32[8,2]{0,1:T(2,128)S(1)}, f32[8,2]{0,1:T(2,128)S(1)}, u32[]{:S(2)}, u32[]{:S(2)}) collective-permute-start(f32[8,2]{0,1:T(2,128)S(1)} %get-tuple-element.88), channel_id=1, source_target_pairs={{0,16},{4,20},{8,24},{12,28},{16,0},{20,4},{24,8},{28,12},{32,48},... | collective-permute-start | bytes 200 | tf_op jit(solution)/shard_map/ppermute | solution.py:352
  54.3 1.8 %collective-permute-done.8 = f32[8,2]{0,1:T(2,128)S(1)} collective-permute-done((f32[8,2]{0,1:T(2,128)S(1)}, f32[8,2]{0,1:T(2,128)S(1)}, u32[]{:S(2)}, u32[]{:S(2)}) %collective-permute-start.8) | collective-permute-done | bytes 96 | tf_op jit(solution)/shard_map/ppermute | solution.py:352
  56.1 2.3 %collective-permute-start.9 = (bf16[512,768]{1,0:T(8,128)(2,1)}, bf16[512,768]{1,0:T(8,128)(2,1)S(1)}, u32[]{:S(2)}, u32[]{:S(2)}) collective-permute-start(bf16[512,768]{1,0:T(8,128)(2,1)} %collective-permute-done.1), channel_id=1, source_target_pairs={{0,8},{1,9},{2,26},{3,27},{4,28},{5,29},{6,14},{7,15},{8,16},{9,17... | collective-permute-start | bytes 2359304 | tf_op jit(solution)/shard_map/ppermute | solution.py:362
  58.5 2.4 %collective-permute-start.13 = (bf16[768,512]{1,0:T(8,128)(2,1)S(1)}, bf16[768,512]{1,0:T(8,128)(2,1)S(1)}, u32[]{:S(2)}, u32[]{:S(2)}) collective-permute-start(bf16[768,512]{1,0:T(8,128)(2,1)S(1)} %collective-permute-done.2), channel_id=1, source_target_pairs={{2,26},{3,27},{4,28},{5,29},{10,2},{11,3},{12,4},{13,5},{18,10},{1... | collective-permute-start | bytes 2359304 | tf_op jit(solution)/shard_map/ppermute | solution.py:360
  61.0 0.1 dynamic-slice_bitcast_fusion
  61.1 4.5 %collective-permute-start.3 = (bf16[1024,512]{1,0:T(8,128)(2,1)S(1)}, bf16[1024,512]{1,0:T(8,128)(2,1)S(1)}, u32[]{:S(2)}, u32[]{:S(2)}) collective-permute-start(bf16[1024,512]{1,0:T(8,128)(2,1)S(1)} %get-tuple-element.82), channel_id=1, source_target_pairs={{0,1},{1,0},{2,5},{3,4},{4,3},{5,2},{6,7},{7,6},{8,9},{9,8},{10,13... | collective-permute-start | bytes 3145736 | tf_op jit(solution)/shard_map/ppermute | solution.py:322
  65.6 2.9 %collective-permute-done.10 = bf16[512,768]{1,0:T(8,128)(2,1)S(1)} collective-permute-done((bf16[512,768]{1,0:T(8,128)(2,1)}, bf16[512,768]{1,0:T(8,128)(2,1)S(1)}, u32[]{:S(2)}, u32[]{:S(2)}) %collective-permute-start.10) | collective-permute-done | bytes 786464 | tf_op jit(solution)/shard_map/ppermute | solution.py:318
  68.6 9.2 %collective-permute-start.4 = (bf16[1024,512]{1,0:T(8,128)(2,1)S(1)}, bf16[1024,512]{1,0:T(8,128)(2,1)S(1)}, u32[]{:S(2)}, u32[]{:S(2)}) collective-permute-start(bf16[1024,512]{1,0:T(8,128)(2,1)S(1)} %get-tuple-element.81), channel_id=1, source_target_pairs={{2,4},{3,5},{4,2},{5,3},{10,12},{11,13},{12,10},{13,11},{18,20},{1... | collective-permute-start | bytes 3145736 | tf_op jit(solution)/shard_map/ppermute | solution.py:323
  77.8 3.2 %collective-permute-start.11 = (bf16[512,768]{1,0:T(8,128)(2,1)S(1)}, bf16[512,768]{1,0:T(8,128)(2,1)S(1)}, u32[]{:S(2)}, u32[]{:S(2)}) collective-permute-start(bf16[512,768]{1,0:T(8,128)(2,1)S(1)} %collective-permute-done.10), channel_id=1, source_target_pairs={{2,10},{3,11},{4,12},{5,13},{10,18},{11,19},{12,20},{13,21},{18,26... | collective-permute-start | bytes 2359304 | tf_op jit(solution)/shard_map/ppermute | solution.py:363
  81.0 2.4 %broadcast_select_fusion.1 = (bf16[768,512]{1,0:T(8,128)(2,1)}, bf16[768,512]{1,0:T(8,128)(2,1)S(1)}) fusion(bf16[768,512]{1,0:T(8,128)(2,1)} %collective-permute-done.12, bf16[768,512]{1,0:T(8,128)(2,1)} %collective-permute-done, pred[]{:T(512)S(6)} %eq.43), kind=kLoop, calls=%fused_computation.10 | loop fusion | flops 786432 | bytes 3145729 | tf_op jit(solution)/shard_map/jit(_where)/select_n | solution.py:370
  83.5 2.3 %broadcast_select_fusion.3 = (bf16[512,768]{1,0:T(8,128)(2,1)S(1)}, bf16[512,768]{1,0:T(8,128)(2,1)}) fusion(bf16[512,768]{1,0:T(8,128)(2,1)S(1)} %collective-permute-done.9, bf16[512,768]{1,0:T(8,128)(2,1)} %collective-permute-done.1, pred[]{:T(512)S(6)} %eq.43), kind=kLoop, calls=%fused_computation.12 | loop fusion | flops 786432 | bytes 3145729 | tf_op jit(solution)/shard_map/jit(_where)/select_n | solution.py:372
  85.8 3.5 %collective-permute-done.13 = bf16[768,512]{1,0:T(8,128)(2,1)S(1)} collective-permute-done((bf16[768,512]{1,0:T(8,128)(2,1)S(1)}, bf16[768,512]{1,0:T(8,128)(2,1)S(1)}, u32[]{:S(2)}, u32[]{:S(2)}) %collective-permute-start.13) | collective-permute-done | bytes 786464 | tf_op jit(solution)/shard_map/ppermute | solution.py:360
  89.3 0.2 bitcast_select_fusion
  89.5 10.0 %collective-permute-done.11 = bf16[512,768]{1,0:T(8,128)(2,1)S(1)} collective-permute-done((bf16[512,768]{1,0:T(8,128)(2,1)S(1)}, bf16[512,768]{1,0:T(8,128)(2,1)S(1)}, u32[]{:S(2)}, u32[]{:S(2)}) %collective-permute-start.11) | collective-permute-done | bytes 786464 | tf_op jit(solution)/shard_map/ppermute | solution.py:363
  99.5 1.1 bitcast_select_fusion.2
  100.5 1.9 %collective-permute-done.4 = bf16[1024,512]{1,0:T(8,128)(2,1)S(1)} collective-permute-done((bf16[1024,512]{1,0:T(8,128)(2,1)S(1)}, bf16[1024,512]{1,0:T(8,128)(2,1)S(1)}, u32[]{:S(2)}, u32[]{:S(2)}) %collective-permute-start.4) | collective-permute-done | bytes 1048608 | tf_op jit(solution)/shard_map/ppermute | solution.py:323
  102.5 1.1 collective-permute-start.16
  103.6 2.6 %collective-permute-start.17 = (f32[3,768]{1,0:T(4,128)S(1)}, f32[3,768]{1,0:T(4,128)S(1)}, u32[]{:S(2)}, u32[]{:S(2)}) collective-permute-start(f32[3,768]{1,0:T(4,128)S(1)} %pad_maximum_fusion), channel_id=1, source_target_pairs={{2,4},{3,5},{4,2},{5,3},{10,12},{11,13},{12,10},{13,11},{18,20},{1... | collective-permute-start | bytes 27656 | tf_op jit(solution)/shard_map/ppermute | solution.py:367
  106.3 0.8 collective-permute-start.14
  107.1 0.1 broadcast_select_fusion.cb_ref
  107.2 1.3 context_part.1
  108.5 1.3 copy-done.5
  109.9 0.8 copy-done.7
  110.8 2.4 %collective-permute-start.15 = (f32[2,2]{0,1:T(2,128)S(1)}, f32[2,2]{0,1:T(2,128)S(1)}, u32[]{:S(2)}, u32[]{:S(2)}) collective-permute-start(f32[2,2]{0,1:T(2,128)S(1)} %slice.63), channel_id=1, source_target_pairs={{0,64},{4,68},{8,72},{12,76},{16,80},{20,84},{24,88},{28,92},{32,9... | collective-permute-start | bytes 56 | tf_op jit(solution)/shard_map/ppermute | solution.py:339
  113.2 1.6 %copy-done.6 = f32[1024,512]{1,0:T(8,128)S(1)} copy-done((f32[1024,512]{1,0:T(8,128)S(1)}, f32[1024,512]{1,0:T(8,128)}, u32[]{:S(2)}) %copy-start.6) | copy-done | bytes 2097176
  114.8 1.0 copy-done.8
  115.9 6.8 %first_layer.1 = (bf16[1024,512]{1,0:T(8,128)(2,1)S(1)}, bf16[1024,512]{1,0:T(8,128)(2,1)S(1)}, f32[16,1024]{1,0:T(8,128)S(1)}) custom-call(bf16[16,512]{1,0:T(8,128)(2,1)S(1)} %broadcast_in_dim.43.u_ref, f32[1024,512]{1,0:T(8,128)S(1)} %copy-done.6, bf16[512,512]{1,0:T(8,128)(2,1)S(1)} %copy-done.8, bf16[2048,512]{1,0:T(8,128)(2,1)} %bitcast.13.recv_hbm), custom_call_target="tpu_custom_call" | custom-call | flops 15728640000 | bytes 8388608 | tf_op jit(solution)/shard_map/first_layer/pallas_call | solution.py:78
  122.8 0.1 collective-permute-start.18
  122.9 2.3 %collective-permute-start.19 = (f32[1,2]{0,1:T(2,128)S(1)}, f32[1,2]{0,1:T(2,128)S(1)}, u32[]{:S(2)}, u32[]{:S(2)}) collective-permute-start(f32[1,2]{0,1:T(2,128)S(1)} %slice.65), channel_id=1, source_target_pairs={{0,192},{4,196},{8,200},{12,204},{16,208},{20,212},{24,216},{28,22... | collective-permute-start | bytes 32 | tf_op jit(solution)/shard_map/ppermute | solution.py:339
  125.2 2.3 %collective-permute-done.19 = f32[1,2]{0,1:T(2,128)S(1)} collective-permute-done((f32[1,2]{0,1:T(2,128)S(1)}, f32[1,2]{0,1:T(2,128)S(1)}, u32[]{:S(2)}, u32[]{:S(2)}) %collective-permute-start.19) | collective-permute-done | bytes 40 | tf_op jit(solution)/shard_map/ppermute | solution.py:339
  127.5 1.5 collective-permute-start.20
  129.0 2.4 %collective-permute-start.21 = (f32[1,2]{0,1:T(2,128)S(1)}, f32[1,2]{0,1:T(2,128)S(1)}, u32[]{:S(2)}, u32[]{:S(2)}) collective-permute-start(f32[1,2]{0,1:T(2,128)S(1)} %slice_maximum_fusion), channel_id=1, source_target_pairs={{0,3},{1,2},{2,1},{3,0},{4,7},{5,6},{6,5},{7,4},{8,11},{9,10},{10,... | collective-permute-start | bytes 32 | tf_op jit(solution)/shard_map/ppermute | solution.py:344
  131.5 0.1 collective-permute-start.22
  131.6 3.7 %second_layer.1 = (bf16[1024,768]{1,0:T(8,128)(2,1)S(1)}, bf16[1024,768]{1,0:T(8,128)(2,1)S(1)}, bf16[1024,512]{1,0:T(8,128)(2,1)S(1)}) custom-call(bf16[1024,512]{1,0:T(8,128)(2,1)S(1)} %get-tuple-element.60.mine_ref, bf16[1024,512]{1,0:T(8,128)(2,1)S(1)} %collective-permute-done.18.other_ref, bf16[1024,512]{1,0:T(8,128)(2,1)S(1)} %get-tuple-element.63.pay_ref, ...), custom_call_target="tpu_custom_call" | custom-call | flops 15728640000 | bytes 12582912 | tf_op jit(solution)/shard_map/second_layer/pallas_call | solution.py:78
  135.4 2.9 %collective-permute-start.23 = (bf16[1024,512]{1,0:T(8,128)(2,1)S(1)}, bf16[1024,512]{1,0:T(8,128)(2,1)S(1)}, u32[]{:S(2)}, u32[]{:S(2)}) collective-permute-start(bf16[1024,512]{1,0:T(8,128)(2,1)S(1)} %get-tuple-element.70.mine_ref), channel_id=1, source_target_pairs={{0,4},{1,5},{2,6},{3,7},{4,0},{5,1},{6,2},{7,3},{8,12},{9,13},{10,... | collective-permute-start | bytes 3145736 | tf_op jit(solution)/shard_map/ppermute | solution.py:413
  139.0 0.6 fusion.4
  140.2 0.4 collective-permute-done.23.other_ref
  140.6 3.1 %last_layer.1 = f32[16,1024]{1,0:T(8,128)S(1)} custom-call(f32[1]{0:T(128)} %copy.14.coefficient, bf16[1024,512]{1,0:T(8,128)(2,1)S(1)} %get-tuple-element.70.mine_ref, bf16[1024,512]{1,0:T(8,128)(2,1)S(1)} %collective-permute-done.23.other_ref, bf16[1024,512]{1,0:T(8,128)(2,1)S(1)} %get-tuple-element.63.pay_ref, ...), custom_call_target="tpu_custom_call" | custom-call | flops 1879048192 | bytes 10485760 | tf_op jit(solution)/shard_map/last_layer/pallas_call | solution.py:78
  143.7 0.4 collective-permute-start.24
  144.1 0.8 collective-permute-done.24
  145.0 4.2 %collective-permute-start.26 = (f32[1,1024]{1,0:T(1,128)S(1)}, f32[1,1024]{1,0:T(1,128)S(1)}, u32[]{:S(2)}, u32[]{:S(2)}) collective-permute-start(f32[1,1024]{1,0:T(1,128)S(1)} %fusion.7), channel_id=1, source_target_pairs={{2,4},{3,5},{4,2},{5,3},{10,12},{11,13},{12,10},{13,11},{18,20},{1... | collective-permute-start | bytes 12296 | tf_op jit(solution)/shard_map/ppermute | solution.py:422
  149.2 0.8 collective-permute-start.25
  150.0 1.4 collective-permute-done.26
  151.4 2.1 %collective-permute-done.25 = f32[1,1024]{1,0:T(1,128)S(1)} collective-permute-done((f32[1,1024]{1,0:T(1,128)S(1)}, f32[1,1024]{1,0:T(1,128)S(1)}, u32[]{:S(2)}, u32[]{:S(2)}) %collective-permute-start.25) | collective-permute-done | bytes 4128 | tf_op jit(solution)/shard_map/ppermute | solution.py:421
  153.5 0.6 maximum_select_fusion
  (76 shorter events, 0.8 us)
Async XLA Ops:
  0.0 5.3 %copy-start.10 = (bf16[2,512,768]{2,1,0:T(8,128)(2,1)S(1)}, bf16[2,512,768]{2,1,0:T(8,128)(2,1)}, u32[]{:S(2)}) copy-start(bf16[2,512,768]{2,1,0:T(8,128)(2,1)} %param.19) | copy-start | bytes 4718596
  0.0 5.7 %copy-start.17 = (bf16[2,256]{1,0:T(2,128)(2,1)S(1)}, bf16[2,256]{1,0:T(2,128)(2,1)}, u32[]{:S(2)}) copy-start(bf16[2,256]{1,0:T(2,128)(2,1)} %param.12) | copy-start | bytes 3076
  0.0 18.1 %copy-start.18 = (bf16[768]{0:T(1024)(128)(2,1)S(1)}, bf16[768]{0:T(1024)(128)(2,1)}, u32[]{:S(2)}) copy-start(bf16[768]{0:T(1024)(128)(2,1)} %param.21) | copy-start | bytes 4612
  1.3 26.9 %collective-permute-start = (bf16[768,512]{1,0:T(8,128)(2,1)S(1)}, bf16[768,512]{1,0:T(8,128)(2,1)}, u32[]{:S(2)}, u32[]{:S(2)}) collective-permute-start(bf16[768,512]{1,0:T(8,128)(2,1)S(1)} %dynamic-slice_bitcast_fusion.3), channel_id=1, source_target_pairs={{0,1},{1,0},{2,5},{3,4},{4,3},{5,2},{6,7},{7,6},{8,9},{9,8},{10,13... | collective-permute-start | bytes 2359304 | tf_op jit(solution)/shard_map/ppermute | solution.py:304
  5.3 22.9 %collective-permute-start.1 = (bf16[512,768]{1,0:T(8,128)(2,1)S(1)}, bf16[512,768]{1,0:T(8,128)(2,1)}, u32[]{:S(2)}, u32[]{:S(2)}) collective-permute-start(bf16[512,768]{1,0:T(8,128)(2,1)S(1)} %dynamic-slice_bitcast_fusion.2), channel_id=1, source_target_pairs={{0,1},{1,0},{2,5},{3,4},{4,3},{5,2},{6,7},{7,6},{8,9},{9,8},{10,13... | collective-permute-start | bytes 2359304 | tf_op jit(solution)/shard_map/ppermute | solution.py:305
  6.3 21.9 %all-to-all-start = ((bf16[64,2,256]{2,1,0:T(2,128)(2,1)}), bf16[64,2,256]{2,1,0:T(2,128)(2,1)S(1)}, u32[]{:S(2)}, u32[]{:S(2)}) async-start(bf16[64,2,256]{2,1,0:T(2,128)(2,1)} %broadcast_in_dim.41), calls=%async_computation | async-start | bytes 131072 | tf_op jit(solution)/shard_map/all_to_all | solution.py:307
  18.9 9.3 %copy-start.13 = (bf16[2048,256]{1,0:T(8,128)(2,1)S(1)}, bf16[2048,256]{1,0:T(8,128)(2,1)}, u32[]{:S(2)}) copy-start(bf16[2048,256]{1,0:T(8,128)(2,1)} %emb_hbm.1) | copy-start | bytes 3145732
  29.2 29.2 %copy-start.16 = (f32[2,768]{1,0:T(2,128)S(1)}, f32[2,768]{1,0:T(2,128)}, u32[]{:S(2)}) copy-start(f32[2,768]{1,0:T(2,128)} %param.20) | copy-start | bytes 18436
  29.2 31.7 %copy-start.12 = (bf16[2,1024,512]{2,1,0:T(8,128)(2,1)S(1)}, bf16[2,1024,512]{2,1,0:T(8,128)(2,1)}, u32[]{:S(2)}) copy-start(bf16[2,1024,512]{2,1,0:T(8,128)(2,1)} %param.17) | copy-start | bytes 6291460
  29.2 19.5 %collective-permute-start.5 = (f32[32,2]{0,1:T(2,128)S(1)}, f32[32,2]{0,1:T(2,128)S(1)}, u32[]{:S(2)}, u32[]{:S(2)}) collective-permute-start(f32[32,2]{0,1:T(2,128)S(1)} %slice.52), channel_id=1, source_target_pairs={{0,4},{4,0},{8,12},{12,8},{16,20},{20,16},{24,28},{28,24},{32,36},... | collective-permute-start | bytes 776 | tf_op jit(solution)/shard_map/ppermute | solution.py:339
  29.7 28.8 %collective-permute-start.2 = (bf16[768,512]{1,0:T(8,128)(2,1)}, bf16[768,512]{1,0:T(8,128)(2,1)S(1)}, u32[]{:S(2)}, u32[]{:S(2)}) collective-permute-start(bf16[768,512]{1,0:T(8,128)(2,1)} %collective-permute-done), channel_id=1, source_target_pairs={{0,3},{1,2},{6,5},{7,4},{8,11},{9,10},{14,13},{15,12},{16,19},{17,... | collective-permute-start | bytes 2359304 | tf_op jit(solution)/shard_map/ppermute | solution.py:317
  31.1 46.7 %collective-permute-start.12 = (bf16[768,512]{1,0:T(8,128)(2,1)}, bf16[768,512]{1,0:T(8,128)(2,1)}, u32[]{:S(2)}, u32[]{:S(2)}) collective-permute-start(bf16[768,512]{1,0:T(8,128)(2,1)} %collective-permute-done), channel_id=1, source_target_pairs={{0,24},{1,25},{2,10},{3,11},{4,12},{5,13},{6,30},{7,31},{8,0},{9,1... | collective-permute-start | bytes 2359304 | tf_op jit(solution)/shard_map/ppermute | solution.py:359
  31.4 79.3 %all-to-all-start.1 = ((bf16[256,8,512]{2,1,0:T(8,128)(2,1)}), bf16[256,8,512]{2,1,0:T(8,128)(2,1)}, u32[]{:S(2)}, u32[]{:S(2)}) async-start(bf16[256,8,512]{2,1,0:T(8,128)(2,1)} %bitcast.32), calls=%async_computation.1 | async-start | bytes 4194304 | tf_op jit(solution)/shard_map/all_to_all | solution.py:314
  45.4 23.2 %collective-permute-start.10 = (bf16[512,768]{1,0:T(8,128)(2,1)}, bf16[512,768]{1,0:T(8,128)(2,1)S(1)}, u32[]{:S(2)}, u32[]{:S(2)}) collective-permute-start(bf16[512,768]{1,0:T(8,128)(2,1)} %collective-permute-done.1), channel_id=1, source_target_pairs={{2,3},{3,2},{4,5},{5,4},{10,11},{11,10},{12,13},{13,12},{18,19},{1... | collective-permute-start | bytes 2359304 | tf_op jit(solution)/shard_map/ppermute | solution.py:318
  48.8 3.0 %collective-permute-start.6 = (f32[8,2]{0,1:T(2,128)S(1)}, f32[8,2]{0,1:T(2,128)S(1)}, u32[]{:S(2)}, u32[]{:S(2)}) collective-permute-start(f32[8,2]{0,1:T(2,128)S(1)} %get-tuple-element.87), channel_id=1, source_target_pairs={{0,8},{4,12},{8,0},{12,4},{16,24},{20,28},{24,16},{28,20},{32,40},... | collective-permute-start | bytes 200 | tf_op jit(solution)/shard_map/ppermute | solution.py:352
  50.0 4.3 %collective-permute-start.7 = (f32[8,2]{0,1:T(2,128)S(1)}, f32[8,2]{0,1:T(2,128)S(1)}, u32[]{:S(2)}, u32[]{:S(2)}) collective-permute-start(f32[8,2]{0,1:T(2,128)S(1)} %get-tuple-element.89), channel_id=1, source_target_pairs={{0,24},{4,28},{8,16},{12,20},{16,8},{20,12},{24,0},{28,4},{32,56},... | collective-permute-start | bytes 200 | tf_op jit(solution)/shard_map/ppermute | solution.py:352
  51.8 4.3 %collective-permute-start.8 = (f32[8,2]{0,1:T(2,128)S(1)}, f32[8,2]{0,1:T(2,128)S(1)}, u32[]{:S(2)}, u32[]{:S(2)}) collective-permute-start(f32[8,2]{0,1:T(2,128)S(1)} %get-tuple-element.88), channel_id=1, source_target_pairs={{0,16},{4,20},{8,24},{12,28},{16,0},{20,4},{24,8},{28,12},{32,48},... | collective-permute-start | bytes 200 | tf_op jit(solution)/shard_map/ppermute | solution.py:352
  56.1 27.4 %collective-permute-start.9 = (bf16[512,768]{1,0:T(8,128)(2,1)}, bf16[512,768]{1,0:T(8,128)(2,1)S(1)}, u32[]{:S(2)}, u32[]{:S(2)}) collective-permute-start(bf16[512,768]{1,0:T(8,128)(2,1)} %collective-permute-done.1), channel_id=1, source_target_pairs={{0,8},{1,9},{2,26},{3,27},{4,28},{5,29},{6,14},{7,15},{8,16},{9,17... | collective-permute-start | bytes 2359304 | tf_op jit(solution)/shard_map/ppermute | solution.py:362
  58.5 2.6 %copy-start.14 = (bf16[768,512]{1,0:T(8,128)(2,1)}, bf16[768,512]{1,0:T(8,128)(2,1)S(1)}, u32[]{:S(2)}) copy-start(bf16[768,512]{1,0:T(8,128)(2,1)S(1)} %collective-permute-done.2) | copy-start | bytes 2359300
  58.5 30.8 %collective-permute-start.13 = (bf16[768,512]{1,0:T(8,128)(2,1)S(1)}, bf16[768,512]{1,0:T(8,128)(2,1)S(1)}, u32[]{:S(2)}, u32[]{:S(2)}) collective-permute-start(bf16[768,512]{1,0:T(8,128)(2,1)S(1)} %collective-permute-done.2), channel_id=1, source_target_pairs={{2,26},{3,27},{4,28},{5,29},{10,2},{11,3},{12,4},{13,5},{18,10},{1... | collective-permute-start | bytes 2359304 | tf_op jit(solution)/shard_map/ppermute | solution.py:360
  61.1 39.4 %collective-permute-start.3 = (bf16[1024,512]{1,0:T(8,128)(2,1)S(1)}, bf16[1024,512]{1,0:T(8,128)(2,1)S(1)}, u32[]{:S(2)}, u32[]{:S(2)}) collective-permute-start(bf16[1024,512]{1,0:T(8,128)(2,1)S(1)} %get-tuple-element.82), channel_id=1, source_target_pairs={{0,1},{1,0},{2,5},{3,4},{4,3},{5,2},{6,7},{7,6},{8,9},{9,8},{10,13... | collective-permute-start | bytes 3145736 | tf_op jit(solution)/shard_map/ppermute | solution.py:322
  68.6 33.9 %collective-permute-start.4 = (bf16[1024,512]{1,0:T(8,128)(2,1)S(1)}, bf16[1024,512]{1,0:T(8,128)(2,1)S(1)}, u32[]{:S(2)}, u32[]{:S(2)}) collective-permute-start(bf16[1024,512]{1,0:T(8,128)(2,1)S(1)} %get-tuple-element.81), channel_id=1, source_target_pairs={{2,4},{3,5},{4,2},{5,3},{10,12},{11,13},{12,10},{13,11},{18,20},{1... | collective-permute-start | bytes 3145736 | tf_op jit(solution)/shard_map/ppermute | solution.py:323
  77.8 21.6 %collective-permute-start.11 = (bf16[512,768]{1,0:T(8,128)(2,1)S(1)}, bf16[512,768]{1,0:T(8,128)(2,1)S(1)}, u32[]{:S(2)}, u32[]{:S(2)}) collective-permute-start(bf16[512,768]{1,0:T(8,128)(2,1)S(1)} %collective-permute-done.10), channel_id=1, source_target_pairs={{2,10},{3,11},{4,12},{5,13},{10,18},{11,19},{12,20},{13,21},{18,26... | collective-permute-start | bytes 2359304 | tf_op jit(solution)/shard_map/ppermute | solution.py:363
  83.5 5.9 %copy-start.9 = (bf16[2,768,512]{2,1,0:T(8,128)(2,1)S(1)}, bf16[2,768,512]{2,1,0:T(8,128)(2,1)}, u32[]{:S(2)}) copy-start(bf16[2,768,512]{2,1,0:T(8,128)(2,1)} %param.18) | copy-start | bytes 4718596
  83.5 5.9 %copy-start.15 = (bf16[768,512]{1,0:T(8,128)(2,1)S(1)}, bf16[768,512]{1,0:T(8,128)(2,1)}, u32[]{:S(2)}) copy-start(bf16[768,512]{1,0:T(8,128)(2,1)} %copy-done.14) | copy-start | bytes 2359300
  85.8 13.7 %copy-start.11 = (bf16[2,512,768]{2,1,0:T(8,128)(2,1)S(1)}, bf16[2,512,768]{2,1,0:T(8,128)(2,1)}, u32[]{:S(2)}) copy-start(bf16[2,512,768]{2,1,0:T(8,128)(2,1)} %param.19) | copy-start | bytes 4718596
  100.5 6.7 %copy-start = (bf16[1024,512]{1,0:T(8,128)(2,1)}, bf16[1024,512]{1,0:T(8,128)(2,1)S(1)}, u32[]{:S(2)}) copy-start(bf16[1024,512]{1,0:T(8,128)(2,1)S(1)} %collective-permute-done.3.ca_ref) | copy-start | bytes 3145732
  102.5 20.3 %collective-permute-start.16 = (f32[3,768]{1,0:T(4,128)S(1)}, f32[3,768]{1,0:T(4,128)S(1)}, u32[]{:S(2)}, u32[]{:S(2)}) collective-permute-start(f32[3,768]{1,0:T(4,128)S(1)} %pad_maximum_fusion), channel_id=1, source_target_pairs={{0,1},{1,0},{2,5},{3,4},{4,3},{5,2},{6,7},{7,6},{8,9},{9,8},{10,13... | collective-permute-start | bytes 27656 | tf_op jit(solution)/shard_map/ppermute | solution.py:366
  103.6 19.2 %collective-permute-start.17 = (f32[3,768]{1,0:T(4,128)S(1)}, f32[3,768]{1,0:T(4,128)S(1)}, u32[]{:S(2)}, u32[]{:S(2)}) collective-permute-start(f32[3,768]{1,0:T(4,128)S(1)} %pad_maximum_fusion), channel_id=1, source_target_pairs={{2,4},{3,5},{4,2},{5,3},{10,12},{11,13},{12,10},{13,11},{18,20},{1... | collective-permute-start | bytes 27656 | tf_op jit(solution)/shard_map/ppermute | solution.py:367
  106.3 4.4 %collective-permute-start.14 = (f32[4,2]{0,1:T(2,128)S(1)}, f32[4,2]{0,1:T(2,128)S(1)}, u32[]{:S(2)}, u32[]{:S(2)}) collective-permute-start(f32[4,2]{0,1:T(2,128)S(1)} %slice.61), channel_id=1, source_target_pairs={{0,32},{4,36},{8,40},{12,44},{16,48},{20,52},{24,56},{28,60},{32,0... | collective-permute-start | bytes 104 | tf_op jit(solution)/shard_map/ppermute | solution.py:339
  108.5 1.4 copy-start.5
  109.9 0.8 copy-start.7
  110.8 12.0 %collective-permute-start.15 = (f32[2,2]{0,1:T(2,128)S(1)}, f32[2,2]{0,1:T(2,128)S(1)}, u32[]{:S(2)}, u32[]{:S(2)}) collective-permute-start(f32[2,2]{0,1:T(2,128)S(1)} %slice.63), channel_id=1, source_target_pairs={{0,64},{4,68},{8,72},{12,76},{16,80},{20,84},{24,88},{28,92},{32,9... | collective-permute-start | bytes 56 | tf_op jit(solution)/shard_map/ppermute | solution.py:339
  113.2 1.6 %copy-start.6 = (f32[1024,512]{1,0:T(8,128)S(1)}, f32[1024,512]{1,0:T(8,128)}, u32[]{:S(2)}) copy-start(f32[1024,512]{1,0:T(8,128)} %copy-done.5) | copy-start | bytes 6291460
  114.8 1.0 copy-start.8
  115.9 15.8 %copy-start.1 = (bf16[1024,512]{1,0:T(8,128)(2,1)S(1)}, bf16[1024,512]{1,0:T(8,128)(2,1)}, u32[]{:S(2)}) copy-start(bf16[1024,512]{1,0:T(8,128)(2,1)} %copy-done) | copy-start | bytes 3145732
  115.9 15.8 %copy-start.2 = (bf16[512,768]{1,0:T(8,128)(2,1)S(1)}, bf16[512,768]{1,0:T(8,128)(2,1)}, u32[]{:S(2)}) copy-start(bf16[512,768]{1,0:T(8,128)(2,1)} %get-tuple-element.67.ub_ref) | copy-start | bytes 2359300
  115.9 15.8 %copy-start.3 = (bf16[768,512]{1,0:T(8,128)(2,1)S(1)}, bf16[768,512]{1,0:T(8,128)(2,1)}, u32[]{:S(2)}) copy-start(bf16[768,512]{1,0:T(8,128)(2,1)} %get-tuple-element.83.va_ref) | copy-start | bytes 2359300
  115.9 15.8 %copy-start.4 = (bf16[512,768]{1,0:T(8,128)(2,1)S(1)}, bf16[512,768]{1,0:T(8,128)(2,1)}, u32[]{:S(2)}) copy-start(bf16[512,768]{1,0:T(8,128)(2,1)} %get-tuple-element.66.ua_ref) | copy-start | bytes 2359300
  122.8 4.7 %collective-permute-start.18 = (bf16[1024,512]{1,0:T(8,128)(2,1)S(1)}, bf16[1024,512]{1,0:T(8,128)(2,1)S(1)}, u32[]{:S(2)}, u32[]{:S(2)}) collective-permute-start(bf16[1024,512]{1,0:T(8,128)(2,1)S(1)} %get-tuple-element.60.mine_ref), channel_id=1, source_target_pairs={{0,4},{1,5},{2,6},{3,7},{4,0},{5,1},{6,2},{7,3},{8,12},{9,13},{10,... | collective-permute-start | bytes 3145736 | tf_op jit(solution)/shard_map/ppermute | solution.py:405
  122.9 4.6 %collective-permute-start.19 = (f32[1,2]{0,1:T(2,128)S(1)}, f32[1,2]{0,1:T(2,128)S(1)}, u32[]{:S(2)}, u32[]{:S(2)}) collective-permute-start(f32[1,2]{0,1:T(2,128)S(1)} %slice.65), channel_id=1, source_target_pairs={{0,192},{4,196},{8,200},{12,204},{16,208},{20,212},{24,216},{28,22... | collective-permute-start | bytes 32 | tf_op jit(solution)/shard_map/ppermute | solution.py:339
  127.5 7.9 %collective-permute-start.20 = (f32[1,2]{0,1:T(2,128)S(1)}, f32[1,2]{0,1:T(2,128)S(1)}, u32[]{:S(2)}, u32[]{:S(2)}) collective-permute-start(f32[1,2]{0,1:T(2,128)S(1)} %slice_maximum_fusion), channel_id=1, source_target_pairs={{0,1},{1,0},{2,3},{3,2},{4,5},{5,4},{6,7},{7,6},{8,9},{9,8},{10,11... | collective-permute-start | bytes 32 | tf_op jit(solution)/shard_map/ppermute | solution.py:344
  129.0 6.4 %collective-permute-start.21 = (f32[1,2]{0,1:T(2,128)S(1)}, f32[1,2]{0,1:T(2,128)S(1)}, u32[]{:S(2)}, u32[]{:S(2)}) collective-permute-start(f32[1,2]{0,1:T(2,128)S(1)} %slice_maximum_fusion), channel_id=1, source_target_pairs={{0,3},{1,2},{2,1},{3,0},{4,7},{5,6},{6,5},{7,4},{8,11},{9,10},{10,... | collective-permute-start | bytes 32 | tf_op jit(solution)/shard_map/ppermute | solution.py:344
  131.5 3.9 %collective-permute-start.22 = (f32[1,2]{0,1:T(2,128)S(1)}, f32[1,2]{0,1:T(2,128)S(1)}, u32[]{:S(2)}, u32[]{:S(2)}) collective-permute-start(f32[1,2]{0,1:T(2,128)S(1)} %slice_maximum_fusion), channel_id=1, source_target_pairs={{0,2},{1,3},{2,0},{3,1},{4,6},{5,7},{6,4},{7,5},{8,10},{9,11},{10,... | collective-permute-start | bytes 32 | tf_op jit(solution)/shard_map/ppermute | solution.py:344
  135.4 5.2 %collective-permute-start.23 = (bf16[1024,512]{1,0:T(8,128)(2,1)S(1)}, bf16[1024,512]{1,0:T(8,128)(2,1)S(1)}, u32[]{:S(2)}, u32[]{:S(2)}) collective-permute-start(bf16[1024,512]{1,0:T(8,128)(2,1)S(1)} %get-tuple-element.70.mine_ref), channel_id=1, source_target_pairs={{0,4},{1,5},{2,6},{3,7},{4,0},{5,1},{6,2},{7,3},{8,12},{9,13},{10,... | collective-permute-start | bytes 3145736 | tf_op jit(solution)/shard_map/ppermute | solution.py:413
  143.7 1.3 collective-permute-start.24
  145.0 6.4 %collective-permute-start.26 = (f32[1,1024]{1,0:T(1,128)S(1)}, f32[1,1024]{1,0:T(1,128)S(1)}, u32[]{:S(2)}, u32[]{:S(2)}) collective-permute-start(f32[1,1024]{1,0:T(1,128)S(1)} %fusion.7), channel_id=1, source_target_pairs={{2,4},{3,5},{4,2},{5,3},{10,12},{11,13},{12,10},{13,11},{18,20},{1... | collective-permute-start | bytes 12296 | tf_op jit(solution)/shard_map/ppermute | solution.py:422
  149.2 4.3 %collective-permute-start.25 = (f32[1,1024]{1,0:T(1,128)S(1)}, f32[1,1024]{1,0:T(1,128)S(1)}, u32[]{:S(2)}, u32[]{:S(2)}) collective-permute-start(f32[1,1024]{1,0:T(1,128)S(1)} %fusion.7), channel_id=1, source_target_pairs={{0,1},{1,0},{2,5},{3,4},{4,3},{5,2},{6,7},{7,6},{8,9},{9,8},{10,13... | collective-permute-start | bytes 12296 | tf_op jit(solution)/shard_map/ppermute | solution.py:421

commit v12 on v11

--- a/solution.py
+++ b/solution.py
@@ -358,7 +358,7 @@
     small = jnp.concatenate([interaction_offset, final_projection[None, :].astype(F32)], 0)
     v_near_y = move(v_near, perm=y_split)
     v_far_y = move(v_far, perm=y_down)
-    best, u_near_on = lax.optimization_barrier((best, u_near))
+    best, v_near_y, u_near_on = lax.optimization_barrier((best, v_near_y, u_near))
     u_near_y = move(u_near_on, perm=y_mirror)
     u_far_y = move(u_far, perm=y_up)
     ctx_a, best, small = lax.optimization_barrier((ctx_a, best, small))

time: 155 us -> 163 us (1.052)
  waiting for transfers between devices: 28.4 us -> 34.8 us
    ppermute x1, waiting for transfers between devices: 9.95 us -> 0.58 us  [on_device(): u_far_y = move(u_far, perm=y_up)]
    ppermute x1, waiting for transfers between devices: 0.01 us -> 8 us  [on_device(): ctx_a = move(ctx_away, perm=ctx_near)]
    ppermute x1, waiting for transfers between devices: 2.93 us -> 10 us  [on_device(): u_far = move(u_near, perm=away_swap)]
    ppermute x1, starting transfers between devices: 9.23 us -> 2.46 us  [on_device(): ctx_b = move(ctx_own, perm=ctx_far)]
    ppermute x1, starting transfers between devices: 2.41 us -> 5.48 us  [on_device(): v_far_y = move(v_far, perm=y_down)]
    ppermute x1, waiting for transfers between devices: 3.53 us -> 6.43 us  [on_device(): v_far_y = move(v_far, perm=y_down)]
    ppermute x1, starting transfers between devices: 4.51 us -> 7.08 us  [on_device(): ctx_a = move(ctx_away, perm=ctx_near)]
    ppermute x4, starting transfers between devices: 5.97 us -> 8 us  [halve(): return jnp.maximum(best[:half], lax.ppermute(best[half:], 'shard', pairs))]
  transfers between devices with their start and end apart: 29 -> 29, of which waited for: 11 -> 11; matrix products, arithmetic and copies ran while one was open for 6% -> 6% of each run, Pallas kernels for 13% -> 12%
where the time goes in v12:
time: 163 us; the launch traced here: 162 us
  starting transfers between devices  85.5 us (52%)
  waiting for transfers between devices  34.8 us (21%)
  Pallas kernels  23.1 us (14%)
  other arithmetic  8.39 us (5%)
  local copies, waits for them, and re-layouts  8.36 us (5%)
  between operations  1.64 us (1%)
    pallas_call x4, Pallas kernels, call(): pl.pallas_call(kernel, in_specs=[SMEM] * len(scalars) + [VMEM] * len(arra...  15 us
    all_to_all x1, starting transfers between devices, on_device(): recv = lax.all_to_all(parcel, AXES, split_axis=0, concat_axis=0, tiled=True)  14 us
    all_to_all x1, starting transfers between devices, on_device(): lax.all_to_all(users, 'shard', split_axis=0, concat_axis=0, tiled=True)  11.8 us
    ppermute x1, waiting for transfers between devices, on_device(): u_far = move(u_near, perm=away_swap)  10 us
    pallas_call x1, Pallas kernels, pick_rows(): pl.pallas_call(pick_kernel, in_specs=[VMEM, VMEM, ANY, ANY], out_specs=AN...  8.1 us
    ppermute x4, starting transfers between devices, halve(): return jnp.maximum(best[:half], lax.ppermute(best[half:], 'shard', pairs))  8 us
    ppermute x1, waiting for transfers between devices, on_device(): ctx_a = move(ctx_away, perm=ctx_near)  8 us
    ppermute x1, starting transfers between devices, on_device(): ctx_a = move(ctx_away, perm=ctx_near)  7.08 us
  transfers between devices with their start and end apart: 29, of which 11 were waited for; matrix products, arithmetic and copies ran while one was open for 6% of the time, Pallas kernels for 12%

profile of v12, /device:TPU:1, one launch (start us, length us, event | category | flops | bytes accessed | tf_op | source)
XLA Modules:
  0.0 162.3 jit_solution(2663944894112057084)
XLA Ops:
  0.0 1.3 dynamic-slice_bitcast_fusion.3
  1.3 4.0 %collective-permute-start = (bf16[768,512]{1,0:T(8,128)(2,1)S(1)}, bf16[768,512]{1,0:T(8,128)(2,1)}, u32[]{:S(2)}, u32[]{:S(2)}) collective-permute-start(bf16[768,512]{1,0:T(8,128)(2,1)S(1)} %dynamic-slice_bitcast_fusion.3), channel_id=1, source_target_pairs={{0,1},{1,0},{2,5},{3,4},{4,3},{5,2},{6,7},{7,6},{8,9},{9,8},{10,13... | collective-permute-start | bytes 2359304 | tf_op jit(solution)/shard_map/ppermute | solution.py:304
  5.3 0.3 collective-permute-start.1
  5.7 0.7 broadcast_in_dim.41
  6.3 11.8 %all-to-all-start = ((bf16[64,2,256]{2,1,0:T(2,128)(2,1)}), bf16[64,2,256]{2,1,0:T(2,128)(2,1)S(1)}, u32[]{:S(2)}, u32[]{:S(2)}) async-start(bf16[64,2,256]{2,1,0:T(2,128)(2,1)} %broadcast_in_dim.41), calls=%async_computation | async-start | bytes 131072 | tf_op jit(solution)/shard_map/all_to_all | solution.py:307
  18.2 0.7 fusion.2
  18.9 8.1 %pick_rows.1 = bf16[32,2,32,512]{3,2,1,0:T(8,128)(2,1)} custom-call(s32[8,128]{1,0:T(8,128)} %bitcast.33, s32[1,128]{1,0:T(1,128)} %bitcast.34, bf16[2048,256]{1,0:T(8,128)(2,1)} %emb_hbm.1, bf16[2048,768]{1,0:T(8,128)(2,1)} %attr_hbm.1), custom_call_target="tpu_custom_call" | custom-call | flops 4294967296 | bytes 6291456 | tf_op jit(solution)/shard_map/pick_rows/pallas_call | solution.py:144
  27.0 0.1 iota_compare_fusion
  27.1 1.0 all-to-all-done
  28.2 0.6 convolution_reduce_fusion
  28.7 0.1 broadcast_in_dim.45
  29.0 0.4 collective-permute-start.9
  29.4 0.1 select_reduce_fusion
  29.5 1.9 %collective-permute-start.5 = (f32[32,2]{0,1:T(2,128)S(1)}, f32[32,2]{0,1:T(2,128)S(1)}, u32[]{:S(2)}, u32[]{:S(2)}) collective-permute-start(f32[32,2]{0,1:T(2,128)S(1)} %slice.52), channel_id=1, source_target_pairs={{0,4},{4,0},{8,12},{12,8},{16,20},{20,16},{24,28},{28,24},{32,36},... | collective-permute-start | bytes 776 | tf_op jit(solution)/shard_map/ppermute | solution.py:339
  31.4 1.3 collective-permute-start.2
  32.7 14.0 %all-to-all-start.1 = ((bf16[256,8,512]{2,1,0:T(8,128)(2,1)}), bf16[256,8,512]{2,1,0:T(8,128)(2,1)}, u32[]{:S(2)}, u32[]{:S(2)}) async-start(bf16[256,8,512]{2,1,0:T(8,128)(2,1)} %bitcast.32), calls=%async_computation.1 | async-start | bytes 4194304 | tf_op jit(solution)/shard_map/all_to_all | solution.py:314
  46.7 3.3 %collective-permute-start.11 = (bf16[512,768]{1,0:T(8,128)(2,1)}, bf16[512,768]{1,0:T(8,128)(2,1)S(1)}, u32[]{:S(2)}, u32[]{:S(2)}) collective-permute-start(bf16[512,768]{1,0:T(8,128)(2,1)} %collective-permute-done.1), channel_id=1, source_target_pairs={{2,3},{3,2},{4,5},{5,4},{10,11},{11,10},{12,13},{13,12},{18,19},{1... | collective-permute-start | bytes 2359304 | tf_op jit(solution)/shard_map/ppermute | solution.py:318
  50.1 1.2 collective-permute-start.6
  51.3 1.8 %collective-permute-start.7 = (f32[8,2]{0,1:T(2,128)S(1)}, f32[8,2]{0,1:T(2,128)S(1)}, u32[]{:S(2)}, u32[]{:S(2)}) collective-permute-start(f32[8,2]{0,1:T(2,128)S(1)} %get-tuple-element.91), channel_id=1, source_target_pairs={{0,24},{4,28},{8,16},{12,20},{16,8},{20,12},{24,0},{28,4},{32,56},... | collective-permute-start | bytes 200 | tf_op jit(solution)/shard_map/ppermute | solution.py:352
  53.1 2.5 %collective-permute-start.8 = (f32[8,2]{0,1:T(2,128)S(1)}, f32[8,2]{0,1:T(2,128)S(1)}, u32[]{:S(2)}, u32[]{:S(2)}) collective-permute-start(f32[8,2]{0,1:T(2,128)S(1)} %get-tuple-element.90), channel_id=1, source_target_pairs={{0,16},{4,20},{8,24},{12,28},{16,0},{20,4},{24,8},{28,12},{32,48},... | collective-permute-start | bytes 200 | tf_op jit(solution)/shard_map/ppermute | solution.py:352
  55.6 1.8 %collective-permute-done.8 = f32[8,2]{0,1:T(2,128)S(1)} collective-permute-done((f32[8,2]{0,1:T(2,128)S(1)}, f32[8,2]{0,1:T(2,128)S(1)}, u32[]{:S(2)}, u32[]{:S(2)}) %collective-permute-start.8) | collective-permute-done | bytes 96 | tf_op jit(solution)/shard_map/ppermute | solution.py:352
  57.4 2.4 %collective-permute-start.10 = (bf16[512,768]{1,0:T(8,128)(2,1)}, bf16[512,768]{1,0:T(8,128)(2,1)S(1)}, u32[]{:S(2)}, u32[]{:S(2)}) collective-permute-start(bf16[512,768]{1,0:T(8,128)(2,1)} %collective-permute-done.1), channel_id=1, source_target_pairs={{0,8},{1,9},{2,26},{3,27},{4,28},{5,29},{6,14},{7,15},{8,16},{9,17... | collective-permute-start | bytes 2359304 | tf_op jit(solution)/shard_map/ppermute | solution.py:362
  59.9 10.0 %collective-permute-done.11 = bf16[512,768]{1,0:T(8,128)(2,1)S(1)} collective-permute-done((bf16[512,768]{1,0:T(8,128)(2,1)}, bf16[512,768]{1,0:T(8,128)(2,1)S(1)}, u32[]{:S(2)}, u32[]{:S(2)}) %collective-permute-start.11) | collective-permute-done | bytes 786464 | tf_op jit(solution)/shard_map/ppermute | solution.py:318
  69.9 3.2 %collective-permute-start.12 = (bf16[512,768]{1,0:T(8,128)(2,1)S(1)}, bf16[512,768]{1,0:T(8,128)(2,1)S(1)}, u32[]{:S(2)}, u32[]{:S(2)}) collective-permute-start(bf16[512,768]{1,0:T(8,128)(2,1)S(1)} %collective-permute-done.11), channel_id=1, source_target_pairs={{2,10},{3,11},{4,12},{5,13},{10,18},{11,19},{12,20},{13,21},{18,26... | collective-permute-start | bytes 2359304 | tf_op jit(solution)/shard_map/ppermute | solution.py:363
  73.1 0.1 dynamic-slice_bitcast_fusion
  73.3 7.1 %collective-permute-start.3 = (bf16[1024,512]{1,0:T(8,128)(2,1)S(1)}, bf16[1024,512]{1,0:T(8,128)(2,1)S(1)}, u32[]{:S(2)}, u32[]{:S(2)}) collective-permute-start(bf16[1024,512]{1,0:T(8,128)(2,1)S(1)} %get-tuple-element.84), channel_id=1, source_target_pairs={{0,1},{1,0},{2,5},{3,4},{4,3},{5,2},{6,7},{7,6},{8,9},{9,8},{10,13... | collective-permute-start | bytes 3145736 | tf_op jit(solution)/shard_map/ppermute | solution.py:322
  80.3 2.5 %collective-permute-start.4 = (bf16[1024,512]{1,0:T(8,128)(2,1)S(1)}, bf16[1024,512]{1,0:T(8,128)(2,1)S(1)}, u32[]{:S(2)}, u32[]{:S(2)}) collective-permute-start(bf16[1024,512]{1,0:T(8,128)(2,1)S(1)} %get-tuple-element.83), channel_id=1, source_target_pairs={{2,4},{3,5},{4,2},{5,3},{10,12},{11,13},{12,10},{13,11},{18,20},{1... | collective-permute-start | bytes 3145736 | tf_op jit(solution)/shard_map/ppermute | solution.py:323
  82.8 5.5 %collective-permute-start.13 = (bf16[768,512]{1,0:T(8,128)(2,1)}, bf16[768,512]{1,0:T(8,128)(2,1)S(1)}, u32[]{:S(2)}, u32[]{:S(2)}) collective-permute-start(bf16[768,512]{1,0:T(8,128)(2,1)} %collective-permute-done.2), channel_id=1, source_target_pairs={{2,26},{3,27},{4,28},{5,29},{10,2},{11,3},{12,4},{13,5},{18,10},{1... | collective-permute-start | bytes 2359304 | tf_op jit(solution)/shard_map/ppermute | solution.py:360
  88.3 2.2 %broadcast_select_fusion.1 = (bf16[768,512]{1,0:T(8,128)(2,1)}, bf16[768,512]{1,0:T(8,128)(2,1)S(1)}) fusion(bf16[768,512]{1,0:T(8,128)(2,1)S(1)} %collective-permute-done.9, bf16[768,512]{1,0:T(8,128)(2,1)} %collective-permute-done, pred[]{:T(512)S(6)} %eq.43), kind=kLoop, calls=%fused_computation.10 | loop fusion | flops 786432 | bytes 3145729 | tf_op jit(solution)/shard_map/jit(_where)/select_n | solution.py:370
  90.5 2.3 %broadcast_select_fusion.3 = (bf16[512,768]{1,0:T(8,128)(2,1)S(1)}, bf16[512,768]{1,0:T(8,128)(2,1)}) fusion(bf16[512,768]{1,0:T(8,128)(2,1)S(1)} %collective-permute-done.10, bf16[512,768]{1,0:T(8,128)(2,1)} %collective-permute-done.1, pred[]{:T(512)S(6)} %eq.43), kind=kLoop, calls=%fused_computation.12 | loop fusion | flops 786432 | bytes 3145729 | tf_op jit(solution)/shard_map/jit(_where)/select_n | solution.py:372
  92.8 0.6 collective-permute-done.12
  93.4 0.2 bitcast_select_fusion.2
  93.6 6.4 %collective-permute-done.13 = bf16[768,512]{1,0:T(8,128)(2,1)S(1)} collective-permute-done((bf16[768,512]{1,0:T(8,128)(2,1)}, bf16[768,512]{1,0:T(8,128)(2,1)S(1)}, u32[]{:S(2)}, u32[]{:S(2)}) %collective-permute-start.13) | collective-permute-done | bytes 786464 | tf_op jit(solution)/shard_map/ppermute | solution.py:360
  100.0 2.2 %bitcast_select_fusion = (bf16[768,512]{1,0:T(8,128)(2,1)}, bf16[768,512]{1,0:T(8,128)(2,1)S(1)}) fusion(bf16[768,512]{1,0:T(8,128)(2,1)S(1)} %collective-permute-done.13, bf16[768,512]{1,0:T(8,128)(2,1)} %collective-permute-done.2, bf16[2,768,512]{2,1,0:T(8,128)(2,1)S(1)} %copy-done.11, pred[]{:T(512)} %eq.38, pred[]{:T(512)S(6)} %eq.43), kind=kLoop, calls=%fused_computation.4 | loop fusion | flops 1572864 | bytes 4718594 | tf_op jit(solution)/shard_map/jit(_where)/select_n | solution.py:374
  102.2 8.0 %collective-permute-done.3.ca_ref = bf16[1024,512]{1,0:T(8,128)(2,1)S(1)} collective-permute-done((bf16[1024,512]{1,0:T(8,128)(2,1)S(1)}, bf16[1024,512]{1,0:T(8,128)(2,1)S(1)}, u32[]{:S(2)}, u32[]{:S(2)}) %collective-permute-start.3) | collective-permute-done | bytes 1048608 | tf_op jit(solution)/shard_map/ppermute | solution.py:322
  110.2 2.2 %collective-permute-start.16 = (f32[3,768]{1,0:T(4,128)S(1)}, f32[3,768]{1,0:T(4,128)S(1)}, u32[]{:S(2)}, u32[]{:S(2)}) collective-permute-start(f32[3,768]{1,0:T(4,128)S(1)} %pad_maximum_fusion), channel_id=1, source_target_pairs={{0,1},{1,0},{2,5},{3,4},{4,3},{5,2},{6,7},{7,6},{8,9},{9,8},{10,13... | collective-permute-start | bytes 27656 | tf_op jit(solution)/shard_map/ppermute | solution.py:366
  112.4 1.9 %collective-permute-start.17 = (f32[3,768]{1,0:T(4,128)S(1)}, f32[3,768]{1,0:T(4,128)S(1)}, u32[]{:S(2)}, u32[]{:S(2)}) collective-permute-start(f32[3,768]{1,0:T(4,128)S(1)} %pad_maximum_fusion), channel_id=1, source_target_pairs={{2,4},{3,5},{4,2},{5,3},{10,12},{11,13},{12,10},{13,11},{18,20},{1... | collective-permute-start | bytes 27656 | tf_op jit(solution)/shard_map/ppermute | solution.py:367
  114.4 1.0 collective-permute-start.14
  115.5 0.1 broadcast_select_fusion.cb_ref
  115.6 1.3 context_part.1
  116.9 1.4 copy-done.5
  118.2 0.8 copy-done.7
  119.2 2.0 %collective-permute-start.15 = (f32[2,2]{0,1:T(2,128)S(1)}, f32[2,2]{0,1:T(2,128)S(1)}, u32[]{:S(2)}, u32[]{:S(2)}) collective-permute-start(f32[2,2]{0,1:T(2,128)S(1)} %slice.63), channel_id=1, source_target_pairs={{0,64},{4,68},{8,72},{12,76},{16,80},{20,84},{24,88},{28,92},{32,9... | collective-permute-start | bytes 56 | tf_op jit(solution)/shard_map/ppermute | solution.py:339
  121.2 1.6 copy-done.6
  122.8 1.0 copy-done.8
  123.8 6.8 %first_layer.1 = (bf16[1024,512]{1,0:T(8,128)(2,1)S(1)}, bf16[1024,512]{1,0:T(8,128)(2,1)S(1)}, f32[16,1024]{1,0:T(8,128)S(1)}) custom-call(bf16[16,512]{1,0:T(8,128)(2,1)S(1)} %broadcast_in_dim.43.u_ref, f32[1024,512]{1,0:T(8,128)S(1)} %copy-done.6, bf16[512,512]{1,0:T(8,128)(2,1)S(1)} %copy-done.8, bf16[2048,512]{1,0:T(8,128)(2,1)} %bitcast.13.recv_hbm), custom_call_target="tpu_custom_call" | custom-call | flops 15728640000 | bytes 8388608 | tf_op jit(solution)/shard_map/first_layer/pallas_call | solution.py:78
  130.7 0.1 collective-permute-start.18
  130.9 3.0 %collective-permute-start.19 = (f32[1,2]{0,1:T(2,128)S(1)}, f32[1,2]{0,1:T(2,128)S(1)}, u32[]{:S(2)}, u32[]{:S(2)}) collective-permute-start(f32[1,2]{0,1:T(2,128)S(1)} %slice.65), channel_id=1, source_target_pairs={{0,192},{4,196},{8,200},{12,204},{16,208},{20,212},{24,216},{28,22... | collective-permute-start | bytes 32 | tf_op jit(solution)/shard_map/ppermute | solution.py:339
  134.0 1.5 collective-permute-done.19
  135.5 1.3 collective-permute-start.20
  136.8 2.9 %collective-permute-start.21 = (f32[1,2]{0,1:T(2,128)S(1)}, f32[1,2]{0,1:T(2,128)S(1)}, u32[]{:S(2)}, u32[]{:S(2)}) collective-permute-start(f32[1,2]{0,1:T(2,128)S(1)} %slice_maximum_fusion), channel_id=1, source_target_pairs={{0,3},{1,2},{2,1},{3,0},{4,7},{5,6},{6,5},{7,4},{8,11},{9,10},{10,... | collective-permute-start | bytes 32 | tf_op jit(solution)/shard_map/ppermute | solution.py:344
  139.6 0.1 collective-permute-start.22
  139.8 3.7 %second_layer.1 = (bf16[1024,768]{1,0:T(8,128)(2,1)S(1)}, bf16[1024,768]{1,0:T(8,128)(2,1)S(1)}, bf16[1024,512]{1,0:T(8,128)(2,1)S(1)}) custom-call(bf16[1024,512]{1,0:T(8,128)(2,1)S(1)} %get-tuple-element.62.mine_ref, bf16[1024,512]{1,0:T(8,128)(2,1)S(1)} %collective-permute-done.18.other_ref, bf16[1024,512]{1,0:T(8,128)(2,1)S(1)} %get-tuple-element.65.pay_ref, ...), custom_call_target="tpu_custom_call" | custom-call | flops 15728640000 | bytes 12582912 | tf_op jit(solution)/shard_map/second_layer/pallas_call | solution.py:78
  143.6 2.9 %collective-permute-start.23 = (bf16[1024,512]{1,0:T(8,128)(2,1)S(1)}, bf16[1024,512]{1,0:T(8,128)(2,1)S(1)}, u32[]{:S(2)}, u32[]{:S(2)}) collective-permute-start(bf16[1024,512]{1,0:T(8,128)(2,1)S(1)} %get-tuple-element.72.mine_ref), channel_id=1, source_target_pairs={{0,4},{1,5},{2,6},{3,7},{4,0},{5,1},{6,2},{7,3},{8,12},{9,13},{10,... | collective-permute-start | bytes 3145736 | tf_op jit(solution)/shard_map/ppermute | solution.py:413
  147.1 0.5 fusion.4
  148.2 0.6 collective-permute-done.23.other_ref
  148.8 3.1 %last_layer.1 = f32[16,1024]{1,0:T(8,128)S(1)} custom-call(f32[1]{0:T(128)} %copy.14.coefficient, bf16[1024,512]{1,0:T(8,128)(2,1)S(1)} %get-tuple-element.72.mine_ref, bf16[1024,512]{1,0:T(8,128)(2,1)S(1)} %collective-permute-done.23.other_ref, bf16[1024,512]{1,0:T(8,128)(2,1)S(1)} %get-tuple-element.65.pay_ref, ...), custom_call_target="tpu_custom_call" | custom-call | flops 1879048192 | bytes 10485760 | tf_op jit(solution)/shard_map/last_layer/pallas_call | solution.py:78
  151.9 0.4 collective-permute-start.24
  152.3 0.8 collective-permute-done.24
  153.1 4.2 %collective-permute-start.26 = (f32[1,1024]{1,0:T(1,128)S(1)}, f32[1,1024]{1,0:T(1,128)S(1)}, u32[]{:S(2)}, u32[]{:S(2)}) collective-permute-start(f32[1,1024]{1,0:T(1,128)S(1)} %fusion.7), channel_id=1, source_target_pairs={{2,4},{3,5},{4,2},{5,3},{10,12},{11,13},{12,10},{13,11},{18,20},{1... | collective-permute-start | bytes 12296 | tf_op jit(solution)/shard_map/ppermute | solution.py:422
  157.3 0.4 collective-permute-start.25
  157.7 1.9 %collective-permute-done.26 = f32[1,1024]{1,0:T(1,128)S(1)} collective-permute-done((f32[1,1024]{1,0:T(1,128)S(1)}, f32[1,1024]{1,0:T(1,128)S(1)}, u32[]{:S(2)}, u32[]{:S(2)}) %collective-permute-start.26) | collective-permute-done | bytes 4128 | tf_op jit(solution)/shard_map/ppermute | solution.py:422
  159.6 2.1 %collective-permute-done.25 = f32[1,1024]{1,0:T(1,128)S(1)} collective-permute-done((f32[1,1024]{1,0:T(1,128)S(1)}, f32[1,1024]{1,0:T(1,128)S(1)}, u32[]{:S(2)}, u32[]{:S(2)}) %collective-permute-start.25) | collective-permute-done | bytes 4128 | tf_op jit(solution)/shard_map/ppermute | solution.py:421
  161.7 0.6 maximum_select_fusion
  (72 shorter events, 0.7 us)
Async XLA Ops:
  0.0 5.3 %copy-start.9 = (bf16[2,512,768]{2,1,0:T(8,128)(2,1)S(1)}, bf16[2,512,768]{2,1,0:T(8,128)(2,1)}, u32[]{:S(2)}) copy-start(bf16[2,512,768]{2,1,0:T(8,128)(2,1)} %param.19) | copy-start | bytes 4718596
  0.0 5.7 %copy-start.15 = (bf16[2,256]{1,0:T(2,128)(2,1)S(1)}, bf16[2,256]{1,0:T(2,128)(2,1)}, u32[]{:S(2)}) copy-start(bf16[2,256]{1,0:T(2,128)(2,1)} %param.12) | copy-start | bytes 3076
  0.0 18.1 %copy-start.16 = (bf16[768]{0:T(1024)(128)(2,1)S(1)}, bf16[768]{0:T(1024)(128)(2,1)}, u32[]{:S(2)}) copy-start(bf16[768]{0:T(1024)(128)(2,1)} %param.21) | copy-start | bytes 4612
  1.3 26.8 %collective-permute-start = (bf16[768,512]{1,0:T(8,128)(2,1)S(1)}, bf16[768,512]{1,0:T(8,128)(2,1)}, u32[]{:S(2)}, u32[]{:S(2)}) collective-permute-start(bf16[768,512]{1,0:T(8,128)(2,1)S(1)} %dynamic-slice_bitcast_fusion.3), channel_id=1, source_target_pairs={{0,1},{1,0},{2,5},{3,4},{4,3},{5,2},{6,7},{7,6},{8,9},{9,8},{10,13... | collective-permute-start | bytes 2359304 | tf_op jit(solution)/shard_map/ppermute | solution.py:304
  5.3 22.8 %collective-permute-start.1 = (bf16[512,768]{1,0:T(8,128)(2,1)S(1)}, bf16[512,768]{1,0:T(8,128)(2,1)}, u32[]{:S(2)}, u32[]{:S(2)}) collective-permute-start(bf16[512,768]{1,0:T(8,128)(2,1)S(1)} %dynamic-slice_bitcast_fusion.2), channel_id=1, source_target_pairs={{0,1},{1,0},{2,5},{3,4},{4,3},{5,2},{6,7},{7,6},{8,9},{9,8},{10,13... | collective-permute-start | bytes 2359304 | tf_op jit(solution)/shard_map/ppermute | solution.py:305
  6.3 21.8 %all-to-all-start = ((bf16[64,2,256]{2,1,0:T(2,128)(2,1)}), bf16[64,2,256]{2,1,0:T(2,128)(2,1)S(1)}, u32[]{:S(2)}, u32[]{:S(2)}) async-start(bf16[64,2,256]{2,1,0:T(2,128)(2,1)} %broadcast_in_dim.41), calls=%async_computation | async-start | bytes 131072 | tf_op jit(solution)/shard_map/all_to_all | solution.py:307
  18.9 9.3 %copy-start.13 = (bf16[2048,256]{1,0:T(8,128)(2,1)S(1)}, bf16[2048,256]{1,0:T(8,128)(2,1)}, u32[]{:S(2)}) copy-start(bf16[2048,256]{1,0:T(8,128)(2,1)} %emb_hbm.1) | copy-start | bytes 3145732
  29.0 28.5 %collective-permute-start.9 = (bf16[768,512]{1,0:T(8,128)(2,1)}, bf16[768,512]{1,0:T(8,128)(2,1)S(1)}, u32[]{:S(2)}, u32[]{:S(2)}) collective-permute-start(bf16[768,512]{1,0:T(8,128)(2,1)} %collective-permute-done), channel_id=1, source_target_pairs={{0,24},{1,25},{2,10},{3,11},{4,12},{5,13},{6,30},{7,31},{8,0},{9,1... | collective-permute-start | bytes 2359304 | tf_op jit(solution)/shard_map/ppermute | solution.py:359
  29.5 30.3 %copy-start.14 = (f32[2,768]{1,0:T(2,128)S(1)}, f32[2,768]{1,0:T(2,128)}, u32[]{:S(2)}) copy-start(f32[2,768]{1,0:T(2,128)} %param.20) | copy-start | bytes 18436
  29.5 43.6 %copy-start.12 = (bf16[2,1024,512]{2,1,0:T(8,128)(2,1)S(1)}, bf16[2,1024,512]{2,1,0:T(8,128)(2,1)}, u32[]{:S(2)}) copy-start(bf16[2,1024,512]{2,1,0:T(8,128)(2,1)} %param.17) | copy-start | bytes 6291460
  29.5 20.5 %collective-permute-start.5 = (f32[32,2]{0,1:T(2,128)S(1)}, f32[32,2]{0,1:T(2,128)S(1)}, u32[]{:S(2)}, u32[]{:S(2)}) collective-permute-start(f32[32,2]{0,1:T(2,128)S(1)} %slice.52), channel_id=1, source_target_pairs={{0,4},{4,0},{8,12},{12,8},{16,20},{20,16},{24,28},{28,24},{32,36},... | collective-permute-start | bytes 776 | tf_op jit(solution)/shard_map/ppermute | solution.py:339
  31.4 41.7 %collective-permute-start.2 = (bf16[768,512]{1,0:T(8,128)(2,1)}, bf16[768,512]{1,0:T(8,128)(2,1)}, u32[]{:S(2)}, u32[]{:S(2)}) collective-permute-start(bf16[768,512]{1,0:T(8,128)(2,1)} %collective-permute-done), channel_id=1, source_target_pairs={{0,3},{1,2},{6,5},{7,4},{8,11},{9,10},{14,13},{15,12},{16,19},{17,... | collective-permute-start | bytes 2359304 | tf_op jit(solution)/shard_map/ppermute | solution.py:317
  32.7 86.4 %all-to-all-start.1 = ((bf16[256,8,512]{2,1,0:T(8,128)(2,1)}), bf16[256,8,512]{2,1,0:T(8,128)(2,1)}, u32[]{:S(2)}, u32[]{:S(2)}) async-start(bf16[256,8,512]{2,1,0:T(8,128)(2,1)} %bitcast.32), calls=%async_computation.1 | async-start | bytes 4194304 | tf_op jit(solution)/shard_map/all_to_all | solution.py:314
  46.7 23.2 %collective-permute-start.11 = (bf16[512,768]{1,0:T(8,128)(2,1)}, bf16[512,768]{1,0:T(8,128)(2,1)S(1)}, u32[]{:S(2)}, u32[]{:S(2)}) collective-permute-start(bf16[512,768]{1,0:T(8,128)(2,1)} %collective-permute-done.1), channel_id=1, source_target_pairs={{2,3},{3,2},{4,5},{5,4},{10,11},{11,10},{12,13},{13,12},{18,19},{1... | collective-permute-start | bytes 2359304 | tf_op jit(solution)/shard_map/ppermute | solution.py:318
  50.1 3.0 %collective-permute-start.6 = (f32[8,2]{0,1:T(2,128)S(1)}, f32[8,2]{0,1:T(2,128)S(1)}, u32[]{:S(2)}, u32[]{:S(2)}) collective-permute-start(f32[8,2]{0,1:T(2,128)S(1)} %get-tuple-element.89), channel_id=1, source_target_pairs={{0,8},{4,12},{8,0},{12,4},{16,24},{20,28},{24,16},{28,20},{32,40},... | collective-permute-start | bytes 200 | tf_op jit(solution)/shard_map/ppermute | solution.py:352
  51.3 4.3 %collective-permute-start.7 = (f32[8,2]{0,1:T(2,128)S(1)}, f32[8,2]{0,1:T(2,128)S(1)}, u32[]{:S(2)}, u32[]{:S(2)}) collective-permute-start(f32[8,2]{0,1:T(2,128)S(1)} %get-tuple-element.91), channel_id=1, source_target_pairs={{0,24},{4,28},{8,16},{12,20},{16,8},{20,12},{24,0},{28,4},{32,56},... | collective-permute-start | bytes 200 | tf_op jit(solution)/shard_map/ppermute | solution.py:352
  53.1 4.3 %collective-permute-start.8 = (f32[8,2]{0,1:T(2,128)S(1)}, f32[8,2]{0,1:T(2,128)S(1)}, u32[]{:S(2)}, u32[]{:S(2)}) collective-permute-start(f32[8,2]{0,1:T(2,128)S(1)} %get-tuple-element.90), channel_id=1, source_target_pairs={{0,16},{4,20},{8,24},{12,28},{16,0},{20,4},{24,8},{28,12},{32,48},... | collective-permute-start | bytes 200 | tf_op jit(solution)/shard_map/ppermute | solution.py:352
  57.4 33.1 %collective-permute-start.10 = (bf16[512,768]{1,0:T(8,128)(2,1)}, bf16[512,768]{1,0:T(8,128)(2,1)S(1)}, u32[]{:S(2)}, u32[]{:S(2)}) collective-permute-start(bf16[512,768]{1,0:T(8,128)(2,1)} %collective-permute-done.1), channel_id=1, source_target_pairs={{0,8},{1,9},{2,26},{3,27},{4,28},{5,29},{6,14},{7,15},{8,16},{9,17... | collective-permute-start | bytes 2359304 | tf_op jit(solution)/shard_map/ppermute | solution.py:362
  69.9 23.5 %collective-permute-start.12 = (bf16[512,768]{1,0:T(8,128)(2,1)S(1)}, bf16[512,768]{1,0:T(8,128)(2,1)S(1)}, u32[]{:S(2)}, u32[]{:S(2)}) collective-permute-start(bf16[512,768]{1,0:T(8,128)(2,1)S(1)} %collective-permute-done.11), channel_id=1, source_target_pairs={{2,10},{3,11},{4,12},{5,13},{10,18},{11,19},{12,20},{13,21},{18,26... | collective-permute-start | bytes 2359304 | tf_op jit(solution)/shard_map/ppermute | solution.py:363
  73.3 37.0 %collective-permute-start.3 = (bf16[1024,512]{1,0:T(8,128)(2,1)S(1)}, bf16[1024,512]{1,0:T(8,128)(2,1)S(1)}, u32[]{:S(2)}, u32[]{:S(2)}) collective-permute-start(bf16[1024,512]{1,0:T(8,128)(2,1)S(1)} %get-tuple-element.84), channel_id=1, source_target_pairs={{0,1},{1,0},{2,5},{3,4},{4,3},{5,2},{6,7},{7,6},{8,9},{9,8},{10,13... | collective-permute-start | bytes 3145736 | tf_op jit(solution)/shard_map/ppermute | solution.py:322
  80.3 29.9 %collective-permute-start.4 = (bf16[1024,512]{1,0:T(8,128)(2,1)S(1)}, bf16[1024,512]{1,0:T(8,128)(2,1)S(1)}, u32[]{:S(2)}, u32[]{:S(2)}) collective-permute-start(bf16[1024,512]{1,0:T(8,128)(2,1)S(1)} %get-tuple-element.83), channel_id=1, source_target_pairs={{2,4},{3,5},{4,2},{5,3},{10,12},{11,13},{12,10},{13,11},{18,20},{1... | collective-permute-start | bytes 3145736 | tf_op jit(solution)/shard_map/ppermute | solution.py:323
  82.8 17.2 %collective-permute-start.13 = (bf16[768,512]{1,0:T(8,128)(2,1)}, bf16[768,512]{1,0:T(8,128)(2,1)S(1)}, u32[]{:S(2)}, u32[]{:S(2)}) collective-permute-start(bf16[768,512]{1,0:T(8,128)(2,1)} %collective-permute-done.2), channel_id=1, source_target_pairs={{2,26},{3,27},{4,28},{5,29},{10,2},{11,3},{12,4},{13,5},{18,10},{1... | collective-permute-start | bytes 2359304 | tf_op jit(solution)/shard_map/ppermute | solution.py:360
  90.5 2.9 %copy-start.10 = (bf16[2,512,768]{2,1,0:T(8,128)(2,1)S(1)}, bf16[2,512,768]{2,1,0:T(8,128)(2,1)}, u32[]{:S(2)}) copy-start(bf16[2,512,768]{2,1,0:T(8,128)(2,1)} %param.19) | copy-start | bytes 4718596
  92.8 7.2 %copy-start.11 = (bf16[2,768,512]{2,1,0:T(8,128)(2,1)S(1)}, bf16[2,768,512]{2,1,0:T(8,128)(2,1)}, u32[]{:S(2)}) copy-start(bf16[2,768,512]{2,1,0:T(8,128)(2,1)} %param.18) | copy-start | bytes 4718596
  110.2 5.4 %copy-start = (bf16[1024,512]{1,0:T(8,128)(2,1)}, bf16[1024,512]{1,0:T(8,128)(2,1)S(1)}, u32[]{:S(2)}) copy-start(bf16[1024,512]{1,0:T(8,128)(2,1)S(1)} %collective-permute-done.3.ca_ref) | copy-start | bytes 3145732
  110.2 20.5 %collective-permute-start.16 = (f32[3,768]{1,0:T(4,128)S(1)}, f32[3,768]{1,0:T(4,128)S(1)}, u32[]{:S(2)}, u32[]{:S(2)}) collective-permute-start(f32[3,768]{1,0:T(4,128)S(1)} %pad_maximum_fusion), channel_id=1, source_target_pairs={{0,1},{1,0},{2,5},{3,4},{4,3},{5,2},{6,7},{7,6},{8,9},{9,8},{10,13... | collective-permute-start | bytes 27656 | tf_op jit(solution)/shard_map/ppermute | solution.py:366
  112.4 18.3 %collective-permute-start.17 = (f32[3,768]{1,0:T(4,128)S(1)}, f32[3,768]{1,0:T(4,128)S(1)}, u32[]{:S(2)}, u32[]{:S(2)}) collective-permute-start(f32[3,768]{1,0:T(4,128)S(1)} %pad_maximum_fusion), channel_id=1, source_target_pairs={{2,4},{3,5},{4,2},{5,3},{10,12},{11,13},{12,10},{13,11},{18,20},{1... | collective-permute-start | bytes 27656 | tf_op jit(solution)/shard_map/ppermute | solution.py:367
  114.4 4.7 %collective-permute-start.14 = (f32[4,2]{0,1:T(2,128)S(1)}, f32[4,2]{0,1:T(2,128)S(1)}, u32[]{:S(2)}, u32[]{:S(2)}) collective-permute-start(f32[4,2]{0,1:T(2,128)S(1)} %slice.61), channel_id=1, source_target_pairs={{0,32},{4,36},{8,40},{12,44},{16,48},{20,52},{24,56},{28,60},{32,0... | collective-permute-start | bytes 104 | tf_op jit(solution)/shard_map/ppermute | solution.py:339
  116.9 1.4 copy-start.5
  118.2 0.8 copy-start.7
  119.2 11.5 %collective-permute-start.15 = (f32[2,2]{0,1:T(2,128)S(1)}, f32[2,2]{0,1:T(2,128)S(1)}, u32[]{:S(2)}, u32[]{:S(2)}) collective-permute-start(f32[2,2]{0,1:T(2,128)S(1)} %slice.63), channel_id=1, source_target_pairs={{0,64},{4,68},{8,72},{12,76},{16,80},{20,84},{24,88},{28,92},{32,9... | collective-permute-start | bytes 56 | tf_op jit(solution)/shard_map/ppermute | solution.py:339
  121.2 1.6 copy-start.6
  122.8 1.0 copy-start.8
  123.8 15.9 %copy-start.1 = (bf16[1024,512]{1,0:T(8,128)(2,1)S(1)}, bf16[1024,512]{1,0:T(8,128)(2,1)}, u32[]{:S(2)}) copy-start(bf16[1024,512]{1,0:T(8,128)(2,1)} %copy-done) | copy-start | bytes 3145732
  123.8 15.9 %copy-start.2 = (bf16[768,512]{1,0:T(8,128)(2,1)S(1)}, bf16[768,512]{1,0:T(8,128)(2,1)}, u32[]{:S(2)}) copy-start(bf16[768,512]{1,0:T(8,128)(2,1)} %get-tuple-element.79.vb_ref) | copy-start | bytes 2359300
  123.8 15.9 %copy-start.3 = (bf16[768,512]{1,0:T(8,128)(2,1)S(1)}, bf16[768,512]{1,0:T(8,128)(2,1)}, u32[]{:S(2)}) copy-start(bf16[768,512]{1,0:T(8,128)(2,1)} %get-tuple-element.85.va_ref) | copy-start | bytes 2359300
  123.8 15.9 %copy-start.4 = (bf16[512,768]{1,0:T(8,128)(2,1)S(1)}, bf16[512,768]{1,0:T(8,128)(2,1)}, u32[]{:S(2)}) copy-start(bf16[512,768]{1,0:T(8,128)(2,1)} %get-tuple-element.68.ua_ref) | copy-start | bytes 2359300
  130.7 4.7 %collective-permute-start.18 = (bf16[1024,512]{1,0:T(8,128)(2,1)S(1)}, bf16[1024,512]{1,0:T(8,128)(2,1)S(1)}, u32[]{:S(2)}, u32[]{:S(2)}) collective-permute-start(bf16[1024,512]{1,0:T(8,128)(2,1)S(1)} %get-tuple-element.62.mine_ref), channel_id=1, source_target_pairs={{0,4},{1,5},{2,6},{3,7},{4,0},{5,1},{6,2},{7,3},{8,12},{9,13},{10,... | collective-permute-start | bytes 3145736 | tf_op jit(solution)/shard_map/ppermute | solution.py:405
  130.9 4.6 %collective-permute-start.19 = (f32[1,2]{0,1:T(2,128)S(1)}, f32[1,2]{0,1:T(2,128)S(1)}, u32[]{:S(2)}, u32[]{:S(2)}) collective-permute-start(f32[1,2]{0,1:T(2,128)S(1)} %slice.65), channel_id=1, source_target_pairs={{0,192},{4,196},{8,200},{12,204},{16,208},{20,212},{24,216},{28,22... | collective-permute-start | bytes 32 | tf_op jit(solution)/shard_map/ppermute | solution.py:339
  135.5 8.0 %collective-permute-start.20 = (f32[1,2]{0,1:T(2,128)S(1)}, f32[1,2]{0,1:T(2,128)S(1)}, u32[]{:S(2)}, u32[]{:S(2)}) collective-permute-start(f32[1,2]{0,1:T(2,128)S(1)} %slice_maximum_fusion), channel_id=1, source_target_pairs={{0,1},{1,0},{2,3},{3,2},{4,5},{5,4},{6,7},{7,6},{8,9},{9,8},{10,11... | collective-permute-start | bytes 32 | tf_op jit(solution)/shard_map/ppermute | solution.py:344
  136.8 6.8 %collective-permute-start.21 = (f32[1,2]{0,1:T(2,128)S(1)}, f32[1,2]{0,1:T(2,128)S(1)}, u32[]{:S(2)}, u32[]{:S(2)}) collective-permute-start(f32[1,2]{0,1:T(2,128)S(1)} %slice_maximum_fusion), channel_id=1, source_target_pairs={{0,3},{1,2},{2,1},{3,0},{4,7},{5,6},{6,5},{7,4},{8,11},{9,10},{10,... | collective-permute-start | bytes 32 | tf_op jit(solution)/shard_map/ppermute | solution.py:344
  139.6 3.9 %collective-permute-start.22 = (f32[1,2]{0,1:T(2,128)S(1)}, f32[1,2]{0,1:T(2,128)S(1)}, u32[]{:S(2)}, u32[]{:S(2)}) collective-permute-start(f32[1,2]{0,1:T(2,128)S(1)} %slice_maximum_fusion), channel_id=1, source_target_pairs={{0,2},{1,3},{2,0},{3,1},{4,6},{5,7},{6,4},{7,5},{8,10},{9,11},{10,... | collective-permute-start | bytes 32 | tf_op jit(solution)/shard_map/ppermute | solution.py:344
  143.6 5.2 %collective-permute-start.23 = (bf16[1024,512]{1,0:T(8,128)(2,1)S(1)}, bf16[1024,512]{1,0:T(8,128)(2,1)S(1)}, u32[]{:S(2)}, u32[]{:S(2)}) collective-permute-start(bf16[1024,512]{1,0:T(8,128)(2,1)S(1)} %get-tuple-element.72.mine_ref), channel_id=1, source_target_pairs={{0,4},{1,5},{2,6},{3,7},{4,0},{5,1},{6,2},{7,3},{8,12},{9,13},{10,... | collective-permute-start | bytes 3145736 | tf_op jit(solution)/shard_map/ppermute | solution.py:413
  151.9 1.3 collective-permute-start.24
  153.1 6.4 %collective-permute-start.26 = (f32[1,1024]{1,0:T(1,128)S(1)}, f32[1,1024]{1,0:T(1,128)S(1)}, u32[]{:S(2)}, u32[]{:S(2)}) collective-permute-start(f32[1,1024]{1,0:T(1,128)S(1)} %fusion.7), channel_id=1, source_target_pairs={{2,4},{3,5},{4,2},{5,3},{10,12},{11,13},{12,10},{13,11},{18,20},{1... | collective-permute-start | bytes 12296 | tf_op jit(solution)/shard_map/ppermute | solution.py:422
  157.3 4.3 %collective-permute-start.25 = (f32[1,1024]{1,0:T(1,128)S(1)}, f32[1,1024]{1,0:T(1,128)S(1)}, u32[]{:S(2)}, u32[]{:S(2)}) collective-permute-start(f32[1,1024]{1,0:T(1,128)S(1)} %fusion.7), channel_id=1, source_target_pairs={{0,1},{1,0},{2,5},{3,4},{4,3},{5,2},{6,7},{7,6},{8,9},{9,8},{10,13... | collective-permute-start | bytes 12296 | tf_op jit(solution)/shard_map/ppermute | solution.py:421
